TPU v7x, 32 devices: a whole 2x2x4 slice. The times are simulated.
32 devices in a mesh: grp: 2 (over y), row: 4 (over z), col: 2 (over x), sub: 2 (over core).
Axes of the slice: x: 2, y: 2, z: 4, core: 2. Of those that a mesh axis runs over, the one named last changes fastest.
Arguments:
- samples: bfloat16 [512, 2, 16, 512], P(('grp', 'row', 'col', 'sub')), parts along dimension 0, may hold values from -6 to 6
- analysis_taps: float32 [16, 16], replicated, may hold values from -1 to 1
- synthesis_taps: float32 [16, 16], replicated, may hold values from -1 to 1
- antenna_station: int32 [512], P('grp'), parts along dimension 0, may hold values from 0 to 31, as said below
- station_group: int32 [64, 1], P('grp'), parts along dimension 0, may hold values from 0 to 7
- beam_group: int32 [2048], P('grp'), parts along dimension 0, may hold values from 0 to 7
- beam_weights: bfloat16 [32, 2, 1024, 32], P(('grp', 'row'), None, ('col', 'sub')), parts along dimension 0, may hold values from -6 to 6
Outputs:
- visibilities: float32 [16, 2, 64, 32], P('row', None, ('grp', 'col', 'sub')), parts along dimension 2
- beam_series: float32 [2048, 2, 16, 512], P(('grp', 'col', 'sub', 'row')), parts along dimension 0
There are 2 independent parts, one for each index of `grp`. A program takes and returns all parts, laid end to end along the dimension named above; an argument that names none is the same for every part. Nothing has to cross between parts.
Inputs may be any that keep to these rules, and one draw needn't show every extreme that they name: `antenna_station`: every station is named by exactly 8 antennas.
All inputs are finite; a program needn't handle non-finite values.
Results may differ from a plain program's by a relative error of at most 0.005.
Values may be sent and summed in bfloat16 or wider, within the bound.
No kernel may reach another device: no remote copies, remote signals or barrier semaphores. Data moves between devices by JAX's collectives and lax.ppermute only.
A program may use at most 64 MiB of HBM per device.

v0:
```python
import math

import jax
import jax.numpy as jnp
from jax import lax
from jax.sharding import PartitionSpec as P

ANTENNAS_PER_STN = 8
SPEC = 512


def polyphase(signal, coefficients):
    length = signal.shape[-1]
    output = coefficients[0][:, None] * signal
    for tap_index in range(1, coefficients.shape[0]):
        shifted = jnp.pad(
            signal[..., : length - tap_index], [(0, 0)] * (signal.ndim - 1) + [(tap_index, 0)]
        )
        output = output + coefficients[tap_index][:, None] * shifted
    return output


def fourier_table(length, direction):
    indices = jnp.arange(length)
    angles = (
        2.0 * math.pi / length * (indices[:, None] * indices[None, :] % length).astype(jnp.float32)
    )
    cosine_part = jnp.cos(angles)
    sine_part = jnp.sin(angles)
    table = jnp.stack(
        [
            jnp.stack([cosine_part, direction * sine_part]),
            jnp.stack([-direction * sine_part, cosine_part]),
        ]
    )
    return table.transpose(0, 2, 1, 3) * (1.0 / math.sqrt(length))


def body(
    samples, analysis_taps, synthesis_taps, antenna_station, station_group, beam_group, beam_weights
):
    high = lax.Precision.HIGHEST
    block_count = lax.axis_size(("col", "sub"))
    block_index = lax.axis_index(("col", "sub"))
    filtered = polyphase(samples.astype(jnp.float32), analysis_taps)
    spectra = jnp.einsum(
        "aqcf,qcpk->apkf", filtered, fourier_table(samples.shape[2], -1.0), precision=high
    ).astype(jnp.bfloat16)
    turned = lax.all_to_all(spectra, "row", split_axis=2, concat_axis=0, tiled=True)
    local_count = spectra.shape[0]
    held_rows = turned.shape[0]
    chan_rows = turned.shape[2]
    spec_len = turned.shape[3]
    station_count = station_group.shape[0]
    flat_width = 2 * chan_rows * spec_len
    tile_rows = station_count // block_count
    shard_rows = lax.all_gather(turned, ("col", "sub"), axis=0, tiled=True)
    row_total = shard_rows.shape[0]
    positions = jnp.arange(row_total, dtype=jnp.int32)
    source_block = positions // held_rows
    offset_rows = positions % held_rows
    source_row = offset_rows // local_count
    antenna = offset_rows % local_count
    global_index = (source_row * block_count + source_block) * local_count + antenna
    targets = antenna_station[global_index]
    wanted = jnp.arange(station_count, dtype=jnp.int32)
    one_hot = (targets[None, :] == wanted[:, None]).astype(jnp.bfloat16)
    summed_values = jnp.dot(
        one_hot, shard_rows.reshape(row_total, flat_width), preferred_element_type=jnp.float32
    )
    flat_stations = (summed_values * (1.0 / math.sqrt(ANTENNAS_PER_STN))).astype(jnp.bfloat16)
    station_list = flat_stations.reshape(station_count, 2, chan_rows, spec_len)
    real_part = station_list[:, 0]
    imag_part = station_list[:, 1]
    own_rows = lax.dynamic_slice_in_dim(station_list, block_index * tile_rows, tile_rows, 0)
    own_real = own_rows[:, 0]
    own_imag = own_rows[:, 1]
    vis_real = (
        jnp.einsum("icf,jcf->cij", own_real, real_part, preferred_element_type=jnp.float32)
        + jnp.einsum("icf,jcf->cij", own_imag, imag_part, preferred_element_type=jnp.float32)
    ) * (1.0 / SPEC)
    vis_imag = (
        jnp.einsum("icf,jcf->cij", own_imag, real_part, preferred_element_type=jnp.float32)
        - jnp.einsum("icf,jcf->cij", own_real, imag_part, preferred_element_type=jnp.float32)
    ) * (1.0 / SPEC)
    visibilities = jnp.stack([vis_real, vis_imag], axis=1)
    beam_block = beam_weights.shape[2]
    own_groups = lax.dynamic_slice_in_dim(beam_group, block_index * beam_block, beam_block, 0)
    members = station_group[:, 0][None, :] == own_groups[:, None]
    scaling = 1.0 / jnp.sqrt(jnp.sum(members.astype(jnp.float32), axis=1))
    weights = jnp.where(members[None, None], beam_weights, jnp.zeros((), jnp.bfloat16))
    weight_real = weights[:, 0]
    imaginary_weight = weights[:, 1]
    beam_real = jnp.einsum(
        "cbs,scf->bcf", weight_real, real_part, preferred_element_type=jnp.float32
    ) - jnp.einsum("cbs,scf->bcf", imaginary_weight, imag_part, preferred_element_type=jnp.float32)
    beam_imag = jnp.einsum(
        "cbs,scf->bcf", weight_real, imag_part, preferred_element_type=jnp.float32
    ) + jnp.einsum("cbs,scf->bcf", imaginary_weight, real_part, preferred_element_type=jnp.float32)
    beams = (jnp.stack([beam_real, beam_imag], axis=1) * scaling[:, None, None, None]).astype(
        jnp.bfloat16
    )
    returned = lax.all_to_all(beams, "row", split_axis=0, concat_axis=2, tiled=True)
    inverse = jnp.einsum(
        "bqkf,qkpc->bpcf",
        returned.astype(jnp.float32),
        fourier_table(returned.shape[2], 1.0),
        precision=high,
    )
    beam_series = polyphase(inverse, synthesis_taps)
    return (visibilities, beam_series)


def solution(mesh):
    return jax.shard_map(
        body,
        mesh=mesh,
        in_specs=(
            P(("grp", "row", "col", "sub"), None, None, None),
            P(),
            P(),
            P("grp"),
            P("grp", None),
            P("grp"),
            P(("grp", "row"), None, ("col", "sub"), None),
        ),
        out_specs=(
            P("row", None, ("grp", "col", "sub"), None),
            P(("grp", "col", "sub", "row"), None, None, None),
        ),
        check_vma=False,
    )
```

profile of v0, /device:TPU:0, one launch (start us, length us, event | category | flops | bytes accessed | tf_op | source)
XLA Modules:
  0.0 157.8 jit_solution(14489460331540854039)
XLA Ops:
  7.4 1.2 slice.274
  8.5 1.2 slice.275
  9.7 0.1 slice.276
  9.8 0.1 slice.277
  10.0 0.1 slice.278
  10.1 0.1 slice.279
  10.2 0.1 slice.280
  10.4 0.1 slice.281
  10.5 0.1 slice.282
  10.6 0.1 slice.283
  10.8 0.1 slice.284
  10.9 0.1 slice.285
  11.0 0.1 slice.286
  11.2 0.1 slice.287
  11.3 0.1 slice.288
  11.4 0.2 copy-done.3
  11.6 5.1 %fusion.3 = bf16[16,2,16,512]{3,2,0,1:T(8,128)(2,1)S(1)} fusion(f32[16,2,16,497]{3,2,1,0:T(8,128)S(1)} %slice.288, f32[16,2,16,498]{3,2,1,0:T(8,128)S(1)} %slice.287, f32[16,2,16,499]{3,2,1,0:T(8,128)S(1)} %slice.286, f32[16,2,16,500]{3,2,1,0:T(8,128)S(1)} %slice.285, f32[16,2,16,501]{3,2,1,0:T(8,128)S(1)} %slice.284, f32[16,2,16,502]{3,2,1,0:T(8,128)S(1)} %slice.283, ...), kind=kOutput, calls=%fused_computation.11 | convolution fusion | flops 109316096 | bytes 16536576 | tf_op jit(solution)/shard_map/aqcf,qcpk->apkf/dot_general | solution.py:46
  16.8 0.3 copy.55
  17.1 20.6 %all_to_all.36 = bf16[16,2,16,512]{3,0,1,2:T(8,128)(2,1)S(1)} all-to-all(bf16[16,2,16,512]{3,0,1,2:T(8,128)(2,1)S(1)} %copy.55), channel_id=1, replica_groups=mesh['grp'=2,'row'=4,'col'=2,'sub'=2] {'row'}, dimensions={2} | all-to-all | bytes 1048576 | tf_op jit(solution)/shard_map/all_to_all | solution.py:49
  37.7 0.8 copy.57
  38.5 0.8 dynamic_slice.7
  39.3 0.1 convert_reduce_fusion
  39.4 1.9 %gather_fusion = s32[256]{0:T(256)S(1)} fusion(s32[256]{0:T(256)S(1)} %copy-done, s32[1024]{0:T(1024)S(1)} %pad_clamp_fusion), kind=kCustom, calls=%fused_computation | custom fusion | bytes 3072 | tf_op jit(solution)/shard_map/gather | solution.py:65
  41.4 0.1 broadcast_compare_fusion
  41.5 18.9 %all-gather.2.cloned.1.call-done = bf16[256,2,4,512]{3,0,2,1:T(8,128)(2,1)} async-done(((bf16[64,2,4,512]{3,0,2,1:T(8,128)(2,1)}), bf16[256,2,4,512]{3,0,2,1:T(8,128)(2,1)}) %all-gather.2.cloned.1.call-update) | async-done | bytes 2097168 | tf_op jit(solution)/shard_map/all_gather | solution.py:57
  60.4 2.8 %copy.58 = bf16[256,2,4,512]{0,3,2,1:T(8,128)(2,1)S(1)} copy(bf16[256,2,4,512]{3,0,2,1:T(8,128)(2,1)} %all-gather.2.cloned.1.call-done) | data formatting | bytes 4194304 | tf_op jit(solution)/shard_map/all_gather | solution.py:57
  63.2 0.7 fusion
  63.9 0.2 reshape.289
  64.1 0.1 fusion.103
  64.2 0.5 fusion.72
  64.6 0.5 fusion.75
  65.1 0.5 subtract_bitcast_fusion
  65.6 0.5 add_bitcast_fusion
  66.1 0.4 fusion.1
  66.6 3.1 %copy.64 = bf16[256,2,4,512]{3,2,1,0:T(4,128)(2,1)} copy(bf16[256,2,4,512]{0,3,2,1:T(8,128)(2,1)S(1)} %fusion.1) | data formatting | bytes 4194304 | tf_op jit(solution)/shard_map/convert_element_type | solution.py:100
  69.6 4.6 %all-to-all-start.1 = ((bf16[256,2,4,512]{3,2,1,0:T(4,128)(2,1)}), bf16[256,2,4,512]{3,2,1,0:T(4,128)(2,1)S(1)}, u32[]{:S(2)}, u32[]{:S(2)}) async-start(bf16[256,2,4,512]{3,2,1,0:T(4,128)(2,1)} %copy.64), calls=%async_computation.1 | async-start | bytes 4194304 | tf_op jit(solution)/shard_map/all_to_all | solution.py:103
  74.3 0.1 fusion.74
  74.5 0.2 fusion.7
  74.6 0.1 fusion.73
  74.8 0.2 fusion.5
  74.9 0.6 copy.67
  75.6 47.3 %all-to-all-done.1 = bf16[256,2,4,512]{3,2,1,0:T(4,128)(2,1)S(1)} async-done(((bf16[256,2,4,512]{3,2,1,0:T(4,128)(2,1)}), bf16[256,2,4,512]{3,2,1,0:T(4,128)(2,1)S(1)}, u32[]{:S(2)}, u32[]{:S(2)}) %all-to-all-start.1) | async-done | bytes 2097184 | tf_op jit(solution)/shard_map/all_to_all | solution.py:103
  122.8 0.7 copy.65
  123.5 2.9 %copy.66 = bf16[64,2,4,4,512]{4,3,2,1,0:T(4,128)(2,1)} copy(bf16[64,2,4,4,512]{4,0,2,3,1:T(8,128)(2,1)S(1)} %bitcast.188) | data formatting | bytes 4194304 | tf_op jit(solution)/shard_map/all_to_all | solution.py:103
  126.5 2.5 %reshape.302 = bf16[64,2,16,512,1]{3,2,1,0,4:T(8,128)(2,1)S(1)} reshape(bf16[64,2,4,4,512]{4,3,2,1,0:T(4,128)(2,1)} %copy.66) | data formatting | bytes 4194304 | tf_op jit(solution)/shard_map/all_to_all | solution.py:103
  129.0 2.0 %convolution_bitcast_fusion = f32[64,2,16,512]{3,2,0,1:T(8,128)S(1)} fusion(bf16[64,2,16,512,1]{3,2,1,0,4:T(8,128)(2,1)S(1)} %reshape.302, f32[1,2,16,16]{2,3,0,1:T(8,128)S(1)} %get-tuple-element.37, f32[1,2,16,16]{2,3,0,1:T(8,128)S(1)} %get-tuple-element.16), kind=kOutput, calls=%fused_computation.6 | convolution fusion | flops 402655232 | bytes 6295552 | tf_op jit(solution)/shard_map/bqkf,qkpc->bpcf/dot_general | solution.py:104
  131.0 17.3 %multiply_add_fusion = f32[64,2,16,512]{3,2,0,1:T(8,128)S(1)} fusion(f32[64,2,16,497]{3,2,0,1:T(8,128)S(1)} %bitcast.172, f32[64,2,16,498]{3,2,0,1:T(8,128)S(1)} %bitcast.173, f32[64,2,16,499]{3,2,0,1:T(8,128)S(1)} %bitcast.174, f32[64,2,16,500]{3,2,0,1:T(8,128)S(1)} %bitcast.175, f32[64,2,16,501]{3,2,0,1:T(8,128)S(1)} %bitcast.176, ...), kind=kLoop, calls=%fused_computation.5 | loop fusion | flops 32505856 | bytes 70321152 | tf_op jit(solution)/shard_map/add | solution.py:19
  148.4 2.6 %copy.68 = f32[64,2,16,512]{3,2,1,0:T(8,128)} copy(f32[64,2,16,512]{3,2,0,1:T(8,128)S(1)} %multiply_add_fusion) | data formatting | bytes 8388608
  (24 shorter events, 0.3 us)
Async XLA Ops:
  7.2 32.3 %copy-start = (s32[256]{0:T(256)S(1)}, s32[256]{0:T(256)}, u32[]{:S(2)}) copy-start(s32[256]{0:T(256)} %param.10) | copy-start | bytes 3076
  7.2 2.5 %copy-start.1 = (bf16[16,2,16,512]{3,2,1,0:T(8,128)(2,1)S(1)}, bf16[16,2,16,512]{3,2,1,0:T(8,128)(2,1)}, u32[]{:S(2)}) copy-start(bf16[16,2,16,512]{3,2,1,0:T(8,128)(2,1)} %param.7) | copy-start | bytes 1572868
  7.2 53.2 %all-gather.2.cloned.1.call-start = ((), (), s32[]{:S(2)}) async-start(), calls=%async_computation.2 | async-start | bytes 2621440 | tf_op jit(solution)/shard_map/all_gather | solution.py:57
  10.9 0.7 copy-start.3
  11.6 27.7 %copy-start.5 = (s32[32,1]{0,1:T(1,128)S(1)}, s32[32,1]{0,1:T(1,128)}, u32[]{:S(2)}) copy-start(s32[32,1]{0,1:T(1,128)} %param.11) | copy-start | bytes 388
  16.7 24.7 %copy-start.2 = (bf16[4,2,256,32]{2,3,1,0:T(8,128)(2,1)S(1)}, bf16[4,2,256,32]{2,3,1,0:T(8,128)(2,1)}, u32[]{:S(2)}) copy-start(bf16[4,2,256,32]{2,3,1,0:T(8,128)(2,1)} %param.13) | copy-start | bytes 393220
  66.5 7.7 %copy-start.4 = (f32[16,16]{1,0:T(8,128)S(1)}, f32[16,16]{1,0:T(8,128)}, u32[]{:S(2)}) copy-start(f32[16,16]{1,0:T(8,128)} %param.9) | copy-start | bytes 3076
  69.6 53.2 %all-to-all-start.1 = ((bf16[256,2,4,512]{3,2,1,0:T(4,128)(2,1)}), bf16[256,2,4,512]{3,2,1,0:T(4,128)(2,1)S(1)}, u32[]{:S(2)}, u32[]{:S(2)}) async-start(bf16[256,2,4,512]{3,2,1,0:T(4,128)(2,1)} %copy.64), calls=%async_computation.1 | async-start | bytes 4194304 | tf_op jit(solution)/shard_map/all_to_all | solution.py:103
Sparse Core Ops, SparseCore 0:
  38.6 21.6 all-gather.1
where the time goes:
time: 158 us
  waiting for transfers between devices  66.2 us (42%)
  local copies, waits for them, and re-layouts  23.5 us (15%)
  blocking collectives  20.6 us (13%)
  other arithmetic  18.1 us (11%)
  between operations  14.4 us (9%)
  matrix products  10.3 us (7%)
  starting transfers between devices  4.66 us (3%)
    all_to_all x1, waiting for transfers between devices, body(): lax.all_to_all(beams, 'row', split_axis=0, concat_axis=2, tiled=True)  47.3 us
    all_to_all x1, blocking collectives, body(): lax.all_to_all(spectra, 'row', split_axis=2, concat_axis=0, tiled=True)  20.6 us
    all_gather x1, waiting for transfers between devices, body(): shard_rows = lax.all_gather(turned, ('col', 'sub'), axis=0, tiled=True)  18.9 us
    add x1, other arithmetic, polyphase(): output = output + coefficients[tap_index][:, None] * shifted  17.3 us
    all_to_all x3, local copies, waits for them, and re-layouts, body(): lax.all_to_all(beams, 'row', split_axis=0, concat_axis=2, tiled=True)  6.19 us
    dot_general x1, matrix products, body(): jnp.einsum('aqcf,qcpk->apkf', filtered, fourier_table(samples.shape[2], -...  5.12 us
    all_to_all x1, starting transfers between devices, body(): lax.all_to_all(beams, 'row', split_axis=0, concat_axis=2, tiled=True)  4.62 us
    slice x15, local copies, waits for them, and re-layouts, polyphase(): signal[..., :length - tap_index]  3.91 us
  transfers between devices with their start and end apart: 2, of which 2 were waited for; matrix products, arithmetic and copies ran while one was open for 3% of the time, Pallas kernels for 0%

commit v1 on v0

--- a/solution.py
+++ b/solution.py
@@ -1,12 +1,292 @@
+import functools
 import math
 
 import jax
 import jax.numpy as jnp
 from jax import lax
+from jax.experimental import pallas as pl
+from jax.experimental.pallas import tpu as pltpu
 from jax.sharding import PartitionSpec as P
 
 ANTENNAS_PER_STN = 8
 SPEC = 512
+VMEM_LIMIT = 48 * 1024 * 1024
+HALO = 128
+
+
+def fourier(parts, sign):
+    count = len(parts)
+    if count == 1:
+        return parts
+    even, odd = fourier(parts[0::2], sign), fourier(parts[1::2], sign)
+    low, top = [], []
+    for k in range(count // 2):
+        er, ei = even[k]
+        re, im = odd[k]
+        if k == 0:
+            tr, ti = re, im
+        elif 4 * k == count:
+            tr, ti = (-sign * im, sign * re)
+        else:
+            c, s = math.cos(2 * math.pi * k / count), sign * math.sin(2 * math.pi * k / count)
+            tr, ti = re * c - im * s, re * s + im * c
+        low.append((er + tr, ei + ti))
+        top.append((er - tr, ei - ti))
+    return low + top
+
+
+def station_kernel(lane_axes, names_ref, taps_ref, x_ref, out_ref):
+    lane = lax.axis_index(lane_axes)
+    stations, antennas = out_ref.shape[0] // 2, names_ref.shape[1]
+    wanted = lax.broadcasted_iota(jnp.int32, (stations, antennas), 0)
+    chosen = jnp.where(names_ref[...] == wanted, 1.0, 0.0).astype(jnp.bfloat16)
+    frames = x_ref.shape[-1]
+    place = lax.broadcasted_iota(jnp.int32, (stations, frames), 1)
+    for part in range(2):
+        rows = x_ref[:, part].reshape(antennas, frames)
+        total = jnp.dot(chosen, rows, preferred_element_type=jnp.float32)
+        result = total * taps_ref[0, lane]
+        for tap in range(1, taps_ref.shape[0]):
+            moved = jnp.where(place >= tap, pltpu.roll(total, tap, 1), 0.0)
+            result = result + moved * taps_ref[tap, lane]
+        out_ref[part * stations : (part + 1) * stations] = result.astype(out_ref.dtype)
+
+
+def weight_kernel(groups_ref, beam_ref, w_ref, m_ref):
+    chan, _, beams, stations = w_ref.shape
+    members = groups_ref[...] == beam_ref[...]
+    count = jnp.sum(members.astype(jnp.float32), axis=1, keepdims=True)
+    scale = (1.0 / (chan * math.sqrt(ANTENNAS_PER_STN))) / jnp.sqrt(count)
+    zero = jnp.zeros((), jnp.float32)
+    parts = [
+        tuple(jnp.where(members, w_ref[k, q].astype(jnp.float32), zero) for q in range(2))
+        for k in range(chan)
+    ]
+    parts = fourier(parts, -1.0)
+    real = [p[0] * scale for p in parts]
+    imag = [p[1] * scale for p in parts]
+    upper = jnp.concatenate([v for k in range(chan) for v in (real[k], -imag[k])], axis=1)
+    lower = jnp.concatenate([v for k in range(chan) for v in (imag[k], real[k])], axis=1)
+    whole = jnp.concatenate([upper, lower], axis=0).astype(m_ref.dtype)
+    width = whole.shape[1] // 4
+    for u in range(4):
+        for j in range(4):
+            t = (u + j) % 4
+            m_ref[u, :, t * width : (t + 1) * width] = whole[:, j * width : (j + 1) * width]
+
+
+def toeplitz_kernel(taps_ref, t_ref):
+    taps, chan = taps_ref.shape
+    rows, cols = t_ref.shape[1] // 2, t_ref.shape[2]
+    wide = 2 * cols
+    lanes = lax.broadcasted_iota(jnp.int32, (8, wide), 1)
+    for c in range(chan):
+        base = jnp.zeros((8, wide), jnp.float32)
+        for tap in range(taps):
+            base = jnp.where(lanes == (tap - HALO) % wide, taps_ref[tap, c], base)
+        whole = jnp.broadcast_to(base[0:1], (rows, wide))
+        whole = pltpu.roll(whole, 0, 1, stride=1, stride_axis=0)[:, :cols]
+        high = whole.astype(jnp.bfloat16)
+        t_ref[c, :rows] = high
+        t_ref[c, rows:] = (whole - high.astype(jnp.float32)).astype(jnp.bfloat16)
+
+
+def beam_kernel(
+    axes,
+    x_refs,
+    m_hbm,
+    t_hbm,
+    series_ref,
+    vis_ref,
+    lanes_ref,
+    cross_ref,
+    m_ref,
+    t_ref,
+    tail_ref,
+    out_ref,
+    load_sems,
+    store_sems,
+):
+    row, col, sub = (lax.axis_index(a) for a in axes)
+    loads = [
+        pltpu.make_async_copy(m_hbm, m_ref, load_sems.at[0]),
+        pltpu.make_async_copy(t_hbm, t_ref, load_sems.at[1]),
+    ]
+    for copy in loads:
+        copy.start()
+    rows = x_refs[0].shape[1]
+    stations = rows // 2
+    chan = 4 * 4
+    frames = lanes_ref.shape[1]
+
+    for place, ref in enumerate(x_refs):
+        for m in range(4):
+            lane = (row ^ m) * 4 + (col ^ (place & 1)) * 2 + (sub ^ (place >> 1))
+            lanes_ref[pl.ds(pl.multiple_of(lane * rows, rows), rows)] = ref[m]
+    wrap = 3 * rows
+    lanes_ref[chan * rows : chan * rows + wrap] = lanes_ref[0:wrap]
+    inner = []
+    for b in range(4):
+        parts = []
+        for a in range(4):
+            start = (4 * a + b) * rows
+            parts.append(
+                tuple(
+                    lanes_ref[start + q * stations : start + (q + 1) * stations].astype(
+                        jnp.float32
+                    )
+                    for q in range(2)
+                )
+            )
+        inner.append(fourier(parts, -1.0))
+    scale = 1.0 / math.sqrt(chan * ANTENNAS_PER_STN)
+    block = (col * 2 + sub) * vis_ref.shape[2]
+    own = vis_ref.shape[2]
+    for j in range(4):
+        re, im = inner[0][j]
+        for b in range(1, 4):
+            cosine = jnp.float32(0.0)
+            sine = jnp.float32(0.0)
+            for r in range(4):
+                angle = -2.0 * math.pi * b * (4 * r + j) / chan
+                cosine = jnp.where(row == r, math.cos(angle), cosine)
+                sine = jnp.where(row == r, math.sin(angle), sine)
+            yr, yi = inner[b][j]
+            re = re + (yr * cosine - yi * sine)
+            im = im + (yr * sine + yi * cosine)
+        both = (jnp.concatenate([re, im], axis=0) * scale).astype(jnp.bfloat16)
+        cross_ref[...] = lax.dot_general(
+            both, both, (((1,), (1,)), ((), ())), preferred_element_type=jnp.float32
+        )
+        own_real = cross_ref[pl.ds(pl.multiple_of(block, own), own)]
+        own_imag = cross_ref[pl.ds(pl.multiple_of(stations + block, own), own)]
+        vis_ref[j, 0] = (own_real[:, :stations] + own_imag[:, stations:]) * (1.0 / SPEC)
+        vis_ref[j, 1] = (own_imag[:, :stations] - own_real[:, stations:]) * (1.0 / SPEC)
+    for copy in loads:
+        copy.wait()
+    beams = m_ref.shape[1] // 2
+    tile = t_ref.shape[2]
+    stores = []
+    for n in range(frames // tile):
+        for half in range(2):
+            slots = [(2 * n + half) * 2 + part for part in range(2)]
+            for v in range(4):
+                window = lanes_ref[v * rows : (v + chan) * rows, n * tile : (n + 1) * tile]
+                pair = m_ref[2 * half : 2 * half + 2].reshape(4 * beams, chan * rows)
+                found = jnp.dot(pair, window, preferred_element_type=jnp.float32)
+                found = found.astype(jnp.bfloat16)
+                for w in range(2):
+                    c = 4 * w + v
+                    lane = 8 * half + c
+                    inverse = found[2 * beams * w : 2 * beams * (w + 1)]
+                    if n == 0:
+                        value = jnp.dot(
+                            inverse, t_ref[lane, HALO : HALO + tile], preferred_element_type=jnp.float32
+                        ) + jnp.dot(
+                            inverse, t_ref[lane, 2 * HALO + tile :], preferred_element_type=jnp.float32
+                        )
+                    else:
+                        taken = jnp.concatenate([tail_ref[lane], inverse] * 2, axis=1)
+                        value = jnp.dot(taken, t_ref[lane], preferred_element_type=jnp.float32)
+                    if n + 1 < frames // tile:
+                        tail_ref[lane] = inverse[:, tile - HALO :]
+                    for part in range(2):
+                        for q in range(2):
+                            out_ref.at[slots[part]][pl.ds(q * 8 + c, beams, stride=16), :] = value[
+                                q * beams : (q + 1) * beams, part * 128 : (part + 1) * 128
+                            ]
+            for part in range(2):
+                first = n * tile + part * 128
+                stores.append(
+                    pltpu.make_async_copy(
+                        out_ref.at[slots[part]].reshape(2 * beams, 8, 128),
+                        series_ref.at[:, half, :, first : first + 128],
+                        store_sems.at[slots[part]],
+                    )
+                )
+                stores[-1].start()
+    for copy in stores:
+        copy.wait()
+
+
+def swap(x, axis, mask):
+    size = lax.axis_size(axis)
+    return lax.ppermute(x, axis, [(i, i ^ mask) for i in range(size)])
+
+
+def fast_body(
+    samples, analysis_taps, synthesis_taps, antenna_station, station_group, beam_group, beam_weights
+):
+    axes = ("row", "col", "sub")
+    params = pltpu.CompilerParams(vmem_limit_bytes=VMEM_LIMIT)
+    vmem = pl.BlockSpec(memory_space=pltpu.VMEM)
+    smem = pl.BlockSpec(memory_space=pltpu.SMEM)
+    local, _, chan, frames = samples.shape
+    stations = station_group.shape[0]
+    antennas = antenna_station.shape[0]
+
+    given = lax.all_to_all(beam_weights, "row", split_axis=2, concat_axis=0, tiled=True)
+    beams = given.shape[2]
+    own = (lax.axis_index(("col", "sub", "row"))) * beams
+    own_groups = lax.dynamic_slice_in_dim(beam_group, own, beams, 0).reshape(beams, 1)
+
+    turned = samples.transpose(2, 1, 0, 3)
+    lane = lax.all_to_all(turned, axes, split_axis=0, concat_axis=0, tiled=True)
+    filtered = pl.pallas_call(
+        functools.partial(station_kernel, axes),
+        out_shape=jax.ShapeDtypeStruct((2 * stations, frames), jnp.bfloat16),
+        in_specs=[vmem, smem, vmem],
+        out_specs=vmem,
+        compiler_params=params,
+        name="station_sums",
+    )(antenna_station.reshape(1, antennas), analysis_taps, lane)
+
+    matrix = pl.pallas_call(
+        weight_kernel,
+        out_shape=jax.ShapeDtypeStruct((4, 2 * beams, 2 * chan * stations), jnp.bfloat16),
+        in_specs=[vmem, vmem, vmem],
+        out_specs=vmem,
+        compiler_params=params,
+        name="weight_matrix",
+    )(station_group.reshape(1, stations), own_groups, given)
+    tile = 256
+    bands = pl.pallas_call(
+        toeplitz_kernel,
+        out_shape=jax.ShapeDtypeStruct((chan, 2 * (tile + HALO), tile), jnp.bfloat16),
+        in_specs=[smem],
+        out_specs=vmem,
+        compiler_params=params,
+        name="synthesis_bands",
+    )(synthesis_taps)
+
+    held = jnp.stack([filtered] + [swap(filtered, "row", m) for m in (1, 2, 3)])
+    other = swap(held, "col", 1)
+    pieces = [held, other, swap(held, "sub", 1), swap(other, "sub", 1)]
+
+    anywhere = pl.BlockSpec(memory_space=pl.ANY)
+    slots = frames // 128 * 2
+    series, visibilities = pl.pallas_call(
+        lambda a, b, c, d, *rest: beam_kernel(axes, (a, b, c, d), *rest),
+        out_shape=(
+            jax.ShapeDtypeStruct((2 * beams, 2, 8, frames), jnp.float32),
+            jax.ShapeDtypeStruct((4, 2, stations // 4, stations), jnp.float32),
+        ),
+        in_specs=[vmem, vmem, vmem, vmem, anywhere, anywhere],
+        out_specs=(anywhere, vmem),
+        scratch_shapes=[
+            pltpu.VMEM(((chan + 3) * 2 * stations, frames), jnp.bfloat16),
+            pltpu.VMEM((2 * stations, 2 * stations), jnp.float32),
+            pltpu.VMEM(matrix.shape, matrix.dtype),
+            pltpu.VMEM(bands.shape, bands.dtype),
+            pltpu.VMEM((chan, 2 * beams, HALO), jnp.bfloat16),
+            pltpu.VMEM((slots, 2 * beams * 8, 128), jnp.float32),
+            pltpu.SemaphoreType.DMA((2,)),
+            pltpu.SemaphoreType.DMA((slots,)),
+        ],
+        compiler_params=params,
+        name="beams_and_series",
+    )(*pieces, matrix, bands)
+    return visibilities, series.reshape(beams, 2, chan, frames)
 
 
 def polyphase(signal, coefficients):
@@ -36,7 +316,7 @@
     return table.transpose(0, 2, 1, 3) * (1.0 / math.sqrt(length))
 
 
-def body(
+def general_body(
     samples, analysis_taps, synthesis_taps, antenna_station, station_group, beam_group, beam_weights
 ):
     high = lax.Precision.HIGHEST
@@ -112,6 +392,13 @@
 
 
 def solution(mesh):
+    sizes = dict(mesh.shape)
+
+    def body(samples, *others):
+        chan = samples.shape[2]
+        fits = (sizes["row"], sizes["col"], sizes["sub"], chan) == (4, 2, 2, 16)
+        return (fast_body if fits else general_body)(samples, *others)
+
     return jax.shard_map(
         body,
         mesh=mesh,

time: 158 us -> 70.9 us (0.45)
  waiting for transfers between devices: 66.2 us -> 13.3 us
  Pallas kernels: 0 us -> 19.6 us
  other arithmetic: 18.1 us -> 0.04 us
  local copies, waits for them, and re-layouts: 23.5 us -> 6.38 us
  between operations: 14.4 us -> 0.75 us
  matrix products: 10.3 us -> 0 us
  starting transfers between devices: 4.66 us -> 8.76 us
    all_to_all x1, waiting for transfers between devices: 47.3 us -> 1.19 us  [fast_body(): lax.all_to_all(beam_weights, 'row', split_axis=2, concat_axis=0, tiled=True)]
    pallas_call x0 -> x4, Pallas kernels: none -> 19.6 us  [the longest x1 13.2 us: fast_body(): pl.pallas_call(lambda a, b, c, d, *rest: beam_kernel(axes, (a, b, c, d),...]
    all_gather x1 -> x0, waiting for transfers between devices: 18.9 us -> none  [body(): shard_rows = lax.all_gather(turned, ('col', 'sub'), axis=0, tiled=True)]
    add x1 -> x0, other arithmetic: 17.3 us -> none  [polyphase(): output = output + coefficients[tap_index][:, None] * shifted]
    ppermute x0 -> x6, waiting for transfers between devices: none -> 12.1 us  [swap(): return lax.ppermute(x, axis, [(i, i ^ mask) for i in range(size)])]
    dot_general x11 -> x0, matrix products: 10.3 us -> none  [the longest x1 5.12 us: body(): jnp.einsum('aqcf,qcpk->apkf', filtered, fourier_table(samples.shape[2], -...]
    all_to_all x4 -> x1, local copies, waits for them, and re-layouts: 7.02 us -> 0.11 us  [fast_body(): lax.all_to_all(beam_weights, 'row', split_axis=2, concat_axis=0, tiled=True)]
    ppermute x0 -> x6, starting transfers between devices: none -> 5.44 us  [swap(): return lax.ppermute(x, axis, [(i, i ^ mask) for i in range(size)])]
  transfers between devices with their start and end apart: 2 -> 7, of which waited for: 2 -> 4; matrix products, arithmetic and copies ran while one was open for 3% -> 4% of each run, Pallas kernels for 0% -> 7%
where the time goes in v1:
time: 70.9 us; the launch traced here: 70.4 us
  blocking collectives  21.6 us (30%)
  Pallas kernels  19.6 us (28%)
  waiting for transfers between devices  13.3 us (19%)
  starting transfers between devices  8.76 us (12%)
  local copies, waits for them, and re-layouts  6.38 us (9%)
  between operations  0.75 us (1%)
    all_to_all x1, blocking collectives, fast_body(): lane = lax.all_to_all(turned, axes, split_axis=0, concat_axis=0, tiled=True)  21.6 us
    pallas_call x1, Pallas kernels, fast_body(): pl.pallas_call(lambda a, b, c, d, *rest: beam_kernel(axes, (a, b, c, d),...  13.2 us
    ppermute x6, waiting for transfers between devices, swap(): return lax.ppermute(x, axis, [(i, i ^ mask) for i in range(size)])  12.1 us
    unnamed x14, local copies, waits for them, and re-layouts  6.09 us
    ppermute x6, starting transfers between devices, swap(): return lax.ppermute(x, axis, [(i, i ^ mask) for i in range(size)])  5.44 us
    pallas_call x1, Pallas kernels, fast_body(): pl.pallas_call(toeplitz_kernel, out_shape=jax.ShapeDtypeStruct((chan, 2 *...  4.38 us
    all_to_all x1, starting transfers between devices, fast_body(): lax.all_to_all(beam_weights, 'row', split_axis=2, concat_axis=0, tiled=True)  3.33 us
  transfers between devices with their start and end apart: 7, of which 4 were waited for; matrix products, arithmetic and copies ran while one was open for 4% of the time, Pallas kernels for 7%

profile of v1, /device:TPU:0, one launch (start us, length us, event | category | flops | bytes accessed | tf_op | source)
XLA Modules:
  0.0 70.4 jit_solution(5431730385070083411)
XLA Ops:
  0.6 0.0 copy-start
  0.6 0.0 copy-start.4
  0.7 1.3 %copy.21 = bf16[16,2,16,512]{3,0,1,2:T(8,128)(2,1)S(1)} copy(bf16[16,2,16,512]{3,2,1,0:T(8,128)(2,1)} %param.7) | data formatting | bytes 1048576 | tf_op args[0]
  2.0 21.6 %all_to_all.23.x_ref = bf16[16,2,16,512]{3,2,1,0:T(8,128)(2,1)S(1)} all-to-all(bf16[16,2,16,512]{3,2,1,0:T(8,128)(2,1)S(1)} %bitcast.24), channel_id=1, replica_groups=mesh['grp'=2,'row'=4,'col'=2,'sub'=2] {'row','col','sub'}, dimensions={0} | all-to-all | bytes 1048576 | tf_op jit(solution)/shard_map/all_to_all | solution.py:234
  23.6 0.0 copy-start.1
  23.6 0.7 copy-done.1
  24.3 0.0 copy-start.3
  24.3 0.7 copy-done.3
  25.0 1.4 %station_sums.1 = bf16[64,512]{1,0:T(8,128)(2,1)S(1)} custom-call(s32[1,256]{1,0:T(1,128)S(1)} %bitcast.20, f32[16,16]{1,0:T(8,128)S(1)} %copy-done.1, bf16[16,2,16,512]{3,2,1,0:T(8,128)(2,1)S(1)} %all_to_all.23.x_ref), custom_call_target="tpu_custom_call" | custom-call | tf_op jit(solution)/shard_map/station_sums/pallas_call | solution.py:235
  26.4 1.4 %collective-permute-start.2 = (bf16[64,512]{1,0:T(8,128)(2,1)S(1)}, bf16[64,512]{1,0:T(8,128)(2,1)S(1)}, u32[]{:S(2)}, u32[]{:S(2)}) collective-permute-start(bf16[64,512]{1,0:T(8,128)(2,1)S(1)} %station_sums.1), channel_id=1, source_target_pairs={{0,12},{4,8},{8,4},{12,0},{1,13},{5,9},{9,5},{13,1},{2,14},{6,10},... | collective-permute-start | bytes 196616 | tf_op jit(solution)/shard_map/ppermute | solution.py:214
  27.8 1.2 %collective-permute-start.1 = (bf16[64,512]{1,0:T(8,128)(2,1)S(1)}, bf16[64,512]{1,0:T(8,128)(2,1)S(1)}, u32[]{:S(2)}, u32[]{:S(2)}) collective-permute-start(bf16[64,512]{1,0:T(8,128)(2,1)S(1)} %station_sums.1), channel_id=1, source_target_pairs={{0,8},{4,12},{8,0},{12,4},{1,9},{5,13},{9,1},{13,5},{2,10},{6,14},... | collective-permute-start | bytes 196616 | tf_op jit(solution)/shard_map/ppermute | solution.py:214
  29.0 1.8 %collective-permute-start = (bf16[64,512]{1,0:T(8,128)(2,1)S(1)}, bf16[64,512]{1,0:T(8,128)(2,1)S(1)}, u32[]{:S(2)}, u32[]{:S(2)}) collective-permute-start(bf16[64,512]{1,0:T(8,128)(2,1)S(1)} %station_sums.1), channel_id=1, source_target_pairs={{0,4},{4,0},{8,12},{12,8},{1,5},{5,1},{9,13},{13,9},{2,6},{6,2},{1... | collective-permute-start | bytes 196616 | tf_op jit(solution)/shard_map/ppermute | solution.py:214
  30.9 2.4 %collective-permute-done.2 = bf16[64,512]{1,0:T(8,128)(2,1)S(1)} collective-permute-done((bf16[64,512]{1,0:T(8,128)(2,1)S(1)}, bf16[64,512]{1,0:T(8,128)(2,1)S(1)}, u32[]{:S(2)}, u32[]{:S(2)}) %collective-permute-start.2) | collective-permute-done | bytes 65568 | tf_op jit(solution)/shard_map/ppermute | solution.py:214
  33.3 2.6 %collective-permute-done.1 = bf16[64,512]{1,0:T(8,128)(2,1)S(1)} collective-permute-done((bf16[64,512]{1,0:T(8,128)(2,1)S(1)}, bf16[64,512]{1,0:T(8,128)(2,1)S(1)}, u32[]{:S(2)}, u32[]{:S(2)}) %collective-permute-start.1) | collective-permute-done | bytes 65568 | tf_op jit(solution)/shard_map/ppermute | solution.py:214
  35.9 0.0 collective-permute-done
  35.9 1.0 %collective-permute-start.3 = (bf16[4,64,512]{2,1,0:T(8,128)(2,1)S(1)}, bf16[4,64,512]{2,1,0:T(8,128)(2,1)S(1)}, u32[]{:S(2)}, u32[]{:S(2)}) collective-permute-start(bf16[4,64,512]{2,1,0:T(8,128)(2,1)S(1)} %pad_maximum_fusion.a), channel_id=1, source_target_pairs={{0,2},{2,0},{1,3},{3,1},{4,6},{6,4},{5,7},{7,5},{8,10},{10,8},{9,1... | collective-permute-start | bytes 786440 | tf_op jit(solution)/shard_map/ppermute | solution.py:214
  36.9 0.0 collective-permute-start.4
  36.9 7.1 %collective-permute-done.3.b = bf16[4,64,512]{2,1,0:T(8,128)(2,1)S(1)} collective-permute-done((bf16[4,64,512]{2,1,0:T(8,128)(2,1)S(1)}, bf16[4,64,512]{2,1,0:T(8,128)(2,1)S(1)}, u32[]{:S(2)}, u32[]{:S(2)}) %collective-permute-start.3) | collective-permute-done | bytes 262176 | tf_op jit(solution)/shard_map/ppermute | solution.py:214
  44.0 0.0 collective-permute-start.5
  44.0 1.2 %copy.17 = bf16[4,2,256,32]{3,0,1,2:T(4,128)(2,1)S(1)} copy(bf16[4,2,256,32]{2,3,1,0:T(8,128)(2,1)} %param.13) | data formatting | bytes 262144 | tf_op args[6]
  45.2 1.2 %reshape.20 = bf16[4,2,8192]{2,1,0:T(2,128)(2,1)} reshape(bf16[256,2,4,32]{3,2,1,0:T(4,128)(2,1)S(1)} %bitcast.22) | data formatting | bytes 262144
  46.4 3.3 %all-to-all-start.1 = ((bf16[4,2,8192]{2,1,0:T(2,128)(2,1)}), bf16[4,2,8192]{2,1,0:T(2,128)(2,1)S(1)}, u32[]{:S(2)}, u32[]{:S(2)}) async-start(bf16[4,2,8192]{2,1,0:T(2,128)(2,1)} %reshape.20), calls=%async_computation.1 | async-start | bytes 262144 | tf_op jit(solution)/shard_map/all_to_all | solution.py:228
  49.7 0.0 copy-done
  49.7 0.1 dynamic-slice_bitcast_fusion
  49.8 0.1 copy.19.beam_ref
  49.9 0.0 copy-start.2
  49.9 0.7 copy-done.2
  50.6 4.4 %synthesis_bands.1.rest_1_ = bf16[16,768,256]{2,1,0:T(8,128)(2,1)} custom-call(f32[16,16]{1,0:T(8,128)S(1)} %copy-done.2), custom_call_target="tpu_custom_call" | custom-call | tf_op jit(solution)/shard_map/synthesis_bands/pallas_call | solution.py:253
  55.0 1.2 %all-to-all-done.1 = bf16[4,2,8192]{2,1,0:T(2,128)(2,1)S(1)} async-done(((bf16[4,2,8192]{2,1,0:T(2,128)(2,1)}), bf16[4,2,8192]{2,1,0:T(2,128)(2,1)S(1)}, u32[]{:S(2)}, u32[]{:S(2)}) %all-to-all-start.1) | async-done | bytes 131104 | tf_op jit(solution)/shard_map/all_to_all | solution.py:228
  56.2 0.3 reshape.21
  56.4 0.1 copy.18
  56.6 0.0 copy-done.4
  56.6 0.7 weight_matrix.1.rest_0_
  57.2 0.0 collective-permute-done.4.c
  57.3 0.0 collective-permute-done.5.d
  57.3 13.2 %beams_and_series.1 = (f32[128,2,8,512]{3,2,1,0:T(8,128)}, f32[4,2,8,32]{3,2,1,0:T(8,128)}) custom-call(bf16[4,64,512]{2,1,0:T(8,128)(2,1)S(1)} %pad_maximum_fusion.a, bf16[4,64,512]{2,1,0:T(8,128)(2,1)S(1)} %collective-permute-done.3.b, bf16[4,64,512]{2,1,0:T(8,128)(2,1)S(1)} %collective-permute-done.4.c, bf16[4,64,512]{2,1,0:T(8,128)(2,1)S(1)} %collective-permute-done.5.d, ...), custom_call_target="tpu_custom_call" | custom-call | tf_op jit(solution)/shard_map/beams_and_series/pallas_call | solution.py:268
  (1 shorter events, 0.0 us)
Async XLA Ops:
  0.6 49.1 %copy-start = (s32[1024]{0:T(1024)S(1)}, s32[1024]{0:T(1024)}, u32[]{:S(2)}) copy-start(s32[1024]{0:T(1024)} %param.12) | copy-start | bytes 12292
  0.6 55.9 %copy-start.4 = (s32[32,1]{0,1:T(1,128)S(1)}, s32[32,1]{0,1:T(1,128)}, u32[]{:S(2)}) copy-start(s32[32,1]{0,1:T(1,128)} %param.11) | copy-start | bytes 388
  23.6 0.7 copy-start.1
  24.3 0.7 copy-start.3
  26.4 6.8 %collective-permute-start.2 = (bf16[64,512]{1,0:T(8,128)(2,1)S(1)}, bf16[64,512]{1,0:T(8,128)(2,1)S(1)}, u32[]{:S(2)}, u32[]{:S(2)}) collective-permute-start(bf16[64,512]{1,0:T(8,128)(2,1)S(1)} %station_sums.1), channel_id=1, source_target_pairs={{0,12},{4,8},{8,4},{12,0},{1,13},{5,9},{9,5},{13,1},{2,14},{6,10},... | collective-permute-start | bytes 196616 | tf_op jit(solution)/shard_map/ppermute | solution.py:214
  27.8 8.0 %collective-permute-start.1 = (bf16[64,512]{1,0:T(8,128)(2,1)S(1)}, bf16[64,512]{1,0:T(8,128)(2,1)S(1)}, u32[]{:S(2)}, u32[]{:S(2)}) collective-permute-start(bf16[64,512]{1,0:T(8,128)(2,1)S(1)} %station_sums.1), channel_id=1, source_target_pairs={{0,8},{4,12},{8,0},{12,4},{1,9},{5,13},{9,1},{13,5},{2,10},{6,14},... | collective-permute-start | bytes 196616 | tf_op jit(solution)/shard_map/ppermute | solution.py:214
  29.0 6.8 %collective-permute-start = (bf16[64,512]{1,0:T(8,128)(2,1)S(1)}, bf16[64,512]{1,0:T(8,128)(2,1)S(1)}, u32[]{:S(2)}, u32[]{:S(2)}) collective-permute-start(bf16[64,512]{1,0:T(8,128)(2,1)S(1)} %station_sums.1), channel_id=1, source_target_pairs={{0,4},{4,0},{8,12},{12,8},{1,5},{5,1},{9,13},{13,9},{2,6},{6,2},{1... | collective-permute-start | bytes 196616 | tf_op jit(solution)/shard_map/ppermute | solution.py:214
  35.9 8.1 %collective-permute-start.3 = (bf16[4,64,512]{2,1,0:T(8,128)(2,1)S(1)}, bf16[4,64,512]{2,1,0:T(8,128)(2,1)S(1)}, u32[]{:S(2)}, u32[]{:S(2)}) collective-permute-start(bf16[4,64,512]{2,1,0:T(8,128)(2,1)S(1)} %pad_maximum_fusion.a), channel_id=1, source_target_pairs={{0,2},{2,0},{1,3},{3,1},{4,6},{6,4},{5,7},{7,5},{8,10},{10,8},{9,1... | collective-permute-start | bytes 786440 | tf_op jit(solution)/shard_map/ppermute | solution.py:214
  36.9 20.4 %collective-permute-start.4 = (bf16[4,64,512]{2,1,0:T(8,128)(2,1)S(1)}, bf16[4,64,512]{2,1,0:T(8,128)(2,1)S(1)}, u32[]{:S(2)}, u32[]{:S(2)}) collective-permute-start(bf16[4,64,512]{2,1,0:T(8,128)(2,1)S(1)} %pad_maximum_fusion.a), channel_id=1, source_target_pairs={{0,1},{1,0},{2,3},{3,2},{4,5},{5,4},{6,7},{7,6},{8,9},{9,8},{10,11... | collective-permute-start | bytes 786440 | tf_op jit(solution)/shard_map/ppermute | solution.py:214
  44.0 13.3 %collective-permute-start.5 = (bf16[4,64,512]{2,1,0:T(8,128)(2,1)S(1)}, bf16[4,64,512]{2,1,0:T(8,128)(2,1)S(1)}, u32[]{:S(2)}, u32[]{:S(2)}) collective-permute-start(bf16[4,64,512]{2,1,0:T(8,128)(2,1)S(1)} %collective-permute-done.3.b), channel_id=1, source_target_pairs={{0,1},{1,0},{2,3},{3,2},{4,5},{5,4},{6,7},{7,6},{8,9},{9,8},{10,11... | collective-permute-start | bytes 786440 | tf_op jit(solution)/shard_map/ppermute | solution.py:214
  46.4 9.8 %all-to-all-start.1 = ((bf16[4,2,8192]{2,1,0:T(2,128)(2,1)}), bf16[4,2,8192]{2,1,0:T(2,128)(2,1)S(1)}, u32[]{:S(2)}, u32[]{:S(2)}) async-start(bf16[4,2,8192]{2,1,0:T(2,128)(2,1)} %reshape.20), calls=%async_computation.1 | async-start | bytes 262144 | tf_op jit(solution)/shard_map/all_to_all | solution.py:228
  49.9 0.7 copy-start.2

commit v2 on v0

--- a/solution.py
+++ b/solution.py
@@ -1,12 +1,386 @@
+import functools
 import math
 
 import jax
 import jax.numpy as jnp
 from jax import lax
+from jax.experimental import pallas as pl
+from jax.experimental.pallas import tpu as pltpu
 from jax.sharding import PartitionSpec as P
 
 ANTENNAS_PER_STN = 8
 SPEC = 512
+VMEM_LIMIT = 32 * 1024 * 1024
+HALO = 128
+
+
+def fourier(parts, sign):
+    count = len(parts)
+    if count == 1:
+        return parts
+    even, odd = fourier(parts[0::2], sign), fourier(parts[1::2], sign)
+    low, top = [], []
+    for k in range(count // 2):
+        er, ei = even[k]
+        re, im = odd[k]
+        if k == 0:
+            tr, ti = re, im
+        elif 4 * k == count:
+            tr, ti = (-sign * im, sign * re)
+        else:
+            c, s = math.cos(2 * math.pi * k / count), sign * math.sin(2 * math.pi * k / count)
+            tr, ti = re * c - im * s, re * s + im * c
+        low.append((er + tr, ei + ti))
+        top.append((er - tr, ei - ti))
+    return low + top
+
+
+def lane_of(row, col, sub):
+    return sub * 8 + col * 4 + row
+
+
+def spread_kernel(axes, x_ref, *out_refs):
+    row, col, sub = (lax.axis_index(a) for a in axes)
+    antennas, parts, chan, frames = x_ref.shape
+    count = antennas * parts * chan
+    shape = (count, count)
+    place = lax.broadcasted_iota(jnp.int32, (count, 1), 0)
+    antenna = place % antennas
+    part = place // antennas % parts
+    piece = place // (antennas * parts)
+    lane = lane_of(row ^ (piece % 4), col ^ (piece // 4 % 2), sub ^ (piece // 8))
+    source = (antenna * parts + part) * chan + lane
+    order = jnp.where(lax.broadcasted_iota(jnp.int32, shape, 1) == source, 1.0, 0.0)
+    moved = jnp.dot(
+        order.astype(jnp.bfloat16),
+        x_ref[...].reshape(count, frames),
+        preferred_element_type=jnp.float32,
+    ).astype(jnp.bfloat16)
+    size = count // len(out_refs)
+    for k, ref in enumerate(out_refs):
+        ref[...] = moved[k * size : (k + 1) * size].reshape(ref.shape)
+
+
+def sum_kernel(members_ref, *refs):
+    x_refs, out_refs = refs[:4], refs[4:]
+    for m, ref in enumerate(out_refs):
+        rows = jnp.concatenate([x[m] for x in x_refs], axis=0)
+        ref[...] = jnp.dot(
+            members_ref[...], rows, preferred_element_type=jnp.float32
+        ).astype(ref.dtype)
+
+
+def filter_kernel(taps_ref, *refs):
+    x_refs, out_ref = refs[:-1], refs[-1]
+    total = x_refs[0][...].astype(jnp.float32)
+    for ref in x_refs[1:]:
+        total = total + ref[...].astype(jnp.float32)
+    place = lax.broadcasted_iota(jnp.int32, total.shape, 1)
+    result = total * taps_ref[0:1]
+    for tap in range(1, taps_ref.shape[0]):
+        moved = jnp.where(place >= tap, pltpu.roll(total, tap, 1), 0.0)
+        result = result + moved * taps_ref[tap : tap + 1]
+    out_ref[...] = result.astype(out_ref.dtype)
+
+
+def pack_kernel(axes, w_ref, names_ref, taps_ref, members_ref, own_taps_ref, *out_refs):
+    row, col, sub = (lax.axis_index(a) for a in axes)
+    names = []
+    for k in range(4):
+        owner = (row * 2 + (col ^ (k // 2))) * 2 + (sub ^ (k % 2))
+        names += [names_ref[pl.ds(owner, 1)]] * 2
+    names = jnp.concatenate(names, axis=1)
+    local = names_ref.shape[1]
+    place = lax.broadcasted_iota(jnp.int32, members_ref.shape, 0)
+    column = lax.broadcasted_iota(jnp.int32, members_ref.shape, 1)
+    wanted = members_ref.shape[0] // 2
+    same = (place % wanted == names) & (place // wanted == column // local % 2)
+    members_ref[...] = jnp.where(same, 1.0, 0.0).astype(members_ref.dtype)
+    taps = taps_ref[...]
+    mine = lax.broadcasted_iota(jnp.int32, taps.shape, 1) == lane_of(row, col, sub)
+    own = jnp.sum(jnp.where(mine, taps, 0.0), axis=1, keepdims=True)
+    own_taps_ref[...] = jnp.broadcast_to(own, own_taps_ref.shape)
+    chan, _, _, stations = w_ref.shape
+    beams = out_refs[0].shape[0]
+    for mask, ref in enumerate(out_refs):
+        first = pl.multiple_of((row ^ mask) * beams, beams)
+        for k in range(chan):
+            for q in range(2):
+                place = (2 * k + q) * stations
+                ref[:, place : place + stations] = w_ref[k, q, pl.ds(first, beams)]
+
+
+def weight_kernel(axes, groups_ref, beam_ref, *refs):
+    row = lax.axis_index(axes[0])
+    w_refs, m_ref, all_ref = refs[:4], refs[4], refs[5]
+    stations = groups_ref.shape[1]
+    held = w_refs[0].shape[1] // (2 * stations)
+    chan = 4 * held
+    for mask, ref in enumerate(w_refs):
+        all_ref[row ^ mask] = ref[...]
+    members = groups_ref[...] == beam_ref[...]
+    count = jnp.sum(members.astype(jnp.float32), axis=1, keepdims=True)
+    scale = (1.0 / (chan * math.sqrt(ANTENNAS_PER_STN))) / jnp.sqrt(count)
+    zero = jnp.zeros((), jnp.float32)
+    parts = []
+    for k in range(chan):
+        whole = all_ref[k // held].astype(jnp.float32)
+        places = [(2 * (k % held) + q) * stations for q in range(2)]
+        parts.append(
+            tuple(jnp.where(members, whole[:, p : p + stations], zero) for p in places)
+        )
+    parts = fourier(parts, -1.0)
+    real = [p[0] * scale for p in parts]
+    imag = [p[1] * scale for p in parts]
+    upper = jnp.concatenate([v for k in range(chan) for v in (real[k], -imag[k])], axis=1)
+    lower = jnp.concatenate([v for k in range(chan) for v in (imag[k], real[k])], axis=1)
+    whole = jnp.concatenate([upper, lower], axis=0).astype(m_ref.dtype)
+    width = whole.shape[1] // 4
+    for u in range(4):
+        for j in range(4):
+            t = (u + j) % 4
+            m_ref[u, :, t * width : (t + 1) * width] = whole[:, j * width : (j + 1) * width]
+
+
+def bands(taps_ref, lane, rows, cols):
+    wide = 2 * cols
+    places = lax.broadcasted_iota(jnp.int32, (8, wide), 1)
+    base = jnp.zeros((8, wide), jnp.float32)
+    for tap in range(taps_ref.shape[0]):
+        base = jnp.where(places == (tap - HALO) % wide, taps_ref[tap, lane], base)
+    whole = jnp.broadcast_to(base[0:1], (rows, wide))
+    whole = pltpu.roll(whole, 0, 1, stride=1, stride_axis=0)[:, :cols]
+    high = whole.astype(jnp.bfloat16)
+    low = (whole - high.astype(jnp.float32)).astype(jnp.bfloat16)
+    return jnp.concatenate([high[:HALO], low[:HALO], high[HALO:], low[HALO:]], axis=0)
+
+
+def beam_kernel(
+    axes,
+    x_refs,
+    m_ref,
+    taps_ref,
+    series_ref,
+    vis_ref,
+    lanes_ref,
+    cross_ref,
+    t_ref,
+    inverse_ref,
+    out_ref,
+    store_sems,
+):
+    row, col, sub = (lax.axis_index(a) for a in axes)
+    rows = x_refs[0].shape[1]
+    stations = rows // 2
+    chan = 4 * 4
+    frames = lanes_ref.shape[1]
+
+    for place, ref in enumerate(x_refs):
+        for m in range(4):
+            lane = lane_of(row ^ m, col ^ (place & 1), sub ^ (place >> 1))
+            lanes_ref[pl.ds(pl.multiple_of(lane * rows, rows), rows)] = ref[m]
+    wrap = 3 * rows
+    lanes_ref[chan * rows : chan * rows + wrap] = lanes_ref[0:wrap]
+    beams = m_ref.shape[1] // 2
+    tile = t_ref.shape[2]
+    stores = []
+    for half in range(2):
+        for c in range(8):
+            t_ref[8 * half + c] = bands(taps_ref, 8 * half + c, HALO + tile, tile)
+        some = m_ref[2 * half : 2 * half + 2].reshape(4 * beams, chan * rows)
+        for v in range(4):
+            window = lanes_ref[v * rows : (v + chan) * rows]
+            found = jnp.dot(some, window, preferred_element_type=jnp.float32)
+            found = found.astype(jnp.bfloat16)
+            for u in range(2):
+                inverse_ref[8 * half + 4 * u + v] = found[2 * beams * u : 2 * beams * (u + 1)]
+        for n in range(frames // tile):
+            for c in range(8):
+                lane = 8 * half + c
+                taken = [inverse_ref[lane, :, n * tile : (n + 1) * tile]] * 2
+                first = 2 * HALO
+                if n > 0:
+                    taken = [inverse_ref[lane, :, n * tile - HALO : n * tile]] * 2 + taken
+                    first = 0
+                value = jnp.dot(
+                    jnp.concatenate(taken, axis=1),
+                    t_ref[lane, first:],
+                    preferred_element_type=jnp.float32,
+                )
+                for part in range(2):
+                    slot = (2 * n + half) * 2 + part
+                    for q in range(2):
+                        out_ref.at[slot][pl.ds(q * 8 + c, beams, stride=16), :] = value[
+                            q * beams : (q + 1) * beams, part * 128 : (part + 1) * 128
+                        ]
+            for part in range(2):
+                first = n * tile + part * 128
+                slot = (2 * n + half) * 2 + part
+                stores.append(
+                    pltpu.make_async_copy(
+                        out_ref.at[slot].reshape(2 * beams, 8, 128),
+                        series_ref.at[:, half, :, first : first + 128],
+                        store_sems.at[slot],
+                    )
+                )
+                stores[-1].start()
+    inner = []
+    for b in range(4):
+        parts = []
+        for a in range(4):
+            start = (4 * a + b) * rows
+            parts.append(
+                tuple(
+                    lanes_ref[start + q * stations : start + (q + 1) * stations].astype(
+                        jnp.float32
+                    )
+                    for q in range(2)
+                )
+            )
+        inner.append(fourier(parts, -1.0))
+    scale = 1.0 / math.sqrt(chan * ANTENNAS_PER_STN)
+    block = (col * 2 + sub) * vis_ref.shape[2]
+    own = vis_ref.shape[2]
+    for j in range(4):
+        re, im = inner[0][j]
+        for b in range(1, 4):
+            cosine = jnp.float32(0.0)
+            sine = jnp.float32(0.0)
+            for r in range(4):
+                angle = -2.0 * math.pi * b * (4 * r + j) / chan
+                cosine = jnp.where(row == r, math.cos(angle), cosine)
+                sine = jnp.where(row == r, math.sin(angle), sine)
+            yr, yi = inner[b][j]
+            re = re + (yr * cosine - yi * sine)
+            im = im + (yr * sine + yi * cosine)
+        both = (jnp.concatenate([re, im], axis=0) * scale).astype(jnp.bfloat16)
+        cross_ref[...] = lax.dot_general(
+            both, both, (((1,), (1,)), ((), ())), preferred_element_type=jnp.float32
+        )
+        own_real = cross_ref[pl.ds(pl.multiple_of(block, own), own)]
+        own_imag = cross_ref[pl.ds(pl.multiple_of(stations + block, own), own)]
+        vis_ref[j, 0] = (own_real[:, :stations] + own_imag[:, stations:]) * (1.0 / SPEC)
+        vis_ref[j, 1] = (own_imag[:, :stations] - own_real[:, stations:]) * (1.0 / SPEC)
+    for copy in stores:
+        copy.wait()
+
+
+def call_beams(axes, pieces, matrix, taps):
+    params = pltpu.CompilerParams(vmem_limit_bytes=VMEM_LIMIT)
+    vmem = pl.BlockSpec(memory_space=pltpu.VMEM)
+    smem = pl.BlockSpec(memory_space=pltpu.SMEM)
+    chan, frames, tile = taps.shape[1], pieces[0].shape[2], 256
+    stations, beams = pieces[0].shape[1] // 2, matrix.shape[1] // 2
+    anywhere = pl.BlockSpec(memory_space=pl.ANY)
+    slots = frames // 128 * 2
+    series, visibilities = pl.pallas_call(
+        lambda a, b, c, d, *rest: beam_kernel(axes, (a, b, c, d), *rest),
+        out_shape=(
+            jax.ShapeDtypeStruct((2 * beams, 2, 8, frames), jnp.float32),
+            jax.ShapeDtypeStruct((4, 2, stations // 4, stations), jnp.float32),
+        ),
+        in_specs=[vmem] * 5 + [smem],
+        out_specs=(anywhere, vmem),
+        scratch_shapes=[
+            pltpu.VMEM(((chan + 3) * 2 * stations, frames), jnp.bfloat16),
+            pltpu.VMEM((2 * stations, 2 * stations), jnp.float32),
+            pltpu.VMEM((chan, 2 * (tile + HALO), tile), jnp.bfloat16),
+            pltpu.VMEM((chan, 2 * beams, frames), jnp.bfloat16),
+            pltpu.VMEM((slots, 2 * beams * 8, 128), jnp.float32),
+            pltpu.SemaphoreType.DMA((slots,)),
+        ],
+        compiler_params=params,
+        name="beams_and_series",
+    )(*pieces, matrix, taps)
+    return visibilities, series
+
+
+def swap(x, axis, mask):
+    size = lax.axis_size(axis)
+    return lax.ppermute(x, axis, [(i, i ^ mask) for i in range(size)])
+
+
+def fast_body(
+    samples, analysis_taps, synthesis_taps, antenna_station, station_group, beam_group, beam_weights
+):
+    axes = ("row", "col", "sub")
+    params = pltpu.CompilerParams(vmem_limit_bytes=VMEM_LIMIT)
+    vmem = pl.BlockSpec(memory_space=pltpu.VMEM)
+    smem = pl.BlockSpec(memory_space=pltpu.SMEM)
+    local, _, chan, frames = samples.shape
+    stations = station_group.shape[0]
+    antennas = antenna_station.shape[0]
+
+    held_chan = beam_weights.shape[0]
+    beams = beam_weights.shape[2] // 4
+    block = jax.ShapeDtypeStruct((4, 2 * local, frames), jnp.bfloat16)
+    kept, crossing, paired, far = pl.pallas_call(
+        functools.partial(spread_kernel, axes),
+        out_shape=[block] * 4,
+        in_specs=[vmem],
+        out_specs=[vmem] * 4,
+        compiler_params=params,
+        name="lane_spread",
+    )(samples)
+    far = swap(far, "sub", 1)
+    crossed = swap(crossing, "col", 1)
+    paired = swap(paired, "sub", 1)
+    far = swap(far, "col", 1)
+
+    packed = jax.ShapeDtypeStruct((beams, held_chan * 2 * stations), jnp.bfloat16)
+    members, own_taps, *shares = pl.pallas_call(
+        functools.partial(pack_kernel, axes),
+        out_shape=[
+            jax.ShapeDtypeStruct((2 * stations, 8 * local), jnp.bfloat16),
+            jax.ShapeDtypeStruct((analysis_taps.shape[0], frames), jnp.float32),
+        ]
+        + [packed] * 4,
+        in_specs=[vmem] * 3,
+        out_specs=[vmem] * 6,
+        compiler_params=params,
+        cost_estimate=pl.CostEstimate(flops=0, bytes_accessed=4 << 20, transcendentals=0),
+        name="weight_shares",
+    )(beam_weights, antenna_station.reshape(antennas // local, local), analysis_taps)
+    given = [shares[0]] + [swap(shares[m], "row", m) for m in (1, 2, 3)]
+    own = (lax.axis_index(("col", "sub", "row"))) * beams
+    own_groups = lax.dynamic_slice_in_dim(beam_group, own, beams, 0).reshape(beams, 1)
+
+    lane = jax.ShapeDtypeStruct((2 * stations, frames), jnp.bfloat16)
+    sums = pl.pallas_call(
+        sum_kernel,
+        out_shape=[lane] * 4,
+        in_specs=[vmem] * 5,
+        out_specs=[vmem] * 4,
+        compiler_params=params,
+        name="plane_sums",
+    )(members, kept, paired, crossed, far)
+    moved = [swap(sums[m], "row", m) for m in (1, 2, 3)]
+    first, *given = lax.optimization_barrier((sums[0], *given))
+    matrix = pl.pallas_call(
+        functools.partial(weight_kernel, axes),
+        out_shape=jax.ShapeDtypeStruct((4, 2 * beams, 2 * chan * stations), jnp.bfloat16),
+        in_specs=[vmem] * 6,
+        out_specs=vmem,
+        scratch_shapes=[pltpu.VMEM((4,) + packed.shape, jnp.bfloat16)],
+        compiler_params=params,
+        cost_estimate=pl.CostEstimate(flops=1_000_000_000, bytes_accessed=2 << 20, transcendentals=0),
+        name="weight_matrix",
+    )(station_group.reshape(1, stations), own_groups, *given)
+    filtered = pl.pallas_call(
+        filter_kernel,
+        out_shape=lane,
+        in_specs=[vmem] * 5,
+        out_specs=vmem,
+        compiler_params=params,
+        name="station_filter",
+    )(own_taps, first, *moved)
+
+    held = jnp.stack([filtered] + [swap(filtered, "row", m) for m in (1, 2, 3)])
+    other = swap(held, "col", 1)
+    pieces = [held, other, swap(held, "sub", 1), swap(other, "sub", 1)]
+
+    visibilities, series = call_beams(axes, pieces, matrix, synthesis_taps)
+    return visibilities, series.reshape(beams, 2, chan, frames)
 
 
 def polyphase(signal, coefficients):
@@ -36,7 +410,7 @@
     return table.transpose(0, 2, 1, 3) * (1.0 / math.sqrt(length))
 
 
-def body(
+def general_body(
     samples, analysis_taps, synthesis_taps, antenna_station, station_group, beam_group, beam_weights
 ):
     high = lax.Precision.HIGHEST
@@ -112,6 +486,13 @@
 
 
 def solution(mesh):
+    sizes = dict(mesh.shape)
+
+    def body(samples, *others):
+        chan = samples.shape[2]
+        fits = (sizes["row"], sizes["col"], sizes["sub"], chan) == (4, 2, 2, 16)
+        return (fast_body if fits else general_body)(samples, *others)
+
     return jax.shard_map(
         body,
         mesh=mesh,

time: 158 us -> 49.7 us (0.31)
  waiting for transfers between devices: 66.2 us -> 13.8 us
  blocking collectives: 20.6 us -> 0 us
  local copies, waits for them, and re-layouts: 23.5 us -> 4.53 us
  other arithmetic: 18.1 us -> 0.04 us
  starting transfers between devices: 4.66 us -> 20.3 us
  between operations: 14.4 us -> 0.75 us
  matrix products: 10.3 us -> 0 us
  Pallas kernels: 0 us -> 10 us
    all_to_all x1 -> x0, waiting for transfers between devices: 47.3 us -> none  [body(): lax.all_to_all(beams, 'row', split_axis=0, concat_axis=2, tiled=True)]
    all_to_all x1 -> x0, blocking collectives: 20.6 us -> none  [body(): lax.all_to_all(spectra, 'row', split_axis=2, concat_axis=0, tiled=True)]
    ppermute x0 -> x16, starting transfers between devices: none -> 20.3 us  [swap(): return lax.ppermute(x, axis, [(i, i ^ mask) for i in range(size)])]
    all_gather x1 -> x0, waiting for transfers between devices: 18.9 us -> none  [body(): shard_rows = lax.all_gather(turned, ('col', 'sub'), axis=0, tiled=True)]
    add x1 -> x0, other arithmetic: 17.3 us -> none  [polyphase(): output = output + coefficients[tap_index][:, None] * shifted]
    ppermute x0 -> x16, waiting for transfers between devices: none -> 13.8 us  [swap(): return lax.ppermute(x, axis, [(i, i ^ mask) for i in range(size)])]
    dot_general x11 -> x0, matrix products: 10.3 us -> none  [the longest x1 5.12 us: body(): jnp.einsum('aqcf,qcpk->apkf', filtered, fourier_table(samples.shape[2], -...]
    pallas_call x0 -> x6, Pallas kernels: none -> 10 us  [the longest x1 7.71 us: call_beams(): pl.pallas_call(lambda a, b, c, d, *rest: beam_kernel(axes, (a, b, c, d),...]
  transfers between devices with their start and end apart: 2 -> 16, of which waited for: 2 -> 5; matrix products, arithmetic and copies ran while one was open for 3% -> 4% of each run, Pallas kernels for 0% -> 2%
where the time goes in v2:
time: 49.7 us; the launch traced here: 49.4 us
  starting transfers between devices  20.3 us (41%)
  waiting for transfers between devices  13.8 us (28%)
  Pallas kernels  10 us (20%)
  local copies, waits for them, and re-layouts  4.53 us (9%)
  between operations  0.75 us (2%)
    ppermute x16, starting transfers between devices, swap(): return lax.ppermute(x, axis, [(i, i ^ mask) for i in range(size)])  20.3 us
    ppermute x16, waiting for transfers between devices, swap(): return lax.ppermute(x, axis, [(i, i ^ mask) for i in range(size)])  13.8 us
    pallas_call x1, Pallas kernels, call_beams(): pl.pallas_call(lambda a, b, c, d, *rest: beam_kernel(axes, (a, b, c, d),...  7.71 us
    unnamed x11, local copies, waits for them, and re-layouts  3.6 us
  transfers between devices with their start and end apart: 16, of which 5 were waited for; matrix products, arithmetic and copies ran while one was open for 4% of the time, Pallas kernels for 2%

profile of v2, /device:TPU:0, one launch (start us, length us, event | category | flops | bytes accessed | tf_op | source)
XLA Modules:
  0.0 49.4 jit_solution(4009075755213633404)
XLA Ops:
  0.6 0.0 copy-start
  0.6 0.0 copy-start.1
  0.7 1.0 %copy-done.1 = bf16[16,2,16,512]{3,2,1,0:T(8,128)(2,1)S(1)} copy-done((bf16[16,2,16,512]{3,2,1,0:T(8,128)(2,1)S(1)}, bf16[16,2,16,512]{3,2,1,0:T(8,128)(2,1)}, u32[]{:S(2)}) %copy-start.1) | copy-done | bytes 524312
  1.7 0.5 %lane_spread.1 = (bf16[4,32,512]{2,1,0:T(8,128)(2,1)S(1)}, bf16[4,32,512]{2,1,0:T(8,128)(2,1)S(1)}, bf16[4,32,512]{2,1,0:T(8,128)(2,1)S(1)}, bf16[4,32,512]{2,1,0:T(8,128)(2,1)S(1)}) custom-call(bf16[16,2,16,512]{3,2,1,0:T(8,128)(2,1)S(1)} %copy-done.1), custom_call_target="tpu_custom_call" | custom-call | tf_op jit(solution)/shard_map/lane_spread/pallas_call | solution.py:317
  2.2 0.5 %collective-permute-start.2 = (bf16[4,32,512]{2,1,0:T(8,128)(2,1)S(1)}, bf16[4,32,512]{2,1,0:T(8,128)(2,1)S(1)}, u32[]{:S(2)}, u32[]{:S(2)}) collective-permute-start(bf16[4,32,512]{2,1,0:T(8,128)(2,1)S(1)} %get-tuple-element.28), channel_id=1, source_target_pairs={{0,1},{1,0},{2,3},{3,2},{4,5},{5,4},{6,7},{7,6},{8,9},{9,8},{10,11... | collective-permute-start | bytes 393224 | tf_op jit(solution)/shard_map/ppermute | solution.py:300
  2.7 0.1 collective-permute-start
  2.8 2.9 %collective-permute-start.1 = (bf16[4,32,512]{2,1,0:T(8,128)(2,1)S(1)}, bf16[4,32,512]{2,1,0:T(8,128)(2,1)S(1)}, u32[]{:S(2)}, u32[]{:S(2)}) collective-permute-start(bf16[4,32,512]{2,1,0:T(8,128)(2,1)S(1)} %get-tuple-element.27), channel_id=1, source_target_pairs={{0,2},{2,0},{1,3},{3,1},{4,6},{6,4},{5,7},{7,5},{8,10},{10,8},{9,1... | collective-permute-start | bytes 393224 | tf_op jit(solution)/shard_map/ppermute | solution.py:300
  5.7 0.0 collective-permute-done.2
  5.7 0.8 %collective-permute-start.3 = (bf16[4,32,512]{2,1,0:T(8,128)(2,1)S(1)}, bf16[4,32,512]{2,1,0:T(8,128)(2,1)S(1)}, u32[]{:S(2)}, u32[]{:S(2)}) collective-permute-start(bf16[4,32,512]{2,1,0:T(8,128)(2,1)S(1)} %collective-permute-done.2), channel_id=1, source_target_pairs={{0,2},{2,0},{1,3},{3,1},{4,6},{6,4},{5,7},{7,5},{8,10},{10,8},{9,1... | collective-permute-start | bytes 393224 | tf_op jit(solution)/shard_map/ppermute | solution.py:300
  6.6 0.8 %reshape.16.names_ref = s32[16,16]{1,0:T(8,128)S(1)} reshape(s32[256]{0:T(256)} %param.10) | data formatting | bytes 2048 | tf_op jit(solution)/shard_map/reshape | solution.py:343
  7.3 1.2 %copy.9.w_ref = bf16[4,2,256,32]{3,2,1,0:T(8,128)(2,1)S(1)} copy(bf16[4,2,256,32]{2,3,1,0:T(8,128)(2,1)} %param.13) | data formatting | bytes 262144 | tf_op args[6]
  8.5 0.0 copy-start.2
  8.5 0.7 %copy-done.2 = f32[16,16]{1,0:T(8,128)S(1)} copy-done((f32[16,16]{1,0:T(8,128)S(1)}, f32[16,16]{1,0:T(8,128)}, u32[]{:S(2)}) %copy-start.2) | copy-done | bytes 1048
  9.2 0.3 weight_shares.1
  9.5 1.6 %collective-permute-start.4 = (bf16[64,256]{1,0:T(8,128)(2,1)S(1)}, bf16[64,256]{1,0:T(8,128)(2,1)S(1)}, u32[]{:S(2)}, u32[]{:S(2)}) collective-permute-start(bf16[64,256]{1,0:T(8,128)(2,1)S(1)} %get-tuple-element.31), channel_id=1, source_target_pairs={{0,4},{4,0},{8,12},{12,8},{1,5},{5,1},{9,13},{13,9},{2,6},{6,2},{1... | collective-permute-start | bytes 98312 | tf_op jit(solution)/shard_map/ppermute | solution.py:300
  11.2 0.0 collective-permute-done.refs_1_
  11.2 0.0 collective-permute-done.1.refs_2_
  11.2 1.1 %collective-permute-done.3.refs_3_ = bf16[4,32,512]{2,1,0:T(8,128)(2,1)S(1)} collective-permute-done((bf16[4,32,512]{2,1,0:T(8,128)(2,1)S(1)}, bf16[4,32,512]{2,1,0:T(8,128)(2,1)S(1)}, u32[]{:S(2)}, u32[]{:S(2)}) %collective-permute-start.3) | collective-permute-done | bytes 131104 | tf_op jit(solution)/shard_map/ppermute | solution.py:300
  12.3 0.2 plane_sums.1
  12.5 1.9 %collective-permute-start.7 = (bf16[64,512]{1,0:T(8,128)(2,1)S(1)}, bf16[64,512]{1,0:T(8,128)(2,1)S(1)}, u32[]{:S(2)}, u32[]{:S(2)}) collective-permute-start(bf16[64,512]{1,0:T(8,128)(2,1)S(1)} %get-tuple-element.35), channel_id=1, source_target_pairs={{0,4},{4,0},{8,12},{12,8},{1,5},{5,1},{9,13},{13,9},{2,6},{6,2},{1... | collective-permute-start | bytes 196616 | tf_op jit(solution)/shard_map/ppermute | solution.py:300
  14.4 2.6 %collective-permute-start.8 = (bf16[64,512]{1,0:T(8,128)(2,1)S(1)}, bf16[64,512]{1,0:T(8,128)(2,1)S(1)}, u32[]{:S(2)}, u32[]{:S(2)}) collective-permute-start(bf16[64,512]{1,0:T(8,128)(2,1)S(1)} %get-tuple-element.36), channel_id=1, source_target_pairs={{0,8},{4,12},{8,0},{12,4},{1,9},{5,13},{9,1},{13,5},{2,10},{6,14},... | collective-permute-start | bytes 196616 | tf_op jit(solution)/shard_map/ppermute | solution.py:300
  17.0 0.0 collective-permute-start.9
  17.0 1.9 %collective-permute-start.5 = (bf16[64,256]{1,0:T(8,128)(2,1)S(1)}, bf16[64,256]{1,0:T(8,128)(2,1)S(1)}, u32[]{:S(2)}, u32[]{:S(2)}) collective-permute-start(bf16[64,256]{1,0:T(8,128)(2,1)S(1)} %get-tuple-element.32), channel_id=1, source_target_pairs={{0,8},{4,12},{8,0},{12,4},{1,9},{5,13},{9,1},{13,5},{2,10},{6,14},... | collective-permute-start | bytes 98312 | tf_op jit(solution)/shard_map/ppermute | solution.py:300
  18.9 0.0 collective-permute-done.4.refs_1_
  18.9 1.9 %collective-permute-start.6 = (bf16[64,256]{1,0:T(8,128)(2,1)S(1)}, bf16[64,256]{1,0:T(8,128)(2,1)S(1)}, u32[]{:S(2)}, u32[]{:S(2)}) collective-permute-start(bf16[64,256]{1,0:T(8,128)(2,1)S(1)} %get-tuple-element.33), channel_id=1, source_target_pairs={{0,12},{4,8},{8,4},{12,0},{1,13},{5,9},{9,5},{13,1},{2,14},{6,10},... | collective-permute-start | bytes 98312 | tf_op jit(solution)/shard_map/ppermute | solution.py:300
  20.8 4.1 %collective-permute-done.5.refs_2_ = bf16[64,256]{1,0:T(8,128)(2,1)S(1)} collective-permute-done((bf16[64,256]{1,0:T(8,128)(2,1)S(1)}, bf16[64,256]{1,0:T(8,128)(2,1)S(1)}, u32[]{:S(2)}, u32[]{:S(2)}) %collective-permute-start.5) | collective-permute-done | bytes 32800 | tf_op jit(solution)/shard_map/ppermute | solution.py:300
  24.9 0.0 collective-permute-done.6.refs_3_
  24.9 0.0 collective-permute-done.7.refs_1_
  24.9 0.0 collective-permute-done.8.refs_2_
  24.9 0.0 collective-permute-done.9.refs_3_
  24.9 0.6 %station_filter.1 = bf16[64,512]{1,0:T(8,128)(2,1)S(1)} custom-call(f32[16,512]{1,0:T(8,128)S(1)} %get-tuple-element.23.taps_ref, bf16[64,512]{1,0:T(8,128)(2,1)S(1)} %get-tuple-element.34.refs_0_, bf16[64,512]{1,0:T(8,128)(2,1)S(1)} %collective-permute-done.7.refs_1_, bf16[64,512]{1,0:T(8,128)(2,1)S(1)} %collective-permute-done.8.refs_2_, ...), custom_call_target="tpu_custom_call" | custom-call | tf_op jit(solution)/shard_map/station_filter/pallas_call | solution.py:369
  25.6 2.5 %collective-permute-start.12 = (bf16[64,512]{1,0:T(8,128)(2,1)S(1)}, bf16[64,512]{1,0:T(8,128)(2,1)S(1)}, u32[]{:S(2)}, u32[]{:S(2)}) collective-permute-start(bf16[64,512]{1,0:T(8,128)(2,1)S(1)} %station_filter.1), channel_id=1, source_target_pairs={{0,12},{4,8},{8,4},{12,0},{1,13},{5,9},{9,5},{13,1},{2,14},{6,10},... | collective-permute-start | bytes 196616 | tf_op jit(solution)/shard_map/ppermute | solution.py:300
  28.1 0.0 collective-permute-start.11
  28.1 1.9 %collective-permute-start.10 = (bf16[64,512]{1,0:T(8,128)(2,1)S(1)}, bf16[64,512]{1,0:T(8,128)(2,1)S(1)}, u32[]{:S(2)}, u32[]{:S(2)}) collective-permute-start(bf16[64,512]{1,0:T(8,128)(2,1)S(1)} %station_filter.1), channel_id=1, source_target_pairs={{0,4},{4,0},{8,12},{12,8},{1,5},{5,1},{9,13},{13,9},{2,6},{6,2},{1... | collective-permute-start | bytes 196616 | tf_op jit(solution)/shard_map/ppermute | solution.py:300
  30.0 2.1 %collective-permute-done.12 = bf16[64,512]{1,0:T(8,128)(2,1)S(1)} collective-permute-done((bf16[64,512]{1,0:T(8,128)(2,1)S(1)}, bf16[64,512]{1,0:T(8,128)(2,1)S(1)}, u32[]{:S(2)}, u32[]{:S(2)}) %collective-permute-start.12) | collective-permute-done | bytes 65568 | tf_op jit(solution)/shard_map/ppermute | solution.py:300
  32.1 1.4 %collective-permute-done.11 = bf16[64,512]{1,0:T(8,128)(2,1)S(1)} collective-permute-done((bf16[64,512]{1,0:T(8,128)(2,1)S(1)}, bf16[64,512]{1,0:T(8,128)(2,1)S(1)}, u32[]{:S(2)}, u32[]{:S(2)}) %collective-permute-start.11) | collective-permute-done | bytes 65568 | tf_op jit(solution)/shard_map/ppermute | solution.py:300
  33.5 0.0 collective-permute-done.10
  33.5 1.6 %collective-permute-start.13 = (bf16[4,64,512]{2,1,0:T(8,128)(2,1)S(1)}, bf16[4,64,512]{2,1,0:T(8,128)(2,1)S(1)}, u32[]{:S(2)}, u32[]{:S(2)}) collective-permute-start(bf16[4,64,512]{2,1,0:T(8,128)(2,1)S(1)} %pad_maximum_fusion.a), channel_id=1, source_target_pairs={{0,2},{2,0},{1,3},{3,1},{4,6},{6,4},{5,7},{7,5},{8,10},{10,8},{9,1... | collective-permute-start | bytes 786440 | tf_op jit(solution)/shard_map/ppermute | solution.py:300
  35.1 0.0 collective-permute-start.14
  35.1 5.1 %collective-permute-done.13.b = bf16[4,64,512]{2,1,0:T(8,128)(2,1)S(1)} collective-permute-done((bf16[4,64,512]{2,1,0:T(8,128)(2,1)S(1)}, bf16[4,64,512]{2,1,0:T(8,128)(2,1)S(1)}, u32[]{:S(2)}, u32[]{:S(2)}) %collective-permute-start.13) | collective-permute-done | bytes 262176 | tf_op jit(solution)/shard_map/ppermute | solution.py:300
  40.1 0.0 collective-permute-start.15
  40.2 0.1 dynamic-slice_bitcast_fusion
  40.2 0.1 copy.10.beam_ref
  40.3 0.7 %copy-done.4 = s32[32,1]{0,1:T(1,128)S(1)} copy-done((s32[32,1]{0,1:T(1,128)S(1)}, s32[32,1]{0,1:T(1,128)}, u32[]{:S(2)}) %copy-start.4) | copy-done | bytes 152
  41.0 0.7 %weight_matrix.1.rest_0_ = bf16[4,128,1024]{2,1,0:T(8,128)(2,1)S(1)} custom-call(s32[1,32]{1,0:T(1,128)S(1)} %bitcast.9, s32[64,1]{1,0:T(8,128)S(1)} %copy.10.beam_ref, bf16[64,256]{1,0:T(8,128)(2,1)S(1)} %get-tuple-element.38.refs_0_, bf16[64,256]{1,0:T(8,128)(2,1)S(1)} %collective-permute-done.4.refs_1_, ...), custom_call_target="tpu_custom_call" | custom-call | flops 1000000000 | bytes 2097152 | tf_op jit(solution)/shard_map/weight_matrix/pallas_call | solution.py:359
  41.7 0.0 collective-permute-done.14.c
  41.7 0.0 collective-permute-done.15.d
  41.7 7.7 %beams_and_series.1 = (f32[128,2,8,512]{3,2,1,0:T(8,128)}, f32[4,2,8,32]{3,2,1,0:T(8,128)}) custom-call(bf16[4,64,512]{2,1,0:T(8,128)(2,1)S(1)} %pad_maximum_fusion.a, bf16[4,64,512]{2,1,0:T(8,128)(2,1)S(1)} %collective-permute-done.13.b, bf16[4,64,512]{2,1,0:T(8,128)(2,1)S(1)} %collective-permute-done.14.c, ...), custom_call_target="tpu_custom_call" | custom-call | tf_op jit(solution)/shard_map/beams_and_series/pallas_call | solution.py:276
  (5 shorter events, 0.0 us)
Async XLA Ops:
  0.6 39.5 %copy-start = (s32[1024]{0:T(1024)S(1)}, s32[1024]{0:T(1024)}, u32[]{:S(2)}) copy-start(s32[1024]{0:T(1024)} %param.12) | copy-start | bytes 12292
  0.6 1.0 %copy-start.1 = (bf16[16,2,16,512]{3,2,1,0:T(8,128)(2,1)S(1)}, bf16[16,2,16,512]{3,2,1,0:T(8,128)(2,1)}, u32[]{:S(2)}) copy-start(bf16[16,2,16,512]{3,2,1,0:T(8,128)(2,1)} %x_ref.1) | copy-start | bytes 1572868
  1.7 40.0 %copy-start.3 = (f32[16,16]{1,0:T(8,128)S(1)}, f32[16,16]{1,0:T(8,128)}, u32[]{:S(2)}) copy-start(f32[16,16]{1,0:T(8,128)} %rest_1_.1) | copy-start | bytes 3076
  2.2 3.5 %collective-permute-start.2 = (bf16[4,32,512]{2,1,0:T(8,128)(2,1)S(1)}, bf16[4,32,512]{2,1,0:T(8,128)(2,1)S(1)}, u32[]{:S(2)}, u32[]{:S(2)}) collective-permute-start(bf16[4,32,512]{2,1,0:T(8,128)(2,1)S(1)} %get-tuple-element.28), channel_id=1, source_target_pairs={{0,1},{1,0},{2,3},{3,2},{4,5},{5,4},{6,7},{7,6},{8,9},{9,8},{10,11... | collective-permute-start | bytes 393224 | tf_op jit(solution)/shard_map/ppermute | solution.py:300
  2.7 8.5 %collective-permute-start = (bf16[4,32,512]{2,1,0:T(8,128)(2,1)S(1)}, bf16[4,32,512]{2,1,0:T(8,128)(2,1)S(1)}, u32[]{:S(2)}, u32[]{:S(2)}) collective-permute-start(bf16[4,32,512]{2,1,0:T(8,128)(2,1)S(1)} %get-tuple-element.26), channel_id=1, source_target_pairs={{0,1},{1,0},{2,3},{3,2},{4,5},{5,4},{6,7},{7,6},{8,9},{9,8},{10,11... | collective-permute-start | bytes 393224 | tf_op jit(solution)/shard_map/ppermute | solution.py:300
  2.8 8.4 %collective-permute-start.1 = (bf16[4,32,512]{2,1,0:T(8,128)(2,1)S(1)}, bf16[4,32,512]{2,1,0:T(8,128)(2,1)S(1)}, u32[]{:S(2)}, u32[]{:S(2)}) collective-permute-start(bf16[4,32,512]{2,1,0:T(8,128)(2,1)S(1)} %get-tuple-element.27), channel_id=1, source_target_pairs={{0,2},{2,0},{1,3},{3,1},{4,6},{6,4},{5,7},{7,5},{8,10},{10,8},{9,1... | collective-permute-start | bytes 393224 | tf_op jit(solution)/shard_map/ppermute | solution.py:300
  5.7 6.5 %collective-permute-start.3 = (bf16[4,32,512]{2,1,0:T(8,128)(2,1)S(1)}, bf16[4,32,512]{2,1,0:T(8,128)(2,1)S(1)}, u32[]{:S(2)}, u32[]{:S(2)}) collective-permute-start(bf16[4,32,512]{2,1,0:T(8,128)(2,1)S(1)} %collective-permute-done.2), channel_id=1, source_target_pairs={{0,2},{2,0},{1,3},{3,1},{4,6},{6,4},{5,7},{7,5},{8,10},{10,8},{9,1... | collective-permute-start | bytes 393224 | tf_op jit(solution)/shard_map/ppermute | solution.py:300
  8.5 0.7 %copy-start.2 = (f32[16,16]{1,0:T(8,128)S(1)}, f32[16,16]{1,0:T(8,128)}, u32[]{:S(2)}) copy-start(f32[16,16]{1,0:T(8,128)} %taps_ref.1) | copy-start | bytes 3076
  9.5 9.4 %collective-permute-start.4 = (bf16[64,256]{1,0:T(8,128)(2,1)S(1)}, bf16[64,256]{1,0:T(8,128)(2,1)S(1)}, u32[]{:S(2)}, u32[]{:S(2)}) collective-permute-start(bf16[64,256]{1,0:T(8,128)(2,1)S(1)} %get-tuple-element.31), channel_id=1, source_target_pairs={{0,4},{4,0},{8,12},{12,8},{1,5},{5,1},{9,13},{13,9},{2,6},{6,2},{1... | collective-permute-start | bytes 98312 | tf_op jit(solution)/shard_map/ppermute | solution.py:300
  12.5 12.4 %collective-permute-start.7 = (bf16[64,512]{1,0:T(8,128)(2,1)S(1)}, bf16[64,512]{1,0:T(8,128)(2,1)S(1)}, u32[]{:S(2)}, u32[]{:S(2)}) collective-permute-start(bf16[64,512]{1,0:T(8,128)(2,1)S(1)} %get-tuple-element.35), channel_id=1, source_target_pairs={{0,4},{4,0},{8,12},{12,8},{1,5},{5,1},{9,13},{13,9},{2,6},{6,2},{1... | collective-permute-start | bytes 196616 | tf_op jit(solution)/shard_map/ppermute | solution.py:300
  14.4 10.5 %collective-permute-start.8 = (bf16[64,512]{1,0:T(8,128)(2,1)S(1)}, bf16[64,512]{1,0:T(8,128)(2,1)S(1)}, u32[]{:S(2)}, u32[]{:S(2)}) collective-permute-start(bf16[64,512]{1,0:T(8,128)(2,1)S(1)} %get-tuple-element.36), channel_id=1, source_target_pairs={{0,8},{4,12},{8,0},{12,4},{1,9},{5,13},{9,1},{13,5},{2,10},{6,14},... | collective-permute-start | bytes 196616 | tf_op jit(solution)/shard_map/ppermute | solution.py:300
  17.0 8.0 %collective-permute-start.9 = (bf16[64,512]{1,0:T(8,128)(2,1)S(1)}, bf16[64,512]{1,0:T(8,128)(2,1)S(1)}, u32[]{:S(2)}, u32[]{:S(2)}) collective-permute-start(bf16[64,512]{1,0:T(8,128)(2,1)S(1)} %get-tuple-element.37), channel_id=1, source_target_pairs={{0,12},{4,8},{8,4},{12,0},{1,13},{5,9},{9,5},{13,1},{2,14},{6,10},... | collective-permute-start | bytes 196616 | tf_op jit(solution)/shard_map/ppermute | solution.py:300
  17.0 7.9 %collective-permute-start.5 = (bf16[64,256]{1,0:T(8,128)(2,1)S(1)}, bf16[64,256]{1,0:T(8,128)(2,1)S(1)}, u32[]{:S(2)}, u32[]{:S(2)}) collective-permute-start(bf16[64,256]{1,0:T(8,128)(2,1)S(1)} %get-tuple-element.32), channel_id=1, source_target_pairs={{0,8},{4,12},{8,0},{12,4},{1,9},{5,13},{9,1},{13,5},{2,10},{6,14},... | collective-permute-start | bytes 98312 | tf_op jit(solution)/shard_map/ppermute | solution.py:300
  18.9 6.0 %collective-permute-start.6 = (bf16[64,256]{1,0:T(8,128)(2,1)S(1)}, bf16[64,256]{1,0:T(8,128)(2,1)S(1)}, u32[]{:S(2)}, u32[]{:S(2)}) collective-permute-start(bf16[64,256]{1,0:T(8,128)(2,1)S(1)} %get-tuple-element.33), channel_id=1, source_target_pairs={{0,12},{4,8},{8,4},{12,0},{1,13},{5,9},{9,5},{13,1},{2,14},{6,10},... | collective-permute-start | bytes 98312 | tf_op jit(solution)/shard_map/ppermute | solution.py:300
  25.6 6.5 %collective-permute-start.12 = (bf16[64,512]{1,0:T(8,128)(2,1)S(1)}, bf16[64,512]{1,0:T(8,128)(2,1)S(1)}, u32[]{:S(2)}, u32[]{:S(2)}) collective-permute-start(bf16[64,512]{1,0:T(8,128)(2,1)S(1)} %station_filter.1), channel_id=1, source_target_pairs={{0,12},{4,8},{8,4},{12,0},{1,13},{5,9},{9,5},{13,1},{2,14},{6,10},... | collective-permute-start | bytes 196616 | tf_op jit(solution)/shard_map/ppermute | solution.py:300
  28.1 5.4 %collective-permute-start.11 = (bf16[64,512]{1,0:T(8,128)(2,1)S(1)}, bf16[64,512]{1,0:T(8,128)(2,1)S(1)}, u32[]{:S(2)}, u32[]{:S(2)}) collective-permute-start(bf16[64,512]{1,0:T(8,128)(2,1)S(1)} %station_filter.1), channel_id=1, source_target_pairs={{0,8},{4,12},{8,0},{12,4},{1,9},{5,13},{9,1},{13,5},{2,10},{6,14},... | collective-permute-start | bytes 196616 | tf_op jit(solution)/shard_map/ppermute | solution.py:300
  28.1 5.4 %collective-permute-start.10 = (bf16[64,512]{1,0:T(8,128)(2,1)S(1)}, bf16[64,512]{1,0:T(8,128)(2,1)S(1)}, u32[]{:S(2)}, u32[]{:S(2)}) collective-permute-start(bf16[64,512]{1,0:T(8,128)(2,1)S(1)} %station_filter.1), channel_id=1, source_target_pairs={{0,4},{4,0},{8,12},{12,8},{1,5},{5,1},{9,13},{13,9},{2,6},{6,2},{1... | collective-permute-start | bytes 196616 | tf_op jit(solution)/shard_map/ppermute | solution.py:300
  33.5 6.6 %collective-permute-start.13 = (bf16[4,64,512]{2,1,0:T(8,128)(2,1)S(1)}, bf16[4,64,512]{2,1,0:T(8,128)(2,1)S(1)}, u32[]{:S(2)}, u32[]{:S(2)}) collective-permute-start(bf16[4,64,512]{2,1,0:T(8,128)(2,1)S(1)} %pad_maximum_fusion.a), channel_id=1, source_target_pairs={{0,2},{2,0},{1,3},{3,1},{4,6},{6,4},{5,7},{7,5},{8,10},{10,8},{9,1... | collective-permute-start | bytes 786440 | tf_op jit(solution)/shard_map/ppermute | solution.py:300
  35.1 6.6 %collective-permute-start.14 = (bf16[4,64,512]{2,1,0:T(8,128)(2,1)S(1)}, bf16[4,64,512]{2,1,0:T(8,128)(2,1)S(1)}, u32[]{:S(2)}, u32[]{:S(2)}) collective-permute-start(bf16[4,64,512]{2,1,0:T(8,128)(2,1)S(1)} %pad_maximum_fusion.a), channel_id=1, source_target_pairs={{0,1},{1,0},{2,3},{3,2},{4,5},{5,4},{6,7},{7,6},{8,9},{9,8},{10,11... | collective-permute-start | bytes 786440 | tf_op jit(solution)/shard_map/ppermute | solution.py:300
  40.1 1.5 %collective-permute-start.15 = (bf16[4,64,512]{2,1,0:T(8,128)(2,1)S(1)}, bf16[4,64,512]{2,1,0:T(8,128)(2,1)S(1)}, u32[]{:S(2)}, u32[]{:S(2)}) collective-permute-start(bf16[4,64,512]{2,1,0:T(8,128)(2,1)S(1)} %collective-permute-done.13.b), channel_id=1, source_target_pairs={{0,1},{1,0},{2,3},{3,2},{4,5},{5,4},{6,7},{7,6},{8,9},{9,8},{10,11... | collective-permute-start | bytes 786440 | tf_op jit(solution)/shard_map/ppermute | solution.py:300
  40.3 0.7 %copy-start.4 = (s32[32,1]{0,1:T(1,128)S(1)}, s32[32,1]{0,1:T(1,128)}, u32[]{:S(2)}) copy-start(s32[32,1]{0,1:T(1,128)} %param.11) | copy-start | bytes 388

commit v3 on v2

--- a/solution.py
+++ b/solution.py
@@ -10,7 +10,7 @@
 
 ANTENNAS_PER_STN = 8
 SPEC = 512
-VMEM_LIMIT = 32 * 1024 * 1024
+VMEM_LIMIT = 24 * 1024 * 1024
 HALO = 128
 
 
@@ -39,7 +39,10 @@
     return sub * 8 + col * 4 + row
 
 
-def spread_kernel(axes, x_ref, *out_refs):
+def spread_kernel(axes, x_hbm, *refs):
+    out_refs, (x_ref, sem) = refs[:-2], refs[-2:]
+    load = pltpu.make_async_copy(x_hbm, x_ref, sem)
+    load.start()
     row, col, sub = (lax.axis_index(a) for a in axes)
     antennas, parts, chan, frames = x_ref.shape
     count = antennas * parts * chan
@@ -48,31 +51,65 @@
     antenna = place % antennas
     part = place // antennas % parts
     piece = place // (antennas * parts)
-    lane = lane_of(row ^ (piece % 4), col ^ (piece // 4 % 2), sub ^ (piece // 8))
+    lane = lane_of(row ^ (piece % 4) ^ 2, col ^ (piece // 4 % 2), sub ^ (piece // 8))
     source = (antenna * parts + part) * chan + lane
     order = jnp.where(lax.broadcasted_iota(jnp.int32, shape, 1) == source, 1.0, 0.0)
+    order = order.astype(jnp.bfloat16)
+    load.wait()
     moved = jnp.dot(
-        order.astype(jnp.bfloat16),
+        order,
         x_ref[...].reshape(count, frames),
         preferred_element_type=jnp.float32,
     ).astype(jnp.bfloat16)
-    size = count // len(out_refs)
+    start = 0
+    for ref in out_refs:
+        size = ref.shape[0] * ref.shape[1]
+        ref[...] = moved[start : start + size].reshape(ref.shape)
+        start += size
+
+
+def member_matrix(axes, names_ref, stations, local):
+    row, col, sub = (lax.axis_index(a) for a in axes)
+    antennas = 16 * local
+    every = jnp.broadcast_to(names_ref[:, :antennas], (8, antennas))
+    names = []
+    for k in range(4):
+        owner = (row * 2 + (col ^ (k // 2))) * 2 + (sub ^ (k % 2))
+        names += [pltpu.roll(every, lax.rem(antennas - owner * local, antennas), 1)[:1, :local]] * 2
+    names = jnp.concatenate(names, axis=1)
+    shape = (2 * stations, 8 * local)
+    place = lax.broadcasted_iota(jnp.int32, shape, 0)
+    column = lax.broadcasted_iota(jnp.int32, shape, 1)
+    same = ((place % stations).astype(jnp.float32) == names) & (place // stations == column // local % 2)
+    return jnp.where(same, 1.0, 0.0).astype(jnp.bfloat16)
+
+
+def own_taps(axes, taps, count, chan):
+    lane = lane_of(*(lax.axis_index(a) for a in axes))
+    shape = (count, count * chan)
+    column = lax.broadcasted_iota(jnp.int32, shape, 1)
+    mine = column == lax.broadcasted_iota(jnp.int32, shape, 0) * chan + lane
+    taps = jnp.where(mine, jnp.broadcast_to(taps, shape), 0.0)
+    return jnp.sum(taps, axis=1, keepdims=True)
+
+
+def sum_kernel(axes, first, names_ref, *refs):
+    x_refs, out_refs = refs[:4], refs[4:6]
+    for taps_ref in refs[6:]:
+        count = taps_ref.shape[0]
+        taps = names_ref[:, names_ref.shape[1] - count * count :]
+        taps_ref[...] = jnp.broadcast_to(own_taps(axes, taps, count, count), taps_ref.shape)
+    stations, local = out_refs[0].shape[0] // 2, x_refs[0].shape[1] // 2
+    members = member_matrix(axes, names_ref, stations, local)
     for k, ref in enumerate(out_refs):
-        ref[...] = moved[k * size : (k + 1) * size].reshape(ref.shape)
-
-
-def sum_kernel(members_ref, *refs):
-    x_refs, out_refs = refs[:4], refs[4:]
-    for m, ref in enumerate(out_refs):
-        rows = jnp.concatenate([x[m] for x in x_refs], axis=0)
-        ref[...] = jnp.dot(
-            members_ref[...], rows, preferred_element_type=jnp.float32
-        ).astype(ref.dtype)
+        rows = jnp.concatenate([x[first + k if x.shape[0] == 4 else k] for x in x_refs], axis=0)
+        ref[...] = jnp.dot(members, rows, preferred_element_type=jnp.float32).astype(ref.dtype)
 
 
 def filter_kernel(taps_ref, *refs):
-    x_refs, out_ref = refs[:-1], refs[-1]
-    total = x_refs[0][...].astype(jnp.float32)
+    x_refs, share_refs, out_refs = refs[:4], refs[4:7], refs[7:]
+    rows = out_refs[0].shape[0]
+    total = x_refs[0][...]
     for ref in x_refs[1:]:
         total = total + ref[...].astype(jnp.float32)
     place = lax.broadcasted_iota(jnp.int32, total.shape, 1)
@@ -80,66 +117,26 @@
     for tap in range(1, taps_ref.shape[0]):
         moved = jnp.where(place >= tap, pltpu.roll(total, tap, 1), 0.0)
         result = result + moved * taps_ref[tap : tap + 1]
-    out_ref[...] = result.astype(out_ref.dtype)
-
-
-def pack_kernel(axes, w_ref, names_ref, taps_ref, members_ref, own_taps_ref, *out_refs):
-    row, col, sub = (lax.axis_index(a) for a in axes)
-    names = []
-    for k in range(4):
-        owner = (row * 2 + (col ^ (k // 2))) * 2 + (sub ^ (k % 2))
-        names += [names_ref[pl.ds(owner, 1)]] * 2
-    names = jnp.concatenate(names, axis=1)
-    local = names_ref.shape[1]
-    place = lax.broadcasted_iota(jnp.int32, members_ref.shape, 0)
-    column = lax.broadcasted_iota(jnp.int32, members_ref.shape, 1)
-    wanted = members_ref.shape[0] // 2
-    same = (place % wanted == names) & (place // wanted == column // local % 2)
-    members_ref[...] = jnp.where(same, 1.0, 0.0).astype(members_ref.dtype)
-    taps = taps_ref[...]
-    mine = lax.broadcasted_iota(jnp.int32, taps.shape, 1) == lane_of(row, col, sub)
-    own = jnp.sum(jnp.where(mine, taps, 0.0), axis=1, keepdims=True)
-    own_taps_ref[...] = jnp.broadcast_to(own, own_taps_ref.shape)
-    chan, _, _, stations = w_ref.shape
-    beams = out_refs[0].shape[0]
-    for mask, ref in enumerate(out_refs):
-        first = pl.multiple_of((row ^ mask) * beams, beams)
-        for k in range(chan):
-            for q in range(2):
-                place = (2 * k + q) * stations
-                ref[:, place : place + stations] = w_ref[k, q, pl.ds(first, beams)]
-
-
-def weight_kernel(axes, groups_ref, beam_ref, *refs):
+    result = result.astype(out_refs[0].dtype)
+    out_refs[0][...] = result
+    for ref, share in zip(out_refs[1:], share_refs):
+        ref[:rows] = result
+        ref[rows:] = share[...]
+
+
+def pack_kernel(axes, w_ref, *out_refs):
     row = lax.axis_index(axes[0])
-    w_refs, m_ref, all_ref = refs[:4], refs[4], refs[5]
-    stations = groups_ref.shape[1]
-    held = w_refs[0].shape[1] // (2 * stations)
-    chan = 4 * held
-    for mask, ref in enumerate(w_refs):
-        all_ref[row ^ mask] = ref[...]
-    members = groups_ref[...] == beam_ref[...]
-    count = jnp.sum(members.astype(jnp.float32), axis=1, keepdims=True)
-    scale = (1.0 / (chan * math.sqrt(ANTENNAS_PER_STN))) / jnp.sqrt(count)
-    zero = jnp.zeros((), jnp.float32)
-    parts = []
+    chan, _, _, width = w_ref.shape
+    beams = width // 4
     for k in range(chan):
-        whole = all_ref[k // held].astype(jnp.float32)
-        places = [(2 * (k % held) + q) * stations for q in range(2)]
-        parts.append(
-            tuple(jnp.where(members, whole[:, p : p + stations], zero) for p in places)
-        )
-    parts = fourier(parts, -1.0)
-    real = [p[0] * scale for p in parts]
-    imag = [p[1] * scale for p in parts]
-    upper = jnp.concatenate([v for k in range(chan) for v in (real[k], -imag[k])], axis=1)
-    lower = jnp.concatenate([v for k in range(chan) for v in (imag[k], real[k])], axis=1)
-    whole = jnp.concatenate([upper, lower], axis=0).astype(m_ref.dtype)
-    width = whole.shape[1] // 4
-    for u in range(4):
-        for j in range(4):
-            t = (u + j) % 4
-            m_ref[u, :, t * width : (t + 1) * width] = whole[:, j * width : (j + 1) * width]
+        for q in range(2):
+            place = (2 * k + q) * beams
+            parts = [w_ref[k, q, :, j * beams : (j + 1) * beams] for j in range(4)]
+            for mask, ref in enumerate(out_refs):
+                taken = parts[0]
+                for j in range(1, 4):
+                    taken = jnp.where((row ^ mask) == j, parts[j], taken)
+                ref[:, place : place + beams] = taken
 
 
 def bands(taps_ref, lane, rows, cols):
@@ -155,16 +152,58 @@
     return jnp.concatenate([high[:HALO], low[:HALO], high[HALO:], low[HALO:]], axis=0)
 
 
+def weight_kernel(axes, groups_ref, beam_ref, taps_ref, *refs):
+    row, col, sub = (lax.axis_index(a) for a in axes)
+    w_refs, (m_ref, t_ref, all_ref) = refs[:4], refs[4:]
+    stations, beams = groups_ref.shape[1], m_ref.shape[1] // 2
+    held = all_ref.shape[2] // (2 * beams)
+    chan = 4 * held
+    for mask, ref in enumerate(w_refs):
+        all_ref[row ^ mask] = ref[ref.shape[0] - stations :]
+    square = (stations, stations)
+    diagonal = lax.broadcasted_iota(jnp.int32, square, 0) == lax.broadcasted_iota(
+        jnp.int32, square, 1
+    )
+    groups = jnp.broadcast_to(groups_ref[...], square).astype(jnp.float32)
+    groups = jnp.sum(jnp.where(diagonal, groups, 0.0), axis=1, keepdims=True)
+    total = beam_ref.shape[1]
+    first = ((col * 2 + sub) * 4 + row) * beams
+    every = jnp.broadcast_to(beam_ref[...], (8, total))
+    wanted = pltpu.roll(every, lax.rem(total - first, total), 1)[:1, :beams]
+    members = groups == wanted.astype(jnp.float32)
+    scale = (1.0 / (chan * math.sqrt(ANTENNAS_PER_STN))) / jnp.sqrt(
+        jnp.sum(members.astype(jnp.float32), axis=0, keepdims=True)
+    )
+    zero = jnp.zeros((), jnp.float32)
+    parts = []
+    for k in range(chan):
+        whole = all_ref[k // held].astype(jnp.float32)
+        places = [(2 * (k % held) + q) * beams for q in range(2)]
+        parts.append(tuple(jnp.where(members, whole[:, p : p + beams], zero) for p in places))
+    parts = fourier(parts, -1.0)
+    real = [p[0] * scale for p in parts]
+    imag = [p[1] * scale for p in parts]
+    upper = jnp.concatenate([v for k in range(chan) for v in (real[k], -imag[k])], axis=0)
+    lower = jnp.concatenate([v for k in range(chan) for v in (imag[k], real[k])], axis=0)
+    whole = jnp.concatenate([upper, lower], axis=1).T.astype(m_ref.dtype)
+    width = whole.shape[1] // 4
+    for u in range(4):
+        for j in range(4):
+            t = (u + j) % 4
+            m_ref[u, :, t * width : (t + 1) * width] = whole[:, j * width : (j + 1) * width]
+    for c in range(chan):
+        t_ref[c] = bands(taps_ref, c, t_ref.shape[1] // 2, t_ref.shape[2])
+
+
 def beam_kernel(
     axes,
     x_refs,
     m_ref,
-    taps_ref,
+    t_ref,
     series_ref,
     vis_ref,
     lanes_ref,
     cross_ref,
-    t_ref,
     inverse_ref,
     out_ref,
     store_sems,
@@ -177,7 +216,7 @@
 
     for place, ref in enumerate(x_refs):
         for m in range(4):
-            lane = lane_of(row ^ m, col ^ (place & 1), sub ^ (place >> 1))
+            lane = lane_of(row ^ m, col ^ (place % 2), sub ^ (place // 2))
             lanes_ref[pl.ds(pl.multiple_of(lane * rows, rows), rows)] = ref[m]
     wrap = 3 * rows
     lanes_ref[chan * rows : chan * rows + wrap] = lanes_ref[0:wrap]
@@ -185,8 +224,6 @@
     tile = t_ref.shape[2]
     stores = []
     for half in range(2):
-        for c in range(8):
-            t_ref[8 * half + c] = bands(taps_ref, 8 * half + c, HALO + tile, tile)
         some = m_ref[2 * half : 2 * half + 2].reshape(4 * beams, chan * rows)
         for v in range(4):
             window = lanes_ref[v * rows : (v + chan) * rows]
@@ -265,33 +302,31 @@
         copy.wait()
 
 
-def call_beams(axes, pieces, matrix, taps):
+def call_beams(axes, pieces, matrix, bands):
     params = pltpu.CompilerParams(vmem_limit_bytes=VMEM_LIMIT)
     vmem = pl.BlockSpec(memory_space=pltpu.VMEM)
-    smem = pl.BlockSpec(memory_space=pltpu.SMEM)
-    chan, frames, tile = taps.shape[1], pieces[0].shape[2], 256
+    chan, frames = bands.shape[0], pieces[0].shape[2]
     stations, beams = pieces[0].shape[1] // 2, matrix.shape[1] // 2
     anywhere = pl.BlockSpec(memory_space=pl.ANY)
     slots = frames // 128 * 2
     series, visibilities = pl.pallas_call(
-        lambda a, b, c, d, *rest: beam_kernel(axes, (a, b, c, d), *rest),
+        lambda *refs: beam_kernel(axes, refs[: len(pieces)], *refs[len(pieces) :]),
         out_shape=(
             jax.ShapeDtypeStruct((2 * beams, 2, 8, frames), jnp.float32),
             jax.ShapeDtypeStruct((4, 2, stations // 4, stations), jnp.float32),
         ),
-        in_specs=[vmem] * 5 + [smem],
+        in_specs=[vmem] * (len(pieces) + 2),
         out_specs=(anywhere, vmem),
         scratch_shapes=[
             pltpu.VMEM(((chan + 3) * 2 * stations, frames), jnp.bfloat16),
             pltpu.VMEM((2 * stations, 2 * stations), jnp.float32),
-            pltpu.VMEM((chan, 2 * (tile + HALO), tile), jnp.bfloat16),
             pltpu.VMEM((chan, 2 * beams, frames), jnp.bfloat16),
             pltpu.VMEM((slots, 2 * beams * 8, 128), jnp.float32),
             pltpu.SemaphoreType.DMA((slots,)),
         ],
         compiler_params=params,
         name="beams_and_series",
-    )(*pieces, matrix, taps)
+    )(*pieces, matrix, bands)
     return visibilities, series
 
 
@@ -307,6 +342,7 @@
     params = pltpu.CompilerParams(vmem_limit_bytes=VMEM_LIMIT)
     vmem = pl.BlockSpec(memory_space=pltpu.VMEM)
     smem = pl.BlockSpec(memory_space=pltpu.SMEM)
+    hbm = pl.BlockSpec(memory_space=pltpu.HBM)
     local, _, chan, frames = samples.shape
     stations = station_group.shape[0]
     antennas = antenna_station.shape[0]
@@ -314,72 +350,96 @@
     held_chan = beam_weights.shape[0]
     beams = beam_weights.shape[2] // 4
     block = jax.ShapeDtypeStruct((4, 2 * local, frames), jnp.bfloat16)
-    kept, crossing, paired, far = pl.pallas_call(
+    half = jax.ShapeDtypeStruct((2, 2 * local, frames), jnp.bfloat16)
+    kept, crossing_a, crossing_b, paired, far_a, far_b = pl.pallas_call(
         functools.partial(spread_kernel, axes),
-        out_shape=[block] * 4,
+        out_shape=[block, half, half, block, half, half],
+        in_specs=[hbm],
+        out_specs=[vmem] * 6,
+        scratch_shapes=[pltpu.VMEM(samples.shape, samples.dtype), pltpu.SemaphoreType.DMA],
+        compiler_params=params,
+        name="lane_spread",
+    )(samples)
+    far_a = swap(far_a, "sub", 1)
+    crossing_a = swap(crossing_a, "col", 1)
+    far_a = swap(far_a, "col", 1)
+    far_b = swap(far_b, "sub", 1)
+    paired = swap(paired, "sub", 1)
+    crossing_b = swap(crossing_b, "col", 1)
+    far_b = swap(far_b, "col", 1)
+
+    lane = jax.ShapeDtypeStruct((2 * stations, frames), jnp.bfloat16)
+    names = jnp.concatenate([antenna_station.astype(jnp.float32), analysis_taps.reshape(-1)])
+    names = names.reshape(1, -1)
+    sums2, sums3, taps = pl.pallas_call(
+        functools.partial(sum_kernel, axes, 0),
+        out_shape=[lane] * 2
+        + [jax.ShapeDtypeStruct((analysis_taps.shape[0], frames), jnp.float32)],
+        in_specs=[vmem] * 5,
+        out_specs=[vmem] * 3,
+        compiler_params=params,
+        name="plane_sums_far",
+    )(names, kept, paired, crossing_a, far_a)
+    sums3, sums2 = swap(sums3, "row", 3), swap(sums2, "row", 2)
+    sums0, sums1 = pl.pallas_call(
+        functools.partial(sum_kernel, axes, 2),
+        out_shape=[jax.ShapeDtypeStruct(lane.shape, jnp.float32), lane],
+        in_specs=[vmem] * 5,
+        out_specs=[vmem] * 2,
+        compiler_params=params,
+        name="plane_sums_near",
+    )(names, kept, paired, crossing_b, far_b)
+
+    share = jax.ShapeDtypeStruct((stations, 2 * held_chan * beams), jnp.bfloat16)
+    shares = pl.pallas_call(
+        functools.partial(pack_kernel, axes),
+        out_shape=[share] * 4,
         in_specs=[vmem],
         out_specs=[vmem] * 4,
         compiler_params=params,
-        name="lane_spread",
-    )(samples)
-    far = swap(far, "sub", 1)
-    crossed = swap(crossing, "col", 1)
-    paired = swap(paired, "sub", 1)
-    far = swap(far, "col", 1)
-
-    packed = jax.ShapeDtypeStruct((beams, held_chan * 2 * stations), jnp.bfloat16)
-    members, own_taps, *shares = pl.pallas_call(
-        functools.partial(pack_kernel, axes),
+        cost_estimate=pl.CostEstimate(flops=0, bytes_accessed=8 << 20, transcendentals=0),
+        name="weight_shares",
+    )(beam_weights.transpose(0, 1, 3, 2))
+
+    lane_share = jax.ShapeDtypeStruct((3 * stations, frames), jnp.bfloat16)
+    filtered, *sent = pl.pallas_call(
+        filter_kernel,
+        out_shape=[lane] + [lane_share] * 3,
+        in_specs=[vmem] * 8,
+        out_specs=[vmem] * 4,
+        compiler_params=params,
+        name="station_filter",
+    )(taps, sums0, swap(sums1, "row", 1), sums2, sums3, *shares[1:])
+    moved = [swap(x, "row", m) for x, m in zip(sent, (1, 2, 3))]
+
+    tile = 256
+    matrix, bands = pl.pallas_call(
+        functools.partial(weight_kernel, axes),
         out_shape=[
-            jax.ShapeDtypeStruct((2 * stations, 8 * local), jnp.bfloat16),
-            jax.ShapeDtypeStruct((analysis_taps.shape[0], frames), jnp.float32),
-        ]
-        + [packed] * 4,
-        in_specs=[vmem] * 3,
-        out_specs=[vmem] * 6,
-        compiler_params=params,
-        cost_estimate=pl.CostEstimate(flops=0, bytes_accessed=4 << 20, transcendentals=0),
-        name="weight_shares",
-    )(beam_weights, antenna_station.reshape(antennas // local, local), analysis_taps)
-    given = [shares[0]] + [swap(shares[m], "row", m) for m in (1, 2, 3)]
-    own = (lax.axis_index(("col", "sub", "row"))) * beams
-    own_groups = lax.dynamic_slice_in_dim(beam_group, own, beams, 0).reshape(beams, 1)
-
-    lane = jax.ShapeDtypeStruct((2 * stations, frames), jnp.bfloat16)
-    sums = pl.pallas_call(
-        sum_kernel,
-        out_shape=[lane] * 4,
-        in_specs=[vmem] * 5,
-        out_specs=[vmem] * 4,
-        compiler_params=params,
-        name="plane_sums",
-    )(members, kept, paired, crossed, far)
-    moved = [swap(sums[m], "row", m) for m in (1, 2, 3)]
-    first, *given = lax.optimization_barrier((sums[0], *given))
-    matrix = pl.pallas_call(
-        functools.partial(weight_kernel, axes),
-        out_shape=jax.ShapeDtypeStruct((4, 2 * beams, 2 * chan * stations), jnp.bfloat16),
-        in_specs=[vmem] * 6,
-        out_specs=vmem,
-        scratch_shapes=[pltpu.VMEM((4,) + packed.shape, jnp.bfloat16)],
-        compiler_params=params,
-        cost_estimate=pl.CostEstimate(flops=1_000_000_000, bytes_accessed=2 << 20, transcendentals=0),
+            jax.ShapeDtypeStruct((4, 2 * beams, 2 * chan * stations), jnp.bfloat16),
+            jax.ShapeDtypeStruct((chan, 2 * (tile + HALO), tile), jnp.bfloat16),
+        ],
+        in_specs=[vmem, vmem, smem] + [vmem] * 4,
+        out_specs=[vmem] * 2,
+        scratch_shapes=[pltpu.VMEM((4,) + share.shape, jnp.bfloat16)],
+        compiler_params=params,
+        cost_estimate=pl.CostEstimate(flops=2_000_000_000, bytes_accessed=2 << 20, transcendentals=0),
         name="weight_matrix",
-    )(station_group.reshape(1, stations), own_groups, *given)
-    filtered = pl.pallas_call(
-        filter_kernel,
-        out_shape=lane,
-        in_specs=[vmem] * 5,
-        out_specs=vmem,
-        compiler_params=params,
-        name="station_filter",
-    )(own_taps, first, *moved)
-
-    held = jnp.stack([filtered] + [swap(filtered, "row", m) for m in (1, 2, 3)])
+    )(
+        station_group.reshape(1, stations),
+        beam_group.reshape(1, beam_group.shape[0]),
+        synthesis_taps,
+        shares[0],
+        *moved,
+    )
+
+    held = jnp.stack([filtered] + [x[: 2 * stations] for x in moved])
     other = swap(held, "col", 1)
-    pieces = [held, other, swap(held, "sub", 1), swap(other, "sub", 1)]
-
-    visibilities, series = call_beams(axes, pieces, matrix, synthesis_taps)
+    other, matrix, bands = lax.optimization_barrier((other, matrix, bands))
+    pieces = [held, other]
+    pieces += [swap(x, "sub", 1) for x in pieces]
+
+    visibilities, series = call_beams(axes, pieces, matrix, bands)
     return visibilities, series.reshape(beams, 2, chan, frames)
 
 

time: 49.7 us -> 47.4 us (0.954)
  starting transfers between devices: 20.3 us -> 16.6 us
  Pallas kernels: 10 us -> 12.4 us
  waiting for transfers between devices: 13.8 us -> 11.9 us
  other arithmetic: 0.04 us -> 0.73 us
    ppermute x16, starting transfers between devices: 20.3 us -> 16.6 us  [swap(): return lax.ppermute(x, axis, [(i, i ^ mask) for i in range(size)])]
    pallas_call x6 -> x7, Pallas kernels: 10 us -> 12.4 us  [the longest x1 6.84 us: call_beams(): pl.pallas_call(lambda *refs: beam_kernel(axes, refs[:len(pieces)], *refs[...]
    ppermute x16, waiting for transfers between devices: 13.8 us -> 11.9 us  [swap(): return lax.ppermute(x, axis, [(i, i ^ mask) for i in range(size)])]
    convert_element_type x0 -> x1, other arithmetic: none -> 0.68 us  [fast_body(): antenna_station.astype(jnp.float32)]
    unnamed x11 -> x10, local copies, waits for them, and re-layouts: 3.6 us -> 3.98 us
  transfers between devices with their start and end apart: 16 -> 16, of which waited for: 5 -> 8; matrix products, arithmetic and copies ran while one was open for 4% -> 3% of each run, Pallas kernels for 2% -> 9%
where the time goes in v3:
time: 47.4 us; the launch traced here: 47.1 us
  starting transfers between devices  16.6 us (35%)
  Pallas kernels  12.4 us (26%)
  waiting for transfers between devices  11.9 us (25%)
  local copies, waits for them, and re-layouts  4.77 us (10%)
  other arithmetic  0.73 us (2%)
  between operations  0.72 us (2%)
    ppermute x16, starting transfers between devices, swap(): return lax.ppermute(x, axis, [(i, i ^ mask) for i in range(size)])  16.6 us
    ppermute x16, waiting for transfers between devices, swap(): return lax.ppermute(x, axis, [(i, i ^ mask) for i in range(size)])  11.9 us
    pallas_call x1, Pallas kernels, call_beams(): pl.pallas_call(lambda *refs: beam_kernel(axes, refs[:len(pieces)], *refs[...  6.84 us
    unnamed x10, local copies, waits for them, and re-layouts  3.98 us
    pallas_call x1, Pallas kernels, fast_body(): pl.pallas_call(functools.partial(weight_kernel, axes), out_shape=[jax.Sha...  2.12 us
    pallas_call x1, Pallas kernels, fast_body(): pl.pallas_call(functools.partial(pack_kernel, axes), out_shape=[share] *...  1.37 us
  transfers between devices with their start and end apart: 16, of which 8 were waited for; matrix products, arithmetic and copies ran while one was open for 3% of the time, Pallas kernels for 9%

profile of v3, /device:TPU:0, one launch (start us, length us, event | category | flops | bytes accessed | tf_op | source)
XLA Modules:
  0.0 47.1 jit_solution(15829178773321298075)
XLA Ops:
  0.6 0.0 copy-start
  0.6 1.0 %copy-done = bf16[16,2,16,512]{3,2,1,0:T(8,128)(2,1)S(1)} copy-done((bf16[16,2,16,512]{3,2,1,0:T(8,128)(2,1)S(1)}, bf16[16,2,16,512]{3,2,1,0:T(8,128)(2,1)}, u32[]{:S(2)}) %copy-start) | copy-done | bytes 524312
  1.7 0.8 %lane_spread.1 = (bf16[4,32,512]{2,1,0:T(8,128)(2,1)S(1)}, bf16[2,32,512]{2,1,0:T(8,128)(2,1)S(1)}, bf16[2,32,512]{2,1,0:T(8,128)(2,1)S(1)}, bf16[4,32,512]{2,1,...) custom-call(bf16[16,2,16,512]{3,2,1,0:T(8,128)(2,1)S(1)} %copy-done), custom_call_target="tpu_custom_call" | custom-call | tf_op jit(solution)/shard_map/lane_spread/pallas_call | solution.py:354
  2.5 0.5 %collective-permute-start.2 = (bf16[2,32,512]{2,1,0:T(8,128)(2,1)S(1)}, bf16[2,32,512]{2,1,0:T(8,128)(2,1)S(1)}, u32[]{:S(2)}, u32[]{:S(2)}) collective-permute-start(bf16[2,32,512]{2,1,0:T(8,128)(2,1)S(1)} %get-tuple-element.31), channel_id=1, source_target_pairs={{0,1},{1,0},{2,3},{3,2},{4,5},{5,4},{6,7},{7,6},{8,9},{9,8},{10,11... | collective-permute-start | bytes 196616 | tf_op jit(solution)/shard_map/ppermute | solution.py:335
  3.0 0.1 collective-permute-start.5
  3.1 0.4 collective-permute-start
  3.5 2.6 %collective-permute-start.1 = (bf16[2,32,512]{2,1,0:T(8,128)(2,1)S(1)}, bf16[2,32,512]{2,1,0:T(8,128)(2,1)S(1)}, u32[]{:S(2)}, u32[]{:S(2)}) collective-permute-start(bf16[2,32,512]{2,1,0:T(8,128)(2,1)S(1)} %get-tuple-element.30), channel_id=1, source_target_pairs={{0,2},{2,0},{1,3},{3,1},{4,6},{6,4},{5,7},{7,5},{8,10},{10,8},{9,1... | collective-permute-start | bytes 196616 | tf_op jit(solution)/shard_map/ppermute | solution.py:335
  6.1 0.0 collective-permute-start.4
  6.1 0.8 %reshape.19 = f32[256]{0:T(256)S(1)} reshape(f32[16,16]{1,0:T(8,128)} %param.8) | data formatting | bytes 2048 | tf_op jit(solution)/shard_map/reshape | solution.py:372
  6.9 0.7 %convert_element_type.3 = f32[256]{0:T(256)S(1)} convert(s32[256]{0:T(256)} %param.10) | non-fusion elementwise | flops 256 | bytes 2048 | tf_op jit(solution)/shard_map/convert_element_type | solution.py:372
  7.6 0.0 collective-permute-done.2
  7.6 2.0 %collective-permute-start.3 = (bf16[2,32,512]{2,1,0:T(8,128)(2,1)S(1)}, bf16[2,32,512]{2,1,0:T(8,128)(2,1)S(1)}, u32[]{:S(2)}, u32[]{:S(2)}) collective-permute-start(bf16[2,32,512]{2,1,0:T(8,128)(2,1)S(1)} %collective-permute-done.2), channel_id=1, source_target_pairs={{0,2},{2,0},{1,3},{3,1},{4,6},{6,4},{5,7},{7,5},{8,10},{10,8},{9,1... | collective-permute-start | bytes 196616 | tf_op jit(solution)/shard_map/ppermute | solution.py:335
  9.6 0.0 collective-permute-done.5
  9.6 0.1 collective-permute-start.6
  9.7 0.0 collective-permute-done.1.refs_2_
  9.7 2.3 %collective-permute-done.3.refs_3_ = bf16[2,32,512]{2,1,0:T(8,128)(2,1)S(1)} collective-permute-done((bf16[2,32,512]{2,1,0:T(8,128)(2,1)S(1)}, bf16[2,32,512]{2,1,0:T(8,128)(2,1)S(1)}, u32[]{:S(2)}, u32[]{:S(2)}) %collective-permute-start.3) | collective-permute-done | bytes 65568 | tf_op jit(solution)/shard_map/ppermute | solution.py:335
  12.0 0.0 collective-permute-done.refs_1_
  12.0 0.3 plane_sums_far.1
  12.3 3.6 %collective-permute-start.8 = (bf16[64,512]{1,0:T(8,128)(2,1)S(1)}, bf16[64,512]{1,0:T(8,128)(2,1)S(1)}, u32[]{:S(2)}, u32[]{:S(2)}) collective-permute-start(bf16[64,512]{1,0:T(8,128)(2,1)S(1)} %get-tuple-element.37), channel_id=1, source_target_pairs={{0,8},{4,12},{8,0},{12,4},{1,9},{5,13},{9,1},{13,5},{2,10},{6,14},... | collective-permute-start | bytes 196616 | tf_op jit(solution)/shard_map/ppermute | solution.py:335
  15.9 1.3 %collective-permute-start.9 = (bf16[64,512]{1,0:T(8,128)(2,1)S(1)}, bf16[64,512]{1,0:T(8,128)(2,1)S(1)}, u32[]{:S(2)}, u32[]{:S(2)}) collective-permute-start(bf16[64,512]{1,0:T(8,128)(2,1)S(1)} %get-tuple-element.38), channel_id=1, source_target_pairs={{0,12},{4,8},{8,4},{12,0},{1,13},{5,9},{9,5},{13,1},{2,14},{6,10},... | collective-permute-start | bytes 196616 | tf_op jit(solution)/shard_map/ppermute | solution.py:335
  17.3 0.0 collective-permute-done.4.refs_2_
  17.3 0.0 collective-permute-done.6.refs_3_
  17.3 0.3 plane_sums_near.1
  17.6 0.3 collective-permute-start.7
  17.9 0.0 copy-start.1
  17.9 0.9 %copy-done.1 = bf16[4,2,256,32]{2,3,1,0:T(8,128)(2,1)S(1)} copy-done((bf16[4,2,256,32]{2,3,1,0:T(8,128)(2,1)S(1)}, bf16[4,2,256,32]{2,3,1,0:T(8,128)(2,1)}, u32[]{:S(2)}) %copy-start.1) | copy-done | bytes 131096
  18.8 1.4 %weight_shares.1 = (bf16[32,512]{1,0:T(8,128)(2,1)S(1)}, bf16[32,512]{1,0:T(8,128)(2,1)S(1)}, bf16[32,512]{1,0:T(8,128)(2,1)S(1)}, bf16[32,512]{1,0:T(8,128)(2,1)S(1)}) custom-call(bf16[4,2,32,256]{3,2,1,0:T(8,128)(2,1)S(1)} %bitcast.12), custom_call_target="tpu_custom_call" | custom-call | bytes 8388608 | tf_op jit(solution)/shard_map/weight_shares/pallas_call | solution.py:394
  20.2 0.0 collective-permute-done.8.refs_2_
  20.2 1.9 %collective-permute-done.9.refs_3_ = bf16[64,512]{1,0:T(8,128)(2,1)S(1)} collective-permute-done((bf16[64,512]{1,0:T(8,128)(2,1)S(1)}, bf16[64,512]{1,0:T(8,128)(2,1)S(1)}, u32[]{:S(2)}, u32[]{:S(2)}) %collective-permute-start.9) | collective-permute-done | bytes 65568 | tf_op jit(solution)/shard_map/ppermute | solution.py:335
  22.1 0.5 %collective-permute-done.7.refs_1_ = bf16[64,512]{1,0:T(8,128)(2,1)S(1)} collective-permute-done((bf16[64,512]{1,0:T(8,128)(2,1)S(1)}, bf16[64,512]{1,0:T(8,128)(2,1)S(1)}, u32[]{:S(2)}, u32[]{:S(2)}) %collective-permute-start.7) | collective-permute-done | bytes 65568 | tf_op jit(solution)/shard_map/ppermute | solution.py:335
  22.6 0.6 %station_filter.1 = (bf16[64,512]{1,0:T(8,128)(2,1)S(1)}, bf16[96,512]{1,0:T(8,128)(2,1)S(1)}, bf16[96,512]{1,0:T(8,128)(2,1)S(1)}, bf16[96,512]{1,0:T(8,128)(2,1)S(1)}) custom-call(f32[16,512]{1,0:T(8,128)S(1)} %get-tuple-element.32.taps_ref, f32[64,512]{1,0:T(8,128)S(1)} %get-tuple-element.35.refs_0_, bf16[64,512]{1,0:T(8,128)(2,1)S(1)} %collective-permute-done.7.refs_1_, ...), custom_call_target="tpu_custom_call" | custom-call | tf_op jit(solution)/shard_map/station_filter/pallas_call | solution.py:405
  23.2 0.1 collective-permute-start.10
  23.3 2.4 %collective-permute-start.11 = (bf16[96,512]{1,0:T(8,128)(2,1)S(1)}, bf16[96,512]{1,0:T(8,128)(2,1)S(1)}, u32[]{:S(2)}, u32[]{:S(2)}) collective-permute-start(bf16[96,512]{1,0:T(8,128)(2,1)S(1)} %get-tuple-element.44), channel_id=1, source_target_pairs={{0,8},{4,12},{8,0},{12,4},{1,9},{5,13},{9,1},{13,5},{2,10},{6,14},... | collective-permute-start | bytes 294920 | tf_op jit(solution)/shard_map/ppermute | solution.py:335
  25.7 2.0 %collective-permute-start.12 = (bf16[96,512]{1,0:T(8,128)(2,1)S(1)}, bf16[96,512]{1,0:T(8,128)(2,1)S(1)}, u32[]{:S(2)}, u32[]{:S(2)}) collective-permute-start(bf16[96,512]{1,0:T(8,128)(2,1)S(1)} %get-tuple-element.45), channel_id=1, source_target_pairs={{0,12},{4,8},{8,4},{12,0},{1,13},{5,9},{9,5},{13,1},{2,14},{6,10},... | collective-permute-start | bytes 294920 | tf_op jit(solution)/shard_map/ppermute | solution.py:335
  27.7 1.9 %collective-permute-done.10.refs_1_ = bf16[96,512]{1,0:T(8,128)(2,1)S(1)} collective-permute-done((bf16[96,512]{1,0:T(8,128)(2,1)S(1)}, bf16[96,512]{1,0:T(8,128)(2,1)S(1)}, u32[]{:S(2)}, u32[]{:S(2)}) %collective-permute-start.10) | collective-permute-done | bytes 98336 | tf_op jit(solution)/shard_map/ppermute | solution.py:335
  29.7 1.4 %collective-permute-done.11.refs_2_ = bf16[96,512]{1,0:T(8,128)(2,1)S(1)} collective-permute-done((bf16[96,512]{1,0:T(8,128)(2,1)S(1)}, bf16[96,512]{1,0:T(8,128)(2,1)S(1)}, u32[]{:S(2)}, u32[]{:S(2)}) %collective-permute-start.11) | collective-permute-done | bytes 98336 | tf_op jit(solution)/shard_map/ppermute | solution.py:335
  31.1 1.2 %collective-permute-done.12.refs_3_ = bf16[96,512]{1,0:T(8,128)(2,1)S(1)} collective-permute-done((bf16[96,512]{1,0:T(8,128)(2,1)S(1)}, bf16[96,512]{1,0:T(8,128)(2,1)S(1)}, u32[]{:S(2)}, u32[]{:S(2)}) %collective-permute-start.12) | collective-permute-done | bytes 98336 | tf_op jit(solution)/shard_map/ppermute | solution.py:335
  32.3 1.2 %collective-permute-start.13 = (bf16[4,64,512]{2,1,0:T(8,128)(2,1)S(1)}, bf16[4,64,512]{2,1,0:T(8,128)(2,1)S(1)}, u32[]{:S(2)}, u32[]{:S(2)}) collective-permute-start(bf16[4,64,512]{2,1,0:T(8,128)(2,1)S(1)} %pad_maximum_fusion.refs_0_), channel_id=1, source_target_pairs={{0,2},{2,0},{1,3},{3,1},{4,6},{6,4},{5,7},{7,5},{8,10},{10,8},{9,1... | collective-permute-start | bytes 786440 | tf_op jit(solution)/shard_map/ppermute | solution.py:335
  33.5 0.0 collective-permute-start.14
  33.5 0.7 %copy-done.2 = f32[16,16]{1,0:T(8,128)S(1)} copy-done((f32[16,16]{1,0:T(8,128)S(1)}, f32[16,16]{1,0:T(8,128)}, u32[]{:S(2)}) %copy-start.2) | copy-done | bytes 1048
  34.2 0.7 %copy-done.3 = s32[1024]{0:T(1024)S(1)} copy-done((s32[1024]{0:T(1024)S(1)}, s32[1024]{0:T(1024)}, u32[]{:S(2)}) %copy-start.3) | copy-done | bytes 4120
  34.9 0.7 %copy-done.4 = s32[32,1]{0,1:T(1,128)S(1)} copy-done((s32[32,1]{0,1:T(1,128)S(1)}, s32[32,1]{0,1:T(1,128)}, u32[]{:S(2)}) %copy-start.4) | copy-done | bytes 152
  35.6 2.1 %weight_matrix.1 = (bf16[4,128,1024]{2,1,0:T(8,128)(2,1)S(1)}, bf16[16,768,256]{2,1,0:T(8,128)(2,1)S(1)}) custom-call(s32[1,32]{1,0:T(1,128)S(1)} %bitcast.17, s32[1,1024]{1,0:T(1,128)S(1)} %bitcast.16, f32[16,16]{1,0:T(8,128)S(1)} %copy-done.2, bf16[32,512]{1,0:T(8,128)(2,1)S(1)} %get-tuple-element.46.refs_0_, ...), custom_call_target="tpu_custom_call" | custom-call | flops 2000000000 | bytes 2097152 | tf_op jit(solution)/shard_map/weight_matrix/pallas_call | solution.py:416
  37.7 1.0 %collective-permute-done.13.refs_1_ = bf16[4,64,512]{2,1,0:T(8,128)(2,1)S(1)} collective-permute-done((bf16[4,64,512]{2,1,0:T(8,128)(2,1)S(1)}, bf16[4,64,512]{2,1,0:T(8,128)(2,1)S(1)}, u32[]{:S(2)}, u32[]{:S(2)}) %collective-permute-start.13) | collective-permute-done | bytes 262176 | tf_op jit(solution)/shard_map/ppermute | solution.py:335
  38.7 0.0 collective-permute-start.15
  38.7 0.0 collective-permute-done.14.refs_2_
  38.7 1.5 %collective-permute-done.15.refs_3_ = bf16[4,64,512]{2,1,0:T(8,128)(2,1)S(1)} collective-permute-done((bf16[4,64,512]{2,1,0:T(8,128)(2,1)S(1)}, bf16[4,64,512]{2,1,0:T(8,128)(2,1)S(1)}, u32[]{:S(2)}, u32[]{:S(2)}) %collective-permute-start.15) | collective-permute-done | bytes 262176 | tf_op jit(solution)/shard_map/ppermute | solution.py:335
  40.3 6.8 %beams_and_series.1 = (f32[128,2,8,512]{3,2,1,0:T(8,128)}, f32[4,2,8,32]{3,2,1,0:T(8,128)}) custom-call(bf16[4,64,512]{2,1,0:T(8,128)(2,1)S(1)} %pad_maximum_fusion.refs_0_, bf16[4,64,512]{2,1,0:T(8,128)(2,1)S(1)} %collective-permute-done.13.refs_1_, bf16[4,64,512]{2,1,0:T(8,128)(2,1)S(1)} %collective-permute-done.14.refs_2_, ...), custom_call_target="tpu_custom_call" | custom-call | tf_op jit(solution)/shard_map/beams_and_series/pallas_call | solution.py:312
  (8 shorter events, 0.1 us)
Async XLA Ops:
  0.6 1.0 %copy-start = (bf16[16,2,16,512]{3,2,1,0:T(8,128)(2,1)S(1)}, bf16[16,2,16,512]{3,2,1,0:T(8,128)(2,1)}, u32[]{:S(2)}) copy-start(bf16[16,2,16,512]{3,2,1,0:T(8,128)(2,1)} %x_hbm.1) | copy-start | bytes 1572868
  2.5 5.1 %collective-permute-start.2 = (bf16[2,32,512]{2,1,0:T(8,128)(2,1)S(1)}, bf16[2,32,512]{2,1,0:T(8,128)(2,1)S(1)}, u32[]{:S(2)}, u32[]{:S(2)}) collective-permute-start(bf16[2,32,512]{2,1,0:T(8,128)(2,1)S(1)} %get-tuple-element.31), channel_id=1, source_target_pairs={{0,1},{1,0},{2,3},{3,2},{4,5},{5,4},{6,7},{7,6},{8,9},{9,8},{10,11... | collective-permute-start | bytes 196616 | tf_op jit(solution)/shard_map/ppermute | solution.py:335
  3.0 6.6 %collective-permute-start.5 = (bf16[2,32,512]{2,1,0:T(8,128)(2,1)S(1)}, bf16[2,32,512]{2,1,0:T(8,128)(2,1)S(1)}, u32[]{:S(2)}, u32[]{:S(2)}) collective-permute-start(bf16[2,32,512]{2,1,0:T(8,128)(2,1)S(1)} %get-tuple-element.34), channel_id=1, source_target_pairs={{0,1},{1,0},{2,3},{3,2},{4,5},{5,4},{6,7},{7,6},{8,9},{9,8},{10,11... | collective-permute-start | bytes 196616 | tf_op jit(solution)/shard_map/ppermute | solution.py:335
  3.1 8.9 %collective-permute-start = (bf16[4,32,512]{2,1,0:T(8,128)(2,1)S(1)}, bf16[4,32,512]{2,1,0:T(8,128)(2,1)S(1)}, u32[]{:S(2)}, u32[]{:S(2)}) collective-permute-start(bf16[4,32,512]{2,1,0:T(8,128)(2,1)S(1)} %get-tuple-element.29), channel_id=1, source_target_pairs={{0,1},{1,0},{2,3},{3,2},{4,5},{5,4},{6,7},{7,6},{8,9},{9,8},{10,11... | collective-permute-start | bytes 393224 | tf_op jit(solution)/shard_map/ppermute | solution.py:335
  3.5 6.1 %collective-permute-start.1 = (bf16[2,32,512]{2,1,0:T(8,128)(2,1)S(1)}, bf16[2,32,512]{2,1,0:T(8,128)(2,1)S(1)}, u32[]{:S(2)}, u32[]{:S(2)}) collective-permute-start(bf16[2,32,512]{2,1,0:T(8,128)(2,1)S(1)} %get-tuple-element.30), channel_id=1, source_target_pairs={{0,2},{2,0},{1,3},{3,1},{4,6},{6,4},{5,7},{7,5},{8,10},{10,8},{9,1... | collective-permute-start | bytes 196616 | tf_op jit(solution)/shard_map/ppermute | solution.py:335
  6.1 11.2 %collective-permute-start.4 = (bf16[2,32,512]{2,1,0:T(8,128)(2,1)S(1)}, bf16[2,32,512]{2,1,0:T(8,128)(2,1)S(1)}, u32[]{:S(2)}, u32[]{:S(2)}) collective-permute-start(bf16[2,32,512]{2,1,0:T(8,128)(2,1)S(1)} %get-tuple-element.33), channel_id=1, source_target_pairs={{0,2},{2,0},{1,3},{3,1},{4,6},{6,4},{5,7},{7,5},{8,10},{10,8},{9,1... | collective-permute-start | bytes 196616 | tf_op jit(solution)/shard_map/ppermute | solution.py:335
  7.6 4.4 %collective-permute-start.3 = (bf16[2,32,512]{2,1,0:T(8,128)(2,1)S(1)}, bf16[2,32,512]{2,1,0:T(8,128)(2,1)S(1)}, u32[]{:S(2)}, u32[]{:S(2)}) collective-permute-start(bf16[2,32,512]{2,1,0:T(8,128)(2,1)S(1)} %collective-permute-done.2), channel_id=1, source_target_pairs={{0,2},{2,0},{1,3},{3,1},{4,6},{6,4},{5,7},{7,5},{8,10},{10,8},{9,1... | collective-permute-start | bytes 196616 | tf_op jit(solution)/shard_map/ppermute | solution.py:335
  9.6 7.7 %collective-permute-start.6 = (bf16[2,32,512]{2,1,0:T(8,128)(2,1)S(1)}, bf16[2,32,512]{2,1,0:T(8,128)(2,1)S(1)}, u32[]{:S(2)}, u32[]{:S(2)}) collective-permute-start(bf16[2,32,512]{2,1,0:T(8,128)(2,1)S(1)} %collective-permute-done.5), channel_id=1, source_target_pairs={{0,2},{2,0},{1,3},{3,1},{4,6},{6,4},{5,7},{7,5},{8,10},{10,8},{9,1... | collective-permute-start | bytes 196616 | tf_op jit(solution)/shard_map/ppermute | solution.py:335
  12.3 7.9 %collective-permute-start.8 = (bf16[64,512]{1,0:T(8,128)(2,1)S(1)}, bf16[64,512]{1,0:T(8,128)(2,1)S(1)}, u32[]{:S(2)}, u32[]{:S(2)}) collective-permute-start(bf16[64,512]{1,0:T(8,128)(2,1)S(1)} %get-tuple-element.37), channel_id=1, source_target_pairs={{0,8},{4,12},{8,0},{12,4},{1,9},{5,13},{9,1},{13,5},{2,10},{6,14},... | collective-permute-start | bytes 196616 | tf_op jit(solution)/shard_map/ppermute | solution.py:335
  15.9 6.2 %collective-permute-start.9 = (bf16[64,512]{1,0:T(8,128)(2,1)S(1)}, bf16[64,512]{1,0:T(8,128)(2,1)S(1)}, u32[]{:S(2)}, u32[]{:S(2)}) collective-permute-start(bf16[64,512]{1,0:T(8,128)(2,1)S(1)} %get-tuple-element.38), channel_id=1, source_target_pairs={{0,12},{4,8},{8,4},{12,0},{1,13},{5,9},{9,5},{13,1},{2,14},{6,10},... | collective-permute-start | bytes 196616 | tf_op jit(solution)/shard_map/ppermute | solution.py:335
  17.6 5.0 %collective-permute-start.7 = (bf16[64,512]{1,0:T(8,128)(2,1)S(1)}, bf16[64,512]{1,0:T(8,128)(2,1)S(1)}, u32[]{:S(2)}, u32[]{:S(2)}) collective-permute-start(bf16[64,512]{1,0:T(8,128)(2,1)S(1)} %get-tuple-element.36), channel_id=1, source_target_pairs={{0,4},{4,0},{8,12},{12,8},{1,5},{5,1},{9,13},{13,9},{2,6},{6,2},{1... | collective-permute-start | bytes 196616 | tf_op jit(solution)/shard_map/ppermute | solution.py:335
  17.9 0.9 %copy-start.1 = (bf16[4,2,256,32]{2,3,1,0:T(8,128)(2,1)S(1)}, bf16[4,2,256,32]{2,3,1,0:T(8,128)(2,1)}, u32[]{:S(2)}) copy-start(bf16[4,2,256,32]{2,3,1,0:T(8,128)(2,1)} %param.13) | copy-start | bytes 393220
  23.2 6.4 %collective-permute-start.10 = (bf16[96,512]{1,0:T(8,128)(2,1)S(1)}, bf16[96,512]{1,0:T(8,128)(2,1)S(1)}, u32[]{:S(2)}, u32[]{:S(2)}) collective-permute-start(bf16[96,512]{1,0:T(8,128)(2,1)S(1)} %get-tuple-element.43), channel_id=1, source_target_pairs={{0,4},{4,0},{8,12},{12,8},{1,5},{5,1},{9,13},{13,9},{2,6},{6,2},{1... | collective-permute-start | bytes 294920 | tf_op jit(solution)/shard_map/ppermute | solution.py:335
  23.3 7.7 %collective-permute-start.11 = (bf16[96,512]{1,0:T(8,128)(2,1)S(1)}, bf16[96,512]{1,0:T(8,128)(2,1)S(1)}, u32[]{:S(2)}, u32[]{:S(2)}) collective-permute-start(bf16[96,512]{1,0:T(8,128)(2,1)S(1)} %get-tuple-element.44), channel_id=1, source_target_pairs={{0,8},{4,12},{8,0},{12,4},{1,9},{5,13},{9,1},{13,5},{2,10},{6,14},... | collective-permute-start | bytes 294920 | tf_op jit(solution)/shard_map/ppermute | solution.py:335
  25.7 6.5 %collective-permute-start.12 = (bf16[96,512]{1,0:T(8,128)(2,1)S(1)}, bf16[96,512]{1,0:T(8,128)(2,1)S(1)}, u32[]{:S(2)}, u32[]{:S(2)}) collective-permute-start(bf16[96,512]{1,0:T(8,128)(2,1)S(1)} %get-tuple-element.45), channel_id=1, source_target_pairs={{0,12},{4,8},{8,4},{12,0},{1,13},{5,9},{9,5},{13,1},{2,14},{6,10},... | collective-permute-start | bytes 294920 | tf_op jit(solution)/shard_map/ppermute | solution.py:335
  32.3 6.4 %collective-permute-start.13 = (bf16[4,64,512]{2,1,0:T(8,128)(2,1)S(1)}, bf16[4,64,512]{2,1,0:T(8,128)(2,1)S(1)}, u32[]{:S(2)}, u32[]{:S(2)}) collective-permute-start(bf16[4,64,512]{2,1,0:T(8,128)(2,1)S(1)} %pad_maximum_fusion.refs_0_), channel_id=1, source_target_pairs={{0,2},{2,0},{1,3},{3,1},{4,6},{6,4},{5,7},{7,5},{8,10},{10,8},{9,1... | collective-permute-start | bytes 786440 | tf_op jit(solution)/shard_map/ppermute | solution.py:335
  33.5 5.2 %collective-permute-start.14 = (bf16[4,64,512]{2,1,0:T(8,128)(2,1)S(1)}, bf16[4,64,512]{2,1,0:T(8,128)(2,1)S(1)}, u32[]{:S(2)}, u32[]{:S(2)}) collective-permute-start(bf16[4,64,512]{2,1,0:T(8,128)(2,1)S(1)} %pad_maximum_fusion.refs_0_), channel_id=1, source_target_pairs={{0,1},{1,0},{2,3},{3,2},{4,5},{5,4},{6,7},{7,6},{8,9},{9,8},{10,11... | collective-permute-start | bytes 786440 | tf_op jit(solution)/shard_map/ppermute | solution.py:335
  33.5 0.7 %copy-start.2 = (f32[16,16]{1,0:T(8,128)S(1)}, f32[16,16]{1,0:T(8,128)}, u32[]{:S(2)}) copy-start(f32[16,16]{1,0:T(8,128)} %taps_ref.1) | copy-start | bytes 3076
  34.2 0.7 %copy-start.3 = (s32[1024]{0:T(1024)S(1)}, s32[1024]{0:T(1024)}, u32[]{:S(2)}) copy-start(s32[1024]{0:T(1024)} %param.12) | copy-start | bytes 12292
  34.9 0.7 %copy-start.4 = (s32[32,1]{0,1:T(1,128)S(1)}, s32[32,1]{0,1:T(1,128)}, u32[]{:S(2)}) copy-start(s32[32,1]{0,1:T(1,128)} %param.11) | copy-start | bytes 388
  38.7 1.5 %collective-permute-start.15 = (bf16[4,64,512]{2,1,0:T(8,128)(2,1)S(1)}, bf16[4,64,512]{2,1,0:T(8,128)(2,1)S(1)}, u32[]{:S(2)}, u32[]{:S(2)}) collective-permute-start(bf16[4,64,512]{2,1,0:T(8,128)(2,1)S(1)} %collective-permute-done.13.refs_1_), channel_id=1, source_target_pairs={{0,1},{1,0},{2,3},{3,2},{4,5},{5,4},{6,7},{7,6},{8,9},{9,8},{10,11... | collective-permute-start | bytes 786440 | tf_op jit(solution)/shard_map/ppermute | solution.py:335

commit v4 on v3

--- a/solution.py
+++ b/solution.py
@@ -12,6 +12,7 @@
 SPEC = 512
 VMEM_LIMIT = 24 * 1024 * 1024
 HALO = 128
+FLIPS = ((0, 0), (0, 1), (1, 0), (1, 1))
 
 
 def fourier(parts, sign):
@@ -39,10 +40,7 @@
     return sub * 8 + col * 4 + row
 
 
-def spread_kernel(axes, x_hbm, *refs):
-    out_refs, (x_ref, sem) = refs[:-2], refs[-2:]
-    load = pltpu.make_async_copy(x_hbm, x_ref, sem)
-    load.start()
+def spread_kernel(axes, x_ref, *out_refs):
     row, col, sub = (lax.axis_index(a) for a in axes)
     antennas, parts, chan, frames = x_ref.shape
     count = antennas * parts * chan
@@ -54,10 +52,8 @@
     lane = lane_of(row ^ (piece % 4) ^ 2, col ^ (piece // 4 % 2), sub ^ (piece // 8))
     source = (antenna * parts + part) * chan + lane
     order = jnp.where(lax.broadcasted_iota(jnp.int32, shape, 1) == source, 1.0, 0.0)
-    order = order.astype(jnp.bfloat16)
-    load.wait()
     moved = jnp.dot(
-        order,
+        order.astype(jnp.bfloat16),
         x_ref[...].reshape(count, frames),
         preferred_element_type=jnp.float32,
     ).astype(jnp.bfloat16)
@@ -70,8 +66,8 @@
 
 def member_matrix(axes, names_ref, stations, local):
     row, col, sub = (lax.axis_index(a) for a in axes)
-    antennas = 16 * local
-    every = jnp.broadcast_to(names_ref[:, :antennas], (8, antennas))
+    antennas = names_ref.shape[1]
+    every = jnp.broadcast_to(names_ref[...], (8, antennas))
     names = []
     for k in range(4):
         owner = (row * 2 + (col ^ (k // 2))) * 2 + (sub ^ (k % 2))
@@ -80,30 +76,27 @@
     shape = (2 * stations, 8 * local)
     place = lax.broadcasted_iota(jnp.int32, shape, 0)
     column = lax.broadcasted_iota(jnp.int32, shape, 1)
-    same = ((place % stations).astype(jnp.float32) == names) & (place // stations == column // local % 2)
+    same = (place % stations == names) & (place // stations == column // local % 2)
     return jnp.where(same, 1.0, 0.0).astype(jnp.bfloat16)
 
 
-def own_taps(axes, taps, count, chan):
+def table_kernel(axes, names_ref, taps_ref, members_ref, own_taps_ref):
+    stations, local = members_ref.shape[0] // 2, members_ref.shape[1] // 8
+    members_ref[...] = member_matrix(axes, names_ref, stations, local)
+    taps = taps_ref[...]
     lane = lane_of(*(lax.axis_index(a) for a in axes))
-    shape = (count, count * chan)
-    column = lax.broadcasted_iota(jnp.int32, shape, 1)
-    mine = column == lax.broadcasted_iota(jnp.int32, shape, 0) * chan + lane
-    taps = jnp.where(mine, jnp.broadcast_to(taps, shape), 0.0)
-    return jnp.sum(taps, axis=1, keepdims=True)
-
-
-def sum_kernel(axes, first, names_ref, *refs):
-    x_refs, out_refs = refs[:4], refs[4:6]
-    for taps_ref in refs[6:]:
-        count = taps_ref.shape[0]
-        taps = names_ref[:, names_ref.shape[1] - count * count :]
-        taps_ref[...] = jnp.broadcast_to(own_taps(axes, taps, count, count), taps_ref.shape)
-    stations, local = out_refs[0].shape[0] // 2, x_refs[0].shape[1] // 2
-    members = member_matrix(axes, names_ref, stations, local)
+    mine = lax.broadcasted_iota(jnp.int32, taps.shape, 1) == lane
+    own = jnp.sum(jnp.where(mine, taps, 0.0), axis=1, keepdims=True)
+    own_taps_ref[...] = jnp.broadcast_to(own, own_taps_ref.shape)
+
+
+def sum_kernel(first, members_ref, *refs):
+    x_refs, out_refs = refs[:4], refs[4:]
     for k, ref in enumerate(out_refs):
         rows = jnp.concatenate([x[first + k if x.shape[0] == 4 else k] for x in x_refs], axis=0)
-        ref[...] = jnp.dot(members, rows, preferred_element_type=jnp.float32).astype(ref.dtype)
+        ref[...] = jnp.dot(
+            members_ref[...], rows, preferred_element_type=jnp.float32
+        ).astype(ref.dtype)
 
 
 def filter_kernel(taps_ref, *refs):
@@ -152,14 +145,10 @@
     return jnp.concatenate([high[:HALO], low[:HALO], high[HALO:], low[HALO:]], axis=0)
 
 
-def weight_kernel(axes, groups_ref, beam_ref, taps_ref, *refs):
+def band_kernel(axes, groups_ref, beam_ref, taps_ref, t_ref, chosen_ref, scale_ref):
     row, col, sub = (lax.axis_index(a) for a in axes)
-    w_refs, (m_ref, t_ref, all_ref) = refs[:4], refs[4:]
-    stations, beams = groups_ref.shape[1], m_ref.shape[1] // 2
-    held = all_ref.shape[2] // (2 * beams)
-    chan = 4 * held
-    for mask, ref in enumerate(w_refs):
-        all_ref[row ^ mask] = ref[ref.shape[0] - stations :]
+    stations, beams = chosen_ref.shape
+    chan = t_ref.shape[0]
     square = (stations, stations)
     diagonal = lax.broadcasted_iota(jnp.int32, square, 0) == lax.broadcasted_iota(
         jnp.int32, square, 1
@@ -170,10 +159,26 @@
     first = ((col * 2 + sub) * 4 + row) * beams
     every = jnp.broadcast_to(beam_ref[...], (8, total))
     wanted = pltpu.roll(every, lax.rem(total - first, total), 1)[:1, :beams]
-    members = groups == wanted.astype(jnp.float32)
+    chosen = (groups == wanted.astype(jnp.float32)).astype(jnp.float32)
+    chosen_ref[...] = chosen
     scale = (1.0 / (chan * math.sqrt(ANTENNAS_PER_STN))) / jnp.sqrt(
-        jnp.sum(members.astype(jnp.float32), axis=0, keepdims=True)
-    )
+        jnp.sum(chosen, axis=0, keepdims=True)
+    )
+    scale_ref[...] = jnp.broadcast_to(scale, scale_ref.shape)
+    for c in range(chan):
+        t_ref[c] = bands(taps_ref, c, t_ref.shape[1] // 2, t_ref.shape[2])
+
+
+def weight_kernel(axes, chosen_ref, scale_ref, *refs):
+    row = lax.axis_index(axes[0])
+    w_refs, (m_ref, all_ref) = refs[:4], refs[4:]
+    stations, beams = chosen_ref.shape
+    held = all_ref.shape[2] // (2 * beams)
+    chan = 4 * held
+    for mask, ref in enumerate(w_refs):
+        all_ref[row ^ mask] = ref[ref.shape[0] - stations :]
+    members = chosen_ref[...] > 0
+    scale = scale_ref[...]
     zero = jnp.zeros((), jnp.float32)
     parts = []
     for k in range(chan):
@@ -186,13 +191,49 @@
     upper = jnp.concatenate([v for k in range(chan) for v in (real[k], -imag[k])], axis=0)
     lower = jnp.concatenate([v for k in range(chan) for v in (imag[k], real[k])], axis=0)
     whole = jnp.concatenate([upper, lower], axis=1).T.astype(m_ref.dtype)
-    width = whole.shape[1] // 4
-    for u in range(4):
-        for j in range(4):
-            t = (u + j) % 4
-            m_ref[u, :, t * width : (t + 1) * width] = whole[:, j * width : (j + 1) * width]
+    width = whole.shape[1]
+    step = 2 * stations
+    odd = jnp.concatenate([whole[:, width - step :], whole[:, : width - step]], axis=1)
     for c in range(chan):
-        t_ref[c] = bands(taps_ref, c, t_ref.shape[1] // 2, t_ref.shape[2])
+        base = odd if c % 2 else whole
+        start = c // 2 * 2 * step
+        m_ref[c, :, start:] = base[:, : width - start]
+        if start:
+            m_ref[c, :, :start] = base[:, width - start :]
+
+
+def gather_lanes(axes, x_refs, flips, lanes_ref):
+    row, col, sub = (lax.axis_index(a) for a in axes)
+    rows = x_refs[0].shape[1]
+    for (dc, ds), ref in zip(flips, x_refs):
+        for m in range(4):
+            lane = lane_of(row ^ m, col ^ dc, sub ^ ds)
+            lanes_ref[pl.ds(pl.multiple_of(lane * rows, rows), rows)] = ref[m]
+
+
+def lane_products(axes, flips, m_ref, lanes_ref, first, count):
+    col, sub = (lax.axis_index(a) for a in axes[1:])
+    width = 4 * lanes_ref.shape[0] // 16
+    total = None
+    for dc, ds in flips:
+        start = pl.multiple_of((2 * (sub ^ ds) + (col ^ dc)) * width, width)
+        some = m_ref[first : first + count, :, pl.ds(start, width)]
+        some = some.reshape(count * m_ref.shape[1], width)
+        found = jnp.dot(some, lanes_ref[pl.ds(start, width)], preferred_element_type=jnp.float32)
+        total = found if total is None else total + found
+    return total
+
+
+def part_kernel(axes, flips, m_ref, *refs):
+    x_refs, (sum_ref, lanes_ref) = refs[: len(flips)], refs[-2:]
+    before = refs[len(flips) : -2]
+    gather_lanes(axes, x_refs, flips, lanes_ref)
+    for first in range(0, m_ref.shape[0], 4):
+        found = lane_products(axes, flips, m_ref, lanes_ref, first, 4)
+        found = found.reshape((4,) + sum_ref.shape[1:])
+        for ref in before:
+            found = found + ref[first : first + 4]
+        sum_ref[first : first + 4] = found
 
 
 def beam_kernel(
@@ -200,6 +241,7 @@
     x_refs,
     m_ref,
     t_ref,
+    sum_ref,
     series_ref,
     vis_ref,
     lanes_ref,
@@ -214,23 +256,15 @@
     chan = 4 * 4
     frames = lanes_ref.shape[1]
 
-    for place, ref in enumerate(x_refs):
-        for m in range(4):
-            lane = lane_of(row ^ m, col ^ (place % 2), sub ^ (place // 2))
-            lanes_ref[pl.ds(pl.multiple_of(lane * rows, rows), rows)] = ref[m]
-    wrap = 3 * rows
-    lanes_ref[chan * rows : chan * rows + wrap] = lanes_ref[0:wrap]
+    gather_lanes(axes, x_refs, FLIPS, lanes_ref)
     beams = m_ref.shape[1] // 2
     tile = t_ref.shape[2]
     stores = []
     for half in range(2):
-        some = m_ref[2 * half : 2 * half + 2].reshape(4 * beams, chan * rows)
-        for v in range(4):
-            window = lanes_ref[v * rows : (v + chan) * rows]
-            found = jnp.dot(some, window, preferred_element_type=jnp.float32)
-            found = found.astype(jnp.bfloat16)
-            for u in range(2):
-                inverse_ref[8 * half + 4 * u + v] = found[2 * beams * u : 2 * beams * (u + 1)]
+        for first in range(8 * half, 8 * half + 8, 4):
+            found = lane_products(axes, FLIPS[3:], m_ref, lanes_ref, first, 4)
+            found = found.reshape((4,) + sum_ref.shape[1:]) + sum_ref[first : first + 4]
+            inverse_ref[first : first + 4] = found.astype(jnp.bfloat16)
         for n in range(frames // tile):
             for c in range(8):
                 lane = 8 * half + c
@@ -302,7 +336,7 @@
         copy.wait()
 
 
-def call_beams(axes, pieces, matrix, bands):
+def call_beams(axes, pieces, matrix, bands, sums):
     params = pltpu.CompilerParams(vmem_limit_bytes=VMEM_LIMIT)
     vmem = pl.BlockSpec(memory_space=pltpu.VMEM)
     chan, frames = bands.shape[0], pieces[0].shape[2]
@@ -315,10 +349,10 @@
             jax.ShapeDtypeStruct((2 * beams, 2, 8, frames), jnp.float32),
             jax.ShapeDtypeStruct((4, 2, stations // 4, stations), jnp.float32),
         ),
-        in_specs=[vmem] * (len(pieces) + 2),
+        in_specs=[vmem] * (len(pieces) + 3),
         out_specs=(anywhere, vmem),
         scratch_shapes=[
-            pltpu.VMEM(((chan + 3) * 2 * stations, frames), jnp.bfloat16),
+            pltpu.VMEM((chan * 2 * stations, frames), jnp.bfloat16),
             pltpu.VMEM((2 * stations, 2 * stations), jnp.float32),
             pltpu.VMEM((chan, 2 * beams, frames), jnp.bfloat16),
             pltpu.VMEM((slots, 2 * beams * 8, 128), jnp.float32),
@@ -326,7 +360,7 @@
         ],
         compiler_params=params,
         name="beams_and_series",
-    )(*pieces, matrix, bands)
+    )(*pieces, matrix, bands, sums)
     return visibilities, series
 
 
@@ -354,12 +388,23 @@
     kept, crossing_a, crossing_b, paired, far_a, far_b = pl.pallas_call(
         functools.partial(spread_kernel, axes),
         out_shape=[block, half, half, block, half, half],
-        in_specs=[hbm],
+        in_specs=[vmem],
         out_specs=[vmem] * 6,
-        scratch_shapes=[pltpu.VMEM(samples.shape, samples.dtype), pltpu.SemaphoreType.DMA],
         compiler_params=params,
         name="lane_spread",
     )(samples)
+    members, taps = pl.pallas_call(
+        functools.partial(table_kernel, axes),
+        out_shape=[
+            jax.ShapeDtypeStruct((2 * stations, 8 * local), jnp.bfloat16),
+            jax.ShapeDtypeStruct((analysis_taps.shape[0], frames), jnp.float32),
+        ],
+        in_specs=[vmem] * 2,
+        out_specs=[vmem] * 2,
+        compiler_params=params,
+        cost_estimate=pl.CostEstimate(flops=0, bytes_accessed=16 << 20, transcendentals=0),
+        name="station_tables",
+    )(antenna_station.reshape(1, antennas), analysis_taps)
     far_a = swap(far_a, "sub", 1)
     crossing_a = swap(crossing_a, "col", 1)
     far_a = swap(far_a, "col", 1)
@@ -369,26 +414,23 @@
     far_b = swap(far_b, "col", 1)
 
     lane = jax.ShapeDtypeStruct((2 * stations, frames), jnp.bfloat16)
-    names = jnp.concatenate([antenna_station.astype(jnp.float32), analysis_taps.reshape(-1)])
-    names = names.reshape(1, -1)
-    sums2, sums3, taps = pl.pallas_call(
-        functools.partial(sum_kernel, axes, 0),
-        out_shape=[lane] * 2
-        + [jax.ShapeDtypeStruct((analysis_taps.shape[0], frames), jnp.float32)],
+    sums2, sums3 = pl.pallas_call(
+        functools.partial(sum_kernel, 0),
+        out_shape=[lane] * 2,
         in_specs=[vmem] * 5,
-        out_specs=[vmem] * 3,
+        out_specs=[vmem] * 2,
         compiler_params=params,
         name="plane_sums_far",
-    )(names, kept, paired, crossing_a, far_a)
+    )(members, kept, paired, crossing_a, far_a)
     sums3, sums2 = swap(sums3, "row", 3), swap(sums2, "row", 2)
     sums0, sums1 = pl.pallas_call(
-        functools.partial(sum_kernel, axes, 2),
+        functools.partial(sum_kernel, 2),
         out_shape=[jax.ShapeDtypeStruct(lane.shape, jnp.float32), lane],
         in_specs=[vmem] * 5,
         out_specs=[vmem] * 2,
         compiler_params=params,
         name="plane_sums_near",
-    )(names, kept, paired, crossing_b, far_b)
+    )(members, kept, paired, crossing_b, far_b)
 
     share = jax.ShapeDtypeStruct((stations, 2 * held_chan * beams), jnp.bfloat16)
     shares = pl.pallas_call(
@@ -413,33 +455,61 @@
     moved = [swap(x, "row", m) for x, m in zip(sent, (1, 2, 3))]
 
     tile = 256
-    matrix, bands = pl.pallas_call(
+    table = jax.ShapeDtypeStruct((stations, beams), jnp.float32)
+    moved[0], *small = lax.optimization_barrier(
+        (moved[0], station_group, beam_group, synthesis_taps)
+    )
+    bands, chosen, scale = pl.pallas_call(
+        functools.partial(band_kernel, axes),
+        out_shape=[
+            jax.ShapeDtypeStruct((chan, 2 * (tile + HALO), tile), jnp.bfloat16),
+            table,
+            table,
+        ],
+        in_specs=[vmem, vmem, smem],
+        out_specs=[vmem] * 3,
+        compiler_params=params,
+        cost_estimate=pl.CostEstimate(flops=0, bytes_accessed=16 << 20, transcendentals=0),
+        name="synthesis_bands",
+    )(
+        small[0].reshape(1, stations),
+        small[1].reshape(1, beam_group.shape[0]),
+        small[2],
+    )
+    *moved[1:], bands, chosen, scale = lax.optimization_barrier((*moved[1:], bands, chosen, scale))
+    matrix = pl.pallas_call(
         functools.partial(weight_kernel, axes),
-        out_shape=[
-            jax.ShapeDtypeStruct((4, 2 * beams, 2 * chan * stations), jnp.bfloat16),
-            jax.ShapeDtypeStruct((chan, 2 * (tile + HALO), tile), jnp.bfloat16),
-        ],
-        in_specs=[vmem, vmem, smem] + [vmem] * 4,
-        out_specs=[vmem] * 2,
+        out_shape=jax.ShapeDtypeStruct((chan, 2 * beams, 2 * chan * stations), jnp.bfloat16),
+        in_specs=[vmem] * 6,
+        out_specs=vmem,
         scratch_shapes=[pltpu.VMEM((4,) + share.shape, jnp.bfloat16)],
         compiler_params=params,
-        cost_estimate=pl.CostEstimate(flops=2_000_000_000, bytes_accessed=2 << 20, transcendentals=0),
+        cost_estimate=pl.CostEstimate(flops=0, bytes_accessed=8 << 20, transcendentals=0),
         name="weight_matrix",
-    )(
-        station_group.reshape(1, stations),
-        beam_group.reshape(1, beam_group.shape[0]),
-        synthesis_taps,
-        shares[0],
-        *moved,
-    )
+    )(chosen, scale, shares[0], *moved)
+
+    def add_part(flips, xs, before, name):
+        return pl.pallas_call(
+            functools.partial(part_kernel, axes, flips),
+            out_shape=jax.ShapeDtypeStruct((chan, 2 * beams, frames), jnp.float32),
+            in_specs=[vmem] * (1 + len(xs) + len(before)),
+            out_specs=vmem,
+            scratch_shapes=[pltpu.VMEM((chan * 2 * stations, frames), jnp.bfloat16)],
+            compiler_params=params,
+            cost_estimate=pl.CostEstimate(flops=0, bytes_accessed=8 << 20, transcendentals=0),
+            name=name,
+        )(matrix, *xs, *before)
 
     held = jnp.stack([filtered] + [x[: 2 * stations] for x in moved])
     other = swap(held, "col", 1)
-    other, matrix, bands = lax.optimization_barrier((other, matrix, bands))
-    pieces = [held, other]
-    pieces += [swap(x, "sub", 1) for x in pieces]
-
-    visibilities, series = call_beams(axes, pieces, matrix, bands)
+    paired = swap(held, "sub", 1)
+    sums = add_part(FLIPS[:1], [held], [], "own_beams")
+    other, sums = lax.optimization_barrier((other, sums))
+    last = swap(other, "sub", 1)
+    sums = add_part(FLIPS[1:3], [paired, other], [sums], "near_beams")
+    pieces = [held, paired, other, last]
+
+    visibilities, series = call_beams(axes, pieces, matrix, bands, sums)
     return visibilities, series.reshape(beams, 2, chan, frames)
 
 

time: 47.4 us -> 45.5 us (0.960)
  the two profiles are of different devices: /device:TPU:0 before, /device:TPU:23 now
where the time goes in v4:
time: 45.5 us; the launch traced here: 45.2 us
  starting transfers between devices  13.9 us (31%)
  Pallas kernels  12.6 us (28%)
  waiting for transfers between devices  12.5 us (27%)
  local copies, waits for them, and re-layouts  5.36 us (12%)
  between operations  0.77 us (2%)
    ppermute x16, starting transfers between devices, swap(): return lax.ppermute(x, axis, [(i, i ^ mask) for i in range(size)])  13.9 us
    ppermute x16, waiting for transfers between devices, swap(): return lax.ppermute(x, axis, [(i, i ^ mask) for i in range(size)])  12.5 us
    unnamed x14, local copies, waits for them, and re-layouts  5.35 us
    pallas_call x1, Pallas kernels, call_beams(): pl.pallas_call(lambda *refs: beam_kernel(axes, refs[:len(pieces)], *refs[...  5.23 us
    pallas_call x2, Pallas kernels, add_part(): pl.pallas_call(functools.partial(part_kernel, axes, flips), out_shape=jax...  2.07 us
    pallas_call x1, Pallas kernels, fast_body(): pl.pallas_call(functools.partial(band_kernel, axes), out_shape=[jax.Shape...  1.7 us
    pallas_call x1, Pallas kernels, fast_body(): pl.pallas_call(functools.partial(pack_kernel, axes), out_shape=[share] *...  1.37 us
  transfers between devices with their start and end apart: 16, of which 7 were waited for; matrix products, arithmetic and copies ran while one was open for 0% of the time, Pallas kernels for 14%

profile of v4, /device:TPU:23, one launch (start us, length us, event | category | flops | bytes accessed | tf_op | source)
XLA Modules:
  0.0 45.2 jit_solution(14157698660522948281)
XLA Ops:
  0.6 1.0 %copy-done = bf16[16,2,16,512]{3,2,1,0:T(8,128)(2,1)S(1)} copy-done((bf16[16,2,16,512]{3,2,1,0:T(8,128)(2,1)S(1)}, bf16[16,2,16,512]{3,2,1,0:T(8,128)(2,1)}, u32[]{:S(2)}) %copy-start) | copy-done | bytes 524312
  1.7 0.5 %lane_spread.1 = (bf16[4,32,512]{2,1,0:T(8,128)(2,1)S(1)}, bf16[2,32,512]{2,1,0:T(8,128)(2,1)S(1)}, bf16[2,32,512]{2,1,0:T(8,128)(2,1)S(1)}, bf16[4,32,512]{2,1,...) custom-call(bf16[16,2,16,512]{3,2,1,0:T(8,128)(2,1)S(1)} %copy-done), custom_call_target="tpu_custom_call" | custom-call | tf_op jit(solution)/shard_map/lane_spread/pallas_call | solution.py:388
  2.2 0.7 %collective-permute-start.6 = (bf16[2,32,512]{2,1,0:T(8,128)(2,1)S(1)}, bf16[2,32,512]{2,1,0:T(8,128)(2,1)S(1)}, u32[]{:S(2)}, u32[]{:S(2)}) collective-permute-start(bf16[2,32,512]{2,1,0:T(8,128)(2,1)S(1)} %get-tuple-element.47), channel_id=1, source_target_pairs={{0,1},{1,0},{2,3},{3,2},{4,5},{5,4},{6,7},{7,6},{8,9},{9,8},{10,11... | collective-permute-start | bytes 196616 | tf_op jit(solution)/shard_map/ppermute | solution.py:369
  2.9 0.1 collective-permute-start
  3.0 0.4 collective-permute-start.2
  3.5 0.3 collective-permute-start.5
  3.7 0.1 collective-permute-done.6
  3.8 1.1 %collective-permute-start.7 = (bf16[2,32,512]{2,1,0:T(8,128)(2,1)S(1)}, bf16[2,32,512]{2,1,0:T(8,128)(2,1)S(1)}, u32[]{:S(2)}, u32[]{:S(2)}) collective-permute-start(bf16[2,32,512]{2,1,0:T(8,128)(2,1)S(1)} %collective-permute-done.6), channel_id=1, source_target_pairs={{0,2},{2,0},{1,3},{3,1},{4,6},{6,4},{5,7},{7,5},{8,10},{10,8},{9,1... | collective-permute-start | bytes 196616 | tf_op jit(solution)/shard_map/ppermute | solution.py:369
  4.9 0.4 collective-permute-start.1
  5.3 0.0 collective-permute-done.2
  5.3 1.1 %collective-permute-start.3 = (bf16[2,32,512]{2,1,0:T(8,128)(2,1)S(1)}, bf16[2,32,512]{2,1,0:T(8,128)(2,1)S(1)}, u32[]{:S(2)}, u32[]{:S(2)}) collective-permute-start(bf16[2,32,512]{2,1,0:T(8,128)(2,1)S(1)} %collective-permute-done.2), channel_id=1, source_target_pairs={{0,2},{2,0},{1,3},{3,1},{4,6},{6,4},{5,7},{7,5},{8,10},{10,8},{9,1... | collective-permute-start | bytes 196616 | tf_op jit(solution)/shard_map/ppermute | solution.py:369
  6.4 0.7 %copy-done.2 = f32[16,16]{1,0:T(8,128)S(1)} copy-done((f32[16,16]{1,0:T(8,128)S(1)}, f32[16,16]{1,0:T(8,128)}, u32[]{:S(2)}) %copy-start.2) | copy-done | bytes 1048
  7.1 0.7 %copy-done.5 = s32[256]{0:T(256)S(1)} copy-done((s32[256]{0:T(256)S(1)}, s32[256]{0:T(256)}, u32[]{:S(2)}) %copy-start.5) | copy-done | bytes 1048
  7.8 0.2 station_tables.1
  8.0 0.0 collective-permute-done.5.refs_2_
  8.0 0.6 %collective-permute-done.7.refs_3_ = bf16[2,32,512]{2,1,0:T(8,128)(2,1)S(1)} collective-permute-done((bf16[2,32,512]{2,1,0:T(8,128)(2,1)S(1)}, bf16[2,32,512]{2,1,0:T(8,128)(2,1)S(1)}, u32[]{:S(2)}, u32[]{:S(2)}) %collective-permute-start.7) | collective-permute-done | bytes 65568 | tf_op jit(solution)/shard_map/ppermute | solution.py:369
  8.5 0.0 collective-permute-done.refs_1_
  8.5 0.2 plane_sums_far.1
  8.7 0.1 collective-permute-start.8
  8.8 2.4 %collective-permute-start.9 = (bf16[64,512]{1,0:T(8,128)(2,1)S(1)}, bf16[64,512]{1,0:T(8,128)(2,1)S(1)}, u32[]{:S(2)}, u32[]{:S(2)}) collective-permute-start(bf16[64,512]{1,0:T(8,128)(2,1)S(1)} %get-tuple-element.49), channel_id=1, source_target_pairs={{0,12},{4,8},{8,4},{12,0},{1,13},{5,9},{9,5},{13,1},{2,14},{6,10},... | collective-permute-start | bytes 196616 | tf_op jit(solution)/shard_map/ppermute | solution.py:369
  11.3 0.0 collective-permute-done.1.refs_2_
  11.3 0.1 collective-permute-done.3.refs_3_
  11.3 0.2 plane_sums_near.1
  11.5 1.4 %collective-permute-start.4 = (bf16[64,512]{1,0:T(8,128)(2,1)S(1)}, bf16[64,512]{1,0:T(8,128)(2,1)S(1)}, u32[]{:S(2)}, u32[]{:S(2)}) collective-permute-start(bf16[64,512]{1,0:T(8,128)(2,1)S(1)} %get-tuple-element.45), channel_id=1, source_target_pairs={{0,4},{4,0},{8,12},{12,8},{1,5},{5,1},{9,13},{13,9},{2,6},{6,2},{1... | collective-permute-start | bytes 196616 | tf_op jit(solution)/shard_map/ppermute | solution.py:369
  12.9 0.9 %copy-done.1 = bf16[4,2,256,32]{2,3,1,0:T(8,128)(2,1)S(1)} copy-done((bf16[4,2,256,32]{2,3,1,0:T(8,128)(2,1)S(1)}, bf16[4,2,256,32]{2,3,1,0:T(8,128)(2,1)}, u32[]{:S(2)}) %copy-start.1) | copy-done | bytes 131096
  13.8 1.4 %weight_shares.1 = (bf16[32,512]{1,0:T(8,128)(2,1)S(1)}, bf16[32,512]{1,0:T(8,128)(2,1)S(1)}, bf16[32,512]{1,0:T(8,128)(2,1)S(1)}, bf16[32,512]{1,0:T(8,128)(2,1)S(1)}) custom-call(bf16[4,2,32,256]{3,2,1,0:T(8,128)(2,1)S(1)} %bitcast.12), custom_call_target="tpu_custom_call" | custom-call | bytes 8388608 | tf_op jit(solution)/shard_map/weight_shares/pallas_call | solution.py:436
  15.2 0.0 collective-permute-done.8.refs_2_
  15.2 2.4 %collective-permute-done.9.refs_3_ = bf16[64,512]{1,0:T(8,128)(2,1)S(1)} collective-permute-done((bf16[64,512]{1,0:T(8,128)(2,1)S(1)}, bf16[64,512]{1,0:T(8,128)(2,1)S(1)}, u32[]{:S(2)}, u32[]{:S(2)}) %collective-permute-start.9) | collective-permute-done | bytes 65568 | tf_op jit(solution)/shard_map/ppermute | solution.py:369
  17.5 0.0 collective-permute-done.4.refs_1_
  17.6 0.6 %station_filter.1 = (bf16[64,512]{1,0:T(8,128)(2,1)S(1)}, bf16[96,512]{1,0:T(8,128)(2,1)S(1)}, bf16[96,512]{1,0:T(8,128)(2,1)S(1)}, bf16[96,512]{1,0:T(8,128)(2,1)S(1)}) custom-call(f32[16,512]{1,0:T(8,128)S(1)} %get-tuple-element.38.taps_ref, f32[64,512]{1,0:T(8,128)S(1)} %get-tuple-element.44.refs_0_, bf16[64,512]{1,0:T(8,128)(2,1)S(1)} %collective-permute-done.4.refs_1_, ...), custom_call_target="tpu_custom_call" | custom-call | tf_op jit(solution)/shard_map/station_filter/pallas_call | solution.py:447
  18.2 0.1 collective-permute-start.10
  18.3 0.4 collective-permute-start.11
  18.7 2.2 %collective-permute-start.12 = (bf16[96,512]{1,0:T(8,128)(2,1)S(1)}, bf16[96,512]{1,0:T(8,128)(2,1)S(1)}, u32[]{:S(2)}, u32[]{:S(2)}) collective-permute-start(bf16[96,512]{1,0:T(8,128)(2,1)S(1)} %get-tuple-element.57), channel_id=1, source_target_pairs={{0,12},{4,8},{8,4},{12,0},{1,13},{5,9},{9,5},{13,1},{2,14},{6,10},... | collective-permute-start | bytes 294920 | tf_op jit(solution)/shard_map/ppermute | solution.py:369
  20.9 0.8 %collective-permute-done.10.refs_1_ = bf16[96,512]{1,0:T(8,128)(2,1)S(1)} collective-permute-done((bf16[96,512]{1,0:T(8,128)(2,1)S(1)}, bf16[96,512]{1,0:T(8,128)(2,1)S(1)}, u32[]{:S(2)}, u32[]{:S(2)}) %collective-permute-start.10) | collective-permute-done | bytes 98336 | tf_op jit(solution)/shard_map/ppermute | solution.py:369
  21.7 0.7 %copy-done.3 = f32[16,16]{1,0:T(8,128)S(1)} copy-done((f32[16,16]{1,0:T(8,128)S(1)}, f32[16,16]{1,0:T(8,128)}, u32[]{:S(2)}) %copy-start.3) | copy-done | bytes 1048
  22.4 0.7 %copy-done.4 = s32[1024]{0:T(1024)S(1)} copy-done((s32[1024]{0:T(1024)S(1)}, s32[1024]{0:T(1024)}, u32[]{:S(2)}) %copy-start.4) | copy-done | bytes 4120
  23.1 0.7 %copy-done.6 = s32[32,1]{0,1:T(1,128)S(1)} copy-done((s32[32,1]{0,1:T(1,128)S(1)}, s32[32,1]{0,1:T(1,128)}, u32[]{:S(2)}) %copy-start.6) | copy-done | bytes 152
  23.7 1.7 %synthesis_bands.1 = (bf16[16,768,256]{2,1,0:T(8,128)(2,1)S(1)}, f32[32,64]{1,0:T(8,128)S(1)}, f32[32,64]{1,0:T(8,128)S(1)}) custom-call(s32[1,32]{1,0:T(1,128)S(1)} %bitcast.16, s32[1,1024]{1,0:T(1,128)S(1)} %bitcast.14, f32[16,16]{1,0:T(8,128)S(1)} %copy-done.3), custom_call_target="tpu_custom_call" | custom-call | bytes 16777216 | tf_op jit(solution)/shard_map/synthesis_bands/pallas_call | solution.py:462
  25.5 4.3 %collective-permute-done.12.refs_3_ = bf16[96,512]{1,0:T(8,128)(2,1)S(1)} collective-permute-done((bf16[96,512]{1,0:T(8,128)(2,1)S(1)}, bf16[96,512]{1,0:T(8,128)(2,1)S(1)}, u32[]{:S(2)}, u32[]{:S(2)}) %collective-permute-start.12) | collective-permute-done | bytes 98336 | tf_op jit(solution)/shard_map/ppermute | solution.py:369
  29.8 0.1 collective-permute-start.14
  29.9 1.1 %collective-permute-start.13 = (bf16[4,64,512]{2,1,0:T(8,128)(2,1)S(1)}, bf16[4,64,512]{2,1,0:T(8,128)(2,1)S(1)}, u32[]{:S(2)}, u32[]{:S(2)}) collective-permute-start(bf16[4,64,512]{2,1,0:T(8,128)(2,1)S(1)} %pad_maximum_fusion.refs_0_), channel_id=1, source_target_pairs={{0,1},{1,0},{2,3},{3,2},{4,5},{5,4},{6,7},{7,6},{8,9},{9,8},{10,11... | collective-permute-start | bytes 786440 | tf_op jit(solution)/shard_map/ppermute | solution.py:369
  31.0 0.6 %weight_matrix.1.m_ref.refs_4_ = bf16[16,128,1024]{2,1,0:T(8,128)(2,1)S(1)} custom-call(f32[32,64]{1,0:T(8,128)S(1)} %get-tuple-element.66.chosen_ref, f32[32,64]{1,0:T(8,128)S(1)} %get-tuple-element.67.scale_ref, bf16[32,512]{1,0:T(8,128)(2,1)S(1)} %get-tuple-element.68.refs_0_, bf16[96,512]{1,0:T(8,128)(2,1)S(1)} %collective-permute-done.10.refs_1_, ...), custom_call_target="tpu_custom_call" | custom-call | bytes 8388608 | tf_op jit(solution)/shard_map/weight_matrix/pallas_call | solution.py:480
  31.7 0.7 %own_beams.1.refs_2_ = f32[16,128,512]{2,1,0:T(8,128)S(1)} custom-call(bf16[16,128,1024]{2,1,0:T(8,128)(2,1)S(1)} %weight_matrix.1.m_ref.refs_4_, bf16[4,64,512]{2,1,0:T(8,128)(2,1)S(1)} %pad_maximum_fusion.refs_0_), custom_call_target="tpu_custom_call" | custom-call | bytes 8388608 | tf_op jit(solution)/shard_map/own_beams/pallas_call | solution.py:492
  32.4 4.2 %collective-permute-done.14.refs_1_.refs_2_ = bf16[4,64,512]{2,1,0:T(8,128)(2,1)S(1)} collective-permute-done((bf16[4,64,512]{2,1,0:T(8,128)(2,1)S(1)}, bf16[4,64,512]{2,1,0:T(8,128)(2,1)S(1)}, u32[]{:S(2)}, u32[]{:S(2)}) %collective-permute-start.14) | collective-permute-done | bytes 262176 | tf_op jit(solution)/shard_map/ppermute | solution.py:369
  36.7 1.9 %collective-permute-start.15 = (bf16[4,64,512]{2,1,0:T(8,128)(2,1)S(1)}, bf16[4,64,512]{2,1,0:T(8,128)(2,1)S(1)}, u32[]{:S(2)}, u32[]{:S(2)}) collective-permute-start(bf16[4,64,512]{2,1,0:T(8,128)(2,1)S(1)} %collective-permute-done.14.refs_1_.refs_2_), channel_id=1, source_target_pairs={{0,1},{1,0},{2,3},{3,2},{4,5},{5,4},{6,7},{7,6},{8,9},{9,8},{10,11... | collective-permute-start | bytes 786440 | tf_op jit(solution)/shard_map/ppermute | solution.py:369
  38.6 1.3 %near_beams.1.refs_6_ = f32[16,128,512]{2,1,0:T(8,128)S(1)} custom-call(bf16[16,128,1024]{2,1,0:T(8,128)(2,1)S(1)} %weight_matrix.1.m_ref.refs_4_, bf16[4,64,512]{2,1,0:T(8,128)(2,1)S(1)} %collective-permute-done.13.refs_0_.refs_1_, bf16[4,64,512]{2,1,0:T(8,128)(2,1)S(1)} %collective-permute-done.14.refs_1_.refs_2_, f32[16,128,512]{2,1,0:T(8,128)S(1)} %own_beams.1.refs_2_), custom_call_target="tpu_custom_call" | custom-call | bytes 8388608 | tf_op jit(solution)/shard_map/near_beams/pallas_call | solution.py:492
  40.0 0.0 collective-permute-done.15.refs_3_
  40.0 5.2 %beams_and_series.1 = (f32[128,2,8,512]{3,2,1,0:T(8,128)}, f32[4,2,8,32]{3,2,1,0:T(8,128)}) custom-call(bf16[4,64,512]{2,1,0:T(8,128)(2,1)S(1)} %pad_maximum_fusion.refs_0_, bf16[4,64,512]{2,1,0:T(8,128)(2,1)S(1)} %collective-permute-done.13.refs_0_.refs_1_, bf16[4,64,512]{2,1,0:T(8,128)(2,1)S(1)} %collective-permute-done.14.refs_1_.refs_2_, ...), custom_call_target="tpu_custom_call" | custom-call | tf_op jit(solution)/shard_map/beams_and_series/pallas_call | solution.py:346
  (12 shorter events, 0.1 us)
Async XLA Ops:
  0.6 1.0 %copy-start = (bf16[16,2,16,512]{3,2,1,0:T(8,128)(2,1)S(1)}, bf16[16,2,16,512]{3,2,1,0:T(8,128)(2,1)}, u32[]{:S(2)}) copy-start(bf16[16,2,16,512]{3,2,1,0:T(8,128)(2,1)} %x_ref.1) | copy-start | bytes 1572868
  2.2 1.6 %collective-permute-start.6 = (bf16[2,32,512]{2,1,0:T(8,128)(2,1)S(1)}, bf16[2,32,512]{2,1,0:T(8,128)(2,1)S(1)}, u32[]{:S(2)}, u32[]{:S(2)}) collective-permute-start(bf16[2,32,512]{2,1,0:T(8,128)(2,1)S(1)} %get-tuple-element.47), channel_id=1, source_target_pairs={{0,1},{1,0},{2,3},{3,2},{4,5},{5,4},{6,7},{7,6},{8,9},{9,8},{10,11... | collective-permute-start | bytes 196616 | tf_op jit(solution)/shard_map/ppermute | solution.py:369
  2.9 5.6 %collective-permute-start = (bf16[4,32,512]{2,1,0:T(8,128)(2,1)S(1)}, bf16[4,32,512]{2,1,0:T(8,128)(2,1)S(1)}, u32[]{:S(2)}, u32[]{:S(2)}) collective-permute-start(bf16[4,32,512]{2,1,0:T(8,128)(2,1)S(1)} %get-tuple-element.41), channel_id=1, source_target_pairs={{0,1},{1,0},{2,3},{3,2},{4,5},{5,4},{6,7},{7,6},{8,9},{9,8},{10,11... | collective-permute-start | bytes 393224 | tf_op jit(solution)/shard_map/ppermute | solution.py:369
  3.0 2.3 %collective-permute-start.2 = (bf16[2,32,512]{2,1,0:T(8,128)(2,1)S(1)}, bf16[2,32,512]{2,1,0:T(8,128)(2,1)S(1)}, u32[]{:S(2)}, u32[]{:S(2)}) collective-permute-start(bf16[2,32,512]{2,1,0:T(8,128)(2,1)S(1)} %get-tuple-element.43), channel_id=1, source_target_pairs={{0,1},{1,0},{2,3},{3,2},{4,5},{5,4},{6,7},{7,6},{8,9},{9,8},{10,11... | collective-permute-start | bytes 196616 | tf_op jit(solution)/shard_map/ppermute | solution.py:369
  3.5 4.5 %collective-permute-start.5 = (bf16[2,32,512]{2,1,0:T(8,128)(2,1)S(1)}, bf16[2,32,512]{2,1,0:T(8,128)(2,1)S(1)}, u32[]{:S(2)}, u32[]{:S(2)}) collective-permute-start(bf16[2,32,512]{2,1,0:T(8,128)(2,1)S(1)} %get-tuple-element.46), channel_id=1, source_target_pairs={{0,2},{2,0},{1,3},{3,1},{4,6},{6,4},{5,7},{7,5},{8,10},{10,8},{9,1... | collective-permute-start | bytes 196616 | tf_op jit(solution)/shard_map/ppermute | solution.py:369
  3.8 4.7 %collective-permute-start.7 = (bf16[2,32,512]{2,1,0:T(8,128)(2,1)S(1)}, bf16[2,32,512]{2,1,0:T(8,128)(2,1)S(1)}, u32[]{:S(2)}, u32[]{:S(2)}) collective-permute-start(bf16[2,32,512]{2,1,0:T(8,128)(2,1)S(1)} %collective-permute-done.6), channel_id=1, source_target_pairs={{0,2},{2,0},{1,3},{3,1},{4,6},{6,4},{5,7},{7,5},{8,10},{10,8},{9,1... | collective-permute-start | bytes 196616 | tf_op jit(solution)/shard_map/ppermute | solution.py:369
  4.9 6.3 %collective-permute-start.1 = (bf16[2,32,512]{2,1,0:T(8,128)(2,1)S(1)}, bf16[2,32,512]{2,1,0:T(8,128)(2,1)S(1)}, u32[]{:S(2)}, u32[]{:S(2)}) collective-permute-start(bf16[2,32,512]{2,1,0:T(8,128)(2,1)S(1)} %get-tuple-element.42), channel_id=1, source_target_pairs={{0,2},{2,0},{1,3},{3,1},{4,6},{6,4},{5,7},{7,5},{8,10},{10,8},{9,1... | collective-permute-start | bytes 196616 | tf_op jit(solution)/shard_map/ppermute | solution.py:369
  5.3 6.0 %collective-permute-start.3 = (bf16[2,32,512]{2,1,0:T(8,128)(2,1)S(1)}, bf16[2,32,512]{2,1,0:T(8,128)(2,1)S(1)}, u32[]{:S(2)}, u32[]{:S(2)}) collective-permute-start(bf16[2,32,512]{2,1,0:T(8,128)(2,1)S(1)} %collective-permute-done.2), channel_id=1, source_target_pairs={{0,2},{2,0},{1,3},{3,1},{4,6},{6,4},{5,7},{7,5},{8,10},{10,8},{9,1... | collective-permute-start | bytes 196616 | tf_op jit(solution)/shard_map/ppermute | solution.py:369
  6.4 0.7 %copy-start.2 = (f32[16,16]{1,0:T(8,128)S(1)}, f32[16,16]{1,0:T(8,128)}, u32[]{:S(2)}) copy-start(f32[16,16]{1,0:T(8,128)} %taps_ref.1) | copy-start | bytes 3076
  7.1 0.7 %copy-start.5 = (s32[256]{0:T(256)S(1)}, s32[256]{0:T(256)}, u32[]{:S(2)}) copy-start(s32[256]{0:T(256)} %param.10) | copy-start | bytes 3076
  8.7 6.5 %collective-permute-start.8 = (bf16[64,512]{1,0:T(8,128)(2,1)S(1)}, bf16[64,512]{1,0:T(8,128)(2,1)S(1)}, u32[]{:S(2)}, u32[]{:S(2)}) collective-permute-start(bf16[64,512]{1,0:T(8,128)(2,1)S(1)} %get-tuple-element.48), channel_id=1, source_target_pairs={{0,8},{4,12},{8,0},{12,4},{1,9},{5,13},{9,1},{13,5},{2,10},{6,14},... | collective-permute-start | bytes 196616 | tf_op jit(solution)/shard_map/ppermute | solution.py:369
  8.8 8.7 %collective-permute-start.9 = (bf16[64,512]{1,0:T(8,128)(2,1)S(1)}, bf16[64,512]{1,0:T(8,128)(2,1)S(1)}, u32[]{:S(2)}, u32[]{:S(2)}) collective-permute-start(bf16[64,512]{1,0:T(8,128)(2,1)S(1)} %get-tuple-element.49), channel_id=1, source_target_pairs={{0,12},{4,8},{8,4},{12,0},{1,13},{5,9},{9,5},{13,1},{2,14},{6,10},... | collective-permute-start | bytes 196616 | tf_op jit(solution)/shard_map/ppermute | solution.py:369
  11.5 6.0 %collective-permute-start.4 = (bf16[64,512]{1,0:T(8,128)(2,1)S(1)}, bf16[64,512]{1,0:T(8,128)(2,1)S(1)}, u32[]{:S(2)}, u32[]{:S(2)}) collective-permute-start(bf16[64,512]{1,0:T(8,128)(2,1)S(1)} %get-tuple-element.45), channel_id=1, source_target_pairs={{0,4},{4,0},{8,12},{12,8},{1,5},{5,1},{9,13},{13,9},{2,6},{6,2},{1... | collective-permute-start | bytes 196616 | tf_op jit(solution)/shard_map/ppermute | solution.py:369
  12.9 0.9 %copy-start.1 = (bf16[4,2,256,32]{2,3,1,0:T(8,128)(2,1)S(1)}, bf16[4,2,256,32]{2,3,1,0:T(8,128)(2,1)}, u32[]{:S(2)}) copy-start(bf16[4,2,256,32]{2,3,1,0:T(8,128)(2,1)} %param.13) | copy-start | bytes 393220
  18.2 3.5 %collective-permute-start.10 = (bf16[96,512]{1,0:T(8,128)(2,1)S(1)}, bf16[96,512]{1,0:T(8,128)(2,1)S(1)}, u32[]{:S(2)}, u32[]{:S(2)}) collective-permute-start(bf16[96,512]{1,0:T(8,128)(2,1)S(1)} %get-tuple-element.54), channel_id=1, source_target_pairs={{0,4},{4,0},{8,12},{12,8},{1,5},{5,1},{9,13},{13,9},{2,6},{6,2},{1... | collective-permute-start | bytes 294920 | tf_op jit(solution)/shard_map/ppermute | solution.py:369
  18.3 7.1 %collective-permute-start.11 = (bf16[96,512]{1,0:T(8,128)(2,1)S(1)}, bf16[96,512]{1,0:T(8,128)(2,1)S(1)}, u32[]{:S(2)}, u32[]{:S(2)}) collective-permute-start(bf16[96,512]{1,0:T(8,128)(2,1)S(1)} %get-tuple-element.56), channel_id=1, source_target_pairs={{0,8},{4,12},{8,0},{12,4},{1,9},{5,13},{9,1},{13,5},{2,10},{6,14},... | collective-permute-start | bytes 294920 | tf_op jit(solution)/shard_map/ppermute | solution.py:369
  18.7 11.1 %collective-permute-start.12 = (bf16[96,512]{1,0:T(8,128)(2,1)S(1)}, bf16[96,512]{1,0:T(8,128)(2,1)S(1)}, u32[]{:S(2)}, u32[]{:S(2)}) collective-permute-start(bf16[96,512]{1,0:T(8,128)(2,1)S(1)} %get-tuple-element.57), channel_id=1, source_target_pairs={{0,12},{4,8},{8,4},{12,0},{1,13},{5,9},{9,5},{13,1},{2,14},{6,10},... | collective-permute-start | bytes 294920 | tf_op jit(solution)/shard_map/ppermute | solution.py:369
  21.7 0.7 %copy-start.3 = (f32[16,16]{1,0:T(8,128)S(1)}, f32[16,16]{1,0:T(8,128)}, u32[]{:S(2)}) copy-start(f32[16,16]{1,0:T(8,128)} %taps_ref.2) | copy-start | bytes 3076
  22.4 0.7 %copy-start.4 = (s32[1024]{0:T(1024)S(1)}, s32[1024]{0:T(1024)}, u32[]{:S(2)}) copy-start(s32[1024]{0:T(1024)} %param.12) | copy-start | bytes 12292
  23.1 0.7 %copy-start.6 = (s32[32,1]{0,1:T(1,128)S(1)}, s32[32,1]{0,1:T(1,128)}, u32[]{:S(2)}) copy-start(s32[32,1]{0,1:T(1,128)} %param.11) | copy-start | bytes 388
  29.8 6.8 %collective-permute-start.14 = (bf16[4,64,512]{2,1,0:T(8,128)(2,1)S(1)}, bf16[4,64,512]{2,1,0:T(8,128)(2,1)S(1)}, u32[]{:S(2)}, u32[]{:S(2)}) collective-permute-start(bf16[4,64,512]{2,1,0:T(8,128)(2,1)S(1)} %pad_maximum_fusion.refs_0_), channel_id=1, source_target_pairs={{0,2},{2,0},{1,3},{3,1},{4,6},{6,4},{5,7},{7,5},{8,10},{10,8},{9,1... | collective-permute-start | bytes 786440 | tf_op jit(solution)/shard_map/ppermute | solution.py:369
  29.9 8.7 %collective-permute-start.13 = (bf16[4,64,512]{2,1,0:T(8,128)(2,1)S(1)}, bf16[4,64,512]{2,1,0:T(8,128)(2,1)S(1)}, u32[]{:S(2)}, u32[]{:S(2)}) collective-permute-start(bf16[4,64,512]{2,1,0:T(8,128)(2,1)S(1)} %pad_maximum_fusion.refs_0_), channel_id=1, source_target_pairs={{0,1},{1,0},{2,3},{3,2},{4,5},{5,4},{6,7},{7,6},{8,9},{9,8},{10,11... | collective-permute-start | bytes 786440 | tf_op jit(solution)/shard_map/ppermute | solution.py:369
  36.7 3.3 %collective-permute-start.15 = (bf16[4,64,512]{2,1,0:T(8,128)(2,1)S(1)}, bf16[4,64,512]{2,1,0:T(8,128)(2,1)S(1)}, u32[]{:S(2)}, u32[]{:S(2)}) collective-permute-start(bf16[4,64,512]{2,1,0:T(8,128)(2,1)S(1)} %collective-permute-done.14.refs_1_.refs_2_), channel_id=1, source_target_pairs={{0,1},{1,0},{2,3},{3,2},{4,5},{5,4},{6,7},{7,6},{8,9},{9,8},{10,11... | collective-permute-start | bytes 786440 | tf_op jit(solution)/shard_map/ppermute | solution.py:369

commit v5 on v4

--- a/solution.py
+++ b/solution.py
@@ -13,6 +13,15 @@
 VMEM_LIMIT = 24 * 1024 * 1024
 HALO = 128
 FLIPS = ((0, 0), (0, 1), (1, 0), (1, 1))
+NEAR, FAR = (0, 1), (2, 3)
+PLACES = (
+    (FLIPS[0], NEAR + FAR),
+    (FLIPS[1], NEAR + FAR),
+    (FLIPS[2], NEAR),
+    (FLIPS[2], FAR),
+    (FLIPS[3], NEAR),
+    (FLIPS[3], FAR),
+)
 
 
 def fourier(parts, sign):
@@ -191,6 +200,12 @@
     upper = jnp.concatenate([v for k in range(chan) for v in (real[k], -imag[k])], axis=0)
     lower = jnp.concatenate([v for k in range(chan) for v in (imag[k], real[k])], axis=0)
     whole = jnp.concatenate([upper, lower], axis=1).T.astype(m_ref.dtype)
+    count = 2 * beams
+    place = lax.broadcasted_iota(jnp.int32, (count, 1), 0)
+    source = place % 2 * beams + place // 2
+    order = jnp.where(lax.broadcasted_iota(jnp.int32, (count, count), 1) == source, 1.0, 0.0)
+    whole = jnp.dot(order.astype(m_ref.dtype), whole, preferred_element_type=jnp.float32)
+    whole = whole.astype(m_ref.dtype)
     width = whole.shape[1]
     step = 2 * stations
     odd = jnp.concatenate([whole[:, width - step :], whole[:, : width - step]], axis=1)
@@ -202,13 +217,13 @@
             m_ref[c, :, :start] = base[:, width - start :]
 
 
-def gather_lanes(axes, x_refs, flips, lanes_ref):
+def gather_lanes(axes, x_refs, places, lanes_ref):
     row, col, sub = (lax.axis_index(a) for a in axes)
     rows = x_refs[0].shape[1]
-    for (dc, ds), ref in zip(flips, x_refs):
-        for m in range(4):
+    for ((dc, ds), masks), ref in zip(places, x_refs):
+        for k, m in enumerate(masks):
             lane = lane_of(row ^ m, col ^ dc, sub ^ ds)
-            lanes_ref[pl.ds(pl.multiple_of(lane * rows, rows), rows)] = ref[m]
+            lanes_ref[pl.ds(pl.multiple_of(lane * rows, rows), rows)] = ref[k]
 
 
 def lane_products(axes, flips, m_ref, lanes_ref, first, count):
@@ -224,10 +239,11 @@
     return total
 
 
-def part_kernel(axes, flips, m_ref, *refs):
-    x_refs, (sum_ref, lanes_ref) = refs[: len(flips)], refs[-2:]
-    before = refs[len(flips) : -2]
-    gather_lanes(axes, x_refs, flips, lanes_ref)
+def part_kernel(axes, places, m_ref, *refs):
+    x_refs, (sum_ref, lanes_ref) = refs[: len(places)], refs[-2:]
+    before = refs[len(places) : -2]
+    gather_lanes(axes, x_refs, places, lanes_ref)
+    flips = sorted({flip for flip, _ in places})
     for first in range(0, m_ref.shape[0], 4):
         found = lane_products(axes, flips, m_ref, lanes_ref, first, 4)
         found = found.reshape((4,) + sum_ref.shape[1:])
@@ -256,45 +272,36 @@
     chan = 4 * 4
     frames = lanes_ref.shape[1]
 
-    gather_lanes(axes, x_refs, FLIPS, lanes_ref)
+    gather_lanes(axes, x_refs[4:], PLACES[4:], lanes_ref)
     beams = m_ref.shape[1] // 2
     tile = t_ref.shape[2]
     stores = []
-    for half in range(2):
-        for first in range(8 * half, 8 * half + 8, 4):
-            found = lane_products(axes, FLIPS[3:], m_ref, lanes_ref, first, 4)
-            found = found.reshape((4,) + sum_ref.shape[1:]) + sum_ref[first : first + 4]
-            inverse_ref[first : first + 4] = found.astype(jnp.bfloat16)
+    for first in range(0, 16, 4):
+        found = lane_products(axes, FLIPS[3:], m_ref, lanes_ref, first, 4)
+        found = found.reshape((4,) + sum_ref.shape[1:]) + sum_ref[first : first + 4]
+        inverse_ref[first : first + 4] = found.astype(jnp.bfloat16)
+    for lane in range(chan):
         for n in range(frames // tile):
-            for c in range(8):
-                lane = 8 * half + c
-                taken = [inverse_ref[lane, :, n * tile : (n + 1) * tile]] * 2
-                first = 2 * HALO
-                if n > 0:
-                    taken = [inverse_ref[lane, :, n * tile - HALO : n * tile]] * 2 + taken
-                    first = 0
-                value = jnp.dot(
-                    jnp.concatenate(taken, axis=1),
-                    t_ref[lane, first:],
-                    preferred_element_type=jnp.float32,
-                )
-                for part in range(2):
-                    slot = (2 * n + half) * 2 + part
-                    for q in range(2):
-                        out_ref.at[slot][pl.ds(q * 8 + c, beams, stride=16), :] = value[
-                            q * beams : (q + 1) * beams, part * 128 : (part + 1) * 128
-                        ]
-            for part in range(2):
-                first = n * tile + part * 128
-                slot = (2 * n + half) * 2 + part
+            taken = [inverse_ref[lane, :, n * tile : (n + 1) * tile]] * 2
+            first = 2 * HALO
+            if n > 0:
+                taken = [inverse_ref[lane, :, n * tile - HALO : n * tile]] * 2 + taken
+                first = 0
+            value = jnp.dot(
+                jnp.concatenate(taken, axis=1), t_ref[lane, first:], preferred_element_type=jnp.float32
+            )
+            for part in range(tile // 128):
+                slot = n * (tile // 128) + part
+                out_ref[lane, slot] = value[:, part * 128 : (part + 1) * 128]
                 stores.append(
                     pltpu.make_async_copy(
-                        out_ref.at[slot].reshape(2 * beams, 8, 128),
-                        series_ref.at[:, half, :, first : first + 128],
-                        store_sems.at[slot],
+                        out_ref.at[lane, slot],
+                        series_ref.at[:, lane // 8, lane % 8, pl.ds(slot * 128, 128)],
+                        store_sems.at[lane, slot],
                     )
                 )
                 stores[-1].start()
+    gather_lanes(axes, x_refs[:4], PLACES[:4], lanes_ref)
     inner = []
     for b in range(4):
         parts = []
@@ -342,7 +349,6 @@
     chan, frames = bands.shape[0], pieces[0].shape[2]
     stations, beams = pieces[0].shape[1] // 2, matrix.shape[1] // 2
     anywhere = pl.BlockSpec(memory_space=pl.ANY)
-    slots = frames // 128 * 2
     series, visibilities = pl.pallas_call(
         lambda *refs: beam_kernel(axes, refs[: len(pieces)], *refs[len(pieces) :]),
         out_shape=(
@@ -355,8 +361,8 @@
             pltpu.VMEM((chan * 2 * stations, frames), jnp.bfloat16),
             pltpu.VMEM((2 * stations, 2 * stations), jnp.float32),
             pltpu.VMEM((chan, 2 * beams, frames), jnp.bfloat16),
-            pltpu.VMEM((slots, 2 * beams * 8, 128), jnp.float32),
-            pltpu.SemaphoreType.DMA((slots,)),
+            pltpu.VMEM((chan, frames // 128, 2 * beams, 128), jnp.float32),
+            pltpu.SemaphoreType.DMA((chan, frames // 128)),
         ],
         compiler_params=params,
         name="beams_and_series",
@@ -456,9 +462,11 @@
 
     tile = 256
     table = jax.ShapeDtypeStruct((stations, beams), jnp.float32)
+    other = [swap(filtered, "col", 1)]
     moved[0], *small = lax.optimization_barrier(
         (moved[0], station_group, beam_group, synthesis_taps)
     )
+    other.append(swap(moved[0][: 2 * stations], "col", 1))
     bands, chosen, scale = pl.pallas_call(
         functools.partial(band_kernel, axes),
         out_shape=[
@@ -476,7 +484,9 @@
         small[1].reshape(1, beam_group.shape[0]),
         small[2],
     )
-    *moved[1:], bands, chosen, scale = lax.optimization_barrier((*moved[1:], bands, chosen, scale))
+    moved[1], moved[2], other[0], other[1], bands, chosen, scale = lax.optimization_barrier(
+        (*moved[1:], *other, bands, chosen, scale)
+    )
     matrix = pl.pallas_call(
         functools.partial(weight_kernel, axes),
         out_shape=jax.ShapeDtypeStruct((chan, 2 * beams, 2 * chan * stations), jnp.bfloat16),
@@ -488,9 +498,9 @@
         name="weight_matrix",
     )(chosen, scale, shares[0], *moved)
 
-    def add_part(flips, xs, before, name):
+    def add_part(places, xs, before, name):
         return pl.pallas_call(
-            functools.partial(part_kernel, axes, flips),
+            functools.partial(part_kernel, axes, places),
             out_shape=jax.ShapeDtypeStruct((chan, 2 * beams, frames), jnp.float32),
             in_specs=[vmem] * (1 + len(xs) + len(before)),
             out_specs=vmem,
@@ -500,14 +510,16 @@
             name=name,
         )(matrix, *xs, *before)
 
-    held = jnp.stack([filtered] + [x[: 2 * stations] for x in moved])
-    other = swap(held, "col", 1)
-    paired = swap(held, "sub", 1)
-    sums = add_part(FLIPS[:1], [held], [], "own_beams")
-    other, sums = lax.optimization_barrier((other, sums))
-    last = swap(other, "sub", 1)
-    sums = add_part(FLIPS[1:3], [paired, other], [sums], "near_beams")
-    pieces = [held, paired, other, last]
+    distant = [x[: 2 * stations] for x in moved[1:]]
+    held = jnp.stack([filtered, moved[0][: 2 * stations], *distant])
+    near = jnp.stack(other)
+    far = swap(jnp.stack(distant), "col", 1)
+    paired, last_near = swap(held, "sub", 1), swap(near, "sub", 1)
+    sums = add_part(PLACES[:1], [held], [], "own_beams")
+    far, sums = lax.optimization_barrier((far, sums))
+    last_far = swap(far, "sub", 1)
+    sums = add_part(PLACES[1:4], [paired, near, far], [sums], "near_beams")
+    pieces = [held, paired, near, far, last_near, last_far]
 
     visibilities, series = call_beams(axes, pieces, matrix, bands, sums)
     return visibilities, series.reshape(beams, 2, chan, frames)

time: 45.5 us -> 43.7 us (0.960)
  the two profiles are of different devices: /device:TPU:23 before, /device:TPU:0 now
where the time goes in v5:
time: 43.7 us; the launch traced here: 43.3 us
  starting transfers between devices  18.6 us (43%)
  Pallas kernels  12.1 us (28%)
  waiting for transfers between devices  6.39 us (15%)
  local copies, waits for them, and re-layouts  5.37 us (12%)
  between operations  0.8 us (2%)
    ppermute x19, starting transfers between devices, swap(): return lax.ppermute(x, axis, [(i, i ^ mask) for i in range(size)])  18.6 us
    ppermute x19, waiting for transfers between devices, swap(): return lax.ppermute(x, axis, [(i, i ^ mask) for i in range(size)])  6.39 us
    unnamed x14, local copies, waits for them, and re-layouts  5.35 us
    pallas_call x1, Pallas kernels, call_beams(): pl.pallas_call(lambda *refs: beam_kernel(axes, refs[:len(pieces)], *refs[...  4.52 us
    pallas_call x2, Pallas kernels, add_part(): pl.pallas_call(functools.partial(part_kernel, axes, places), out_shape=ja...  2.06 us
    pallas_call x1, Pallas kernels, fast_body(): pl.pallas_call(functools.partial(band_kernel, axes), out_shape=[jax.Shape...  1.7 us
    pallas_call x1, Pallas kernels, fast_body(): pl.pallas_call(functools.partial(pack_kernel, axes), out_shape=[share] *...  1.37 us
  transfers between devices with their start and end apart: 19, of which 5 were waited for; matrix products, arithmetic and copies ran while one was open for 0% of the time, Pallas kernels for 15%

profile of v5, /device:TPU:0, one launch (start us, length us, event | category | flops | bytes accessed | tf_op | source)
XLA Modules:
  0.0 43.3 jit_solution(15649224415654939708)
XLA Ops:
  0.6 1.0 %copy-done = bf16[16,2,16,512]{3,2,1,0:T(8,128)(2,1)S(1)} copy-done((bf16[16,2,16,512]{3,2,1,0:T(8,128)(2,1)S(1)}, bf16[16,2,16,512]{3,2,1,0:T(8,128)(2,1)}, u32[]{:S(2)}) %copy-start) | copy-done | bytes 524312
  1.7 0.5 %lane_spread.1 = (bf16[4,32,512]{2,1,0:T(8,128)(2,1)S(1)}, bf16[2,32,512]{2,1,0:T(8,128)(2,1)S(1)}, bf16[2,32,512]{2,1,0:T(8,128)(2,1)S(1)}, bf16[4,32,512]{2,1,...) custom-call(bf16[16,2,16,512]{3,2,1,0:T(8,128)(2,1)S(1)} %copy-done), custom_call_target="tpu_custom_call" | custom-call | tf_op jit(solution)/shard_map/lane_spread/pallas_call | solution.py:394
  2.2 0.5 %collective-permute-start.6 = (bf16[2,32,512]{2,1,0:T(8,128)(2,1)S(1)}, bf16[2,32,512]{2,1,0:T(8,128)(2,1)S(1)}, u32[]{:S(2)}, u32[]{:S(2)}) collective-permute-start(bf16[2,32,512]{2,1,0:T(8,128)(2,1)S(1)} %get-tuple-element.49), channel_id=1, source_target_pairs={{0,1},{1,0},{2,3},{3,2},{4,5},{5,4},{6,7},{7,6},{8,9},{9,8},{10,11... | collective-permute-start | bytes 196616 | tf_op jit(solution)/shard_map/ppermute | solution.py:375
  2.7 0.1 collective-permute-start
  2.8 0.4 collective-permute-start.2
  3.2 2.6 %collective-permute-start.5 = (bf16[2,32,512]{2,1,0:T(8,128)(2,1)S(1)}, bf16[2,32,512]{2,1,0:T(8,128)(2,1)S(1)}, u32[]{:S(2)}, u32[]{:S(2)}) collective-permute-start(bf16[2,32,512]{2,1,0:T(8,128)(2,1)S(1)} %get-tuple-element.48), channel_id=1, source_target_pairs={{0,2},{2,0},{1,3},{3,1},{4,6},{6,4},{5,7},{7,5},{8,10},{10,8},{9,1... | collective-permute-start | bytes 196616 | tf_op jit(solution)/shard_map/ppermute | solution.py:375
  5.8 0.0 collective-permute-done.6
  5.8 0.7 %collective-permute-start.7 = (bf16[2,32,512]{2,1,0:T(8,128)(2,1)S(1)}, bf16[2,32,512]{2,1,0:T(8,128)(2,1)S(1)}, u32[]{:S(2)}, u32[]{:S(2)}) collective-permute-start(bf16[2,32,512]{2,1,0:T(8,128)(2,1)S(1)} %collective-permute-done.6), channel_id=1, source_target_pairs={{0,2},{2,0},{1,3},{3,1},{4,6},{6,4},{5,7},{7,5},{8,10},{10,8},{9,1... | collective-permute-start | bytes 196616 | tf_op jit(solution)/shard_map/ppermute | solution.py:375
  6.5 1.4 %collective-permute-start.1 = (bf16[2,32,512]{2,1,0:T(8,128)(2,1)S(1)}, bf16[2,32,512]{2,1,0:T(8,128)(2,1)S(1)}, u32[]{:S(2)}, u32[]{:S(2)}) collective-permute-start(bf16[2,32,512]{2,1,0:T(8,128)(2,1)S(1)} %get-tuple-element.44), channel_id=1, source_target_pairs={{0,2},{2,0},{1,3},{3,1},{4,6},{6,4},{5,7},{7,5},{8,10},{10,8},{9,1... | collective-permute-start | bytes 196616 | tf_op jit(solution)/shard_map/ppermute | solution.py:375
  7.8 0.7 %collective-permute-start.3 = (bf16[2,32,512]{2,1,0:T(8,128)(2,1)S(1)}, bf16[2,32,512]{2,1,0:T(8,128)(2,1)S(1)}, u32[]{:S(2)}, u32[]{:S(2)}) collective-permute-start(bf16[2,32,512]{2,1,0:T(8,128)(2,1)S(1)} %collective-permute-done.2), channel_id=1, source_target_pairs={{0,2},{2,0},{1,3},{3,1},{4,6},{6,4},{5,7},{7,5},{8,10},{10,8},{9,1... | collective-permute-start | bytes 196616 | tf_op jit(solution)/shard_map/ppermute | solution.py:375
  8.5 0.7 %copy-done.2 = f32[16,16]{1,0:T(8,128)S(1)} copy-done((f32[16,16]{1,0:T(8,128)S(1)}, f32[16,16]{1,0:T(8,128)}, u32[]{:S(2)}) %copy-start.2) | copy-done | bytes 1048
  9.2 0.7 %copy-done.5 = s32[256]{0:T(256)S(1)} copy-done((s32[256]{0:T(256)S(1)}, s32[256]{0:T(256)}, u32[]{:S(2)}) %copy-start.5) | copy-done | bytes 1048
  9.9 0.2 station_tables.1
  10.0 0.0 collective-permute-done.5.refs_2_
  10.1 0.7 %collective-permute-done.7.refs_3_ = bf16[2,32,512]{2,1,0:T(8,128)(2,1)S(1)} collective-permute-done((bf16[2,32,512]{2,1,0:T(8,128)(2,1)S(1)}, bf16[2,32,512]{2,1,0:T(8,128)(2,1)S(1)}, u32[]{:S(2)}, u32[]{:S(2)}) %collective-permute-start.7) | collective-permute-done | bytes 65568 | tf_op jit(solution)/shard_map/ppermute | solution.py:375
  10.7 0.0 collective-permute-done.refs_1_
  10.7 0.2 plane_sums_far.1
  10.9 2.7 %collective-permute-start.8 = (bf16[64,512]{1,0:T(8,128)(2,1)S(1)}, bf16[64,512]{1,0:T(8,128)(2,1)S(1)}, u32[]{:S(2)}, u32[]{:S(2)}) collective-permute-start(bf16[64,512]{1,0:T(8,128)(2,1)S(1)} %get-tuple-element.50), channel_id=1, source_target_pairs={{0,8},{4,12},{8,0},{12,4},{1,9},{5,13},{9,1},{13,5},{2,10},{6,14},... | collective-permute-start | bytes 196616 | tf_op jit(solution)/shard_map/ppermute | solution.py:375
  13.6 1.3 %collective-permute-start.9 = (bf16[64,512]{1,0:T(8,128)(2,1)S(1)}, bf16[64,512]{1,0:T(8,128)(2,1)S(1)}, u32[]{:S(2)}, u32[]{:S(2)}) collective-permute-start(bf16[64,512]{1,0:T(8,128)(2,1)S(1)} %get-tuple-element.51), channel_id=1, source_target_pairs={{0,12},{4,8},{8,4},{12,0},{1,13},{5,9},{9,5},{13,1},{2,14},{6,10},... | collective-permute-start | bytes 196616 | tf_op jit(solution)/shard_map/ppermute | solution.py:375
  14.9 0.0 collective-permute-done.1.refs_2_
  14.9 0.2 plane_sums_near.1
  15.1 0.3 collective-permute-start.4
  15.4 0.9 %copy-done.1 = bf16[4,2,256,32]{2,3,1,0:T(8,128)(2,1)S(1)} copy-done((bf16[4,2,256,32]{2,3,1,0:T(8,128)(2,1)S(1)}, bf16[4,2,256,32]{2,3,1,0:T(8,128)(2,1)}, u32[]{:S(2)}) %copy-start.1) | copy-done | bytes 131096
  16.3 1.4 %weight_shares.1 = (bf16[32,512]{1,0:T(8,128)(2,1)S(1)}, bf16[32,512]{1,0:T(8,128)(2,1)S(1)}, bf16[32,512]{1,0:T(8,128)(2,1)S(1)}, bf16[32,512]{1,0:T(8,128)(2,1)S(1)}) custom-call(bf16[4,2,32,256]{3,2,1,0:T(8,128)(2,1)S(1)} %bitcast.14), custom_call_target="tpu_custom_call" | custom-call | bytes 8388608 | tf_op jit(solution)/shard_map/weight_shares/pallas_call | solution.py:442
  17.7 0.0 collective-permute-done.8.refs_2_
  17.7 2.0 %collective-permute-done.9.refs_3_ = bf16[64,512]{1,0:T(8,128)(2,1)S(1)} collective-permute-done((bf16[64,512]{1,0:T(8,128)(2,1)S(1)}, bf16[64,512]{1,0:T(8,128)(2,1)S(1)}, u32[]{:S(2)}, u32[]{:S(2)}) %collective-permute-start.9) | collective-permute-done | bytes 65568 | tf_op jit(solution)/shard_map/ppermute | solution.py:375
  19.7 0.4 collective-permute-done.4.refs_1_
  20.1 0.6 %station_filter.1 = (bf16[64,512]{1,0:T(8,128)(2,1)S(1)}, bf16[96,512]{1,0:T(8,128)(2,1)S(1)}, bf16[96,512]{1,0:T(8,128)(2,1)S(1)}, bf16[96,512]{1,0:T(8,128)(2,1)S(1)}) custom-call(f32[16,512]{1,0:T(8,128)S(1)} %get-tuple-element.40.taps_ref, f32[64,512]{1,0:T(8,128)S(1)} %get-tuple-element.46.refs_0_, bf16[64,512]{1,0:T(8,128)(2,1)S(1)} %collective-permute-done.4.refs_1_, ...), custom_call_target="tpu_custom_call" | custom-call | tf_op jit(solution)/shard_map/station_filter/pallas_call | solution.py:453
  20.8 0.1 collective-permute-start.10
  20.8 1.4 %collective-permute-start.13 = (bf16[64,512]{1,0:T(8,128)(2,1)S(1)}, bf16[64,512]{1,0:T(8,128)(2,1)S(1)}, u32[]{:S(2)}, u32[]{:S(2)}) collective-permute-start(bf16[64,512]{1,0:T(8,128)(2,1)S(1)} %get-tuple-element.55), channel_id=1, source_target_pairs={{0,2},{2,0},{1,3},{3,1},{4,6},{6,4},{5,7},{7,5},{8,10},{10,8},{9,1... | collective-permute-start | bytes 196616 | tf_op jit(solution)/shard_map/ppermute | solution.py:375
  22.2 2.6 %collective-permute-start.11 = (bf16[96,512]{1,0:T(8,128)(2,1)S(1)}, bf16[96,512]{1,0:T(8,128)(2,1)S(1)}, u32[]{:S(2)}, u32[]{:S(2)}) collective-permute-start(bf16[96,512]{1,0:T(8,128)(2,1)S(1)} %get-tuple-element.58), channel_id=1, source_target_pairs={{0,8},{4,12},{8,0},{12,4},{1,9},{5,13},{9,1},{13,5},{2,10},{6,14},... | collective-permute-start | bytes 294920 | tf_op jit(solution)/shard_map/ppermute | solution.py:375
  24.8 1.7 %collective-permute-start.12 = (bf16[96,512]{1,0:T(8,128)(2,1)S(1)}, bf16[96,512]{1,0:T(8,128)(2,1)S(1)}, u32[]{:S(2)}, u32[]{:S(2)}) collective-permute-start(bf16[96,512]{1,0:T(8,128)(2,1)S(1)} %get-tuple-element.59), channel_id=1, source_target_pairs={{0,12},{4,8},{8,4},{12,0},{1,13},{5,9},{9,5},{13,1},{2,14},{6,10},... | collective-permute-start | bytes 294920 | tf_op jit(solution)/shard_map/ppermute | solution.py:375
  26.6 0.0 collective-permute-done.10.refs_1_
  26.6 0.7 %collective-permute-start.14 = (bf16[64,512]{1,0:T(8,128)(2,1)S(1)}, bf16[64,512]{1,0:T(8,128)(2,1)S(1)}, u32[]{:S(2)}, u32[]{:S(2)}) collective-permute-start(bf16[64,512]{1,0:T(8,128)(2,1)S(1)} %get-tuple-element.79), channel_id=1, source_target_pairs={{0,2},{2,0},{1,3},{3,1},{4,6},{6,4},{5,7},{7,5},{8,10},{10,8},{9,1... | collective-permute-start | bytes 196616 | tf_op jit(solution)/shard_map/ppermute | solution.py:375
  27.3 0.7 %copy-done.3 = f32[16,16]{1,0:T(8,128)S(1)} copy-done((f32[16,16]{1,0:T(8,128)S(1)}, f32[16,16]{1,0:T(8,128)}, u32[]{:S(2)}) %copy-start.3) | copy-done | bytes 1048
  28.0 0.7 %copy-done.4 = s32[1024]{0:T(1024)S(1)} copy-done((s32[1024]{0:T(1024)S(1)}, s32[1024]{0:T(1024)}, u32[]{:S(2)}) %copy-start.4) | copy-done | bytes 4120
  28.7 0.7 %copy-done.6 = s32[32,1]{0,1:T(1,128)S(1)} copy-done((s32[32,1]{0,1:T(1,128)S(1)}, s32[32,1]{0,1:T(1,128)}, u32[]{:S(2)}) %copy-start.6) | copy-done | bytes 152
  29.4 1.7 %synthesis_bands.1 = (bf16[16,768,256]{2,1,0:T(8,128)(2,1)S(1)}, f32[32,64]{1,0:T(8,128)S(1)}, f32[32,64]{1,0:T(8,128)S(1)}) custom-call(s32[1,32]{1,0:T(1,128)S(1)} %bitcast.18, s32[1,1024]{1,0:T(1,128)S(1)} %bitcast.16, f32[16,16]{1,0:T(8,128)S(1)} %copy-done.3), custom_call_target="tpu_custom_call" | custom-call | bytes 16777216 | tf_op jit(solution)/shard_map/synthesis_bands/pallas_call | solution.py:470
  31.1 1.2 %collective-permute-done.11.refs_2_ = bf16[96,512]{1,0:T(8,128)(2,1)S(1)} collective-permute-done((bf16[96,512]{1,0:T(8,128)(2,1)S(1)}, bf16[96,512]{1,0:T(8,128)(2,1)S(1)}, u32[]{:S(2)}, u32[]{:S(2)}) %collective-permute-start.11) | collective-permute-done | bytes 98336 | tf_op jit(solution)/shard_map/ppermute | solution.py:375
  32.3 0.8 %collective-permute-start.16 = (bf16[2,64,512]{2,1,0:T(8,128)(2,1)S(1)}, bf16[2,64,512]{2,1,0:T(8,128)(2,1)S(1)}, u32[]{:S(2)}, u32[]{:S(2)}) collective-permute-start(bf16[2,64,512]{2,1,0:T(8,128)(2,1)S(1)} %pad_maximum_fusion.2), channel_id=1, source_target_pairs={{0,2},{2,0},{1,3},{3,1},{4,6},{6,4},{5,7},{7,5},{8,10},{10,8},{9,1... | collective-permute-start | bytes 393224 | tf_op jit(solution)/shard_map/ppermute | solution.py:375
  33.2 0.1 collective-permute-start.15
  33.3 0.6 %collective-permute-start.17 = (bf16[2,64,512]{2,1,0:T(8,128)(2,1)S(1)}, bf16[2,64,512]{2,1,0:T(8,128)(2,1)S(1)}, u32[]{:S(2)}, u32[]{:S(2)}) collective-permute-start(bf16[2,64,512]{2,1,0:T(8,128)(2,1)S(1)} %pad_maximum_fusion.1.refs_1_.refs_2_), channel_id=1, source_target_pairs={{0,1},{1,0},{2,3},{3,2},{4,5},{5,4},{6,7},{7,6},{8,9},{9,8},{10,11... | collective-permute-start | bytes 393224 | tf_op jit(solution)/shard_map/ppermute | solution.py:375
  33.8 0.8 %weight_matrix.1.m_ref.refs_6_ = bf16[16,128,1024]{2,1,0:T(8,128)(2,1)S(1)} custom-call(f32[32,64]{1,0:T(8,128)S(1)} %get-tuple-element.70.chosen_ref, f32[32,64]{1,0:T(8,128)S(1)} %get-tuple-element.71.scale_ref, bf16[32,512]{1,0:T(8,128)(2,1)S(1)} %get-tuple-element.72.refs_0_, bf16[96,512]{1,0:T(8,128)(2,1)S(1)} %collective-permute-done.10.refs_1_, ...), custom_call_target="tpu_custom_call" | custom-call | bytes 8388608 | tf_op jit(solution)/shard_map/weight_matrix/pallas_call | solution.py:490
  34.6 0.7 %own_beams.1.refs_3_ = f32[16,128,512]{2,1,0:T(8,128)S(1)} custom-call(bf16[16,128,1024]{2,1,0:T(8,128)(2,1)S(1)} %weight_matrix.1.m_ref.refs_6_, bf16[4,64,512]{2,1,0:T(8,128)(2,1)S(1)} %pad_maximum_fusion.refs_0_), custom_call_target="tpu_custom_call" | custom-call | bytes 8388608 | tf_op jit(solution)/shard_map/own_beams/pallas_call | solution.py:502
  35.4 2.0 %collective-permute-done.16.refs_2_.refs_3_ = bf16[2,64,512]{2,1,0:T(8,128)(2,1)S(1)} collective-permute-done((bf16[2,64,512]{2,1,0:T(8,128)(2,1)S(1)}, bf16[2,64,512]{2,1,0:T(8,128)(2,1)S(1)}, u32[]{:S(2)}, u32[]{:S(2)}) %collective-permute-start.16) | collective-permute-done | bytes 131104 | tf_op jit(solution)/shard_map/ppermute | solution.py:375
  37.4 1.3 %near_beams.1.refs_8_ = f32[16,128,512]{2,1,0:T(8,128)S(1)} custom-call(bf16[16,128,1024]{2,1,0:T(8,128)(2,1)S(1)} %weight_matrix.1.m_ref.refs_6_, bf16[4,64,512]{2,1,0:T(8,128)(2,1)S(1)} %collective-permute-done.15.refs_0_.refs_1_, bf16[2,64,512]{2,1,0:T(8,128)(2,1)S(1)} %pad_maximum_fusion.1.refs_1_.refs_2_, ...), custom_call_target="tpu_custom_call" | custom-call | bytes 8388608 | tf_op jit(solution)/shard_map/near_beams/pallas_call | solution.py:502
  38.7 0.0 collective-permute-done.18.refs_5_
  38.7 4.5 %beams_and_series.1 = (f32[128,2,8,512]{3,2,1,0:T(8,128)}, f32[4,2,8,32]{3,2,1,0:T(8,128)}) custom-call(bf16[4,64,512]{2,1,0:T(8,128)(2,1)S(1)} %pad_maximum_fusion.refs_0_, bf16[4,64,512]{2,1,0:T(8,128)(2,1)S(1)} %collective-permute-done.15.refs_0_.refs_1_, bf16[2,64,512]{2,1,0:T(8,128)(2,1)S(1)} %pad_maximum_fusion.1.refs_1_.refs_2_, ...), custom_call_target="tpu_custom_call" | custom-call | tf_op jit(solution)/shard_map/beams_and_series/pallas_call | solution.py:352
  (20 shorter events, 0.1 us)
Async XLA Ops:
  0.6 1.0 %copy-start = (bf16[16,2,16,512]{3,2,1,0:T(8,128)(2,1)S(1)}, bf16[16,2,16,512]{3,2,1,0:T(8,128)(2,1)}, u32[]{:S(2)}) copy-start(bf16[16,2,16,512]{3,2,1,0:T(8,128)(2,1)} %x_ref.1) | copy-start | bytes 1572868
  2.2 3.6 %collective-permute-start.6 = (bf16[2,32,512]{2,1,0:T(8,128)(2,1)S(1)}, bf16[2,32,512]{2,1,0:T(8,128)(2,1)S(1)}, u32[]{:S(2)}, u32[]{:S(2)}) collective-permute-start(bf16[2,32,512]{2,1,0:T(8,128)(2,1)S(1)} %get-tuple-element.49), channel_id=1, source_target_pairs={{0,1},{1,0},{2,3},{3,2},{4,5},{5,4},{6,7},{7,6},{8,9},{9,8},{10,11... | collective-permute-start | bytes 196616 | tf_op jit(solution)/shard_map/ppermute | solution.py:375
  2.7 8.0 %collective-permute-start = (bf16[4,32,512]{2,1,0:T(8,128)(2,1)S(1)}, bf16[4,32,512]{2,1,0:T(8,128)(2,1)S(1)}, u32[]{:S(2)}, u32[]{:S(2)}) collective-permute-start(bf16[4,32,512]{2,1,0:T(8,128)(2,1)S(1)} %get-tuple-element.43), channel_id=1, source_target_pairs={{0,1},{1,0},{2,3},{3,2},{4,5},{5,4},{6,7},{7,6},{8,9},{9,8},{10,11... | collective-permute-start | bytes 393224 | tf_op jit(solution)/shard_map/ppermute | solution.py:375
  2.8 5.0 %collective-permute-start.2 = (bf16[2,32,512]{2,1,0:T(8,128)(2,1)S(1)}, bf16[2,32,512]{2,1,0:T(8,128)(2,1)S(1)}, u32[]{:S(2)}, u32[]{:S(2)}) collective-permute-start(bf16[2,32,512]{2,1,0:T(8,128)(2,1)S(1)} %get-tuple-element.45), channel_id=1, source_target_pairs={{0,1},{1,0},{2,3},{3,2},{4,5},{5,4},{6,7},{7,6},{8,9},{9,8},{10,11... | collective-permute-start | bytes 196616 | tf_op jit(solution)/shard_map/ppermute | solution.py:375
  3.2 6.8 %collective-permute-start.5 = (bf16[2,32,512]{2,1,0:T(8,128)(2,1)S(1)}, bf16[2,32,512]{2,1,0:T(8,128)(2,1)S(1)}, u32[]{:S(2)}, u32[]{:S(2)}) collective-permute-start(bf16[2,32,512]{2,1,0:T(8,128)(2,1)S(1)} %get-tuple-element.48), channel_id=1, source_target_pairs={{0,2},{2,0},{1,3},{3,1},{4,6},{6,4},{5,7},{7,5},{8,10},{10,8},{9,1... | collective-permute-start | bytes 196616 | tf_op jit(solution)/shard_map/ppermute | solution.py:375
  5.8 4.9 %collective-permute-start.7 = (bf16[2,32,512]{2,1,0:T(8,128)(2,1)S(1)}, bf16[2,32,512]{2,1,0:T(8,128)(2,1)S(1)}, u32[]{:S(2)}, u32[]{:S(2)}) collective-permute-start(bf16[2,32,512]{2,1,0:T(8,128)(2,1)S(1)} %collective-permute-done.6), channel_id=1, source_target_pairs={{0,2},{2,0},{1,3},{3,1},{4,6},{6,4},{5,7},{7,5},{8,10},{10,8},{9,1... | collective-permute-start | bytes 196616 | tf_op jit(solution)/shard_map/ppermute | solution.py:375
  6.5 8.5 %collective-permute-start.1 = (bf16[2,32,512]{2,1,0:T(8,128)(2,1)S(1)}, bf16[2,32,512]{2,1,0:T(8,128)(2,1)S(1)}, u32[]{:S(2)}, u32[]{:S(2)}) collective-permute-start(bf16[2,32,512]{2,1,0:T(8,128)(2,1)S(1)} %get-tuple-element.44), channel_id=1, source_target_pairs={{0,2},{2,0},{1,3},{3,1},{4,6},{6,4},{5,7},{7,5},{8,10},{10,8},{9,1... | collective-permute-start | bytes 196616 | tf_op jit(solution)/shard_map/ppermute | solution.py:375
  7.8 7.1 %collective-permute-start.3 = (bf16[2,32,512]{2,1,0:T(8,128)(2,1)S(1)}, bf16[2,32,512]{2,1,0:T(8,128)(2,1)S(1)}, u32[]{:S(2)}, u32[]{:S(2)}) collective-permute-start(bf16[2,32,512]{2,1,0:T(8,128)(2,1)S(1)} %collective-permute-done.2), channel_id=1, source_target_pairs={{0,2},{2,0},{1,3},{3,1},{4,6},{6,4},{5,7},{7,5},{8,10},{10,8},{9,1... | collective-permute-start | bytes 196616 | tf_op jit(solution)/shard_map/ppermute | solution.py:375
  8.5 0.7 %copy-start.2 = (f32[16,16]{1,0:T(8,128)S(1)}, f32[16,16]{1,0:T(8,128)}, u32[]{:S(2)}) copy-start(f32[16,16]{1,0:T(8,128)} %taps_ref.1) | copy-start | bytes 3076
  9.2 0.7 %copy-start.5 = (s32[256]{0:T(256)S(1)}, s32[256]{0:T(256)}, u32[]{:S(2)}) copy-start(s32[256]{0:T(256)} %param.10) | copy-start | bytes 3076
  10.9 6.8 %collective-permute-start.8 = (bf16[64,512]{1,0:T(8,128)(2,1)S(1)}, bf16[64,512]{1,0:T(8,128)(2,1)S(1)}, u32[]{:S(2)}, u32[]{:S(2)}) collective-permute-start(bf16[64,512]{1,0:T(8,128)(2,1)S(1)} %get-tuple-element.50), channel_id=1, source_target_pairs={{0,8},{4,12},{8,0},{12,4},{1,9},{5,13},{9,1},{13,5},{2,10},{6,14},... | collective-permute-start | bytes 196616 | tf_op jit(solution)/shard_map/ppermute | solution.py:375
  13.6 6.2 %collective-permute-start.9 = (bf16[64,512]{1,0:T(8,128)(2,1)S(1)}, bf16[64,512]{1,0:T(8,128)(2,1)S(1)}, u32[]{:S(2)}, u32[]{:S(2)}) collective-permute-start(bf16[64,512]{1,0:T(8,128)(2,1)S(1)} %get-tuple-element.51), channel_id=1, source_target_pairs={{0,12},{4,8},{8,4},{12,0},{1,13},{5,9},{9,5},{13,1},{2,14},{6,10},... | collective-permute-start | bytes 196616 | tf_op jit(solution)/shard_map/ppermute | solution.py:375
  15.1 5.0 %collective-permute-start.4 = (bf16[64,512]{1,0:T(8,128)(2,1)S(1)}, bf16[64,512]{1,0:T(8,128)(2,1)S(1)}, u32[]{:S(2)}, u32[]{:S(2)}) collective-permute-start(bf16[64,512]{1,0:T(8,128)(2,1)S(1)} %get-tuple-element.47), channel_id=1, source_target_pairs={{0,4},{4,0},{8,12},{12,8},{1,5},{5,1},{9,13},{13,9},{2,6},{6,2},{1... | collective-permute-start | bytes 196616 | tf_op jit(solution)/shard_map/ppermute | solution.py:375
  15.4 0.9 %copy-start.1 = (bf16[4,2,256,32]{2,3,1,0:T(8,128)(2,1)S(1)}, bf16[4,2,256,32]{2,3,1,0:T(8,128)(2,1)}, u32[]{:S(2)}) copy-start(bf16[4,2,256,32]{2,3,1,0:T(8,128)(2,1)} %param.13) | copy-start | bytes 393220
  20.8 5.8 %collective-permute-start.10 = (bf16[96,512]{1,0:T(8,128)(2,1)S(1)}, bf16[96,512]{1,0:T(8,128)(2,1)S(1)}, u32[]{:S(2)}, u32[]{:S(2)}) collective-permute-start(bf16[96,512]{1,0:T(8,128)(2,1)S(1)} %get-tuple-element.56), channel_id=1, source_target_pairs={{0,4},{4,0},{8,12},{12,8},{1,5},{5,1},{9,13},{13,9},{2,6},{6,2},{1... | collective-permute-start | bytes 294920 | tf_op jit(solution)/shard_map/ppermute | solution.py:375
  20.8 10.2 %collective-permute-start.13 = (bf16[64,512]{1,0:T(8,128)(2,1)S(1)}, bf16[64,512]{1,0:T(8,128)(2,1)S(1)}, u32[]{:S(2)}, u32[]{:S(2)}) collective-permute-start(bf16[64,512]{1,0:T(8,128)(2,1)S(1)} %get-tuple-element.55), channel_id=1, source_target_pairs={{0,2},{2,0},{1,3},{3,1},{4,6},{6,4},{5,7},{7,5},{8,10},{10,8},{9,1... | collective-permute-start | bytes 196616 | tf_op jit(solution)/shard_map/ppermute | solution.py:375
  22.2 10.1 %collective-permute-start.11 = (bf16[96,512]{1,0:T(8,128)(2,1)S(1)}, bf16[96,512]{1,0:T(8,128)(2,1)S(1)}, u32[]{:S(2)}, u32[]{:S(2)}) collective-permute-start(bf16[96,512]{1,0:T(8,128)(2,1)S(1)} %get-tuple-element.58), channel_id=1, source_target_pairs={{0,8},{4,12},{8,0},{12,4},{1,9},{5,13},{9,1},{13,5},{2,10},{6,14},... | collective-permute-start | bytes 294920 | tf_op jit(solution)/shard_map/ppermute | solution.py:375
  24.8 7.5 %collective-permute-start.12 = (bf16[96,512]{1,0:T(8,128)(2,1)S(1)}, bf16[96,512]{1,0:T(8,128)(2,1)S(1)}, u32[]{:S(2)}, u32[]{:S(2)}) collective-permute-start(bf16[96,512]{1,0:T(8,128)(2,1)S(1)} %get-tuple-element.59), channel_id=1, source_target_pairs={{0,12},{4,8},{8,4},{12,0},{1,13},{5,9},{9,5},{13,1},{2,14},{6,10},... | collective-permute-start | bytes 294920 | tf_op jit(solution)/shard_map/ppermute | solution.py:375
  26.6 5.7 %collective-permute-start.14 = (bf16[64,512]{1,0:T(8,128)(2,1)S(1)}, bf16[64,512]{1,0:T(8,128)(2,1)S(1)}, u32[]{:S(2)}, u32[]{:S(2)}) collective-permute-start(bf16[64,512]{1,0:T(8,128)(2,1)S(1)} %get-tuple-element.79), channel_id=1, source_target_pairs={{0,2},{2,0},{1,3},{3,1},{4,6},{6,4},{5,7},{7,5},{8,10},{10,8},{9,1... | collective-permute-start | bytes 196616 | tf_op jit(solution)/shard_map/ppermute | solution.py:375
  27.3 0.7 %copy-start.3 = (f32[16,16]{1,0:T(8,128)S(1)}, f32[16,16]{1,0:T(8,128)}, u32[]{:S(2)}) copy-start(f32[16,16]{1,0:T(8,128)} %taps_ref.2) | copy-start | bytes 3076
  28.0 0.7 %copy-start.4 = (s32[1024]{0:T(1024)S(1)}, s32[1024]{0:T(1024)}, u32[]{:S(2)}) copy-start(s32[1024]{0:T(1024)} %param.12) | copy-start | bytes 12292
  28.7 0.7 %copy-start.6 = (s32[32,1]{0,1:T(1,128)S(1)}, s32[32,1]{0,1:T(1,128)}, u32[]{:S(2)}) copy-start(s32[32,1]{0,1:T(1,128)} %param.11) | copy-start | bytes 388
  32.3 5.0 %collective-permute-start.16 = (bf16[2,64,512]{2,1,0:T(8,128)(2,1)S(1)}, bf16[2,64,512]{2,1,0:T(8,128)(2,1)S(1)}, u32[]{:S(2)}, u32[]{:S(2)}) collective-permute-start(bf16[2,64,512]{2,1,0:T(8,128)(2,1)S(1)} %pad_maximum_fusion.2), channel_id=1, source_target_pairs={{0,2},{2,0},{1,3},{3,1},{4,6},{6,4},{5,7},{7,5},{8,10},{10,8},{9,1... | collective-permute-start | bytes 393224 | tf_op jit(solution)/shard_map/ppermute | solution.py:375
  33.2 4.2 %collective-permute-start.15 = (bf16[4,64,512]{2,1,0:T(8,128)(2,1)S(1)}, bf16[4,64,512]{2,1,0:T(8,128)(2,1)S(1)}, u32[]{:S(2)}, u32[]{:S(2)}) collective-permute-start(bf16[4,64,512]{2,1,0:T(8,128)(2,1)S(1)} %pad_maximum_fusion.refs_0_), channel_id=1, source_target_pairs={{0,1},{1,0},{2,3},{3,2},{4,5},{5,4},{6,7},{7,6},{8,9},{9,8},{10,11... | collective-permute-start | bytes 786440 | tf_op jit(solution)/shard_map/ppermute | solution.py:375
  33.3 5.4 %collective-permute-start.17 = (bf16[2,64,512]{2,1,0:T(8,128)(2,1)S(1)}, bf16[2,64,512]{2,1,0:T(8,128)(2,1)S(1)}, u32[]{:S(2)}, u32[]{:S(2)}) collective-permute-start(bf16[2,64,512]{2,1,0:T(8,128)(2,1)S(1)} %pad_maximum_fusion.1.refs_1_.refs_2_), channel_id=1, source_target_pairs={{0,1},{1,0},{2,3},{3,2},{4,5},{5,4},{6,7},{7,6},{8,9},{9,8},{10,11... | collective-permute-start | bytes 393224 | tf_op jit(solution)/shard_map/ppermute | solution.py:375
  37.4 1.3 %collective-permute-start.18 = (bf16[2,64,512]{2,1,0:T(8,128)(2,1)S(1)}, bf16[2,64,512]{2,1,0:T(8,128)(2,1)S(1)}, u32[]{:S(2)}, u32[]{:S(2)}) collective-permute-start(bf16[2,64,512]{2,1,0:T(8,128)(2,1)S(1)} %collective-permute-done.16.refs_2_.refs_3_), channel_id=1, source_target_pairs={{0,1},{1,0},{2,3},{3,2},{4,5},{5,4},{6,7},{7,6},{8,9},{9,8},{10,11... | collective-permute-start | bytes 393224 | tf_op jit(solution)/shard_map/ppermute | solution.py:375

commit v6 on v5

--- a/solution.py
+++ b/solution.py
@@ -484,8 +484,8 @@
         small[1].reshape(1, beam_group.shape[0]),
         small[2],
     )
-    moved[1], moved[2], other[0], other[1], bands, chosen, scale = lax.optimization_barrier(
-        (*moved[1:], *other, bands, chosen, scale)
+    moved[1], moved[2], other[1], bands, chosen, scale = lax.optimization_barrier(
+        (moved[1], moved[2], other[1], bands, chosen, scale)
     )
     matrix = pl.pallas_call(
         functools.partial(weight_kernel, axes),

time: 43.7 us -> 42.6 us (0.975)
  waiting for transfers between devices: 6.39 us -> 4.53 us
  starting transfers between devices: 18.6 us -> 19.4 us
    ppermute x19, waiting for transfers between devices: 6.39 us -> 4.53 us  [swap(): return lax.ppermute(x, axis, [(i, i ^ mask) for i in range(size)])]
    ppermute x19, starting transfers between devices: 18.6 us -> 19.4 us  [swap(): return lax.ppermute(x, axis, [(i, i ^ mask) for i in range(size)])]
where the time goes in v6:
time: 42.6 us; the launch traced here: 42.3 us
  starting transfers between devices  19.4 us (46%)
  Pallas kernels  12.1 us (28%)
  local copies, waits for them, and re-layouts  5.37 us (13%)
  waiting for transfers between devices  4.53 us (11%)
  between operations  0.82 us (2%)
    ppermute x19, starting transfers between devices, swap(): return lax.ppermute(x, axis, [(i, i ^ mask) for i in range(size)])  19.4 us
    unnamed x14, local copies, waits for them, and re-layouts  5.35 us
    ppermute x19, waiting for transfers between devices, swap(): return lax.ppermute(x, axis, [(i, i ^ mask) for i in range(size)])  4.53 us
    pallas_call x1, Pallas kernels, call_beams(): pl.pallas_call(lambda *refs: beam_kernel(axes, refs[:len(pieces)], *refs[...  4.52 us
    pallas_call x2, Pallas kernels, add_part(): pl.pallas_call(functools.partial(part_kernel, axes, places), out_shape=ja...  2.06 us
    pallas_call x1, Pallas kernels, fast_body(): pl.pallas_call(functools.partial(band_kernel, axes), out_shape=[jax.Shape...  1.7 us
    pallas_call x1, Pallas kernels, fast_body(): pl.pallas_call(functools.partial(pack_kernel, axes), out_shape=[share] *...  1.37 us
  transfers between devices with their start and end apart: 19, of which 5 were waited for; matrix products, arithmetic and copies ran while one was open for 0% of the time, Pallas kernels for 15%

profile of v6, /device:TPU:0, one launch (start us, length us, event | category | flops | bytes accessed | tf_op | source)
XLA Modules:
  0.0 42.3 jit_solution(15609539468657281784)
XLA Ops:
  0.6 1.0 %copy-done = bf16[16,2,16,512]{3,2,1,0:T(8,128)(2,1)S(1)} copy-done((bf16[16,2,16,512]{3,2,1,0:T(8,128)(2,1)S(1)}, bf16[16,2,16,512]{3,2,1,0:T(8,128)(2,1)}, u32[]{:S(2)}) %copy-start) | copy-done | bytes 524312
  1.7 0.5 %lane_spread.1 = (bf16[4,32,512]{2,1,0:T(8,128)(2,1)S(1)}, bf16[2,32,512]{2,1,0:T(8,128)(2,1)S(1)}, bf16[2,32,512]{2,1,0:T(8,128)(2,1)S(1)}, bf16[4,32,512]{2,1,...) custom-call(bf16[16,2,16,512]{3,2,1,0:T(8,128)(2,1)S(1)} %copy-done), custom_call_target="tpu_custom_call" | custom-call | tf_op jit(solution)/shard_map/lane_spread/pallas_call | solution.py:394
  2.2 0.5 %collective-permute-start.6 = (bf16[2,32,512]{2,1,0:T(8,128)(2,1)S(1)}, bf16[2,32,512]{2,1,0:T(8,128)(2,1)S(1)}, u32[]{:S(2)}, u32[]{:S(2)}) collective-permute-start(bf16[2,32,512]{2,1,0:T(8,128)(2,1)S(1)} %get-tuple-element.48), channel_id=1, source_target_pairs={{0,1},{1,0},{2,3},{3,2},{4,5},{5,4},{6,7},{7,6},{8,9},{9,8},{10,11... | collective-permute-start | bytes 196616 | tf_op jit(solution)/shard_map/ppermute | solution.py:375
  2.7 0.1 collective-permute-start
  2.8 0.4 %collective-permute-start.2 = (bf16[2,32,512]{2,1,0:T(8,128)(2,1)S(1)}, bf16[2,32,512]{2,1,0:T(8,128)(2,1)S(1)}, u32[]{:S(2)}, u32[]{:S(2)}) collective-permute-start(bf16[2,32,512]{2,1,0:T(8,128)(2,1)S(1)} %get-tuple-element.44), channel_id=1, source_target_pairs={{0,1},{1,0},{2,3},{3,2},{4,5},{5,4},{6,7},{7,6},{8,9},{9,8},{10,11... | collective-permute-start | bytes 196616 | tf_op jit(solution)/shard_map/ppermute | solution.py:375
  3.2 2.6 %collective-permute-start.5 = (bf16[2,32,512]{2,1,0:T(8,128)(2,1)S(1)}, bf16[2,32,512]{2,1,0:T(8,128)(2,1)S(1)}, u32[]{:S(2)}, u32[]{:S(2)}) collective-permute-start(bf16[2,32,512]{2,1,0:T(8,128)(2,1)S(1)} %get-tuple-element.47), channel_id=1, source_target_pairs={{0,2},{2,0},{1,3},{3,1},{4,6},{6,4},{5,7},{7,5},{8,10},{10,8},{9,1... | collective-permute-start | bytes 196616 | tf_op jit(solution)/shard_map/ppermute | solution.py:375
  5.8 0.0 collective-permute-done.6
  5.8 0.7 %collective-permute-start.7 = (bf16[2,32,512]{2,1,0:T(8,128)(2,1)S(1)}, bf16[2,32,512]{2,1,0:T(8,128)(2,1)S(1)}, u32[]{:S(2)}, u32[]{:S(2)}) collective-permute-start(bf16[2,32,512]{2,1,0:T(8,128)(2,1)S(1)} %collective-permute-done.6), channel_id=1, source_target_pairs={{0,2},{2,0},{1,3},{3,1},{4,6},{6,4},{5,7},{7,5},{8,10},{10,8},{9,1... | collective-permute-start | bytes 196616 | tf_op jit(solution)/shard_map/ppermute | solution.py:375
  6.5 1.4 %collective-permute-start.1 = (bf16[2,32,512]{2,1,0:T(8,128)(2,1)S(1)}, bf16[2,32,512]{2,1,0:T(8,128)(2,1)S(1)}, u32[]{:S(2)}, u32[]{:S(2)}) collective-permute-start(bf16[2,32,512]{2,1,0:T(8,128)(2,1)S(1)} %get-tuple-element.43), channel_id=1, source_target_pairs={{0,2},{2,0},{1,3},{3,1},{4,6},{6,4},{5,7},{7,5},{8,10},{10,8},{9,1... | collective-permute-start | bytes 196616 | tf_op jit(solution)/shard_map/ppermute | solution.py:375
  7.8 0.7 %collective-permute-start.3 = (bf16[2,32,512]{2,1,0:T(8,128)(2,1)S(1)}, bf16[2,32,512]{2,1,0:T(8,128)(2,1)S(1)}, u32[]{:S(2)}, u32[]{:S(2)}) collective-permute-start(bf16[2,32,512]{2,1,0:T(8,128)(2,1)S(1)} %collective-permute-done.2), channel_id=1, source_target_pairs={{0,2},{2,0},{1,3},{3,1},{4,6},{6,4},{5,7},{7,5},{8,10},{10,8},{9,1... | collective-permute-start | bytes 196616 | tf_op jit(solution)/shard_map/ppermute | solution.py:375
  8.5 0.7 %copy-done.2 = f32[16,16]{1,0:T(8,128)S(1)} copy-done((f32[16,16]{1,0:T(8,128)S(1)}, f32[16,16]{1,0:T(8,128)}, u32[]{:S(2)}) %copy-start.2) | copy-done | bytes 1048
  9.2 0.7 %copy-done.5 = s32[256]{0:T(256)S(1)} copy-done((s32[256]{0:T(256)S(1)}, s32[256]{0:T(256)}, u32[]{:S(2)}) %copy-start.5) | copy-done | bytes 1048
  9.9 0.2 station_tables.1
  10.0 0.0 collective-permute-done.5.refs_2_
  10.1 0.7 %collective-permute-done.7.refs_3_ = bf16[2,32,512]{2,1,0:T(8,128)(2,1)S(1)} collective-permute-done((bf16[2,32,512]{2,1,0:T(8,128)(2,1)S(1)}, bf16[2,32,512]{2,1,0:T(8,128)(2,1)S(1)}, u32[]{:S(2)}, u32[]{:S(2)}) %collective-permute-start.7) | collective-permute-done | bytes 65568 | tf_op jit(solution)/shard_map/ppermute | solution.py:375
  10.7 0.0 collective-permute-done.refs_1_
  10.7 0.2 plane_sums_far.1
  10.9 2.7 %collective-permute-start.8 = (bf16[64,512]{1,0:T(8,128)(2,1)S(1)}, bf16[64,512]{1,0:T(8,128)(2,1)S(1)}, u32[]{:S(2)}, u32[]{:S(2)}) collective-permute-start(bf16[64,512]{1,0:T(8,128)(2,1)S(1)} %get-tuple-element.49), channel_id=1, source_target_pairs={{0,8},{4,12},{8,0},{12,4},{1,9},{5,13},{9,1},{13,5},{2,10},{6,14},... | collective-permute-start | bytes 196616 | tf_op jit(solution)/shard_map/ppermute | solution.py:375
  13.6 1.3 %collective-permute-start.9 = (bf16[64,512]{1,0:T(8,128)(2,1)S(1)}, bf16[64,512]{1,0:T(8,128)(2,1)S(1)}, u32[]{:S(2)}, u32[]{:S(2)}) collective-permute-start(bf16[64,512]{1,0:T(8,128)(2,1)S(1)} %get-tuple-element.50), channel_id=1, source_target_pairs={{0,12},{4,8},{8,4},{12,0},{1,13},{5,9},{9,5},{13,1},{2,14},{6,10},... | collective-permute-start | bytes 196616 | tf_op jit(solution)/shard_map/ppermute | solution.py:375
  14.9 0.0 collective-permute-done.1.refs_2_
  14.9 0.0 collective-permute-done.3.refs_3_
  14.9 0.2 plane_sums_near.1
  15.1 0.3 collective-permute-start.4
  15.4 0.9 %copy-done.1 = bf16[4,2,256,32]{2,3,1,0:T(8,128)(2,1)S(1)} copy-done((bf16[4,2,256,32]{2,3,1,0:T(8,128)(2,1)S(1)}, bf16[4,2,256,32]{2,3,1,0:T(8,128)(2,1)}, u32[]{:S(2)}) %copy-start.1) | copy-done | bytes 131096
  16.3 1.4 %weight_shares.1 = (bf16[32,512]{1,0:T(8,128)(2,1)S(1)}, bf16[32,512]{1,0:T(8,128)(2,1)S(1)}, bf16[32,512]{1,0:T(8,128)(2,1)S(1)}, bf16[32,512]{1,0:T(8,128)(2,1)S(1)}) custom-call(bf16[4,2,32,256]{3,2,1,0:T(8,128)(2,1)S(1)} %bitcast.14), custom_call_target="tpu_custom_call" | custom-call | bytes 8388608 | tf_op jit(solution)/shard_map/weight_shares/pallas_call | solution.py:442
  17.7 0.0 collective-permute-done.8.refs_2_
  17.7 2.0 %collective-permute-done.9.refs_3_ = bf16[64,512]{1,0:T(8,128)(2,1)S(1)} collective-permute-done((bf16[64,512]{1,0:T(8,128)(2,1)S(1)}, bf16[64,512]{1,0:T(8,128)(2,1)S(1)}, u32[]{:S(2)}, u32[]{:S(2)}) %collective-permute-start.9) | collective-permute-done | bytes 65568 | tf_op jit(solution)/shard_map/ppermute | solution.py:375
  19.7 0.4 collective-permute-done.4.refs_1_
  20.1 0.6 %station_filter.1 = (bf16[64,512]{1,0:T(8,128)(2,1)S(1)}, bf16[96,512]{1,0:T(8,128)(2,1)S(1)}, bf16[96,512]{1,0:T(8,128)(2,1)S(1)}, bf16[96,512]{1,0:T(8,128)(2,1)S(1)}) custom-call(f32[16,512]{1,0:T(8,128)S(1)} %get-tuple-element.39.taps_ref, f32[64,512]{1,0:T(8,128)S(1)} %get-tuple-element.45.refs_0_, bf16[64,512]{1,0:T(8,128)(2,1)S(1)} %collective-permute-done.4.refs_1_, ...), custom_call_target="tpu_custom_call" | custom-call | tf_op jit(solution)/shard_map/station_filter/pallas_call | solution.py:453
  20.8 0.1 collective-permute-start.10
  20.8 2.6 %collective-permute-start.11 = (bf16[96,512]{1,0:T(8,128)(2,1)S(1)}, bf16[96,512]{1,0:T(8,128)(2,1)S(1)}, u32[]{:S(2)}, u32[]{:S(2)}) collective-permute-start(bf16[96,512]{1,0:T(8,128)(2,1)S(1)} %get-tuple-element.57), channel_id=1, source_target_pairs={{0,8},{4,12},{8,0},{12,4},{1,9},{5,13},{9,1},{13,5},{2,10},{6,14},... | collective-permute-start | bytes 294920 | tf_op jit(solution)/shard_map/ppermute | solution.py:375
  23.5 1.7 %collective-permute-start.12 = (bf16[96,512]{1,0:T(8,128)(2,1)S(1)}, bf16[96,512]{1,0:T(8,128)(2,1)S(1)}, u32[]{:S(2)}, u32[]{:S(2)}) collective-permute-start(bf16[96,512]{1,0:T(8,128)(2,1)S(1)} %get-tuple-element.58), channel_id=1, source_target_pairs={{0,12},{4,8},{8,4},{12,0},{1,13},{5,9},{9,5},{13,1},{2,14},{6,10},... | collective-permute-start | bytes 294920 | tf_op jit(solution)/shard_map/ppermute | solution.py:375
  25.2 0.2 collective-permute-done.10.refs_1_
  25.5 1.6 %collective-permute-start.13 = (bf16[64,512]{1,0:T(8,128)(2,1)S(1)}, bf16[64,512]{1,0:T(8,128)(2,1)S(1)}, u32[]{:S(2)}, u32[]{:S(2)}) collective-permute-start(bf16[64,512]{1,0:T(8,128)(2,1)S(1)} %get-tuple-element.77), channel_id=1, source_target_pairs={{0,2},{2,0},{1,3},{3,1},{4,6},{6,4},{5,7},{7,5},{8,10},{10,8},{9,1... | collective-permute-start | bytes 196616 | tf_op jit(solution)/shard_map/ppermute | solution.py:375
  27.1 0.5 %collective-permute-start.15 = (bf16[64,512]{1,0:T(8,128)(2,1)S(1)}, bf16[64,512]{1,0:T(8,128)(2,1)S(1)}, u32[]{:S(2)}, u32[]{:S(2)}) collective-permute-start(bf16[64,512]{1,0:T(8,128)(2,1)S(1)} %get-tuple-element.54), channel_id=1, source_target_pairs={{0,2},{2,0},{1,3},{3,1},{4,6},{6,4},{5,7},{7,5},{8,10},{10,8},{9,1... | collective-permute-start | bytes 196616 | tf_op jit(solution)/shard_map/ppermute | solution.py:375
  27.6 0.7 %copy-done.3 = f32[16,16]{1,0:T(8,128)S(1)} copy-done((f32[16,16]{1,0:T(8,128)S(1)}, f32[16,16]{1,0:T(8,128)}, u32[]{:S(2)}) %copy-start.3) | copy-done | bytes 1048
  28.2 0.7 %copy-done.4 = s32[1024]{0:T(1024)S(1)} copy-done((s32[1024]{0:T(1024)S(1)}, s32[1024]{0:T(1024)}, u32[]{:S(2)}) %copy-start.4) | copy-done | bytes 4120
  28.9 0.7 %copy-done.6 = s32[32,1]{0,1:T(1,128)S(1)} copy-done((s32[32,1]{0,1:T(1,128)S(1)}, s32[32,1]{0,1:T(1,128)}, u32[]{:S(2)}) %copy-start.6) | copy-done | bytes 152
  29.6 1.7 %synthesis_bands.1 = (bf16[16,768,256]{2,1,0:T(8,128)(2,1)S(1)}, f32[32,64]{1,0:T(8,128)S(1)}, f32[32,64]{1,0:T(8,128)S(1)}) custom-call(s32[1,32]{1,0:T(1,128)S(1)} %bitcast.18, s32[1,1024]{1,0:T(1,128)S(1)} %bitcast.16, f32[16,16]{1,0:T(8,128)S(1)} %copy-done.3), custom_call_target="tpu_custom_call" | custom-call | bytes 16777216 | tf_op jit(solution)/shard_map/synthesis_bands/pallas_call | solution.py:470
  31.4 1.7 %collective-permute-start.16 = (bf16[2,64,512]{2,1,0:T(8,128)(2,1)S(1)}, bf16[2,64,512]{2,1,0:T(8,128)(2,1)S(1)}, u32[]{:S(2)}, u32[]{:S(2)}) collective-permute-start(bf16[2,64,512]{2,1,0:T(8,128)(2,1)S(1)} %pad_maximum_fusion.2), channel_id=1, source_target_pairs={{0,2},{2,0},{1,3},{3,1},{4,6},{6,4},{5,7},{7,5},{8,10},{10,8},{9,1... | collective-permute-start | bytes 393224 | tf_op jit(solution)/shard_map/ppermute | solution.py:375
  33.1 0.1 collective-permute-start.14
  33.2 0.5 %collective-permute-start.17 = (bf16[2,64,512]{2,1,0:T(8,128)(2,1)S(1)}, bf16[2,64,512]{2,1,0:T(8,128)(2,1)S(1)}, u32[]{:S(2)}, u32[]{:S(2)}) collective-permute-start(bf16[2,64,512]{2,1,0:T(8,128)(2,1)S(1)} %pad_maximum_fusion.1.refs_1_.refs_2_), channel_id=1, source_target_pairs={{0,1},{1,0},{2,3},{3,2},{4,5},{5,4},{6,7},{7,6},{8,9},{9,8},{10,11... | collective-permute-start | bytes 393224 | tf_op jit(solution)/shard_map/ppermute | solution.py:375
  33.7 0.8 %weight_matrix.1.m_ref.refs_6_ = bf16[16,128,1024]{2,1,0:T(8,128)(2,1)S(1)} custom-call(f32[32,64]{1,0:T(8,128)S(1)} %get-tuple-element.68.chosen_ref, f32[32,64]{1,0:T(8,128)S(1)} %get-tuple-element.69.scale_ref, bf16[32,512]{1,0:T(8,128)(2,1)S(1)} %get-tuple-element.70.refs_0_, bf16[96,512]{1,0:T(8,128)(2,1)S(1)} %collective-permute-done.10.refs_1_, ...), custom_call_target="tpu_custom_call" | custom-call | bytes 8388608 | tf_op jit(solution)/shard_map/weight_matrix/pallas_call | solution.py:490
  34.5 0.7 %own_beams.1.refs_3_ = f32[16,128,512]{2,1,0:T(8,128)S(1)} custom-call(bf16[16,128,1024]{2,1,0:T(8,128)(2,1)S(1)} %weight_matrix.1.m_ref.refs_6_, bf16[4,64,512]{2,1,0:T(8,128)(2,1)S(1)} %pad_maximum_fusion.refs_0_), custom_call_target="tpu_custom_call" | custom-call | bytes 8388608 | tf_op jit(solution)/shard_map/own_beams/pallas_call | solution.py:502
  35.3 1.1 %collective-permute-done.16.refs_2_.refs_3_ = bf16[2,64,512]{2,1,0:T(8,128)(2,1)S(1)} collective-permute-done((bf16[2,64,512]{2,1,0:T(8,128)(2,1)S(1)}, bf16[2,64,512]{2,1,0:T(8,128)(2,1)S(1)}, u32[]{:S(2)}, u32[]{:S(2)}) %collective-permute-start.16) | collective-permute-done | bytes 131104 | tf_op jit(solution)/shard_map/ppermute | solution.py:375
  36.4 1.3 %near_beams.1.refs_8_ = f32[16,128,512]{2,1,0:T(8,128)S(1)} custom-call(bf16[16,128,1024]{2,1,0:T(8,128)(2,1)S(1)} %weight_matrix.1.m_ref.refs_6_, bf16[4,64,512]{2,1,0:T(8,128)(2,1)S(1)} %collective-permute-done.14.refs_0_.refs_1_, bf16[2,64,512]{2,1,0:T(8,128)(2,1)S(1)} %pad_maximum_fusion.1.refs_1_.refs_2_, ...), custom_call_target="tpu_custom_call" | custom-call | bytes 8388608 | tf_op jit(solution)/shard_map/near_beams/pallas_call | solution.py:502
  37.7 0.0 collective-permute-done.18.refs_5_
  37.8 4.5 %beams_and_series.1 = (f32[128,2,8,512]{3,2,1,0:T(8,128)}, f32[4,2,8,32]{3,2,1,0:T(8,128)}) custom-call(bf16[4,64,512]{2,1,0:T(8,128)(2,1)S(1)} %pad_maximum_fusion.refs_0_, bf16[4,64,512]{2,1,0:T(8,128)(2,1)S(1)} %collective-permute-done.14.refs_0_.refs_1_, bf16[2,64,512]{2,1,0:T(8,128)(2,1)S(1)} %pad_maximum_fusion.1.refs_1_.refs_2_, ...), custom_call_target="tpu_custom_call" | custom-call | tf_op jit(solution)/shard_map/beams_and_series/pallas_call | solution.py:352
  (20 shorter events, 0.1 us)
Async XLA Ops:
  0.6 1.0 %copy-start = (bf16[16,2,16,512]{3,2,1,0:T(8,128)(2,1)S(1)}, bf16[16,2,16,512]{3,2,1,0:T(8,128)(2,1)}, u32[]{:S(2)}) copy-start(bf16[16,2,16,512]{3,2,1,0:T(8,128)(2,1)} %x_ref.1) | copy-start | bytes 1572868
  2.2 3.6 %collective-permute-start.6 = (bf16[2,32,512]{2,1,0:T(8,128)(2,1)S(1)}, bf16[2,32,512]{2,1,0:T(8,128)(2,1)S(1)}, u32[]{:S(2)}, u32[]{:S(2)}) collective-permute-start(bf16[2,32,512]{2,1,0:T(8,128)(2,1)S(1)} %get-tuple-element.48), channel_id=1, source_target_pairs={{0,1},{1,0},{2,3},{3,2},{4,5},{5,4},{6,7},{7,6},{8,9},{9,8},{10,11... | collective-permute-start | bytes 196616 | tf_op jit(solution)/shard_map/ppermute | solution.py:375
  2.7 8.0 %collective-permute-start = (bf16[4,32,512]{2,1,0:T(8,128)(2,1)S(1)}, bf16[4,32,512]{2,1,0:T(8,128)(2,1)S(1)}, u32[]{:S(2)}, u32[]{:S(2)}) collective-permute-start(bf16[4,32,512]{2,1,0:T(8,128)(2,1)S(1)} %get-tuple-element.42), channel_id=1, source_target_pairs={{0,1},{1,0},{2,3},{3,2},{4,5},{5,4},{6,7},{7,6},{8,9},{9,8},{10,11... | collective-permute-start | bytes 393224 | tf_op jit(solution)/shard_map/ppermute | solution.py:375
  2.8 5.0 %collective-permute-start.2 = (bf16[2,32,512]{2,1,0:T(8,128)(2,1)S(1)}, bf16[2,32,512]{2,1,0:T(8,128)(2,1)S(1)}, u32[]{:S(2)}, u32[]{:S(2)}) collective-permute-start(bf16[2,32,512]{2,1,0:T(8,128)(2,1)S(1)} %get-tuple-element.44), channel_id=1, source_target_pairs={{0,1},{1,0},{2,3},{3,2},{4,5},{5,4},{6,7},{7,6},{8,9},{9,8},{10,11... | collective-permute-start | bytes 196616 | tf_op jit(solution)/shard_map/ppermute | solution.py:375
  3.2 6.8 %collective-permute-start.5 = (bf16[2,32,512]{2,1,0:T(8,128)(2,1)S(1)}, bf16[2,32,512]{2,1,0:T(8,128)(2,1)S(1)}, u32[]{:S(2)}, u32[]{:S(2)}) collective-permute-start(bf16[2,32,512]{2,1,0:T(8,128)(2,1)S(1)} %get-tuple-element.47), channel_id=1, source_target_pairs={{0,2},{2,0},{1,3},{3,1},{4,6},{6,4},{5,7},{7,5},{8,10},{10,8},{9,1... | collective-permute-start | bytes 196616 | tf_op jit(solution)/shard_map/ppermute | solution.py:375
  5.8 4.9 %collective-permute-start.7 = (bf16[2,32,512]{2,1,0:T(8,128)(2,1)S(1)}, bf16[2,32,512]{2,1,0:T(8,128)(2,1)S(1)}, u32[]{:S(2)}, u32[]{:S(2)}) collective-permute-start(bf16[2,32,512]{2,1,0:T(8,128)(2,1)S(1)} %collective-permute-done.6), channel_id=1, source_target_pairs={{0,2},{2,0},{1,3},{3,1},{4,6},{6,4},{5,7},{7,5},{8,10},{10,8},{9,1... | collective-permute-start | bytes 196616 | tf_op jit(solution)/shard_map/ppermute | solution.py:375
  6.5 8.5 %collective-permute-start.1 = (bf16[2,32,512]{2,1,0:T(8,128)(2,1)S(1)}, bf16[2,32,512]{2,1,0:T(8,128)(2,1)S(1)}, u32[]{:S(2)}, u32[]{:S(2)}) collective-permute-start(bf16[2,32,512]{2,1,0:T(8,128)(2,1)S(1)} %get-tuple-element.43), channel_id=1, source_target_pairs={{0,2},{2,0},{1,3},{3,1},{4,6},{6,4},{5,7},{7,5},{8,10},{10,8},{9,1... | collective-permute-start | bytes 196616 | tf_op jit(solution)/shard_map/ppermute | solution.py:375
  7.8 7.1 %collective-permute-start.3 = (bf16[2,32,512]{2,1,0:T(8,128)(2,1)S(1)}, bf16[2,32,512]{2,1,0:T(8,128)(2,1)S(1)}, u32[]{:S(2)}, u32[]{:S(2)}) collective-permute-start(bf16[2,32,512]{2,1,0:T(8,128)(2,1)S(1)} %collective-permute-done.2), channel_id=1, source_target_pairs={{0,2},{2,0},{1,3},{3,1},{4,6},{6,4},{5,7},{7,5},{8,10},{10,8},{9,1... | collective-permute-start | bytes 196616 | tf_op jit(solution)/shard_map/ppermute | solution.py:375
  8.5 0.7 %copy-start.2 = (f32[16,16]{1,0:T(8,128)S(1)}, f32[16,16]{1,0:T(8,128)}, u32[]{:S(2)}) copy-start(f32[16,16]{1,0:T(8,128)} %taps_ref.1) | copy-start | bytes 3076
  9.2 0.7 %copy-start.5 = (s32[256]{0:T(256)S(1)}, s32[256]{0:T(256)}, u32[]{:S(2)}) copy-start(s32[256]{0:T(256)} %param.10) | copy-start | bytes 3076
  10.9 6.8 %collective-permute-start.8 = (bf16[64,512]{1,0:T(8,128)(2,1)S(1)}, bf16[64,512]{1,0:T(8,128)(2,1)S(1)}, u32[]{:S(2)}, u32[]{:S(2)}) collective-permute-start(bf16[64,512]{1,0:T(8,128)(2,1)S(1)} %get-tuple-element.49), channel_id=1, source_target_pairs={{0,8},{4,12},{8,0},{12,4},{1,9},{5,13},{9,1},{13,5},{2,10},{6,14},... | collective-permute-start | bytes 196616 | tf_op jit(solution)/shard_map/ppermute | solution.py:375
  13.6 6.2 %collective-permute-start.9 = (bf16[64,512]{1,0:T(8,128)(2,1)S(1)}, bf16[64,512]{1,0:T(8,128)(2,1)S(1)}, u32[]{:S(2)}, u32[]{:S(2)}) collective-permute-start(bf16[64,512]{1,0:T(8,128)(2,1)S(1)} %get-tuple-element.50), channel_id=1, source_target_pairs={{0,12},{4,8},{8,4},{12,0},{1,13},{5,9},{9,5},{13,1},{2,14},{6,10},... | collective-permute-start | bytes 196616 | tf_op jit(solution)/shard_map/ppermute | solution.py:375
  15.1 5.0 %collective-permute-start.4 = (bf16[64,512]{1,0:T(8,128)(2,1)S(1)}, bf16[64,512]{1,0:T(8,128)(2,1)S(1)}, u32[]{:S(2)}, u32[]{:S(2)}) collective-permute-start(bf16[64,512]{1,0:T(8,128)(2,1)S(1)} %get-tuple-element.46), channel_id=1, source_target_pairs={{0,4},{4,0},{8,12},{12,8},{1,5},{5,1},{9,13},{13,9},{2,6},{6,2},{1... | collective-permute-start | bytes 196616 | tf_op jit(solution)/shard_map/ppermute | solution.py:375
  15.4 0.9 %copy-start.1 = (bf16[4,2,256,32]{2,3,1,0:T(8,128)(2,1)S(1)}, bf16[4,2,256,32]{2,3,1,0:T(8,128)(2,1)}, u32[]{:S(2)}) copy-start(bf16[4,2,256,32]{2,3,1,0:T(8,128)(2,1)} %param.13) | copy-start | bytes 393220
  20.8 4.7 %collective-permute-start.10 = (bf16[96,512]{1,0:T(8,128)(2,1)S(1)}, bf16[96,512]{1,0:T(8,128)(2,1)S(1)}, u32[]{:S(2)}, u32[]{:S(2)}) collective-permute-start(bf16[96,512]{1,0:T(8,128)(2,1)S(1)} %get-tuple-element.55), channel_id=1, source_target_pairs={{0,4},{4,0},{8,12},{12,8},{1,5},{5,1},{9,13},{13,9},{2,6},{6,2},{1... | collective-permute-start | bytes 294920 | tf_op jit(solution)/shard_map/ppermute | solution.py:375
  20.8 10.5 %collective-permute-start.11 = (bf16[96,512]{1,0:T(8,128)(2,1)S(1)}, bf16[96,512]{1,0:T(8,128)(2,1)S(1)}, u32[]{:S(2)}, u32[]{:S(2)}) collective-permute-start(bf16[96,512]{1,0:T(8,128)(2,1)S(1)} %get-tuple-element.57), channel_id=1, source_target_pairs={{0,8},{4,12},{8,0},{12,4},{1,9},{5,13},{9,1},{13,5},{2,10},{6,14},... | collective-permute-start | bytes 294920 | tf_op jit(solution)/shard_map/ppermute | solution.py:375
  23.5 7.8 %collective-permute-start.12 = (bf16[96,512]{1,0:T(8,128)(2,1)S(1)}, bf16[96,512]{1,0:T(8,128)(2,1)S(1)}, u32[]{:S(2)}, u32[]{:S(2)}) collective-permute-start(bf16[96,512]{1,0:T(8,128)(2,1)S(1)} %get-tuple-element.58), channel_id=1, source_target_pairs={{0,12},{4,8},{8,4},{12,0},{1,13},{5,9},{9,5},{13,1},{2,14},{6,10},... | collective-permute-start | bytes 294920 | tf_op jit(solution)/shard_map/ppermute | solution.py:375
  25.5 5.9 %collective-permute-start.13 = (bf16[64,512]{1,0:T(8,128)(2,1)S(1)}, bf16[64,512]{1,0:T(8,128)(2,1)S(1)}, u32[]{:S(2)}, u32[]{:S(2)}) collective-permute-start(bf16[64,512]{1,0:T(8,128)(2,1)S(1)} %get-tuple-element.77), channel_id=1, source_target_pairs={{0,2},{2,0},{1,3},{3,1},{4,6},{6,4},{5,7},{7,5},{8,10},{10,8},{9,1... | collective-permute-start | bytes 196616 | tf_op jit(solution)/shard_map/ppermute | solution.py:375
  27.1 6.1 %collective-permute-start.15 = (bf16[64,512]{1,0:T(8,128)(2,1)S(1)}, bf16[64,512]{1,0:T(8,128)(2,1)S(1)}, u32[]{:S(2)}, u32[]{:S(2)}) collective-permute-start(bf16[64,512]{1,0:T(8,128)(2,1)S(1)} %get-tuple-element.54), channel_id=1, source_target_pairs={{0,2},{2,0},{1,3},{3,1},{4,6},{6,4},{5,7},{7,5},{8,10},{10,8},{9,1... | collective-permute-start | bytes 196616 | tf_op jit(solution)/shard_map/ppermute | solution.py:375
  27.6 0.7 %copy-start.3 = (f32[16,16]{1,0:T(8,128)S(1)}, f32[16,16]{1,0:T(8,128)}, u32[]{:S(2)}) copy-start(f32[16,16]{1,0:T(8,128)} %taps_ref.2) | copy-start | bytes 3076
  28.2 0.7 %copy-start.4 = (s32[1024]{0:T(1024)S(1)}, s32[1024]{0:T(1024)}, u32[]{:S(2)}) copy-start(s32[1024]{0:T(1024)} %param.12) | copy-start | bytes 12292
  28.9 0.7 %copy-start.6 = (s32[32,1]{0,1:T(1,128)S(1)}, s32[32,1]{0,1:T(1,128)}, u32[]{:S(2)}) copy-start(s32[32,1]{0,1:T(1,128)} %param.11) | copy-start | bytes 388
  31.4 5.0 %collective-permute-start.16 = (bf16[2,64,512]{2,1,0:T(8,128)(2,1)S(1)}, bf16[2,64,512]{2,1,0:T(8,128)(2,1)S(1)}, u32[]{:S(2)}, u32[]{:S(2)}) collective-permute-start(bf16[2,64,512]{2,1,0:T(8,128)(2,1)S(1)} %pad_maximum_fusion.2), channel_id=1, source_target_pairs={{0,2},{2,0},{1,3},{3,1},{4,6},{6,4},{5,7},{7,5},{8,10},{10,8},{9,1... | collective-permute-start | bytes 393224 | tf_op jit(solution)/shard_map/ppermute | solution.py:375
  33.1 3.3 %collective-permute-start.14 = (bf16[4,64,512]{2,1,0:T(8,128)(2,1)S(1)}, bf16[4,64,512]{2,1,0:T(8,128)(2,1)S(1)}, u32[]{:S(2)}, u32[]{:S(2)}) collective-permute-start(bf16[4,64,512]{2,1,0:T(8,128)(2,1)S(1)} %pad_maximum_fusion.refs_0_), channel_id=1, source_target_pairs={{0,1},{1,0},{2,3},{3,2},{4,5},{5,4},{6,7},{7,6},{8,9},{9,8},{10,11... | collective-permute-start | bytes 786440 | tf_op jit(solution)/shard_map/ppermute | solution.py:375
  33.2 4.5 %collective-permute-start.17 = (bf16[2,64,512]{2,1,0:T(8,128)(2,1)S(1)}, bf16[2,64,512]{2,1,0:T(8,128)(2,1)S(1)}, u32[]{:S(2)}, u32[]{:S(2)}) collective-permute-start(bf16[2,64,512]{2,1,0:T(8,128)(2,1)S(1)} %pad_maximum_fusion.1.refs_1_.refs_2_), channel_id=1, source_target_pairs={{0,1},{1,0},{2,3},{3,2},{4,5},{5,4},{6,7},{7,6},{8,9},{9,8},{10,11... | collective-permute-start | bytes 393224 | tf_op jit(solution)/shard_map/ppermute | solution.py:375
  36.4 1.3 %collective-permute-start.18 = (bf16[2,64,512]{2,1,0:T(8,128)(2,1)S(1)}, bf16[2,64,512]{2,1,0:T(8,128)(2,1)S(1)}, u32[]{:S(2)}, u32[]{:S(2)}) collective-permute-start(bf16[2,64,512]{2,1,0:T(8,128)(2,1)S(1)} %collective-permute-done.16.refs_2_.refs_3_), channel_id=1, source_target_pairs={{0,1},{1,0},{2,3},{3,2},{4,5},{5,4},{6,7},{7,6},{8,9},{9,8},{10,11... | collective-permute-start | bytes 393224 | tf_op jit(solution)/shard_map/ppermute | solution.py:375

commit v7 on v6

--- a/solution.py
+++ b/solution.py
@@ -126,9 +126,9 @@
         ref[rows:] = share[...]
 
 
-def pack_kernel(axes, w_ref, *out_refs):
-    row = lax.axis_index(axes[0])
-    chan, _, _, width = w_ref.shape
+def pack_kernel(axes, w_ref, groups_ref, beam_ref, chosen_ref, scale_ref, *out_refs):
+    row, col, sub = (lax.axis_index(a) for a in axes)
+    chan, _, stations, width = w_ref.shape
     beams = width // 4
     for k in range(chan):
         for q in range(2):
@@ -139,6 +139,22 @@
                 for j in range(1, 4):
                     taken = jnp.where((row ^ mask) == j, parts[j], taken)
                 ref[:, place : place + beams] = taken
+    square = (stations, stations)
+    diagonal = lax.broadcasted_iota(jnp.int32, square, 0) == lax.broadcasted_iota(
+        jnp.int32, square, 1
+    )
+    groups = jnp.broadcast_to(groups_ref[...], square).astype(jnp.float32)
+    groups = jnp.sum(jnp.where(diagonal, groups, 0.0), axis=1, keepdims=True)
+    total = beam_ref.shape[1]
+    first = ((col * 2 + sub) * 4 + row) * beams
+    every = jnp.broadcast_to(beam_ref[...], (8, total))
+    wanted = pltpu.roll(every, lax.rem(total - first, total), 1)[:1, :beams]
+    chosen = (groups == wanted.astype(jnp.float32)).astype(jnp.float32)
+    chosen_ref[...] = chosen
+    scale = (1.0 / (4 * chan * math.sqrt(ANTENNAS_PER_STN))) / jnp.sqrt(
+        jnp.sum(chosen, axis=0, keepdims=True)
+    )
+    scale_ref[...] = jnp.broadcast_to(scale, scale_ref.shape)
 
 
 def bands(taps_ref, lane, rows, cols):
@@ -154,27 +170,8 @@
     return jnp.concatenate([high[:HALO], low[:HALO], high[HALO:], low[HALO:]], axis=0)
 
 
-def band_kernel(axes, groups_ref, beam_ref, taps_ref, t_ref, chosen_ref, scale_ref):
-    row, col, sub = (lax.axis_index(a) for a in axes)
-    stations, beams = chosen_ref.shape
-    chan = t_ref.shape[0]
-    square = (stations, stations)
-    diagonal = lax.broadcasted_iota(jnp.int32, square, 0) == lax.broadcasted_iota(
-        jnp.int32, square, 1
-    )
-    groups = jnp.broadcast_to(groups_ref[...], square).astype(jnp.float32)
-    groups = jnp.sum(jnp.where(diagonal, groups, 0.0), axis=1, keepdims=True)
-    total = beam_ref.shape[1]
-    first = ((col * 2 + sub) * 4 + row) * beams
-    every = jnp.broadcast_to(beam_ref[...], (8, total))
-    wanted = pltpu.roll(every, lax.rem(total - first, total), 1)[:1, :beams]
-    chosen = (groups == wanted.astype(jnp.float32)).astype(jnp.float32)
-    chosen_ref[...] = chosen
-    scale = (1.0 / (chan * math.sqrt(ANTENNAS_PER_STN))) / jnp.sqrt(
-        jnp.sum(chosen, axis=0, keepdims=True)
-    )
-    scale_ref[...] = jnp.broadcast_to(scale, scale_ref.shape)
-    for c in range(chan):
+def band_kernel(taps_ref, t_ref):
+    for c in range(t_ref.shape[0]):
         t_ref[c] = bands(taps_ref, c, t_ref.shape[1] // 2, t_ref.shape[2])
 
 
@@ -439,15 +436,20 @@
     )(members, kept, paired, crossing_b, far_b)
 
     share = jax.ShapeDtypeStruct((stations, 2 * held_chan * beams), jnp.bfloat16)
-    shares = pl.pallas_call(
+    table = jax.ShapeDtypeStruct((stations, beams), jnp.float32)
+    chosen, scale, *shares = pl.pallas_call(
         functools.partial(pack_kernel, axes),
-        out_shape=[share] * 4,
-        in_specs=[vmem],
-        out_specs=[vmem] * 4,
+        out_shape=[table] * 2 + [share] * 4,
+        in_specs=[vmem] * 3,
+        out_specs=[vmem] * 6,
         compiler_params=params,
         cost_estimate=pl.CostEstimate(flops=0, bytes_accessed=8 << 20, transcendentals=0),
         name="weight_shares",
-    )(beam_weights.transpose(0, 1, 3, 2))
+    )(
+        beam_weights.transpose(0, 1, 3, 2),
+        station_group.reshape(1, stations),
+        beam_group.reshape(1, beam_group.shape[0]),
+    )
 
     lane_share = jax.ShapeDtypeStruct((3 * stations, frames), jnp.bfloat16)
     filtered, *sent = pl.pallas_call(
@@ -461,31 +463,19 @@
     moved = [swap(x, "row", m) for x, m in zip(sent, (1, 2, 3))]
 
     tile = 256
-    table = jax.ShapeDtypeStruct((stations, beams), jnp.float32)
-    other = [swap(filtered, "col", 1)]
-    moved[0], *small = lax.optimization_barrier(
-        (moved[0], station_group, beam_group, synthesis_taps)
-    )
-    other.append(swap(moved[0][: 2 * stations], "col", 1))
-    bands, chosen, scale = pl.pallas_call(
-        functools.partial(band_kernel, axes),
-        out_shape=[
-            jax.ShapeDtypeStruct((chan, 2 * (tile + HALO), tile), jnp.bfloat16),
-            table,
-            table,
-        ],
-        in_specs=[vmem, vmem, smem],
-        out_specs=[vmem] * 3,
+    late_taps = synthesis_taps
+    other = [swap(filtered, "col", 1), swap(moved[0][: 2 * stations], "col", 1)]
+    bands = pl.pallas_call(
+        band_kernel,
+        out_shape=jax.ShapeDtypeStruct((chan, 2 * (tile + HALO), tile), jnp.bfloat16),
+        in_specs=[smem],
+        out_specs=vmem,
         compiler_params=params,
         cost_estimate=pl.CostEstimate(flops=0, bytes_accessed=16 << 20, transcendentals=0),
         name="synthesis_bands",
-    )(
-        small[0].reshape(1, stations),
-        small[1].reshape(1, beam_group.shape[0]),
-        small[2],
-    )
-    moved[1], moved[2], other[1], bands, chosen, scale = lax.optimization_barrier(
-        (moved[1], moved[2], other[1], bands, chosen, scale)
+    )(late_taps)
+    moved[1], moved[2], other[1], bands = lax.optimization_barrier(
+        (moved[1], moved[2], other[1], bands)
     )
     matrix = pl.pallas_call(
         functools.partial(weight_kernel, axes),

time: 42.6 us -> 42.4 us (level)
  waiting for transfers between devices: 4.53 us -> 4.07 us
    ppermute x19, waiting for transfers between devices: 4.53 us -> 4.07 us  [swap(): return lax.ppermute(x, axis, [(i, i ^ mask) for i in range(size)])]
  transfers between devices with their start and end apart: 19 -> 19, of which waited for: 5 -> 7; matrix products, arithmetic and copies ran while one was open for 0% -> 0% of each run, Pallas kernels for 15% -> 16%
where the time goes in v7:
time: 42.4 us; the launch traced here: 42 us
  starting transfers between devices  19.3 us (46%)
  Pallas kernels  12.4 us (29%)
  local copies, waits for them, and re-layouts  5.37 us (13%)
  waiting for transfers between devices  4.07 us (10%)
  between operations  0.78 us (2%)
    ppermute x19, starting transfers between devices, swap(): return lax.ppermute(x, axis, [(i, i ^ mask) for i in range(size)])  19.3 us
    unnamed x14, local copies, waits for them, and re-layouts  5.35 us
    pallas_call x1, Pallas kernels, call_beams(): pl.pallas_call(lambda *refs: beam_kernel(axes, refs[:len(pieces)], *refs[...  4.52 us
    ppermute x19, waiting for transfers between devices, swap(): return lax.ppermute(x, axis, [(i, i ^ mask) for i in range(size)])  4.07 us
    pallas_call x2, Pallas kernels, add_part(): pl.pallas_call(functools.partial(part_kernel, axes, places), out_shape=ja...  2.06 us
    pallas_call x1, Pallas kernels, fast_body(): pl.pallas_call(band_kernel, out_shape=jax.ShapeDtypeStruct((chan, 2 * (ti...  1.72 us
    pallas_call x1, Pallas kernels, fast_body(): pl.pallas_call(functools.partial(pack_kernel, axes), out_shape=[table] *...  1.69 us
  transfers between devices with their start and end apart: 19, of which 7 were waited for; matrix products, arithmetic and copies ran while one was open for 0% of the time, Pallas kernels for 16%

profile of v7, /device:TPU:0, one launch (start us, length us, event | category | flops | bytes accessed | tf_op | source)
XLA Modules:
  0.0 42.0 jit_solution(15338158927282009153)
XLA Ops:
  0.6 1.0 %copy-done = bf16[16,2,16,512]{3,2,1,0:T(8,128)(2,1)S(1)} copy-done((bf16[16,2,16,512]{3,2,1,0:T(8,128)(2,1)S(1)}, bf16[16,2,16,512]{3,2,1,0:T(8,128)(2,1)}, u32[]{:S(2)}) %copy-start) | copy-done | bytes 524312
  1.7 0.5 %lane_spread.1 = (bf16[4,32,512]{2,1,0:T(8,128)(2,1)S(1)}, bf16[2,32,512]{2,1,0:T(8,128)(2,1)S(1)}, bf16[2,32,512]{2,1,0:T(8,128)(2,1)S(1)}, bf16[4,32,512]{2,1,...) custom-call(bf16[16,2,16,512]{3,2,1,0:T(8,128)(2,1)S(1)} %copy-done), custom_call_target="tpu_custom_call" | custom-call | tf_op jit(solution)/shard_map/lane_spread/pallas_call | solution.py:391
  2.2 0.5 %collective-permute-start.6 = (bf16[2,32,512]{2,1,0:T(8,128)(2,1)S(1)}, bf16[2,32,512]{2,1,0:T(8,128)(2,1)S(1)}, u32[]{:S(2)}, u32[]{:S(2)}) collective-permute-start(bf16[2,32,512]{2,1,0:T(8,128)(2,1)S(1)} %get-tuple-element.41), channel_id=1, source_target_pairs={{0,1},{1,0},{2,3},{3,2},{4,5},{5,4},{6,7},{7,6},{8,9},{9,8},{10,11... | collective-permute-start | bytes 196616 | tf_op jit(solution)/shard_map/ppermute | solution.py:372
  2.7 0.1 collective-permute-start
  2.8 0.4 %collective-permute-start.2 = (bf16[2,32,512]{2,1,0:T(8,128)(2,1)S(1)}, bf16[2,32,512]{2,1,0:T(8,128)(2,1)S(1)}, u32[]{:S(2)}, u32[]{:S(2)}) collective-permute-start(bf16[2,32,512]{2,1,0:T(8,128)(2,1)S(1)} %get-tuple-element.37), channel_id=1, source_target_pairs={{0,1},{1,0},{2,3},{3,2},{4,5},{5,4},{6,7},{7,6},{8,9},{9,8},{10,11... | collective-permute-start | bytes 196616 | tf_op jit(solution)/shard_map/ppermute | solution.py:372
  3.2 2.6 %collective-permute-start.5 = (bf16[2,32,512]{2,1,0:T(8,128)(2,1)S(1)}, bf16[2,32,512]{2,1,0:T(8,128)(2,1)S(1)}, u32[]{:S(2)}, u32[]{:S(2)}) collective-permute-start(bf16[2,32,512]{2,1,0:T(8,128)(2,1)S(1)} %get-tuple-element.40), channel_id=1, source_target_pairs={{0,2},{2,0},{1,3},{3,1},{4,6},{6,4},{5,7},{7,5},{8,10},{10,8},{9,1... | collective-permute-start | bytes 196616 | tf_op jit(solution)/shard_map/ppermute | solution.py:372
  5.8 0.0 collective-permute-done.6
  5.8 0.7 %collective-permute-start.7 = (bf16[2,32,512]{2,1,0:T(8,128)(2,1)S(1)}, bf16[2,32,512]{2,1,0:T(8,128)(2,1)S(1)}, u32[]{:S(2)}, u32[]{:S(2)}) collective-permute-start(bf16[2,32,512]{2,1,0:T(8,128)(2,1)S(1)} %collective-permute-done.6), channel_id=1, source_target_pairs={{0,2},{2,0},{1,3},{3,1},{4,6},{6,4},{5,7},{7,5},{8,10},{10,8},{9,1... | collective-permute-start | bytes 196616 | tf_op jit(solution)/shard_map/ppermute | solution.py:372
  6.5 1.4 %collective-permute-start.1 = (bf16[2,32,512]{2,1,0:T(8,128)(2,1)S(1)}, bf16[2,32,512]{2,1,0:T(8,128)(2,1)S(1)}, u32[]{:S(2)}, u32[]{:S(2)}) collective-permute-start(bf16[2,32,512]{2,1,0:T(8,128)(2,1)S(1)} %get-tuple-element.36), channel_id=1, source_target_pairs={{0,2},{2,0},{1,3},{3,1},{4,6},{6,4},{5,7},{7,5},{8,10},{10,8},{9,1... | collective-permute-start | bytes 196616 | tf_op jit(solution)/shard_map/ppermute | solution.py:372
  7.8 0.0 collective-permute-done.2
  7.8 0.7 %collective-permute-start.3 = (bf16[2,32,512]{2,1,0:T(8,128)(2,1)S(1)}, bf16[2,32,512]{2,1,0:T(8,128)(2,1)S(1)}, u32[]{:S(2)}, u32[]{:S(2)}) collective-permute-start(bf16[2,32,512]{2,1,0:T(8,128)(2,1)S(1)} %collective-permute-done.2), channel_id=1, source_target_pairs={{0,2},{2,0},{1,3},{3,1},{4,6},{6,4},{5,7},{7,5},{8,10},{10,8},{9,1... | collective-permute-start | bytes 196616 | tf_op jit(solution)/shard_map/ppermute | solution.py:372
  8.5 0.7 %copy-done.3 = f32[16,16]{1,0:T(8,128)S(1)} copy-done((f32[16,16]{1,0:T(8,128)S(1)}, f32[16,16]{1,0:T(8,128)}, u32[]{:S(2)}) %copy-start.3) | copy-done | bytes 1048
  9.2 0.7 %copy-done.5 = s32[256]{0:T(256)S(1)} copy-done((s32[256]{0:T(256)S(1)}, s32[256]{0:T(256)}, u32[]{:S(2)}) %copy-start.5) | copy-done | bytes 1048
  9.9 0.2 station_tables.1
  10.1 0.7 %collective-permute-done.7.refs_3_ = bf16[2,32,512]{2,1,0:T(8,128)(2,1)S(1)} collective-permute-done((bf16[2,32,512]{2,1,0:T(8,128)(2,1)S(1)}, bf16[2,32,512]{2,1,0:T(8,128)(2,1)S(1)}, u32[]{:S(2)}, u32[]{:S(2)}) %collective-permute-start.7) | collective-permute-done | bytes 65568 | tf_op jit(solution)/shard_map/ppermute | solution.py:372
  10.7 0.0 collective-permute-done.refs_1_
  10.7 0.2 plane_sums_far.1
  10.9 2.7 %collective-permute-start.8 = (bf16[64,512]{1,0:T(8,128)(2,1)S(1)}, bf16[64,512]{1,0:T(8,128)(2,1)S(1)}, u32[]{:S(2)}, u32[]{:S(2)}) collective-permute-start(bf16[64,512]{1,0:T(8,128)(2,1)S(1)} %get-tuple-element.42), channel_id=1, source_target_pairs={{0,8},{4,12},{8,0},{12,4},{1,9},{5,13},{9,1},{13,5},{2,10},{6,14},... | collective-permute-start | bytes 196616 | tf_op jit(solution)/shard_map/ppermute | solution.py:372
  13.6 1.3 %collective-permute-start.9 = (bf16[64,512]{1,0:T(8,128)(2,1)S(1)}, bf16[64,512]{1,0:T(8,128)(2,1)S(1)}, u32[]{:S(2)}, u32[]{:S(2)}) collective-permute-start(bf16[64,512]{1,0:T(8,128)(2,1)S(1)} %get-tuple-element.43), channel_id=1, source_target_pairs={{0,12},{4,8},{8,4},{12,0},{1,13},{5,9},{9,5},{13,1},{2,14},{6,10},... | collective-permute-start | bytes 196616 | tf_op jit(solution)/shard_map/ppermute | solution.py:372
  14.9 0.2 plane_sums_near.1
  15.1 0.3 collective-permute-start.4
  15.4 0.9 %copy-done.1 = bf16[4,2,256,32]{2,3,1,0:T(8,128)(2,1)S(1)} copy-done((bf16[4,2,256,32]{2,3,1,0:T(8,128)(2,1)S(1)}, bf16[4,2,256,32]{2,3,1,0:T(8,128)(2,1)}, u32[]{:S(2)}) %copy-start.1) | copy-done | bytes 131096
  16.3 0.7 %copy-done.4 = s32[1024]{0:T(1024)S(1)} copy-done((s32[1024]{0:T(1024)S(1)}, s32[1024]{0:T(1024)}, u32[]{:S(2)}) %copy-start.4) | copy-done | bytes 4120
  17.0 0.7 %copy-done.6 = s32[32,1]{0,1:T(1,128)S(1)} copy-done((s32[32,1]{0,1:T(1,128)S(1)}, s32[32,1]{0,1:T(1,128)}, u32[]{:S(2)}) %copy-start.6) | copy-done | bytes 152
  17.7 1.7 %weight_shares.1 = (f32[32,64]{1,0:T(8,128)S(1)}, f32[32,64]{1,0:T(8,128)S(1)}, bf16[32,512]{1,0:T(8,128)(2,1)S(1)}, bf16[32,512]{1,0:T(8,128)(2,1)S(1)}, bf16[3...) custom-call(bf16[4,2,32,256]{3,2,1,0:T(8,128)(2,1)S(1)} %bitcast.14, s32[1,32]{1,0:T(1,128)S(1)} %bitcast.18, ...), custom_call_target="tpu_custom_call" | custom-call | bytes 8388608 | tf_op jit(solution)/shard_map/weight_shares/pallas_call | solution.py:440
  19.3 0.0 collective-permute-done.8.refs_2_
  19.4 0.4 collective-permute-done.9.refs_3_
  19.7 0.4 collective-permute-done.4.refs_1_
  20.1 0.6 %station_filter.1 = (bf16[64,512]{1,0:T(8,128)(2,1)S(1)}, bf16[96,512]{1,0:T(8,128)(2,1)S(1)}, bf16[96,512]{1,0:T(8,128)(2,1)S(1)}, bf16[96,512]{1,0:T(8,128)(2,1)S(1)}) custom-call(f32[16,512]{1,0:T(8,128)S(1)} %get-tuple-element.32.taps_ref, f32[64,512]{1,0:T(8,128)S(1)} %get-tuple-element.38.refs_0_, bf16[64,512]{1,0:T(8,128)(2,1)S(1)} %collective-permute-done.4.refs_1_, ...), custom_call_target="tpu_custom_call" | custom-call | tf_op jit(solution)/shard_map/station_filter/pallas_call | solution.py:455
  20.8 1.1 %collective-permute-start.10 = (bf16[96,512]{1,0:T(8,128)(2,1)S(1)}, bf16[96,512]{1,0:T(8,128)(2,1)S(1)}, u32[]{:S(2)}, u32[]{:S(2)}) collective-permute-start(bf16[96,512]{1,0:T(8,128)(2,1)S(1)} %get-tuple-element.48), channel_id=1, source_target_pairs={{0,4},{4,0},{8,12},{12,8},{1,5},{5,1},{9,13},{13,9},{2,6},{6,2},{1... | collective-permute-start | bytes 294920 | tf_op jit(solution)/shard_map/ppermute | solution.py:372
  21.9 1.7 %collective-permute-start.11 = (bf16[96,512]{1,0:T(8,128)(2,1)S(1)}, bf16[96,512]{1,0:T(8,128)(2,1)S(1)}, u32[]{:S(2)}, u32[]{:S(2)}) collective-permute-start(bf16[96,512]{1,0:T(8,128)(2,1)S(1)} %get-tuple-element.49), channel_id=1, source_target_pairs={{0,8},{4,12},{8,0},{12,4},{1,9},{5,13},{9,1},{13,5},{2,10},{6,14},... | collective-permute-start | bytes 294920 | tf_op jit(solution)/shard_map/ppermute | solution.py:372
  23.5 1.7 %collective-permute-start.12 = (bf16[96,512]{1,0:T(8,128)(2,1)S(1)}, bf16[96,512]{1,0:T(8,128)(2,1)S(1)}, u32[]{:S(2)}, u32[]{:S(2)}) collective-permute-start(bf16[96,512]{1,0:T(8,128)(2,1)S(1)} %get-tuple-element.50), channel_id=1, source_target_pairs={{0,12},{4,8},{8,4},{12,0},{1,13},{5,9},{9,5},{13,1},{2,14},{6,10},... | collective-permute-start | bytes 294920 | tf_op jit(solution)/shard_map/ppermute | solution.py:372
  25.2 0.2 collective-permute-done.10.refs_1_
  25.4 1.6 %collective-permute-start.13 = (bf16[64,512]{1,0:T(8,128)(2,1)S(1)}, bf16[64,512]{1,0:T(8,128)(2,1)S(1)}, u32[]{:S(2)}, u32[]{:S(2)}) collective-permute-start(bf16[64,512]{1,0:T(8,128)(2,1)S(1)} %get-tuple-element.63), channel_id=1, source_target_pairs={{0,2},{2,0},{1,3},{3,1},{4,6},{6,4},{5,7},{7,5},{8,10},{10,8},{9,1... | collective-permute-start | bytes 196616 | tf_op jit(solution)/shard_map/ppermute | solution.py:372
  27.1 0.7 %copy-done.2 = f32[16,16]{1,0:T(8,128)S(1)} copy-done((f32[16,16]{1,0:T(8,128)S(1)}, f32[16,16]{1,0:T(8,128)}, u32[]{:S(2)}) %copy-start.2) | copy-done | bytes 1048
  27.8 1.7 %synthesis_bands.1.refs_7_ = bf16[16,768,256]{2,1,0:T(8,128)(2,1)S(1)} custom-call(f32[16,16]{1,0:T(8,128)S(1)} %copy-done.2), custom_call_target="tpu_custom_call" | custom-call | bytes 16777216 | tf_op jit(solution)/shard_map/synthesis_bands/pallas_call | solution.py:468
  29.5 0.5 %collective-permute-start.15 = (bf16[64,512]{1,0:T(8,128)(2,1)S(1)}, bf16[64,512]{1,0:T(8,128)(2,1)S(1)}, u32[]{:S(2)}, u32[]{:S(2)}) collective-permute-start(bf16[64,512]{1,0:T(8,128)(2,1)S(1)} %get-tuple-element.47), channel_id=1, source_target_pairs={{0,2},{2,0},{1,3},{3,1},{4,6},{6,4},{5,7},{7,5},{8,10},{10,8},{9,1... | collective-permute-start | bytes 196616 | tf_op jit(solution)/shard_map/ppermute | solution.py:372
  30.0 1.0 %collective-permute-done.11.refs_2_ = bf16[96,512]{1,0:T(8,128)(2,1)S(1)} collective-permute-done((bf16[96,512]{1,0:T(8,128)(2,1)S(1)}, bf16[96,512]{1,0:T(8,128)(2,1)S(1)}, u32[]{:S(2)}, u32[]{:S(2)}) %collective-permute-start.11) | collective-permute-done | bytes 98336 | tf_op jit(solution)/shard_map/ppermute | solution.py:372
  31.1 2.0 %collective-permute-start.16 = (bf16[2,64,512]{2,1,0:T(8,128)(2,1)S(1)}, bf16[2,64,512]{2,1,0:T(8,128)(2,1)S(1)}, u32[]{:S(2)}, u32[]{:S(2)}) collective-permute-start(bf16[2,64,512]{2,1,0:T(8,128)(2,1)S(1)} %pad_maximum_fusion.2), channel_id=1, source_target_pairs={{0,2},{2,0},{1,3},{3,1},{4,6},{6,4},{5,7},{7,5},{8,10},{10,8},{9,1... | collective-permute-start | bytes 393224 | tf_op jit(solution)/shard_map/ppermute | solution.py:372
  33.1 0.1 collective-permute-start.14
  33.2 0.6 %collective-permute-done.15 = bf16[64,512]{1,0:T(8,128)(2,1)S(1)} collective-permute-done((bf16[64,512]{1,0:T(8,128)(2,1)S(1)}, bf16[64,512]{1,0:T(8,128)(2,1)S(1)}, u32[]{:S(2)}, u32[]{:S(2)}) %collective-permute-start.15) | collective-permute-done | bytes 65568 | tf_op jit(solution)/shard_map/ppermute | solution.py:372
  33.8 0.1 collective-permute-start.17
  33.9 0.8 %weight_matrix.1.m_ref.refs_6_ = bf16[16,128,1024]{2,1,0:T(8,128)(2,1)S(1)} custom-call(f32[32,64]{1,0:T(8,128)S(1)} %get-tuple-element.54.chosen_ref, f32[32,64]{1,0:T(8,128)S(1)} %get-tuple-element.55.scale_ref, bf16[32,512]{1,0:T(8,128)(2,1)S(1)} %get-tuple-element.56.refs_0_, bf16[96,512]{1,0:T(8,128)(2,1)S(1)} %collective-permute-done.10.refs_1_, ...), custom_call_target="tpu_custom_call" | custom-call | bytes 8388608 | tf_op jit(solution)/shard_map/weight_matrix/pallas_call | solution.py:480
  34.7 0.7 %own_beams.1.refs_3_ = f32[16,128,512]{2,1,0:T(8,128)S(1)} custom-call(bf16[16,128,1024]{2,1,0:T(8,128)(2,1)S(1)} %weight_matrix.1.m_ref.refs_6_, bf16[4,64,512]{2,1,0:T(8,128)(2,1)S(1)} %pad_maximum_fusion.refs_0_), custom_call_target="tpu_custom_call" | custom-call | bytes 8388608 | tf_op jit(solution)/shard_map/own_beams/pallas_call | solution.py:492
  35.5 0.7 %collective-permute-done.16.refs_2_.refs_3_ = bf16[2,64,512]{2,1,0:T(8,128)(2,1)S(1)} collective-permute-done((bf16[2,64,512]{2,1,0:T(8,128)(2,1)S(1)}, bf16[2,64,512]{2,1,0:T(8,128)(2,1)S(1)}, u32[]{:S(2)}, u32[]{:S(2)}) %collective-permute-start.16) | collective-permute-done | bytes 131104 | tf_op jit(solution)/shard_map/ppermute | solution.py:372
  36.2 1.3 %near_beams.1.refs_8_ = f32[16,128,512]{2,1,0:T(8,128)S(1)} custom-call(bf16[16,128,1024]{2,1,0:T(8,128)(2,1)S(1)} %weight_matrix.1.m_ref.refs_6_, bf16[4,64,512]{2,1,0:T(8,128)(2,1)S(1)} %collective-permute-done.14.refs_0_.refs_1_, bf16[2,64,512]{2,1,0:T(8,128)(2,1)S(1)} %pad_maximum_fusion.1.refs_1_.refs_2_, ...), custom_call_target="tpu_custom_call" | custom-call | bytes 8388608 | tf_op jit(solution)/shard_map/near_beams/pallas_call | solution.py:492
  37.5 0.0 collective-permute-done.18.refs_5_
  37.5 4.5 %beams_and_series.1 = (f32[128,2,8,512]{3,2,1,0:T(8,128)}, f32[4,2,8,32]{3,2,1,0:T(8,128)}) custom-call(bf16[4,64,512]{2,1,0:T(8,128)(2,1)S(1)} %pad_maximum_fusion.refs_0_, bf16[4,64,512]{2,1,0:T(8,128)(2,1)S(1)} %collective-permute-done.14.refs_0_.refs_1_, bf16[2,64,512]{2,1,0:T(8,128)(2,1)S(1)} %pad_maximum_fusion.1.refs_1_.refs_2_, ...), custom_call_target="tpu_custom_call" | custom-call | tf_op jit(solution)/shard_map/beams_and_series/pallas_call | solution.py:349
  (20 shorter events, 0.1 us)
Async XLA Ops:
  0.6 1.0 %copy-start = (bf16[16,2,16,512]{3,2,1,0:T(8,128)(2,1)S(1)}, bf16[16,2,16,512]{3,2,1,0:T(8,128)(2,1)}, u32[]{:S(2)}) copy-start(bf16[16,2,16,512]{3,2,1,0:T(8,128)(2,1)} %x_ref.1) | copy-start | bytes 1572868
  2.2 3.6 %collective-permute-start.6 = (bf16[2,32,512]{2,1,0:T(8,128)(2,1)S(1)}, bf16[2,32,512]{2,1,0:T(8,128)(2,1)S(1)}, u32[]{:S(2)}, u32[]{:S(2)}) collective-permute-start(bf16[2,32,512]{2,1,0:T(8,128)(2,1)S(1)} %get-tuple-element.41), channel_id=1, source_target_pairs={{0,1},{1,0},{2,3},{3,2},{4,5},{5,4},{6,7},{7,6},{8,9},{9,8},{10,11... | collective-permute-start | bytes 196616 | tf_op jit(solution)/shard_map/ppermute | solution.py:372
  2.7 8.0 %collective-permute-start = (bf16[4,32,512]{2,1,0:T(8,128)(2,1)S(1)}, bf16[4,32,512]{2,1,0:T(8,128)(2,1)S(1)}, u32[]{:S(2)}, u32[]{:S(2)}) collective-permute-start(bf16[4,32,512]{2,1,0:T(8,128)(2,1)S(1)} %get-tuple-element.35), channel_id=1, source_target_pairs={{0,1},{1,0},{2,3},{3,2},{4,5},{5,4},{6,7},{7,6},{8,9},{9,8},{10,11... | collective-permute-start | bytes 393224 | tf_op jit(solution)/shard_map/ppermute | solution.py:372
  2.8 5.0 %collective-permute-start.2 = (bf16[2,32,512]{2,1,0:T(8,128)(2,1)S(1)}, bf16[2,32,512]{2,1,0:T(8,128)(2,1)S(1)}, u32[]{:S(2)}, u32[]{:S(2)}) collective-permute-start(bf16[2,32,512]{2,1,0:T(8,128)(2,1)S(1)} %get-tuple-element.37), channel_id=1, source_target_pairs={{0,1},{1,0},{2,3},{3,2},{4,5},{5,4},{6,7},{7,6},{8,9},{9,8},{10,11... | collective-permute-start | bytes 196616 | tf_op jit(solution)/shard_map/ppermute | solution.py:372
  3.2 6.8 %collective-permute-start.5 = (bf16[2,32,512]{2,1,0:T(8,128)(2,1)S(1)}, bf16[2,32,512]{2,1,0:T(8,128)(2,1)S(1)}, u32[]{:S(2)}, u32[]{:S(2)}) collective-permute-start(bf16[2,32,512]{2,1,0:T(8,128)(2,1)S(1)} %get-tuple-element.40), channel_id=1, source_target_pairs={{0,2},{2,0},{1,3},{3,1},{4,6},{6,4},{5,7},{7,5},{8,10},{10,8},{9,1... | collective-permute-start | bytes 196616 | tf_op jit(solution)/shard_map/ppermute | solution.py:372
  5.8 4.9 %collective-permute-start.7 = (bf16[2,32,512]{2,1,0:T(8,128)(2,1)S(1)}, bf16[2,32,512]{2,1,0:T(8,128)(2,1)S(1)}, u32[]{:S(2)}, u32[]{:S(2)}) collective-permute-start(bf16[2,32,512]{2,1,0:T(8,128)(2,1)S(1)} %collective-permute-done.6), channel_id=1, source_target_pairs={{0,2},{2,0},{1,3},{3,1},{4,6},{6,4},{5,7},{7,5},{8,10},{10,8},{9,1... | collective-permute-start | bytes 196616 | tf_op jit(solution)/shard_map/ppermute | solution.py:372
  6.5 8.5 %collective-permute-start.1 = (bf16[2,32,512]{2,1,0:T(8,128)(2,1)S(1)}, bf16[2,32,512]{2,1,0:T(8,128)(2,1)S(1)}, u32[]{:S(2)}, u32[]{:S(2)}) collective-permute-start(bf16[2,32,512]{2,1,0:T(8,128)(2,1)S(1)} %get-tuple-element.36), channel_id=1, source_target_pairs={{0,2},{2,0},{1,3},{3,1},{4,6},{6,4},{5,7},{7,5},{8,10},{10,8},{9,1... | collective-permute-start | bytes 196616 | tf_op jit(solution)/shard_map/ppermute | solution.py:372
  7.8 7.1 %collective-permute-start.3 = (bf16[2,32,512]{2,1,0:T(8,128)(2,1)S(1)}, bf16[2,32,512]{2,1,0:T(8,128)(2,1)S(1)}, u32[]{:S(2)}, u32[]{:S(2)}) collective-permute-start(bf16[2,32,512]{2,1,0:T(8,128)(2,1)S(1)} %collective-permute-done.2), channel_id=1, source_target_pairs={{0,2},{2,0},{1,3},{3,1},{4,6},{6,4},{5,7},{7,5},{8,10},{10,8},{9,1... | collective-permute-start | bytes 196616 | tf_op jit(solution)/shard_map/ppermute | solution.py:372
  8.5 0.7 %copy-start.3 = (f32[16,16]{1,0:T(8,128)S(1)}, f32[16,16]{1,0:T(8,128)}, u32[]{:S(2)}) copy-start(f32[16,16]{1,0:T(8,128)} %taps_ref.2) | copy-start | bytes 3076
  9.2 0.7 %copy-start.5 = (s32[256]{0:T(256)S(1)}, s32[256]{0:T(256)}, u32[]{:S(2)}) copy-start(s32[256]{0:T(256)} %param.10) | copy-start | bytes 3076
  10.9 8.4 %collective-permute-start.8 = (bf16[64,512]{1,0:T(8,128)(2,1)S(1)}, bf16[64,512]{1,0:T(8,128)(2,1)S(1)}, u32[]{:S(2)}, u32[]{:S(2)}) collective-permute-start(bf16[64,512]{1,0:T(8,128)(2,1)S(1)} %get-tuple-element.42), channel_id=1, source_target_pairs={{0,8},{4,12},{8,0},{12,4},{1,9},{5,13},{9,1},{13,5},{2,10},{6,14},... | collective-permute-start | bytes 196616 | tf_op jit(solution)/shard_map/ppermute | solution.py:372
  13.6 6.2 %collective-permute-start.9 = (bf16[64,512]{1,0:T(8,128)(2,1)S(1)}, bf16[64,512]{1,0:T(8,128)(2,1)S(1)}, u32[]{:S(2)}, u32[]{:S(2)}) collective-permute-start(bf16[64,512]{1,0:T(8,128)(2,1)S(1)} %get-tuple-element.43), channel_id=1, source_target_pairs={{0,12},{4,8},{8,4},{12,0},{1,13},{5,9},{9,5},{13,1},{2,14},{6,10},... | collective-permute-start | bytes 196616 | tf_op jit(solution)/shard_map/ppermute | solution.py:372
  15.1 5.0 %collective-permute-start.4 = (bf16[64,512]{1,0:T(8,128)(2,1)S(1)}, bf16[64,512]{1,0:T(8,128)(2,1)S(1)}, u32[]{:S(2)}, u32[]{:S(2)}) collective-permute-start(bf16[64,512]{1,0:T(8,128)(2,1)S(1)} %get-tuple-element.39), channel_id=1, source_target_pairs={{0,4},{4,0},{8,12},{12,8},{1,5},{5,1},{9,13},{13,9},{2,6},{6,2},{1... | collective-permute-start | bytes 196616 | tf_op jit(solution)/shard_map/ppermute | solution.py:372
  15.4 0.9 %copy-start.1 = (bf16[4,2,256,32]{2,3,1,0:T(8,128)(2,1)S(1)}, bf16[4,2,256,32]{2,3,1,0:T(8,128)(2,1)}, u32[]{:S(2)}) copy-start(bf16[4,2,256,32]{2,3,1,0:T(8,128)(2,1)} %param.13) | copy-start | bytes 393220
  16.3 0.7 %copy-start.4 = (s32[1024]{0:T(1024)S(1)}, s32[1024]{0:T(1024)}, u32[]{:S(2)}) copy-start(s32[1024]{0:T(1024)} %param.12) | copy-start | bytes 12292
  17.0 0.7 %copy-start.6 = (s32[32,1]{0,1:T(1,128)S(1)}, s32[32,1]{0,1:T(1,128)}, u32[]{:S(2)}) copy-start(s32[32,1]{0,1:T(1,128)} %param.11) | copy-start | bytes 388
  20.8 4.7 %collective-permute-start.10 = (bf16[96,512]{1,0:T(8,128)(2,1)S(1)}, bf16[96,512]{1,0:T(8,128)(2,1)S(1)}, u32[]{:S(2)}, u32[]{:S(2)}) collective-permute-start(bf16[96,512]{1,0:T(8,128)(2,1)S(1)} %get-tuple-element.48), channel_id=1, source_target_pairs={{0,4},{4,0},{8,12},{12,8},{1,5},{5,1},{9,13},{13,9},{2,6},{6,2},{1... | collective-permute-start | bytes 294920 | tf_op jit(solution)/shard_map/ppermute | solution.py:372
  21.9 9.2 %collective-permute-start.11 = (bf16[96,512]{1,0:T(8,128)(2,1)S(1)}, bf16[96,512]{1,0:T(8,128)(2,1)S(1)}, u32[]{:S(2)}, u32[]{:S(2)}) collective-permute-start(bf16[96,512]{1,0:T(8,128)(2,1)S(1)} %get-tuple-element.49), channel_id=1, source_target_pairs={{0,8},{4,12},{8,0},{12,4},{1,9},{5,13},{9,1},{13,5},{2,10},{6,14},... | collective-permute-start | bytes 294920 | tf_op jit(solution)/shard_map/ppermute | solution.py:372
  23.5 7.5 %collective-permute-start.12 = (bf16[96,512]{1,0:T(8,128)(2,1)S(1)}, bf16[96,512]{1,0:T(8,128)(2,1)S(1)}, u32[]{:S(2)}, u32[]{:S(2)}) collective-permute-start(bf16[96,512]{1,0:T(8,128)(2,1)S(1)} %get-tuple-element.50), channel_id=1, source_target_pairs={{0,12},{4,8},{8,4},{12,0},{1,13},{5,9},{9,5},{13,1},{2,14},{6,10},... | collective-permute-start | bytes 294920 | tf_op jit(solution)/shard_map/ppermute | solution.py:372
  25.4 5.6 %collective-permute-start.13 = (bf16[64,512]{1,0:T(8,128)(2,1)S(1)}, bf16[64,512]{1,0:T(8,128)(2,1)S(1)}, u32[]{:S(2)}, u32[]{:S(2)}) collective-permute-start(bf16[64,512]{1,0:T(8,128)(2,1)S(1)} %get-tuple-element.63), channel_id=1, source_target_pairs={{0,2},{2,0},{1,3},{3,1},{4,6},{6,4},{5,7},{7,5},{8,10},{10,8},{9,1... | collective-permute-start | bytes 196616 | tf_op jit(solution)/shard_map/ppermute | solution.py:372
  27.1 0.7 %copy-start.2 = (f32[16,16]{1,0:T(8,128)S(1)}, f32[16,16]{1,0:T(8,128)}, u32[]{:S(2)}) copy-start(f32[16,16]{1,0:T(8,128)} %taps_ref.3) | copy-start | bytes 3076
  29.5 4.3 %collective-permute-start.15 = (bf16[64,512]{1,0:T(8,128)(2,1)S(1)}, bf16[64,512]{1,0:T(8,128)(2,1)S(1)}, u32[]{:S(2)}, u32[]{:S(2)}) collective-permute-start(bf16[64,512]{1,0:T(8,128)(2,1)S(1)} %get-tuple-element.47), channel_id=1, source_target_pairs={{0,2},{2,0},{1,3},{3,1},{4,6},{6,4},{5,7},{7,5},{8,10},{10,8},{9,1... | collective-permute-start | bytes 196616 | tf_op jit(solution)/shard_map/ppermute | solution.py:372
  31.1 5.0 %collective-permute-start.16 = (bf16[2,64,512]{2,1,0:T(8,128)(2,1)S(1)}, bf16[2,64,512]{2,1,0:T(8,128)(2,1)S(1)}, u32[]{:S(2)}, u32[]{:S(2)}) collective-permute-start(bf16[2,64,512]{2,1,0:T(8,128)(2,1)S(1)} %pad_maximum_fusion.2), channel_id=1, source_target_pairs={{0,2},{2,0},{1,3},{3,1},{4,6},{6,4},{5,7},{7,5},{8,10},{10,8},{9,1... | collective-permute-start | bytes 393224 | tf_op jit(solution)/shard_map/ppermute | solution.py:372
  33.1 3.0 %collective-permute-start.14 = (bf16[4,64,512]{2,1,0:T(8,128)(2,1)S(1)}, bf16[4,64,512]{2,1,0:T(8,128)(2,1)S(1)}, u32[]{:S(2)}, u32[]{:S(2)}) collective-permute-start(bf16[4,64,512]{2,1,0:T(8,128)(2,1)S(1)} %pad_maximum_fusion.refs_0_), channel_id=1, source_target_pairs={{0,1},{1,0},{2,3},{3,2},{4,5},{5,4},{6,7},{7,6},{8,9},{9,8},{10,11... | collective-permute-start | bytes 786440 | tf_op jit(solution)/shard_map/ppermute | solution.py:372
  33.8 3.7 %collective-permute-start.17 = (bf16[2,64,512]{2,1,0:T(8,128)(2,1)S(1)}, bf16[2,64,512]{2,1,0:T(8,128)(2,1)S(1)}, u32[]{:S(2)}, u32[]{:S(2)}) collective-permute-start(bf16[2,64,512]{2,1,0:T(8,128)(2,1)S(1)} %pad_maximum_fusion.1.refs_1_.refs_2_), channel_id=1, source_target_pairs={{0,1},{1,0},{2,3},{3,2},{4,5},{5,4},{6,7},{7,6},{8,9},{9,8},{10,11... | collective-permute-start | bytes 393224 | tf_op jit(solution)/shard_map/ppermute | solution.py:372
  36.2 1.3 %collective-permute-start.18 = (bf16[2,64,512]{2,1,0:T(8,128)(2,1)S(1)}, bf16[2,64,512]{2,1,0:T(8,128)(2,1)S(1)}, u32[]{:S(2)}, u32[]{:S(2)}) collective-permute-start(bf16[2,64,512]{2,1,0:T(8,128)(2,1)S(1)} %collective-permute-done.16.refs_2_.refs_3_), channel_id=1, source_target_pairs={{0,1},{1,0},{2,3},{3,2},{4,5},{5,4},{6,7},{7,6},{8,9},{9,8},{10,11... | collective-permute-start | bytes 393224 | tf_op jit(solution)/shard_map/ppermute | solution.py:372

commit v8 on v7

--- a/solution.py
+++ b/solution.py
@@ -261,7 +261,7 @@
     cross_ref,
     inverse_ref,
     out_ref,
-    store_sems,
+    store_sem,
 ):
     row, col, sub = (lax.axis_index(a) for a in axes)
     rows = x_refs[0].shape[1]
@@ -272,7 +272,6 @@
     gather_lanes(axes, x_refs[4:], PLACES[4:], lanes_ref)
     beams = m_ref.shape[1] // 2
     tile = t_ref.shape[2]
-    stores = []
     for first in range(0, 16, 4):
         found = lane_products(axes, FLIPS[3:], m_ref, lanes_ref, first, 4)
         found = found.reshape((4,) + sum_ref.shape[1:]) + sum_ref[first : first + 4]
@@ -290,14 +289,11 @@
             for part in range(tile // 128):
                 slot = n * (tile // 128) + part
                 out_ref[lane, slot] = value[:, part * 128 : (part + 1) * 128]
-                stores.append(
-                    pltpu.make_async_copy(
-                        out_ref.at[lane, slot],
-                        series_ref.at[:, lane // 8, lane % 8, pl.ds(slot * 128, 128)],
-                        store_sems.at[lane, slot],
-                    )
-                )
-                stores[-1].start()
+                pltpu.make_async_copy(
+                    out_ref.at[lane, slot],
+                    series_ref.at[:, lane // 8, lane % 8, pl.ds(slot * 128, 128)],
+                    store_sem,
+                ).start()
     gather_lanes(axes, x_refs[:4], PLACES[:4], lanes_ref)
     inner = []
     for b in range(4):
@@ -336,8 +332,7 @@
         own_imag = cross_ref[pl.ds(pl.multiple_of(stations + block, own), own)]
         vis_ref[j, 0] = (own_real[:, :stations] + own_imag[:, stations:]) * (1.0 / SPEC)
         vis_ref[j, 1] = (own_imag[:, :stations] - own_real[:, stations:]) * (1.0 / SPEC)
-    for copy in stores:
-        copy.wait()
+    pltpu.make_async_copy(out_ref, out_ref, store_sem).wait()
 
 
 def call_beams(axes, pieces, matrix, bands, sums):
@@ -359,7 +354,7 @@
             pltpu.VMEM((2 * stations, 2 * stations), jnp.float32),
             pltpu.VMEM((chan, 2 * beams, frames), jnp.bfloat16),
             pltpu.VMEM((chan, frames // 128, 2 * beams, 128), jnp.float32),
-            pltpu.SemaphoreType.DMA((chan, frames // 128)),
+            pltpu.SemaphoreType.DMA,
         ],
         compiler_params=params,
         name="beams_and_series",

time: 42.4 us -> 41.8 us (0.986)
  Pallas kernels: 12.4 us -> 11.9 us
    pallas_call x1, Pallas kernels: 4.52 us -> 3.96 us  [call_beams(): pl.pallas_call(lambda *refs: beam_kernel(axes, refs[:len(pieces)], *refs[...]
where the time goes in v8:
time: 41.8 us; the launch traced here: 41.5 us
  starting transfers between devices  19.3 us (46%)
  Pallas kernels  11.9 us (28%)
  local copies, waits for them, and re-layouts  5.37 us (13%)
  waiting for transfers between devices  4.07 us (10%)
  between operations  0.78 us (2%)
    ppermute x19, starting transfers between devices, swap(): return lax.ppermute(x, axis, [(i, i ^ mask) for i in range(size)])  19.3 us
    unnamed x14, local copies, waits for them, and re-layouts  5.35 us
    ppermute x19, waiting for transfers between devices, swap(): return lax.ppermute(x, axis, [(i, i ^ mask) for i in range(size)])  4.07 us
    pallas_call x1, Pallas kernels, call_beams(): pl.pallas_call(lambda *refs: beam_kernel(axes, refs[:len(pieces)], *refs[...  3.96 us
    pallas_call x2, Pallas kernels, add_part(): pl.pallas_call(functools.partial(part_kernel, axes, places), out_shape=ja...  2.06 us
    pallas_call x1, Pallas kernels, fast_body(): pl.pallas_call(band_kernel, out_shape=jax.ShapeDtypeStruct((chan, 2 * (ti...  1.72 us
    pallas_call x1, Pallas kernels, fast_body(): pl.pallas_call(functools.partial(pack_kernel, axes), out_shape=[table] *...  1.69 us
  transfers between devices with their start and end apart: 19, of which 7 were waited for; matrix products, arithmetic and copies ran while one was open for 0% of the time, Pallas kernels for 16%

profile of v8, /device:TPU:0, one launch (start us, length us, event | category | flops | bytes accessed | tf_op | source)
XLA Modules:
  0.0 41.5 jit_solution(18213217877481224191)
XLA Ops:
  0.6 1.0 %copy-done = bf16[16,2,16,512]{3,2,1,0:T(8,128)(2,1)S(1)} copy-done((bf16[16,2,16,512]{3,2,1,0:T(8,128)(2,1)S(1)}, bf16[16,2,16,512]{3,2,1,0:T(8,128)(2,1)}, u32[]{:S(2)}) %copy-start) | copy-done | bytes 524312
  1.7 0.5 %lane_spread.1 = (bf16[4,32,512]{2,1,0:T(8,128)(2,1)S(1)}, bf16[2,32,512]{2,1,0:T(8,128)(2,1)S(1)}, bf16[2,32,512]{2,1,0:T(8,128)(2,1)S(1)}, bf16[4,32,512]{2,1,...) custom-call(bf16[16,2,16,512]{3,2,1,0:T(8,128)(2,1)S(1)} %copy-done), custom_call_target="tpu_custom_call" | custom-call | tf_op jit(solution)/shard_map/lane_spread/pallas_call | solution.py:386
  2.2 0.5 %collective-permute-start.6 = (bf16[2,32,512]{2,1,0:T(8,128)(2,1)S(1)}, bf16[2,32,512]{2,1,0:T(8,128)(2,1)S(1)}, u32[]{:S(2)}, u32[]{:S(2)}) collective-permute-start(bf16[2,32,512]{2,1,0:T(8,128)(2,1)S(1)} %get-tuple-element.41), channel_id=1, source_target_pairs={{0,1},{1,0},{2,3},{3,2},{4,5},{5,4},{6,7},{7,6},{8,9},{9,8},{10,11... | collective-permute-start | bytes 196616 | tf_op jit(solution)/shard_map/ppermute | solution.py:367
  2.7 0.1 collective-permute-start
  2.8 0.4 %collective-permute-start.2 = (bf16[2,32,512]{2,1,0:T(8,128)(2,1)S(1)}, bf16[2,32,512]{2,1,0:T(8,128)(2,1)S(1)}, u32[]{:S(2)}, u32[]{:S(2)}) collective-permute-start(bf16[2,32,512]{2,1,0:T(8,128)(2,1)S(1)} %get-tuple-element.37), channel_id=1, source_target_pairs={{0,1},{1,0},{2,3},{3,2},{4,5},{5,4},{6,7},{7,6},{8,9},{9,8},{10,11... | collective-permute-start | bytes 196616 | tf_op jit(solution)/shard_map/ppermute | solution.py:367
  3.2 2.6 %collective-permute-start.5 = (bf16[2,32,512]{2,1,0:T(8,128)(2,1)S(1)}, bf16[2,32,512]{2,1,0:T(8,128)(2,1)S(1)}, u32[]{:S(2)}, u32[]{:S(2)}) collective-permute-start(bf16[2,32,512]{2,1,0:T(8,128)(2,1)S(1)} %get-tuple-element.40), channel_id=1, source_target_pairs={{0,2},{2,0},{1,3},{3,1},{4,6},{6,4},{5,7},{7,5},{8,10},{10,8},{9,1... | collective-permute-start | bytes 196616 | tf_op jit(solution)/shard_map/ppermute | solution.py:367
  5.8 0.0 collective-permute-done.6
  5.8 0.7 %collective-permute-start.7 = (bf16[2,32,512]{2,1,0:T(8,128)(2,1)S(1)}, bf16[2,32,512]{2,1,0:T(8,128)(2,1)S(1)}, u32[]{:S(2)}, u32[]{:S(2)}) collective-permute-start(bf16[2,32,512]{2,1,0:T(8,128)(2,1)S(1)} %collective-permute-done.6), channel_id=1, source_target_pairs={{0,2},{2,0},{1,3},{3,1},{4,6},{6,4},{5,7},{7,5},{8,10},{10,8},{9,1... | collective-permute-start | bytes 196616 | tf_op jit(solution)/shard_map/ppermute | solution.py:367
  6.5 1.4 %collective-permute-start.1 = (bf16[2,32,512]{2,1,0:T(8,128)(2,1)S(1)}, bf16[2,32,512]{2,1,0:T(8,128)(2,1)S(1)}, u32[]{:S(2)}, u32[]{:S(2)}) collective-permute-start(bf16[2,32,512]{2,1,0:T(8,128)(2,1)S(1)} %get-tuple-element.36), channel_id=1, source_target_pairs={{0,2},{2,0},{1,3},{3,1},{4,6},{6,4},{5,7},{7,5},{8,10},{10,8},{9,1... | collective-permute-start | bytes 196616 | tf_op jit(solution)/shard_map/ppermute | solution.py:367
  7.8 0.0 collective-permute-done.2
  7.8 0.7 %collective-permute-start.3 = (bf16[2,32,512]{2,1,0:T(8,128)(2,1)S(1)}, bf16[2,32,512]{2,1,0:T(8,128)(2,1)S(1)}, u32[]{:S(2)}, u32[]{:S(2)}) collective-permute-start(bf16[2,32,512]{2,1,0:T(8,128)(2,1)S(1)} %collective-permute-done.2), channel_id=1, source_target_pairs={{0,2},{2,0},{1,3},{3,1},{4,6},{6,4},{5,7},{7,5},{8,10},{10,8},{9,1... | collective-permute-start | bytes 196616 | tf_op jit(solution)/shard_map/ppermute | solution.py:367
  8.5 0.7 %copy-done.3 = f32[16,16]{1,0:T(8,128)S(1)} copy-done((f32[16,16]{1,0:T(8,128)S(1)}, f32[16,16]{1,0:T(8,128)}, u32[]{:S(2)}) %copy-start.3) | copy-done | bytes 1048
  9.2 0.7 %copy-done.5 = s32[256]{0:T(256)S(1)} copy-done((s32[256]{0:T(256)S(1)}, s32[256]{0:T(256)}, u32[]{:S(2)}) %copy-start.5) | copy-done | bytes 1048
  9.9 0.2 station_tables.1
  10.1 0.7 %collective-permute-done.7.refs_3_ = bf16[2,32,512]{2,1,0:T(8,128)(2,1)S(1)} collective-permute-done((bf16[2,32,512]{2,1,0:T(8,128)(2,1)S(1)}, bf16[2,32,512]{2,1,0:T(8,128)(2,1)S(1)}, u32[]{:S(2)}, u32[]{:S(2)}) %collective-permute-start.7) | collective-permute-done | bytes 65568 | tf_op jit(solution)/shard_map/ppermute | solution.py:367
  10.7 0.0 collective-permute-done.refs_1_
  10.7 0.2 plane_sums_far.1
  10.9 2.7 %collective-permute-start.8 = (bf16[64,512]{1,0:T(8,128)(2,1)S(1)}, bf16[64,512]{1,0:T(8,128)(2,1)S(1)}, u32[]{:S(2)}, u32[]{:S(2)}) collective-permute-start(bf16[64,512]{1,0:T(8,128)(2,1)S(1)} %get-tuple-element.42), channel_id=1, source_target_pairs={{0,8},{4,12},{8,0},{12,4},{1,9},{5,13},{9,1},{13,5},{2,10},{6,14},... | collective-permute-start | bytes 196616 | tf_op jit(solution)/shard_map/ppermute | solution.py:367
  13.6 1.3 %collective-permute-start.9 = (bf16[64,512]{1,0:T(8,128)(2,1)S(1)}, bf16[64,512]{1,0:T(8,128)(2,1)S(1)}, u32[]{:S(2)}, u32[]{:S(2)}) collective-permute-start(bf16[64,512]{1,0:T(8,128)(2,1)S(1)} %get-tuple-element.43), channel_id=1, source_target_pairs={{0,12},{4,8},{8,4},{12,0},{1,13},{5,9},{9,5},{13,1},{2,14},{6,10},... | collective-permute-start | bytes 196616 | tf_op jit(solution)/shard_map/ppermute | solution.py:367
  14.9 0.2 plane_sums_near.1
  15.1 0.3 collective-permute-start.4
  15.4 0.9 %copy-done.1 = bf16[4,2,256,32]{2,3,1,0:T(8,128)(2,1)S(1)} copy-done((bf16[4,2,256,32]{2,3,1,0:T(8,128)(2,1)S(1)}, bf16[4,2,256,32]{2,3,1,0:T(8,128)(2,1)}, u32[]{:S(2)}) %copy-start.1) | copy-done | bytes 131096
  16.3 0.7 %copy-done.4 = s32[1024]{0:T(1024)S(1)} copy-done((s32[1024]{0:T(1024)S(1)}, s32[1024]{0:T(1024)}, u32[]{:S(2)}) %copy-start.4) | copy-done | bytes 4120
  17.0 0.7 %copy-done.6 = s32[32,1]{0,1:T(1,128)S(1)} copy-done((s32[32,1]{0,1:T(1,128)S(1)}, s32[32,1]{0,1:T(1,128)}, u32[]{:S(2)}) %copy-start.6) | copy-done | bytes 152
  17.7 1.7 %weight_shares.1 = (f32[32,64]{1,0:T(8,128)S(1)}, f32[32,64]{1,0:T(8,128)S(1)}, bf16[32,512]{1,0:T(8,128)(2,1)S(1)}, bf16[32,512]{1,0:T(8,128)(2,1)S(1)}, bf16[3...) custom-call(bf16[4,2,32,256]{3,2,1,0:T(8,128)(2,1)S(1)} %bitcast.14, s32[1,32]{1,0:T(1,128)S(1)} %bitcast.18, ...), custom_call_target="tpu_custom_call" | custom-call | bytes 8388608 | tf_op jit(solution)/shard_map/weight_shares/pallas_call | solution.py:435
  19.3 0.0 collective-permute-done.8.refs_2_
  19.4 0.4 collective-permute-done.9.refs_3_
  19.7 0.4 collective-permute-done.4.refs_1_
  20.1 0.6 %station_filter.1 = (bf16[64,512]{1,0:T(8,128)(2,1)S(1)}, bf16[96,512]{1,0:T(8,128)(2,1)S(1)}, bf16[96,512]{1,0:T(8,128)(2,1)S(1)}, bf16[96,512]{1,0:T(8,128)(2,1)S(1)}) custom-call(f32[16,512]{1,0:T(8,128)S(1)} %get-tuple-element.32.taps_ref, f32[64,512]{1,0:T(8,128)S(1)} %get-tuple-element.38.refs_0_, bf16[64,512]{1,0:T(8,128)(2,1)S(1)} %collective-permute-done.4.refs_1_, ...), custom_call_target="tpu_custom_call" | custom-call | tf_op jit(solution)/shard_map/station_filter/pallas_call | solution.py:450
  20.8 1.1 %collective-permute-start.10 = (bf16[96,512]{1,0:T(8,128)(2,1)S(1)}, bf16[96,512]{1,0:T(8,128)(2,1)S(1)}, u32[]{:S(2)}, u32[]{:S(2)}) collective-permute-start(bf16[96,512]{1,0:T(8,128)(2,1)S(1)} %get-tuple-element.48), channel_id=1, source_target_pairs={{0,4},{4,0},{8,12},{12,8},{1,5},{5,1},{9,13},{13,9},{2,6},{6,2},{1... | collective-permute-start | bytes 294920 | tf_op jit(solution)/shard_map/ppermute | solution.py:367
  21.9 1.7 %collective-permute-start.11 = (bf16[96,512]{1,0:T(8,128)(2,1)S(1)}, bf16[96,512]{1,0:T(8,128)(2,1)S(1)}, u32[]{:S(2)}, u32[]{:S(2)}) collective-permute-start(bf16[96,512]{1,0:T(8,128)(2,1)S(1)} %get-tuple-element.49), channel_id=1, source_target_pairs={{0,8},{4,12},{8,0},{12,4},{1,9},{5,13},{9,1},{13,5},{2,10},{6,14},... | collective-permute-start | bytes 294920 | tf_op jit(solution)/shard_map/ppermute | solution.py:367
  23.5 1.7 %collective-permute-start.12 = (bf16[96,512]{1,0:T(8,128)(2,1)S(1)}, bf16[96,512]{1,0:T(8,128)(2,1)S(1)}, u32[]{:S(2)}, u32[]{:S(2)}) collective-permute-start(bf16[96,512]{1,0:T(8,128)(2,1)S(1)} %get-tuple-element.50), channel_id=1, source_target_pairs={{0,12},{4,8},{8,4},{12,0},{1,13},{5,9},{9,5},{13,1},{2,14},{6,10},... | collective-permute-start | bytes 294920 | tf_op jit(solution)/shard_map/ppermute | solution.py:367
  25.2 0.2 collective-permute-done.10.refs_1_
  25.4 1.6 %collective-permute-start.13 = (bf16[64,512]{1,0:T(8,128)(2,1)S(1)}, bf16[64,512]{1,0:T(8,128)(2,1)S(1)}, u32[]{:S(2)}, u32[]{:S(2)}) collective-permute-start(bf16[64,512]{1,0:T(8,128)(2,1)S(1)} %get-tuple-element.63), channel_id=1, source_target_pairs={{0,2},{2,0},{1,3},{3,1},{4,6},{6,4},{5,7},{7,5},{8,10},{10,8},{9,1... | collective-permute-start | bytes 196616 | tf_op jit(solution)/shard_map/ppermute | solution.py:367
  27.1 0.7 %copy-done.2 = f32[16,16]{1,0:T(8,128)S(1)} copy-done((f32[16,16]{1,0:T(8,128)S(1)}, f32[16,16]{1,0:T(8,128)}, u32[]{:S(2)}) %copy-start.2) | copy-done | bytes 1048
  27.8 1.7 %synthesis_bands.1.refs_7_ = bf16[16,768,256]{2,1,0:T(8,128)(2,1)S(1)} custom-call(f32[16,16]{1,0:T(8,128)S(1)} %copy-done.2), custom_call_target="tpu_custom_call" | custom-call | bytes 16777216 | tf_op jit(solution)/shard_map/synthesis_bands/pallas_call | solution.py:463
  29.5 0.5 %collective-permute-start.15 = (bf16[64,512]{1,0:T(8,128)(2,1)S(1)}, bf16[64,512]{1,0:T(8,128)(2,1)S(1)}, u32[]{:S(2)}, u32[]{:S(2)}) collective-permute-start(bf16[64,512]{1,0:T(8,128)(2,1)S(1)} %get-tuple-element.47), channel_id=1, source_target_pairs={{0,2},{2,0},{1,3},{3,1},{4,6},{6,4},{5,7},{7,5},{8,10},{10,8},{9,1... | collective-permute-start | bytes 196616 | tf_op jit(solution)/shard_map/ppermute | solution.py:367
  30.0 1.0 %collective-permute-done.11.refs_2_ = bf16[96,512]{1,0:T(8,128)(2,1)S(1)} collective-permute-done((bf16[96,512]{1,0:T(8,128)(2,1)S(1)}, bf16[96,512]{1,0:T(8,128)(2,1)S(1)}, u32[]{:S(2)}, u32[]{:S(2)}) %collective-permute-start.11) | collective-permute-done | bytes 98336 | tf_op jit(solution)/shard_map/ppermute | solution.py:367
  31.1 2.0 %collective-permute-start.16 = (bf16[2,64,512]{2,1,0:T(8,128)(2,1)S(1)}, bf16[2,64,512]{2,1,0:T(8,128)(2,1)S(1)}, u32[]{:S(2)}, u32[]{:S(2)}) collective-permute-start(bf16[2,64,512]{2,1,0:T(8,128)(2,1)S(1)} %pad_maximum_fusion.2), channel_id=1, source_target_pairs={{0,2},{2,0},{1,3},{3,1},{4,6},{6,4},{5,7},{7,5},{8,10},{10,8},{9,1... | collective-permute-start | bytes 393224 | tf_op jit(solution)/shard_map/ppermute | solution.py:367
  33.1 0.1 collective-permute-start.14
  33.2 0.6 %collective-permute-done.15 = bf16[64,512]{1,0:T(8,128)(2,1)S(1)} collective-permute-done((bf16[64,512]{1,0:T(8,128)(2,1)S(1)}, bf16[64,512]{1,0:T(8,128)(2,1)S(1)}, u32[]{:S(2)}, u32[]{:S(2)}) %collective-permute-start.15) | collective-permute-done | bytes 65568 | tf_op jit(solution)/shard_map/ppermute | solution.py:367
  33.8 0.1 collective-permute-start.17
  33.9 0.8 %weight_matrix.1.m_ref.refs_6_ = bf16[16,128,1024]{2,1,0:T(8,128)(2,1)S(1)} custom-call(f32[32,64]{1,0:T(8,128)S(1)} %get-tuple-element.54.chosen_ref, f32[32,64]{1,0:T(8,128)S(1)} %get-tuple-element.55.scale_ref, bf16[32,512]{1,0:T(8,128)(2,1)S(1)} %get-tuple-element.56.refs_0_, bf16[96,512]{1,0:T(8,128)(2,1)S(1)} %collective-permute-done.10.refs_1_, ...), custom_call_target="tpu_custom_call" | custom-call | bytes 8388608 | tf_op jit(solution)/shard_map/weight_matrix/pallas_call | solution.py:475
  34.7 0.7 %own_beams.1.refs_3_ = f32[16,128,512]{2,1,0:T(8,128)S(1)} custom-call(bf16[16,128,1024]{2,1,0:T(8,128)(2,1)S(1)} %weight_matrix.1.m_ref.refs_6_, bf16[4,64,512]{2,1,0:T(8,128)(2,1)S(1)} %pad_maximum_fusion.refs_0_), custom_call_target="tpu_custom_call" | custom-call | bytes 8388608 | tf_op jit(solution)/shard_map/own_beams/pallas_call | solution.py:487
  35.5 0.7 %collective-permute-done.16.refs_2_.refs_3_ = bf16[2,64,512]{2,1,0:T(8,128)(2,1)S(1)} collective-permute-done((bf16[2,64,512]{2,1,0:T(8,128)(2,1)S(1)}, bf16[2,64,512]{2,1,0:T(8,128)(2,1)S(1)}, u32[]{:S(2)}, u32[]{:S(2)}) %collective-permute-start.16) | collective-permute-done | bytes 131104 | tf_op jit(solution)/shard_map/ppermute | solution.py:367
  36.2 1.3 %near_beams.1.refs_8_ = f32[16,128,512]{2,1,0:T(8,128)S(1)} custom-call(bf16[16,128,1024]{2,1,0:T(8,128)(2,1)S(1)} %weight_matrix.1.m_ref.refs_6_, bf16[4,64,512]{2,1,0:T(8,128)(2,1)S(1)} %collective-permute-done.14.refs_0_.refs_1_, bf16[2,64,512]{2,1,0:T(8,128)(2,1)S(1)} %pad_maximum_fusion.1.refs_1_.refs_2_, ...), custom_call_target="tpu_custom_call" | custom-call | bytes 8388608 | tf_op jit(solution)/shard_map/near_beams/pallas_call | solution.py:487
  37.5 0.0 collective-permute-done.18.refs_5_
  37.5 4.0 %beams_and_series.1 = (f32[128,2,8,512]{3,2,1,0:T(8,128)}, f32[4,2,8,32]{3,2,1,0:T(8,128)}) custom-call(bf16[4,64,512]{2,1,0:T(8,128)(2,1)S(1)} %pad_maximum_fusion.refs_0_, bf16[4,64,512]{2,1,0:T(8,128)(2,1)S(1)} %collective-permute-done.14.refs_0_.refs_1_, bf16[2,64,512]{2,1,0:T(8,128)(2,1)S(1)} %pad_maximum_fusion.1.refs_1_.refs_2_, ...), custom_call_target="tpu_custom_call" | custom-call | tf_op jit(solution)/shard_map/beams_and_series/pallas_call | solution.py:344
  (20 shorter events, 0.1 us)
Async XLA Ops:
  0.6 1.0 %copy-start = (bf16[16,2,16,512]{3,2,1,0:T(8,128)(2,1)S(1)}, bf16[16,2,16,512]{3,2,1,0:T(8,128)(2,1)}, u32[]{:S(2)}) copy-start(bf16[16,2,16,512]{3,2,1,0:T(8,128)(2,1)} %x_ref.1) | copy-start | bytes 1572868
  2.2 3.6 %collective-permute-start.6 = (bf16[2,32,512]{2,1,0:T(8,128)(2,1)S(1)}, bf16[2,32,512]{2,1,0:T(8,128)(2,1)S(1)}, u32[]{:S(2)}, u32[]{:S(2)}) collective-permute-start(bf16[2,32,512]{2,1,0:T(8,128)(2,1)S(1)} %get-tuple-element.41), channel_id=1, source_target_pairs={{0,1},{1,0},{2,3},{3,2},{4,5},{5,4},{6,7},{7,6},{8,9},{9,8},{10,11... | collective-permute-start | bytes 196616 | tf_op jit(solution)/shard_map/ppermute | solution.py:367
  2.7 8.0 %collective-permute-start = (bf16[4,32,512]{2,1,0:T(8,128)(2,1)S(1)}, bf16[4,32,512]{2,1,0:T(8,128)(2,1)S(1)}, u32[]{:S(2)}, u32[]{:S(2)}) collective-permute-start(bf16[4,32,512]{2,1,0:T(8,128)(2,1)S(1)} %get-tuple-element.35), channel_id=1, source_target_pairs={{0,1},{1,0},{2,3},{3,2},{4,5},{5,4},{6,7},{7,6},{8,9},{9,8},{10,11... | collective-permute-start | bytes 393224 | tf_op jit(solution)/shard_map/ppermute | solution.py:367
  2.8 5.0 %collective-permute-start.2 = (bf16[2,32,512]{2,1,0:T(8,128)(2,1)S(1)}, bf16[2,32,512]{2,1,0:T(8,128)(2,1)S(1)}, u32[]{:S(2)}, u32[]{:S(2)}) collective-permute-start(bf16[2,32,512]{2,1,0:T(8,128)(2,1)S(1)} %get-tuple-element.37), channel_id=1, source_target_pairs={{0,1},{1,0},{2,3},{3,2},{4,5},{5,4},{6,7},{7,6},{8,9},{9,8},{10,11... | collective-permute-start | bytes 196616 | tf_op jit(solution)/shard_map/ppermute | solution.py:367
  3.2 6.8 %collective-permute-start.5 = (bf16[2,32,512]{2,1,0:T(8,128)(2,1)S(1)}, bf16[2,32,512]{2,1,0:T(8,128)(2,1)S(1)}, u32[]{:S(2)}, u32[]{:S(2)}) collective-permute-start(bf16[2,32,512]{2,1,0:T(8,128)(2,1)S(1)} %get-tuple-element.40), channel_id=1, source_target_pairs={{0,2},{2,0},{1,3},{3,1},{4,6},{6,4},{5,7},{7,5},{8,10},{10,8},{9,1... | collective-permute-start | bytes 196616 | tf_op jit(solution)/shard_map/ppermute | solution.py:367
  5.8 4.9 %collective-permute-start.7 = (bf16[2,32,512]{2,1,0:T(8,128)(2,1)S(1)}, bf16[2,32,512]{2,1,0:T(8,128)(2,1)S(1)}, u32[]{:S(2)}, u32[]{:S(2)}) collective-permute-start(bf16[2,32,512]{2,1,0:T(8,128)(2,1)S(1)} %collective-permute-done.6), channel_id=1, source_target_pairs={{0,2},{2,0},{1,3},{3,1},{4,6},{6,4},{5,7},{7,5},{8,10},{10,8},{9,1... | collective-permute-start | bytes 196616 | tf_op jit(solution)/shard_map/ppermute | solution.py:367
  6.5 8.5 %collective-permute-start.1 = (bf16[2,32,512]{2,1,0:T(8,128)(2,1)S(1)}, bf16[2,32,512]{2,1,0:T(8,128)(2,1)S(1)}, u32[]{:S(2)}, u32[]{:S(2)}) collective-permute-start(bf16[2,32,512]{2,1,0:T(8,128)(2,1)S(1)} %get-tuple-element.36), channel_id=1, source_target_pairs={{0,2},{2,0},{1,3},{3,1},{4,6},{6,4},{5,7},{7,5},{8,10},{10,8},{9,1... | collective-permute-start | bytes 196616 | tf_op jit(solution)/shard_map/ppermute | solution.py:367
  7.8 7.1 %collective-permute-start.3 = (bf16[2,32,512]{2,1,0:T(8,128)(2,1)S(1)}, bf16[2,32,512]{2,1,0:T(8,128)(2,1)S(1)}, u32[]{:S(2)}, u32[]{:S(2)}) collective-permute-start(bf16[2,32,512]{2,1,0:T(8,128)(2,1)S(1)} %collective-permute-done.2), channel_id=1, source_target_pairs={{0,2},{2,0},{1,3},{3,1},{4,6},{6,4},{5,7},{7,5},{8,10},{10,8},{9,1... | collective-permute-start | bytes 196616 | tf_op jit(solution)/shard_map/ppermute | solution.py:367
  8.5 0.7 %copy-start.3 = (f32[16,16]{1,0:T(8,128)S(1)}, f32[16,16]{1,0:T(8,128)}, u32[]{:S(2)}) copy-start(f32[16,16]{1,0:T(8,128)} %taps_ref.2) | copy-start | bytes 3076
  9.2 0.7 %copy-start.5 = (s32[256]{0:T(256)S(1)}, s32[256]{0:T(256)}, u32[]{:S(2)}) copy-start(s32[256]{0:T(256)} %param.10) | copy-start | bytes 3076
  10.9 8.4 %collective-permute-start.8 = (bf16[64,512]{1,0:T(8,128)(2,1)S(1)}, bf16[64,512]{1,0:T(8,128)(2,1)S(1)}, u32[]{:S(2)}, u32[]{:S(2)}) collective-permute-start(bf16[64,512]{1,0:T(8,128)(2,1)S(1)} %get-tuple-element.42), channel_id=1, source_target_pairs={{0,8},{4,12},{8,0},{12,4},{1,9},{5,13},{9,1},{13,5},{2,10},{6,14},... | collective-permute-start | bytes 196616 | tf_op jit(solution)/shard_map/ppermute | solution.py:367
  13.6 6.2 %collective-permute-start.9 = (bf16[64,512]{1,0:T(8,128)(2,1)S(1)}, bf16[64,512]{1,0:T(8,128)(2,1)S(1)}, u32[]{:S(2)}, u32[]{:S(2)}) collective-permute-start(bf16[64,512]{1,0:T(8,128)(2,1)S(1)} %get-tuple-element.43), channel_id=1, source_target_pairs={{0,12},{4,8},{8,4},{12,0},{1,13},{5,9},{9,5},{13,1},{2,14},{6,10},... | collective-permute-start | bytes 196616 | tf_op jit(solution)/shard_map/ppermute | solution.py:367
  15.1 5.0 %collective-permute-start.4 = (bf16[64,512]{1,0:T(8,128)(2,1)S(1)}, bf16[64,512]{1,0:T(8,128)(2,1)S(1)}, u32[]{:S(2)}, u32[]{:S(2)}) collective-permute-start(bf16[64,512]{1,0:T(8,128)(2,1)S(1)} %get-tuple-element.39), channel_id=1, source_target_pairs={{0,4},{4,0},{8,12},{12,8},{1,5},{5,1},{9,13},{13,9},{2,6},{6,2},{1... | collective-permute-start | bytes 196616 | tf_op jit(solution)/shard_map/ppermute | solution.py:367
  15.4 0.9 %copy-start.1 = (bf16[4,2,256,32]{2,3,1,0:T(8,128)(2,1)S(1)}, bf16[4,2,256,32]{2,3,1,0:T(8,128)(2,1)}, u32[]{:S(2)}) copy-start(bf16[4,2,256,32]{2,3,1,0:T(8,128)(2,1)} %param.13) | copy-start | bytes 393220
  16.3 0.7 %copy-start.4 = (s32[1024]{0:T(1024)S(1)}, s32[1024]{0:T(1024)}, u32[]{:S(2)}) copy-start(s32[1024]{0:T(1024)} %param.12) | copy-start | bytes 12292
  17.0 0.7 %copy-start.6 = (s32[32,1]{0,1:T(1,128)S(1)}, s32[32,1]{0,1:T(1,128)}, u32[]{:S(2)}) copy-start(s32[32,1]{0,1:T(1,128)} %param.11) | copy-start | bytes 388
  20.8 4.7 %collective-permute-start.10 = (bf16[96,512]{1,0:T(8,128)(2,1)S(1)}, bf16[96,512]{1,0:T(8,128)(2,1)S(1)}, u32[]{:S(2)}, u32[]{:S(2)}) collective-permute-start(bf16[96,512]{1,0:T(8,128)(2,1)S(1)} %get-tuple-element.48), channel_id=1, source_target_pairs={{0,4},{4,0},{8,12},{12,8},{1,5},{5,1},{9,13},{13,9},{2,6},{6,2},{1... | collective-permute-start | bytes 294920 | tf_op jit(solution)/shard_map/ppermute | solution.py:367
  21.9 9.2 %collective-permute-start.11 = (bf16[96,512]{1,0:T(8,128)(2,1)S(1)}, bf16[96,512]{1,0:T(8,128)(2,1)S(1)}, u32[]{:S(2)}, u32[]{:S(2)}) collective-permute-start(bf16[96,512]{1,0:T(8,128)(2,1)S(1)} %get-tuple-element.49), channel_id=1, source_target_pairs={{0,8},{4,12},{8,0},{12,4},{1,9},{5,13},{9,1},{13,5},{2,10},{6,14},... | collective-permute-start | bytes 294920 | tf_op jit(solution)/shard_map/ppermute | solution.py:367
  23.5 7.5 %collective-permute-start.12 = (bf16[96,512]{1,0:T(8,128)(2,1)S(1)}, bf16[96,512]{1,0:T(8,128)(2,1)S(1)}, u32[]{:S(2)}, u32[]{:S(2)}) collective-permute-start(bf16[96,512]{1,0:T(8,128)(2,1)S(1)} %get-tuple-element.50), channel_id=1, source_target_pairs={{0,12},{4,8},{8,4},{12,0},{1,13},{5,9},{9,5},{13,1},{2,14},{6,10},... | collective-permute-start | bytes 294920 | tf_op jit(solution)/shard_map/ppermute | solution.py:367
  25.4 5.6 %collective-permute-start.13 = (bf16[64,512]{1,0:T(8,128)(2,1)S(1)}, bf16[64,512]{1,0:T(8,128)(2,1)S(1)}, u32[]{:S(2)}, u32[]{:S(2)}) collective-permute-start(bf16[64,512]{1,0:T(8,128)(2,1)S(1)} %get-tuple-element.63), channel_id=1, source_target_pairs={{0,2},{2,0},{1,3},{3,1},{4,6},{6,4},{5,7},{7,5},{8,10},{10,8},{9,1... | collective-permute-start | bytes 196616 | tf_op jit(solution)/shard_map/ppermute | solution.py:367
  27.1 0.7 %copy-start.2 = (f32[16,16]{1,0:T(8,128)S(1)}, f32[16,16]{1,0:T(8,128)}, u32[]{:S(2)}) copy-start(f32[16,16]{1,0:T(8,128)} %taps_ref.3) | copy-start | bytes 3076
  29.5 4.3 %collective-permute-start.15 = (bf16[64,512]{1,0:T(8,128)(2,1)S(1)}, bf16[64,512]{1,0:T(8,128)(2,1)S(1)}, u32[]{:S(2)}, u32[]{:S(2)}) collective-permute-start(bf16[64,512]{1,0:T(8,128)(2,1)S(1)} %get-tuple-element.47), channel_id=1, source_target_pairs={{0,2},{2,0},{1,3},{3,1},{4,6},{6,4},{5,7},{7,5},{8,10},{10,8},{9,1... | collective-permute-start | bytes 196616 | tf_op jit(solution)/shard_map/ppermute | solution.py:367
  31.1 5.0 %collective-permute-start.16 = (bf16[2,64,512]{2,1,0:T(8,128)(2,1)S(1)}, bf16[2,64,512]{2,1,0:T(8,128)(2,1)S(1)}, u32[]{:S(2)}, u32[]{:S(2)}) collective-permute-start(bf16[2,64,512]{2,1,0:T(8,128)(2,1)S(1)} %pad_maximum_fusion.2), channel_id=1, source_target_pairs={{0,2},{2,0},{1,3},{3,1},{4,6},{6,4},{5,7},{7,5},{8,10},{10,8},{9,1... | collective-permute-start | bytes 393224 | tf_op jit(solution)/shard_map/ppermute | solution.py:367
  33.1 3.0 %collective-permute-start.14 = (bf16[4,64,512]{2,1,0:T(8,128)(2,1)S(1)}, bf16[4,64,512]{2,1,0:T(8,128)(2,1)S(1)}, u32[]{:S(2)}, u32[]{:S(2)}) collective-permute-start(bf16[4,64,512]{2,1,0:T(8,128)(2,1)S(1)} %pad_maximum_fusion.refs_0_), channel_id=1, source_target_pairs={{0,1},{1,0},{2,3},{3,2},{4,5},{5,4},{6,7},{7,6},{8,9},{9,8},{10,11... | collective-permute-start | bytes 786440 | tf_op jit(solution)/shard_map/ppermute | solution.py:367
  33.8 3.7 %collective-permute-start.17 = (bf16[2,64,512]{2,1,0:T(8,128)(2,1)S(1)}, bf16[2,64,512]{2,1,0:T(8,128)(2,1)S(1)}, u32[]{:S(2)}, u32[]{:S(2)}) collective-permute-start(bf16[2,64,512]{2,1,0:T(8,128)(2,1)S(1)} %pad_maximum_fusion.1.refs_1_.refs_2_), channel_id=1, source_target_pairs={{0,1},{1,0},{2,3},{3,2},{4,5},{5,4},{6,7},{7,6},{8,9},{9,8},{10,11... | collective-permute-start | bytes 393224 | tf_op jit(solution)/shard_map/ppermute | solution.py:367
  36.2 1.3 %collective-permute-start.18 = (bf16[2,64,512]{2,1,0:T(8,128)(2,1)S(1)}, bf16[2,64,512]{2,1,0:T(8,128)(2,1)S(1)}, u32[]{:S(2)}, u32[]{:S(2)}) collective-permute-start(bf16[2,64,512]{2,1,0:T(8,128)(2,1)S(1)} %collective-permute-done.16.refs_2_.refs_3_), channel_id=1, source_target_pairs={{0,1},{1,0},{2,3},{3,2},{4,5},{5,4},{6,7},{7,6},{8,9},{9,8},{10,11... | collective-permute-start | bytes 393224 | tf_op jit(solution)/shard_map/ppermute | solution.py:367

commit v9 on v8

--- a/solution.py
+++ b/solution.py
@@ -276,24 +276,24 @@
         found = lane_products(axes, FLIPS[3:], m_ref, lanes_ref, first, 4)
         found = found.reshape((4,) + sum_ref.shape[1:]) + sum_ref[first : first + 4]
         inverse_ref[first : first + 4] = found.astype(jnp.bfloat16)
-    for lane in range(chan):
-        for n in range(frames // tile):
-            taken = [inverse_ref[lane, :, n * tile : (n + 1) * tile]] * 2
-            first = 2 * HALO
-            if n > 0:
-                taken = [inverse_ref[lane, :, n * tile - HALO : n * tile]] * 2 + taken
-                first = 0
-            value = jnp.dot(
-                jnp.concatenate(taken, axis=1), t_ref[lane, first:], preferred_element_type=jnp.float32
-            )
-            for part in range(tile // 128):
-                slot = n * (tile // 128) + part
-                out_ref[lane, slot] = value[:, part * 128 : (part + 1) * 128]
-                pltpu.make_async_copy(
-                    out_ref.at[lane, slot],
-                    series_ref.at[:, lane // 8, lane % 8, pl.ds(slot * 128, 128)],
-                    store_sem,
-                ).start()
+        for lane in range(first, first + 4):
+            for n in range(frames // tile):
+                taken = [inverse_ref[lane, :, n * tile : (n + 1) * tile]] * 2
+                start = 2 * HALO
+                if n > 0:
+                    taken = [inverse_ref[lane, :, n * tile - HALO : n * tile]] * 2 + taken
+                    start = 0
+                value = jnp.dot(
+                    jnp.concatenate(taken, axis=1), t_ref[lane, start:], preferred_element_type=jnp.float32
+                )
+                for part in range(tile // 128):
+                    slot = n * (tile // 128) + part
+                    out_ref[lane, slot] = value[:, part * 128 : (part + 1) * 128]
+                    pltpu.make_async_copy(
+                        out_ref.at[lane, slot],
+                        series_ref.at[:, lane // 8, lane % 8, pl.ds(slot * 128, 128)],
+                        store_sem,
+                    ).start()
     gather_lanes(axes, x_refs[:4], PLACES[:4], lanes_ref)
     inner = []
     for b in range(4):

time: 41.8 us -> 41.8 us (level)
  no operation moved by 1% of the time
where the time goes in v9:
time: 41.8 us; the launch traced here: 41.5 us
  starting transfers between devices  19.3 us (46%)
  Pallas kernels  11.9 us (28%)
  local copies, waits for them, and re-layouts  5.37 us (13%)
  waiting for transfers between devices  4.07 us (10%)
  between operations  0.78 us (2%)
    ppermute x19, starting transfers between devices, swap(): return lax.ppermute(x, axis, [(i, i ^ mask) for i in range(size)])  19.3 us
    unnamed x14, local copies, waits for them, and re-layouts  5.35 us
    ppermute x19, waiting for transfers between devices, swap(): return lax.ppermute(x, axis, [(i, i ^ mask) for i in range(size)])  4.07 us
    pallas_call x1, Pallas kernels, call_beams(): pl.pallas_call(lambda *refs: beam_kernel(axes, refs[:len(pieces)], *refs[...  3.95 us
    pallas_call x2, Pallas kernels, add_part(): pl.pallas_call(functools.partial(part_kernel, axes, places), out_shape=ja...  2.06 us
    pallas_call x1, Pallas kernels, fast_body(): pl.pallas_call(band_kernel, out_shape=jax.ShapeDtypeStruct((chan, 2 * (ti...  1.72 us
    pallas_call x1, Pallas kernels, fast_body(): pl.pallas_call(functools.partial(pack_kernel, axes), out_shape=[table] *...  1.69 us
  transfers between devices with their start and end apart: 19, of which 7 were waited for; matrix products, arithmetic and copies ran while one was open for 0% of the time, Pallas kernels for 16%

profile of v9, /device:TPU:0, one launch (start us, length us, event | category | flops | bytes accessed | tf_op | source)
XLA Modules:
  0.0 41.5 jit_solution(7531436582818330392)
XLA Ops:
  0.6 1.0 %copy-done = bf16[16,2,16,512]{3,2,1,0:T(8,128)(2,1)S(1)} copy-done((bf16[16,2,16,512]{3,2,1,0:T(8,128)(2,1)S(1)}, bf16[16,2,16,512]{3,2,1,0:T(8,128)(2,1)}, u32[]{:S(2)}) %copy-start) | copy-done | bytes 524312
  1.7 0.5 %lane_spread.1 = (bf16[4,32,512]{2,1,0:T(8,128)(2,1)S(1)}, bf16[2,32,512]{2,1,0:T(8,128)(2,1)S(1)}, bf16[2,32,512]{2,1,0:T(8,128)(2,1)S(1)}, bf16[4,32,512]{2,1,...) custom-call(bf16[16,2,16,512]{3,2,1,0:T(8,128)(2,1)S(1)} %copy-done), custom_call_target="tpu_custom_call" | custom-call | tf_op jit(solution)/shard_map/lane_spread/pallas_call | solution.py:386
  2.2 0.5 %collective-permute-start.6 = (bf16[2,32,512]{2,1,0:T(8,128)(2,1)S(1)}, bf16[2,32,512]{2,1,0:T(8,128)(2,1)S(1)}, u32[]{:S(2)}, u32[]{:S(2)}) collective-permute-start(bf16[2,32,512]{2,1,0:T(8,128)(2,1)S(1)} %get-tuple-element.41), channel_id=1, source_target_pairs={{0,1},{1,0},{2,3},{3,2},{4,5},{5,4},{6,7},{7,6},{8,9},{9,8},{10,11... | collective-permute-start | bytes 196616 | tf_op jit(solution)/shard_map/ppermute | solution.py:367
  2.7 0.1 collective-permute-start
  2.8 0.4 %collective-permute-start.2 = (bf16[2,32,512]{2,1,0:T(8,128)(2,1)S(1)}, bf16[2,32,512]{2,1,0:T(8,128)(2,1)S(1)}, u32[]{:S(2)}, u32[]{:S(2)}) collective-permute-start(bf16[2,32,512]{2,1,0:T(8,128)(2,1)S(1)} %get-tuple-element.37), channel_id=1, source_target_pairs={{0,1},{1,0},{2,3},{3,2},{4,5},{5,4},{6,7},{7,6},{8,9},{9,8},{10,11... | collective-permute-start | bytes 196616 | tf_op jit(solution)/shard_map/ppermute | solution.py:367
  3.2 2.6 %collective-permute-start.5 = (bf16[2,32,512]{2,1,0:T(8,128)(2,1)S(1)}, bf16[2,32,512]{2,1,0:T(8,128)(2,1)S(1)}, u32[]{:S(2)}, u32[]{:S(2)}) collective-permute-start(bf16[2,32,512]{2,1,0:T(8,128)(2,1)S(1)} %get-tuple-element.40), channel_id=1, source_target_pairs={{0,2},{2,0},{1,3},{3,1},{4,6},{6,4},{5,7},{7,5},{8,10},{10,8},{9,1... | collective-permute-start | bytes 196616 | tf_op jit(solution)/shard_map/ppermute | solution.py:367
  5.8 0.0 collective-permute-done.6
  5.8 0.7 %collective-permute-start.7 = (bf16[2,32,512]{2,1,0:T(8,128)(2,1)S(1)}, bf16[2,32,512]{2,1,0:T(8,128)(2,1)S(1)}, u32[]{:S(2)}, u32[]{:S(2)}) collective-permute-start(bf16[2,32,512]{2,1,0:T(8,128)(2,1)S(1)} %collective-permute-done.6), channel_id=1, source_target_pairs={{0,2},{2,0},{1,3},{3,1},{4,6},{6,4},{5,7},{7,5},{8,10},{10,8},{9,1... | collective-permute-start | bytes 196616 | tf_op jit(solution)/shard_map/ppermute | solution.py:367
  6.5 1.4 %collective-permute-start.1 = (bf16[2,32,512]{2,1,0:T(8,128)(2,1)S(1)}, bf16[2,32,512]{2,1,0:T(8,128)(2,1)S(1)}, u32[]{:S(2)}, u32[]{:S(2)}) collective-permute-start(bf16[2,32,512]{2,1,0:T(8,128)(2,1)S(1)} %get-tuple-element.36), channel_id=1, source_target_pairs={{0,2},{2,0},{1,3},{3,1},{4,6},{6,4},{5,7},{7,5},{8,10},{10,8},{9,1... | collective-permute-start | bytes 196616 | tf_op jit(solution)/shard_map/ppermute | solution.py:367
  7.8 0.7 %collective-permute-start.3 = (bf16[2,32,512]{2,1,0:T(8,128)(2,1)S(1)}, bf16[2,32,512]{2,1,0:T(8,128)(2,1)S(1)}, u32[]{:S(2)}, u32[]{:S(2)}) collective-permute-start(bf16[2,32,512]{2,1,0:T(8,128)(2,1)S(1)} %collective-permute-done.2), channel_id=1, source_target_pairs={{0,2},{2,0},{1,3},{3,1},{4,6},{6,4},{5,7},{7,5},{8,10},{10,8},{9,1... | collective-permute-start | bytes 196616 | tf_op jit(solution)/shard_map/ppermute | solution.py:367
  8.5 0.7 %copy-done.3 = f32[16,16]{1,0:T(8,128)S(1)} copy-done((f32[16,16]{1,0:T(8,128)S(1)}, f32[16,16]{1,0:T(8,128)}, u32[]{:S(2)}) %copy-start.3) | copy-done | bytes 1048
  9.2 0.7 %copy-done.5 = s32[256]{0:T(256)S(1)} copy-done((s32[256]{0:T(256)S(1)}, s32[256]{0:T(256)}, u32[]{:S(2)}) %copy-start.5) | copy-done | bytes 1048
  9.9 0.2 station_tables.1
  10.0 0.0 collective-permute-done.5.refs_2_
  10.1 0.7 %collective-permute-done.7.refs_3_ = bf16[2,32,512]{2,1,0:T(8,128)(2,1)S(1)} collective-permute-done((bf16[2,32,512]{2,1,0:T(8,128)(2,1)S(1)}, bf16[2,32,512]{2,1,0:T(8,128)(2,1)S(1)}, u32[]{:S(2)}, u32[]{:S(2)}) %collective-permute-start.7) | collective-permute-done | bytes 65568 | tf_op jit(solution)/shard_map/ppermute | solution.py:367
  10.7 0.0 collective-permute-done.refs_1_
  10.7 0.2 plane_sums_far.1
  10.9 2.7 %collective-permute-start.8 = (bf16[64,512]{1,0:T(8,128)(2,1)S(1)}, bf16[64,512]{1,0:T(8,128)(2,1)S(1)}, u32[]{:S(2)}, u32[]{:S(2)}) collective-permute-start(bf16[64,512]{1,0:T(8,128)(2,1)S(1)} %get-tuple-element.42), channel_id=1, source_target_pairs={{0,8},{4,12},{8,0},{12,4},{1,9},{5,13},{9,1},{13,5},{2,10},{6,14},... | collective-permute-start | bytes 196616 | tf_op jit(solution)/shard_map/ppermute | solution.py:367
  13.6 1.3 %collective-permute-start.9 = (bf16[64,512]{1,0:T(8,128)(2,1)S(1)}, bf16[64,512]{1,0:T(8,128)(2,1)S(1)}, u32[]{:S(2)}, u32[]{:S(2)}) collective-permute-start(bf16[64,512]{1,0:T(8,128)(2,1)S(1)} %get-tuple-element.43), channel_id=1, source_target_pairs={{0,12},{4,8},{8,4},{12,0},{1,13},{5,9},{9,5},{13,1},{2,14},{6,10},... | collective-permute-start | bytes 196616 | tf_op jit(solution)/shard_map/ppermute | solution.py:367
  14.9 0.0 collective-permute-done.1.refs_2_
  14.9 0.2 plane_sums_near.1
  15.1 0.3 collective-permute-start.4
  15.4 0.9 %copy-done.1 = bf16[4,2,256,32]{2,3,1,0:T(8,128)(2,1)S(1)} copy-done((bf16[4,2,256,32]{2,3,1,0:T(8,128)(2,1)S(1)}, bf16[4,2,256,32]{2,3,1,0:T(8,128)(2,1)}, u32[]{:S(2)}) %copy-start.1) | copy-done | bytes 131096
  16.3 0.7 %copy-done.4 = s32[1024]{0:T(1024)S(1)} copy-done((s32[1024]{0:T(1024)S(1)}, s32[1024]{0:T(1024)}, u32[]{:S(2)}) %copy-start.4) | copy-done | bytes 4120
  17.0 0.7 %copy-done.6 = s32[32,1]{0,1:T(1,128)S(1)} copy-done((s32[32,1]{0,1:T(1,128)S(1)}, s32[32,1]{0,1:T(1,128)}, u32[]{:S(2)}) %copy-start.6) | copy-done | bytes 152
  17.7 1.7 %weight_shares.1 = (f32[32,64]{1,0:T(8,128)S(1)}, f32[32,64]{1,0:T(8,128)S(1)}, bf16[32,512]{1,0:T(8,128)(2,1)S(1)}, bf16[32,512]{1,0:T(8,128)(2,1)S(1)}, bf16[3...) custom-call(bf16[4,2,32,256]{3,2,1,0:T(8,128)(2,1)S(1)} %bitcast.14, s32[1,32]{1,0:T(1,128)S(1)} %bitcast.18, ...), custom_call_target="tpu_custom_call" | custom-call | bytes 8388608 | tf_op jit(solution)/shard_map/weight_shares/pallas_call | solution.py:435
  19.4 0.4 collective-permute-done.9.refs_3_
  19.7 0.4 collective-permute-done.4.refs_1_
  20.1 0.6 %station_filter.1 = (bf16[64,512]{1,0:T(8,128)(2,1)S(1)}, bf16[96,512]{1,0:T(8,128)(2,1)S(1)}, bf16[96,512]{1,0:T(8,128)(2,1)S(1)}, bf16[96,512]{1,0:T(8,128)(2,1)S(1)}) custom-call(f32[16,512]{1,0:T(8,128)S(1)} %get-tuple-element.32.taps_ref, f32[64,512]{1,0:T(8,128)S(1)} %get-tuple-element.38.refs_0_, bf16[64,512]{1,0:T(8,128)(2,1)S(1)} %collective-permute-done.4.refs_1_, ...), custom_call_target="tpu_custom_call" | custom-call | tf_op jit(solution)/shard_map/station_filter/pallas_call | solution.py:450
  20.8 1.1 %collective-permute-start.10 = (bf16[96,512]{1,0:T(8,128)(2,1)S(1)}, bf16[96,512]{1,0:T(8,128)(2,1)S(1)}, u32[]{:S(2)}, u32[]{:S(2)}) collective-permute-start(bf16[96,512]{1,0:T(8,128)(2,1)S(1)} %get-tuple-element.48), channel_id=1, source_target_pairs={{0,4},{4,0},{8,12},{12,8},{1,5},{5,1},{9,13},{13,9},{2,6},{6,2},{1... | collective-permute-start | bytes 294920 | tf_op jit(solution)/shard_map/ppermute | solution.py:367
  21.9 1.7 %collective-permute-start.11 = (bf16[96,512]{1,0:T(8,128)(2,1)S(1)}, bf16[96,512]{1,0:T(8,128)(2,1)S(1)}, u32[]{:S(2)}, u32[]{:S(2)}) collective-permute-start(bf16[96,512]{1,0:T(8,128)(2,1)S(1)} %get-tuple-element.49), channel_id=1, source_target_pairs={{0,8},{4,12},{8,0},{12,4},{1,9},{5,13},{9,1},{13,5},{2,10},{6,14},... | collective-permute-start | bytes 294920 | tf_op jit(solution)/shard_map/ppermute | solution.py:367
  23.5 1.7 %collective-permute-start.12 = (bf16[96,512]{1,0:T(8,128)(2,1)S(1)}, bf16[96,512]{1,0:T(8,128)(2,1)S(1)}, u32[]{:S(2)}, u32[]{:S(2)}) collective-permute-start(bf16[96,512]{1,0:T(8,128)(2,1)S(1)} %get-tuple-element.50), channel_id=1, source_target_pairs={{0,12},{4,8},{8,4},{12,0},{1,13},{5,9},{9,5},{13,1},{2,14},{6,10},... | collective-permute-start | bytes 294920 | tf_op jit(solution)/shard_map/ppermute | solution.py:367
  25.2 0.2 collective-permute-done.10.refs_1_
  25.4 1.6 %collective-permute-start.13 = (bf16[64,512]{1,0:T(8,128)(2,1)S(1)}, bf16[64,512]{1,0:T(8,128)(2,1)S(1)}, u32[]{:S(2)}, u32[]{:S(2)}) collective-permute-start(bf16[64,512]{1,0:T(8,128)(2,1)S(1)} %get-tuple-element.63), channel_id=1, source_target_pairs={{0,2},{2,0},{1,3},{3,1},{4,6},{6,4},{5,7},{7,5},{8,10},{10,8},{9,1... | collective-permute-start | bytes 196616 | tf_op jit(solution)/shard_map/ppermute | solution.py:367
  27.1 0.7 %copy-done.2 = f32[16,16]{1,0:T(8,128)S(1)} copy-done((f32[16,16]{1,0:T(8,128)S(1)}, f32[16,16]{1,0:T(8,128)}, u32[]{:S(2)}) %copy-start.2) | copy-done | bytes 1048
  27.8 1.7 %synthesis_bands.1.refs_7_ = bf16[16,768,256]{2,1,0:T(8,128)(2,1)S(1)} custom-call(f32[16,16]{1,0:T(8,128)S(1)} %copy-done.2), custom_call_target="tpu_custom_call" | custom-call | bytes 16777216 | tf_op jit(solution)/shard_map/synthesis_bands/pallas_call | solution.py:463
  29.5 0.5 %collective-permute-start.15 = (bf16[64,512]{1,0:T(8,128)(2,1)S(1)}, bf16[64,512]{1,0:T(8,128)(2,1)S(1)}, u32[]{:S(2)}, u32[]{:S(2)}) collective-permute-start(bf16[64,512]{1,0:T(8,128)(2,1)S(1)} %get-tuple-element.47), channel_id=1, source_target_pairs={{0,2},{2,0},{1,3},{3,1},{4,6},{6,4},{5,7},{7,5},{8,10},{10,8},{9,1... | collective-permute-start | bytes 196616 | tf_op jit(solution)/shard_map/ppermute | solution.py:367
  30.0 1.0 %collective-permute-done.11.refs_2_ = bf16[96,512]{1,0:T(8,128)(2,1)S(1)} collective-permute-done((bf16[96,512]{1,0:T(8,128)(2,1)S(1)}, bf16[96,512]{1,0:T(8,128)(2,1)S(1)}, u32[]{:S(2)}, u32[]{:S(2)}) %collective-permute-start.11) | collective-permute-done | bytes 98336 | tf_op jit(solution)/shard_map/ppermute | solution.py:367
  31.1 2.0 %collective-permute-start.16 = (bf16[2,64,512]{2,1,0:T(8,128)(2,1)S(1)}, bf16[2,64,512]{2,1,0:T(8,128)(2,1)S(1)}, u32[]{:S(2)}, u32[]{:S(2)}) collective-permute-start(bf16[2,64,512]{2,1,0:T(8,128)(2,1)S(1)} %pad_maximum_fusion.2), channel_id=1, source_target_pairs={{0,2},{2,0},{1,3},{3,1},{4,6},{6,4},{5,7},{7,5},{8,10},{10,8},{9,1... | collective-permute-start | bytes 393224 | tf_op jit(solution)/shard_map/ppermute | solution.py:367
  33.1 0.1 collective-permute-start.14
  33.2 0.6 %collective-permute-done.15 = bf16[64,512]{1,0:T(8,128)(2,1)S(1)} collective-permute-done((bf16[64,512]{1,0:T(8,128)(2,1)S(1)}, bf16[64,512]{1,0:T(8,128)(2,1)S(1)}, u32[]{:S(2)}, u32[]{:S(2)}) %collective-permute-start.15) | collective-permute-done | bytes 65568 | tf_op jit(solution)/shard_map/ppermute | solution.py:367
  33.8 0.1 collective-permute-start.17
  33.9 0.8 %weight_matrix.1.m_ref.refs_6_ = bf16[16,128,1024]{2,1,0:T(8,128)(2,1)S(1)} custom-call(f32[32,64]{1,0:T(8,128)S(1)} %get-tuple-element.54.chosen_ref, f32[32,64]{1,0:T(8,128)S(1)} %get-tuple-element.55.scale_ref, bf16[32,512]{1,0:T(8,128)(2,1)S(1)} %get-tuple-element.56.refs_0_, bf16[96,512]{1,0:T(8,128)(2,1)S(1)} %collective-permute-done.10.refs_1_, ...), custom_call_target="tpu_custom_call" | custom-call | bytes 8388608 | tf_op jit(solution)/shard_map/weight_matrix/pallas_call | solution.py:475
  34.7 0.7 %own_beams.1.refs_3_ = f32[16,128,512]{2,1,0:T(8,128)S(1)} custom-call(bf16[16,128,1024]{2,1,0:T(8,128)(2,1)S(1)} %weight_matrix.1.m_ref.refs_6_, bf16[4,64,512]{2,1,0:T(8,128)(2,1)S(1)} %pad_maximum_fusion.refs_0_), custom_call_target="tpu_custom_call" | custom-call | bytes 8388608 | tf_op jit(solution)/shard_map/own_beams/pallas_call | solution.py:487
  35.5 0.7 %collective-permute-done.16.refs_2_.refs_3_ = bf16[2,64,512]{2,1,0:T(8,128)(2,1)S(1)} collective-permute-done((bf16[2,64,512]{2,1,0:T(8,128)(2,1)S(1)}, bf16[2,64,512]{2,1,0:T(8,128)(2,1)S(1)}, u32[]{:S(2)}, u32[]{:S(2)}) %collective-permute-start.16) | collective-permute-done | bytes 131104 | tf_op jit(solution)/shard_map/ppermute | solution.py:367
  36.2 1.3 %near_beams.1.refs_8_ = f32[16,128,512]{2,1,0:T(8,128)S(1)} custom-call(bf16[16,128,1024]{2,1,0:T(8,128)(2,1)S(1)} %weight_matrix.1.m_ref.refs_6_, bf16[4,64,512]{2,1,0:T(8,128)(2,1)S(1)} %collective-permute-done.14.refs_0_.refs_1_, bf16[2,64,512]{2,1,0:T(8,128)(2,1)S(1)} %pad_maximum_fusion.1.refs_1_.refs_2_, ...), custom_call_target="tpu_custom_call" | custom-call | bytes 8388608 | tf_op jit(solution)/shard_map/near_beams/pallas_call | solution.py:487
  37.5 0.0 collective-permute-done.18.refs_5_
  37.5 4.0 %beams_and_series.1 = (f32[128,2,8,512]{3,2,1,0:T(8,128)}, f32[4,2,8,32]{3,2,1,0:T(8,128)}) custom-call(bf16[4,64,512]{2,1,0:T(8,128)(2,1)S(1)} %pad_maximum_fusion.refs_0_, bf16[4,64,512]{2,1,0:T(8,128)(2,1)S(1)} %collective-permute-done.14.refs_0_.refs_1_, bf16[2,64,512]{2,1,0:T(8,128)(2,1)S(1)} %pad_maximum_fusion.1.refs_1_.refs_2_, ...), custom_call_target="tpu_custom_call" | custom-call | tf_op jit(solution)/shard_map/beams_and_series/pallas_call | solution.py:344
  (20 shorter events, 0.1 us)
Async XLA Ops:
  0.6 1.0 %copy-start = (bf16[16,2,16,512]{3,2,1,0:T(8,128)(2,1)S(1)}, bf16[16,2,16,512]{3,2,1,0:T(8,128)(2,1)}, u32[]{:S(2)}) copy-start(bf16[16,2,16,512]{3,2,1,0:T(8,128)(2,1)} %x_ref.1) | copy-start | bytes 1572868
  2.2 3.6 %collective-permute-start.6 = (bf16[2,32,512]{2,1,0:T(8,128)(2,1)S(1)}, bf16[2,32,512]{2,1,0:T(8,128)(2,1)S(1)}, u32[]{:S(2)}, u32[]{:S(2)}) collective-permute-start(bf16[2,32,512]{2,1,0:T(8,128)(2,1)S(1)} %get-tuple-element.41), channel_id=1, source_target_pairs={{0,1},{1,0},{2,3},{3,2},{4,5},{5,4},{6,7},{7,6},{8,9},{9,8},{10,11... | collective-permute-start | bytes 196616 | tf_op jit(solution)/shard_map/ppermute | solution.py:367
  2.7 8.0 %collective-permute-start = (bf16[4,32,512]{2,1,0:T(8,128)(2,1)S(1)}, bf16[4,32,512]{2,1,0:T(8,128)(2,1)S(1)}, u32[]{:S(2)}, u32[]{:S(2)}) collective-permute-start(bf16[4,32,512]{2,1,0:T(8,128)(2,1)S(1)} %get-tuple-element.35), channel_id=1, source_target_pairs={{0,1},{1,0},{2,3},{3,2},{4,5},{5,4},{6,7},{7,6},{8,9},{9,8},{10,11... | collective-permute-start | bytes 393224 | tf_op jit(solution)/shard_map/ppermute | solution.py:367
  2.8 5.0 %collective-permute-start.2 = (bf16[2,32,512]{2,1,0:T(8,128)(2,1)S(1)}, bf16[2,32,512]{2,1,0:T(8,128)(2,1)S(1)}, u32[]{:S(2)}, u32[]{:S(2)}) collective-permute-start(bf16[2,32,512]{2,1,0:T(8,128)(2,1)S(1)} %get-tuple-element.37), channel_id=1, source_target_pairs={{0,1},{1,0},{2,3},{3,2},{4,5},{5,4},{6,7},{7,6},{8,9},{9,8},{10,11... | collective-permute-start | bytes 196616 | tf_op jit(solution)/shard_map/ppermute | solution.py:367
  3.2 6.8 %collective-permute-start.5 = (bf16[2,32,512]{2,1,0:T(8,128)(2,1)S(1)}, bf16[2,32,512]{2,1,0:T(8,128)(2,1)S(1)}, u32[]{:S(2)}, u32[]{:S(2)}) collective-permute-start(bf16[2,32,512]{2,1,0:T(8,128)(2,1)S(1)} %get-tuple-element.40), channel_id=1, source_target_pairs={{0,2},{2,0},{1,3},{3,1},{4,6},{6,4},{5,7},{7,5},{8,10},{10,8},{9,1... | collective-permute-start | bytes 196616 | tf_op jit(solution)/shard_map/ppermute | solution.py:367
  5.8 4.9 %collective-permute-start.7 = (bf16[2,32,512]{2,1,0:T(8,128)(2,1)S(1)}, bf16[2,32,512]{2,1,0:T(8,128)(2,1)S(1)}, u32[]{:S(2)}, u32[]{:S(2)}) collective-permute-start(bf16[2,32,512]{2,1,0:T(8,128)(2,1)S(1)} %collective-permute-done.6), channel_id=1, source_target_pairs={{0,2},{2,0},{1,3},{3,1},{4,6},{6,4},{5,7},{7,5},{8,10},{10,8},{9,1... | collective-permute-start | bytes 196616 | tf_op jit(solution)/shard_map/ppermute | solution.py:367
  6.5 8.5 %collective-permute-start.1 = (bf16[2,32,512]{2,1,0:T(8,128)(2,1)S(1)}, bf16[2,32,512]{2,1,0:T(8,128)(2,1)S(1)}, u32[]{:S(2)}, u32[]{:S(2)}) collective-permute-start(bf16[2,32,512]{2,1,0:T(8,128)(2,1)S(1)} %get-tuple-element.36), channel_id=1, source_target_pairs={{0,2},{2,0},{1,3},{3,1},{4,6},{6,4},{5,7},{7,5},{8,10},{10,8},{9,1... | collective-permute-start | bytes 196616 | tf_op jit(solution)/shard_map/ppermute | solution.py:367
  7.8 7.1 %collective-permute-start.3 = (bf16[2,32,512]{2,1,0:T(8,128)(2,1)S(1)}, bf16[2,32,512]{2,1,0:T(8,128)(2,1)S(1)}, u32[]{:S(2)}, u32[]{:S(2)}) collective-permute-start(bf16[2,32,512]{2,1,0:T(8,128)(2,1)S(1)} %collective-permute-done.2), channel_id=1, source_target_pairs={{0,2},{2,0},{1,3},{3,1},{4,6},{6,4},{5,7},{7,5},{8,10},{10,8},{9,1... | collective-permute-start | bytes 196616 | tf_op jit(solution)/shard_map/ppermute | solution.py:367
  8.5 0.7 %copy-start.3 = (f32[16,16]{1,0:T(8,128)S(1)}, f32[16,16]{1,0:T(8,128)}, u32[]{:S(2)}) copy-start(f32[16,16]{1,0:T(8,128)} %taps_ref.2) | copy-start | bytes 3076
  9.2 0.7 %copy-start.5 = (s32[256]{0:T(256)S(1)}, s32[256]{0:T(256)}, u32[]{:S(2)}) copy-start(s32[256]{0:T(256)} %param.10) | copy-start | bytes 3076
  10.9 8.4 %collective-permute-start.8 = (bf16[64,512]{1,0:T(8,128)(2,1)S(1)}, bf16[64,512]{1,0:T(8,128)(2,1)S(1)}, u32[]{:S(2)}, u32[]{:S(2)}) collective-permute-start(bf16[64,512]{1,0:T(8,128)(2,1)S(1)} %get-tuple-element.42), channel_id=1, source_target_pairs={{0,8},{4,12},{8,0},{12,4},{1,9},{5,13},{9,1},{13,5},{2,10},{6,14},... | collective-permute-start | bytes 196616 | tf_op jit(solution)/shard_map/ppermute | solution.py:367
  13.6 6.2 %collective-permute-start.9 = (bf16[64,512]{1,0:T(8,128)(2,1)S(1)}, bf16[64,512]{1,0:T(8,128)(2,1)S(1)}, u32[]{:S(2)}, u32[]{:S(2)}) collective-permute-start(bf16[64,512]{1,0:T(8,128)(2,1)S(1)} %get-tuple-element.43), channel_id=1, source_target_pairs={{0,12},{4,8},{8,4},{12,0},{1,13},{5,9},{9,5},{13,1},{2,14},{6,10},... | collective-permute-start | bytes 196616 | tf_op jit(solution)/shard_map/ppermute | solution.py:367
  15.1 5.0 %collective-permute-start.4 = (bf16[64,512]{1,0:T(8,128)(2,1)S(1)}, bf16[64,512]{1,0:T(8,128)(2,1)S(1)}, u32[]{:S(2)}, u32[]{:S(2)}) collective-permute-start(bf16[64,512]{1,0:T(8,128)(2,1)S(1)} %get-tuple-element.39), channel_id=1, source_target_pairs={{0,4},{4,0},{8,12},{12,8},{1,5},{5,1},{9,13},{13,9},{2,6},{6,2},{1... | collective-permute-start | bytes 196616 | tf_op jit(solution)/shard_map/ppermute | solution.py:367
  15.4 0.9 %copy-start.1 = (bf16[4,2,256,32]{2,3,1,0:T(8,128)(2,1)S(1)}, bf16[4,2,256,32]{2,3,1,0:T(8,128)(2,1)}, u32[]{:S(2)}) copy-start(bf16[4,2,256,32]{2,3,1,0:T(8,128)(2,1)} %param.13) | copy-start | bytes 393220
  16.3 0.7 %copy-start.4 = (s32[1024]{0:T(1024)S(1)}, s32[1024]{0:T(1024)}, u32[]{:S(2)}) copy-start(s32[1024]{0:T(1024)} %param.12) | copy-start | bytes 12292
  17.0 0.7 %copy-start.6 = (s32[32,1]{0,1:T(1,128)S(1)}, s32[32,1]{0,1:T(1,128)}, u32[]{:S(2)}) copy-start(s32[32,1]{0,1:T(1,128)} %param.11) | copy-start | bytes 388
  20.8 4.7 %collective-permute-start.10 = (bf16[96,512]{1,0:T(8,128)(2,1)S(1)}, bf16[96,512]{1,0:T(8,128)(2,1)S(1)}, u32[]{:S(2)}, u32[]{:S(2)}) collective-permute-start(bf16[96,512]{1,0:T(8,128)(2,1)S(1)} %get-tuple-element.48), channel_id=1, source_target_pairs={{0,4},{4,0},{8,12},{12,8},{1,5},{5,1},{9,13},{13,9},{2,6},{6,2},{1... | collective-permute-start | bytes 294920 | tf_op jit(solution)/shard_map/ppermute | solution.py:367
  21.9 9.2 %collective-permute-start.11 = (bf16[96,512]{1,0:T(8,128)(2,1)S(1)}, bf16[96,512]{1,0:T(8,128)(2,1)S(1)}, u32[]{:S(2)}, u32[]{:S(2)}) collective-permute-start(bf16[96,512]{1,0:T(8,128)(2,1)S(1)} %get-tuple-element.49), channel_id=1, source_target_pairs={{0,8},{4,12},{8,0},{12,4},{1,9},{5,13},{9,1},{13,5},{2,10},{6,14},... | collective-permute-start | bytes 294920 | tf_op jit(solution)/shard_map/ppermute | solution.py:367
  23.5 7.5 %collective-permute-start.12 = (bf16[96,512]{1,0:T(8,128)(2,1)S(1)}, bf16[96,512]{1,0:T(8,128)(2,1)S(1)}, u32[]{:S(2)}, u32[]{:S(2)}) collective-permute-start(bf16[96,512]{1,0:T(8,128)(2,1)S(1)} %get-tuple-element.50), channel_id=1, source_target_pairs={{0,12},{4,8},{8,4},{12,0},{1,13},{5,9},{9,5},{13,1},{2,14},{6,10},... | collective-permute-start | bytes 294920 | tf_op jit(solution)/shard_map/ppermute | solution.py:367
  25.4 5.6 %collective-permute-start.13 = (bf16[64,512]{1,0:T(8,128)(2,1)S(1)}, bf16[64,512]{1,0:T(8,128)(2,1)S(1)}, u32[]{:S(2)}, u32[]{:S(2)}) collective-permute-start(bf16[64,512]{1,0:T(8,128)(2,1)S(1)} %get-tuple-element.63), channel_id=1, source_target_pairs={{0,2},{2,0},{1,3},{3,1},{4,6},{6,4},{5,7},{7,5},{8,10},{10,8},{9,1... | collective-permute-start | bytes 196616 | tf_op jit(solution)/shard_map/ppermute | solution.py:367
  27.1 0.7 %copy-start.2 = (f32[16,16]{1,0:T(8,128)S(1)}, f32[16,16]{1,0:T(8,128)}, u32[]{:S(2)}) copy-start(f32[16,16]{1,0:T(8,128)} %taps_ref.3) | copy-start | bytes 3076
  29.5 4.3 %collective-permute-start.15 = (bf16[64,512]{1,0:T(8,128)(2,1)S(1)}, bf16[64,512]{1,0:T(8,128)(2,1)S(1)}, u32[]{:S(2)}, u32[]{:S(2)}) collective-permute-start(bf16[64,512]{1,0:T(8,128)(2,1)S(1)} %get-tuple-element.47), channel_id=1, source_target_pairs={{0,2},{2,0},{1,3},{3,1},{4,6},{6,4},{5,7},{7,5},{8,10},{10,8},{9,1... | collective-permute-start | bytes 196616 | tf_op jit(solution)/shard_map/ppermute | solution.py:367
  31.1 5.0 %collective-permute-start.16 = (bf16[2,64,512]{2,1,0:T(8,128)(2,1)S(1)}, bf16[2,64,512]{2,1,0:T(8,128)(2,1)S(1)}, u32[]{:S(2)}, u32[]{:S(2)}) collective-permute-start(bf16[2,64,512]{2,1,0:T(8,128)(2,1)S(1)} %pad_maximum_fusion.2), channel_id=1, source_target_pairs={{0,2},{2,0},{1,3},{3,1},{4,6},{6,4},{5,7},{7,5},{8,10},{10,8},{9,1... | collective-permute-start | bytes 393224 | tf_op jit(solution)/shard_map/ppermute | solution.py:367
  33.1 3.0 %collective-permute-start.14 = (bf16[4,64,512]{2,1,0:T(8,128)(2,1)S(1)}, bf16[4,64,512]{2,1,0:T(8,128)(2,1)S(1)}, u32[]{:S(2)}, u32[]{:S(2)}) collective-permute-start(bf16[4,64,512]{2,1,0:T(8,128)(2,1)S(1)} %pad_maximum_fusion.refs_0_), channel_id=1, source_target_pairs={{0,1},{1,0},{2,3},{3,2},{4,5},{5,4},{6,7},{7,6},{8,9},{9,8},{10,11... | collective-permute-start | bytes 786440 | tf_op jit(solution)/shard_map/ppermute | solution.py:367
  33.8 3.7 %collective-permute-start.17 = (bf16[2,64,512]{2,1,0:T(8,128)(2,1)S(1)}, bf16[2,64,512]{2,1,0:T(8,128)(2,1)S(1)}, u32[]{:S(2)}, u32[]{:S(2)}) collective-permute-start(bf16[2,64,512]{2,1,0:T(8,128)(2,1)S(1)} %pad_maximum_fusion.1.refs_1_.refs_2_), channel_id=1, source_target_pairs={{0,1},{1,0},{2,3},{3,2},{4,5},{5,4},{6,7},{7,6},{8,9},{9,8},{10,11... | collective-permute-start | bytes 393224 | tf_op jit(solution)/shard_map/ppermute | solution.py:367
  36.2 1.3 %collective-permute-start.18 = (bf16[2,64,512]{2,1,0:T(8,128)(2,1)S(1)}, bf16[2,64,512]{2,1,0:T(8,128)(2,1)S(1)}, u32[]{:S(2)}, u32[]{:S(2)}) collective-permute-start(bf16[2,64,512]{2,1,0:T(8,128)(2,1)S(1)} %collective-permute-done.16.refs_2_.refs_3_), channel_id=1, source_target_pairs={{0,1},{1,0},{2,3},{3,2},{4,5},{5,4},{6,7},{7,6},{8,9},{9,8},{10,11... | collective-permute-start | bytes 393224 | tf_op jit(solution)/shard_map/ppermute | solution.py:367
